TPU v7x, 32 devices: a whole 2x2x4 slice. The times are simulated.
32 devices in a mesh: rep: 2 (over x), dp: 8 (over z, core), tensor: 2 (over y).
Axes of the slice: x: 2, y: 2, z: 4, core: 2. Of those that a mesh axis runs over, the one named last changes fastest.
Arguments:
- tokens: bfloat16 [16, 1024, 1536], P(('rep', 'dp'), 'tensor'), may hold values from -6 to 6
- norm_gain: float32 [1536], replicated, may hold values from 0.25 to 1.75
- w_query: bfloat16 [1536, 1536], P(None, 'tensor'), may hold values from -0.15625 to 0.15625
- w_keyval: bfloat16 [1536, 512], replicated, may hold values from -0.15625 to 0.15625
- w_out: bfloat16 [1536, 1536], P('tensor'), may hold values from -0.15625 to 0.15625
- kv_pages: bfloat16 [128, 128, 512], P(('rep', 'dp'), 'tensor')
- page_table: int32 [16, 8], P(('rep', 'dp')), may hold values from 0 to 127, as said below
- lengths: int32 [16], P(('rep', 'dp')), may hold values from 1 to 1024, as said below
- starts: int32 [16], P(('rep', 'dp')), may hold values from 1024 to 3968, as said below
Outputs:
- attended: bfloat16 [16, 1024, 1536], P(('rep', 'dp'), 'tensor')
Inputs may be any that keep to these rules, and one draw needn't show every extreme that they name: `page_table`: all 8 pages of a group lie on one replica: its own, or the other one for some groups. Page q is held by the group q // 8 (counted over rep, then dp), whose dp index is within 3 of the group's own, cyclically. `lengths`: some group is full in every draw. `starts`: multiples of 128.
All inputs are finite; a program needn't handle non-finite values.
Results may differ from a plain program's by a relative error of at most 0.034.
Values may be sent and summed in bfloat16 or wider, within the bound.
No kernel may reach another device: no remote copies, remote signals or barrier semaphores. Data moves between devices by JAX's collectives and lax.ppermute only.
A program may use at most 128 MiB of HBM per device.

v0:
```python
import math

import jax
import jax.numpy as jnp
from jax import lax
from jax.sharding import PartitionSpec as P


def rotate_pairs(values, positions, columns_from, head_size):
    rows, cols = values.shape
    column = columns_from + jnp.arange(cols // 2, dtype=jnp.int32) * 2
    within = (column % head_size).astype(jnp.float32)
    inv_freq = jnp.exp(within * (-math.log(10000.0) / head_size))
    angle = positions[:, None] * inv_freq[None, :]
    cosine = jnp.cos(angle)
    sine = jnp.sin(angle)
    pairs = values.reshape(rows, cols // 2, 2)
    first = pairs[:, :, 0]
    second = pairs[:, :, 1]
    turned = jnp.stack([first * cosine - second * sine, first * sine + second * cosine], axis=-1)
    return turned.reshape(rows, cols)


def attend(query, keys, values, first_row, heads, head_size, window):
    rows = query.shape[0]
    count = keys.shape[0]
    q_heads = query.reshape(rows, heads, head_size)
    scores = jnp.einsum("rhd,kd->hrk", q_heads, keys, preferred_element_type=jnp.float32) * (
        1.0 / math.sqrt(head_size)
    )
    row_ids = first_row + jnp.arange(rows, dtype=jnp.int32)
    key_ids = jnp.arange(count, dtype=jnp.int32)
    seen = (key_ids[None, :] >= row_ids[:, None] + 1) & (
        key_ids[None, :] <= row_ids[:, None] + window
    )
    scores = jnp.where(seen[None, :, :], scores, -1e30)
    top = jnp.max(scores, axis=-1, keepdims=True)
    expd = jnp.exp(scores - top)
    total = jnp.sum(expd, axis=-1, keepdims=True)
    probs = (expd / total).astype(jnp.bfloat16)
    mixed = jnp.einsum("hrk,kd->rhd", probs, values, preferred_element_type=jnp.float32)
    return mixed.reshape(rows, heads * head_size).astype(jnp.bfloat16)


def shards(tokens, norm_gain, w_query, w_keyval, w_out, kv_pages, page_table, lengths, starts):
    width = tokens.shape[2]
    head_size = w_keyval.shape[1] // 2
    heads = width // head_size
    part = lax.axis_index("tensor")
    local_rows = tokens.shape[1]
    q_cols = w_query.shape[1]
    start = starts[0]
    length = lengths[0]
    xf = tokens[0].astype(jnp.float32)
    scale = lax.rsqrt(jnp.mean(xf * xf, axis=-1, keepdims=True) + 1e-06)
    normed = (xf * scale * norm_gain).astype(jnp.bfloat16)
    piece = lax.all_gather(normed, "tensor", axis=0, tiled=True)
    positions = (start + jnp.arange(piece.shape[0], dtype=jnp.int32)).astype(jnp.float32)
    query = rotate_pairs(
        jnp.dot(piece, w_query, preferred_element_type=jnp.float32),
        positions,
        part * q_cols,
        head_size,
    )
    keyval = jnp.dot(piece, w_keyval, preferred_element_type=jnp.float32)
    new_keys = rotate_pairs(keyval[:, :head_size], positions, 0, head_size)
    projected = jnp.concatenate([query, new_keys, keyval[:, head_size:]], axis=1).astype(
        jnp.bfloat16
    )
    query_cols = projected[:, :q_cols]
    keys_new = projected[:, q_cols : q_cols + head_size]
    values_new = projected[:, q_cols + head_size :]
    query = lax.all_to_all(query_cols, "tensor", split_axis=0, concat_axis=1, tiled=True)
    table = page_table[0]
    piece = lax.all_gather(kv_pages, ("rep", "dp"), axis=0, tiled=True)
    ident = jnp.arange(piece.shape[0], dtype=jnp.int32)
    onehot = (table[:, None] == ident[None, :]).astype(jnp.bfloat16)
    picked = jnp.einsum("cn,nrk->crk", onehot, piece, preferred_element_type=jnp.float32)
    window_pages = lax.all_gather(picked.astype(jnp.bfloat16), "tensor", axis=1, tiled=True)
    cached = window_pages.reshape(-1, 2 * head_size)
    window = cached.shape[0]
    keys = jnp.concatenate([cached[:, :head_size], keys_new], axis=0)
    values = jnp.concatenate([cached[:, head_size:], values_new], axis=0)
    mixed = attend(query, keys, values, part * local_rows, heads, head_size, window)
    mixed_cols = lax.all_to_all(mixed, "tensor", split_axis=1, concat_axis=0, tiled=True)
    summed = lax.psum_scatter(
        jnp.dot(mixed_cols, w_out, preferred_element_type=jnp.float32).astype(jnp.bfloat16),
        "tensor",
        scatter_dimension=0,
        tiled=True,
    ).astype(jnp.float32)
    live = part * local_rows + jnp.arange(local_rows, dtype=jnp.int32) < length
    return jnp.where(live[:, None], summed, 0.0).astype(jnp.bfloat16)[None]


def solution(mesh):
    placed = (
        P(("rep", "dp"), "tensor", None),
        P(),
        P(None, "tensor"),
        P(),
        P("tensor", None),
        P(("rep", "dp"), "tensor", None),
        P(("rep", "dp"), None),
        P(("rep", "dp")),
        P(("rep", "dp")),
    )
    return jax.shard_map(
        shards,
        mesh=mesh,
        in_specs=placed,
        out_specs=P(("rep", "dp"), "tensor", None),
        check_vma=False,
    )
```

profile of v0, /device:TPU:0, one launch (start us, length us, event | category | flops | bytes accessed | tf_op | source)
XLA Modules:
  0.0 299.3 jit_solution(13291527561778015199)
XLA Ops:
  6.5 0.0 copy-start
  6.5 0.0 all-gather.8.cloned.1.call-start
  6.5 0.0 copy-start.1
  6.5 1.9 fusion.7
  8.5 0.1 copy-done.1
  8.6 0.0 copy-start.3
  8.6 2.3 fusion.9
  10.9 0.0 all-gather.8.cloned.1.call-update
  10.9 0.0 all-gather.4.cloned.1.call-start
  11.0 0.0 copy-done.3
  11.0 1.1 copy.46
  12.1 0.0 all-gather.4.cloned.1.call-update
  12.1 0.0 all-gather.6.cloned.1.call-start
  12.9 2.1 fusion.6
  15.0 43.7 %all-gather.8.cloned.1.call-done = bf16[1024,1536]{1,0:T(8,128)(2,1)} async-done(((bf16[512,1536]{1,0:T(8,128)(2,1)}), bf16[1024,1536]{1,0:T(8,128)(2,1)}) %all-gather.8.cloned.1.call-update) | async-done | bytes 3145744 | tf_op jit(solution)/shard_map/all_gather | solution.py:57
  58.7 6.9 %fusion.59 = f32[1024,768]{0,1:T(8,128)} fusion(bf16[1024,1536]{1,0:T(8,128)(2,1)} %all-gather.8.cloned.1.call-done, bf16[1536,768]{1,0:T(8,128)(2,1)} %param.11), kind=kOutput, calls=%fused_computation.84 | convolution fusion | flops 2415919104 | bytes 8650752 | tf_op jit(solution)/shard_map/dot_general | solution.py:60
  65.6 5.3 %reshape.318 = f32[1024,384,2]{0,2,1:T(2,128)} reshape(f32[1024,768]{0,1:T(8,128)} %fusion.59) | data formatting | bytes 6291456 | tf_op jit(solution)/shard_map/reshape | solution.py:17
  71.0 7.3 %fusion.54 = (f32[1024,384,1]{0,2,1:T(1,128)}, f32[1024,384,1]{0,2,1:T(1,128)}) fusion(f32[1024,384,2]{0,2,1:T(2,128)} %reshape.318), kind=kLoop, calls=%fused_computation.79 | loop fusion | bytes 6291456 | tf_op jit(solution)/shard_map/slice | solution.py:19
  78.3 4.9 %copy.66 = f32[1024,384,1]{1,0,2:T(8,128)} copy(f32[1024,384,1]{0,2,1:T(1,128)} %get-tuple-element.7) | data formatting | bytes 3145728
  83.1 4.2 %fusion.58 = f32[1024,512]{0,1:T(8,128)S(1)} fusion(bf16[1024,1536]{1,0:T(8,128)(2,1)} %all-gather.8.cloned.1.call-done, bf16[1536,512]{1,0:T(8,128)(2,1)} %param.12), kind=kOutput, calls=%fused_computation.83 | convolution fusion | flops 1610612736 | bytes 6815744 | tf_op jit(solution)/shard_map/dot_general | solution.py:65
  87.4 0.0 copy-start.2
  87.4 1.4 copy-done.2
  88.7 1.0 slice.39
  89.8 1.8 reshape.316
  91.6 0.0 copy-start.5
  91.6 4.8 %copy.65 = f32[1024,384,1]{1,0,2:T(8,128)} copy(f32[1024,384,1]{0,2,1:T(1,128)} %get-tuple-element.8) | data formatting | bytes 3145728
  96.5 42.5 %all-gather.4.cloned.1.call-done = bf16[128,64,512]{2,0,1:T(8,128)(2,1)} async-done(((bf16[8,64,512]{2,0,1:T(8,128)(2,1)}), bf16[128,64,512]{2,0,1:T(8,128)(2,1)}) %all-gather.4.cloned.1.call-update) | async-done | bytes 8388624 | tf_op jit(solution)/shard_map/all_gather | solution.py:75
  138.9 0.0 copy-done.5
  138.9 5.4 %convolution_convert_fusion.1 = bf16[8,64,512]{2,0,1:T(8,128)(2,1)} fusion(bf16[128,64,512]{2,0,1:T(8,128)(2,1)} %all-gather.4.cloned.1.call-done, s32[8]{0:T(128)S(1)} %bitcast.70), kind=kOutput, calls=%fused_computation.33 | convolution fusion | flops 67372032 | bytes 8912928 | tf_op jit(solution)/shard_map/cn,nrk->crk/dot_general | solution.py:78
  144.4 0.0 all-gather.6.cloned.1.call-update
  144.4 8.4 %fusion.18 = (bf16[1024,384,1]{1,0,2:T(8,128)(2,1)S(1)}, bf16[1024,384,1]{1,0,2:T(8,128)(2,1)S(1)}) fusion(f32[1024,384,1]{1,0,2:T(8,128)} %copy.66, f32[1024,384,1]{1,0,2:T(8,128)} %copy.65, f32[384]{0:T(512)S(1)} %fusion.38, f32[1024]{0:T(1024)S(1)} %add_convert_fusion), kind=kLoop, calls=%fused_computation.28 | loop fusion | flops 3538944 | bytes 4724224 | tf_op jit(solution)/shard_map/convert.9
  152.8 1.3 pad_maximum_fusion
  154.1 4.9 %copy.55 = bf16[1024,384,2]{0,2,1:T(2,128)(2,1)} copy(bf16[1024,384,2]{1,0,2:T(8,128)(2,1)} %pad_maximum_fusion) | data formatting | bytes 3145728 | tf_op jit(solution)/shard_map/stack | solution.py:20
  159.0 5.7 %all_to_all.24 = bf16[2,512,768]{1,0,2:T(2,128)(2,1)} reshape(bf16[1024,384,2]{0,2,1:T(2,128)(2,1)} %copy.55) | data formatting | bytes 3145728 | tf_op jit(solution)/shard_map/all_to_all | solution.py:73
  164.7 2.8 copy.56
  167.5 4.7 %all-to-all-start = ((bf16[2,512,768]{1,2,0:T(8,128)(2,1)}), bf16[2,512,768]{1,2,0:T(8,128)(2,1)}, u32[]{:S(2)}, u32[]{:S(2)}) async-start(bf16[2,512,768]{1,2,0:T(8,128)(2,1)} %copy.56), calls=%async_computation | async-start | bytes 3145728 | tf_op jit(solution)/shard_map/all_to_all | solution.py:73
  172.2 0.0 reduce-scatter.2.cloned.1.call-start
  172.3 1.8 fusion.56
  174.1 2.1 slice.45
  176.2 1.2 copy.64
  177.4 1.2 copy.63
  178.7 2.4 fusion.30
  181.0 0.1 pad_maximum_fusion.1
  181.1 0.5 copy.51
  181.6 0.2 reshape.317
  181.8 0.2 copy.52
  182.0 0.0 all-gather.6.cloned.1.call-done
  182.0 1.5 copy.47
  183.6 0.9 fusion.55
  184.4 1.0 copy.62
  185.5 6.8 %all-to-all-done = bf16[2,512,768]{1,2,0:T(8,128)(2,1)} async-done(((bf16[2,512,768]{1,2,0:T(8,128)(2,1)}), bf16[2,512,768]{1,2,0:T(8,128)(2,1)}, u32[]{:S(2)}, u32[]{:S(2)}) %all-to-all-start) | async-done | bytes 1572896 | tf_op jit(solution)/shard_map/all_to_all | solution.py:73
  192.2 0.0 copy-start.4
  192.3 14.3 %fusion.57 = (f32[6,512]{1,0:T(8,128)S(1)}, f32[6,512,2048]{1,2,0:T(8,128)}) fusion(pred[512,2048]{0,1:T(8,128)(4,1)} %fusion.6, bf16[512,6,256]{0,2,1:T(8,128)(2,1)} %bitcast.10, bf16[1024,256]{1,0:T(8,128)(2,1)S(1)} %copy.52, bf16[1024,256]{1,0:T(8,128)(2,1)} %get-tuple-element.12), kind=kOutput, calls=%fused_computation.82 | convolution fusion | flops 3248490496 | bytes 28848128 | tf_op jit(solution)/shard_map/sub | solution.py:38
  206.6 0.0 copy-done.4
  206.6 12.9 %fusion.16 = bf16[256,6,512]{2,0,1:T(8,128)(2,1)} fusion(f32[6,512,2048]{1,2,0:T(8,128)} %get-tuple-element.16, f32[6,512]{1,0:T(8,128)S(1)} %get-tuple-element.15, bf16[1024,256]{0,1:T(8,128)(2,1)S(1)} %copy-done.4, bf16[1024,256]{0,1:T(8,128)(2,1)} %copy.62), kind=kOutput, calls=%fused_computation.26 | convolution fusion | flops 3236691968 | bytes 27799552 | tf_op jit(solution)/shard_map/hrk,kd->rhd/dot_general | solution.py:41
  219.5 2.6 copy.59
  222.1 22.7 %all_to_all.32 = bf16[512,2,768]{2,0,1:T(8,128)(2,1)S(1)} all-to-all(bf16[512,2,768]{2,0,1:T(8,128)(2,1)} %copy.59), channel_id=1, replica_groups=mesh['rep'=2,'dp'=8,'tensor'=2] {'tensor'}, dimensions={1} | all-to-all | bytes 3145728 | tf_op jit(solution)/shard_map/all_to_all | solution.py:85
  244.8 0.0 copy-done
  244.9 4.0 %convolution_convert_fusion = bf16[1024,1536]{1,0:T(8,128)(2,1)} fusion(bf16[1024,768]{1,0:T(8,128)(2,1)S(1)} %bitcast.69, bf16[768,1536]{1,0:T(8,128)(2,1)S(1)} %copy-done), kind=kOutput, calls=%fused_computation.14 | convolution fusion | flops 2417491968 | bytes 7077888 | tf_op jit(solution)/shard_map/dot_general | solution.py:87
  248.9 0.0 reduce-scatter.2.cloned.1.call-update
  249.6 40.3 %reduce-scatter.2.cloned.1.call-done = bf16[512,1536]{1,0:T(8,128)(2,1)} async-done(((bf16[1024,1536]{1,0:T(8,128)(2,1)}), bf16[512,1536]{1,0:T(8,128)(2,1)}) %reduce-scatter.2.cloned.1.call-update) | async-done | bytes 1572880 | tf_op jit(solution)/shard_map/reduce_scatter | solution.py:86
  289.9 2.9 fusion.21
  (6 shorter events, 0.1 us)
Async XLA Ops:
  6.5 238.3 %copy-start = (bf16[768,1536]{1,0:T(8,128)(2,1)S(1)}, bf16[768,1536]{1,0:T(8,128)(2,1)}, u32[]{:S(2)}) copy-start(bf16[768,1536]{1,0:T(8,128)(2,1)} %param.13) | copy-start | bytes 7077892
  6.5 52.2 %all-gather.8.cloned.1.call-start = ((), (), s32[]{:S(2)}) async-start(), calls=%async_computation.5 | async-start | bytes 4718592 | tf_op jit(solution)/shard_map/all_gather | solution.py:57
  6.5 2.0 copy-start.1
  8.6 2.4 copy-start.3
  10.9 128.0 %all-gather.4.cloned.1.call-start = ((), (), s32[]{:S(2)}) async-start(), calls=%async_computation.3 | async-start | bytes 8912896 | tf_op jit(solution)/shard_map/all_gather | solution.py:75
  12.1 169.9 %all-gather.6.cloned.1.call-start = ((), (), s32[]{:S(2)}) async-start(), calls=%async_computation.4 | async-start | bytes 1572864 | tf_op jit(solution)/shard_map/all_gather | solution.py:79
  87.4 1.4 copy-start.2
  91.6 47.3 %copy-start.5 = (s32[1,8]{1,0:T(1,128)S(1)}, s32[1,8]{1,0:T(1,128)}, u32[]{:S(2)}) copy-start(s32[1,8]{1,0:T(1,128)} %param.15) | copy-start | bytes 100
  167.5 24.7 %all-to-all-start = ((bf16[2,512,768]{1,2,0:T(8,128)(2,1)}), bf16[2,512,768]{1,2,0:T(8,128)(2,1)}, u32[]{:S(2)}, u32[]{:S(2)}) async-start(bf16[2,512,768]{1,2,0:T(8,128)(2,1)} %copy.56), calls=%async_computation | async-start | bytes 3145728 | tf_op jit(solution)/shard_map/all_to_all | solution.py:73
  172.2 117.7 %reduce-scatter.2.cloned.1.call-start = ((), (), s32[]{:S(2)}) async-start(), calls=%async_computation.6 | async-start | bytes 4718592 | tf_op jit(solution)/shard_map/reduce_scatter | solution.py:86
  192.2 14.3 %copy-start.4 = (bf16[1024,256]{0,1:T(8,128)(2,1)S(1)}, bf16[1024,256]{0,1:T(8,128)(2,1)}, u32[]{:S(2)}) copy-start(bf16[1024,256]{0,1:T(8,128)(2,1)} %slice.45) | copy-start | bytes 1572868
Sparse Core Ops, SparseCore 0:
  11.0 47.6 all-gather.7
  60.8 78.0 all-gather.3
  144.5 19.4 all-gather.5
  249.0 40.8 reduce-scatter.1
where the time goes:
time: 300 us; the launch traced here: 299 us
  waiting for transfers between devices  133 us (44%)
  local copies, waits for them, and re-layouts  54.5 us (18%)
  matrix products  47.8 us (16%)
  blocking collectives  22.7 us (8%)
  other arithmetic  21.4 us (7%)
  between operations  14.6 us (5%)
  starting transfers between devices  4.82 us (2%)
    all_gather x1, waiting for transfers between devices, shards(): piece = lax.all_gather(normed, 'tensor', axis=0, tiled=True)  43.7 us
    all_gather x1, waiting for transfers between devices, shards(): piece = lax.all_gather(kv_pages, ('rep', 'dp'), axis=0, tiled=True)  42.5 us
    reduce_scatter x1, waiting for transfers between devices, shards(): lax.psum_scatter(jnp.dot(mixed_cols, w_out, preferred_element_type=jnp.fl...  40.3 us
    all_to_all x1, blocking collectives, shards(): lax.all_to_all(mixed, 'tensor', split_axis=1, concat_axis=0, tiled=True)  22.7 us
    unnamed x18, local copies, waits for them, and re-layouts  15.8 us
    sub x1, matrix products, attend(): expd = jnp.exp(scores - top)  14.3 us
    dot_general x1, matrix products, attend(): jnp.einsum('hrk,kd->rhd', probs, values, preferred_element_type=jnp.float32)  12.9 us
    another operation x2, other arithmetic  10.8 us
  transfers between devices with their start and end apart: 5, of which 4 were waited for; matrix products, arithmetic and copies ran while one was open for 23% of the time, Pallas kernels for 0%

commit v1 on v0

--- a/solution.py
+++ b/solution.py
@@ -1,9 +1,377 @@
+import functools
 import math
 
 import jax
 import jax.numpy as jnp
 from jax import lax
+from jax.experimental import pallas as pl
+from jax.experimental.pallas import tpu as pltpu
 from jax.sharding import PartitionSpec as P
+
+BF16 = jnp.bfloat16
+F32 = jnp.float32
+MASKED = -1e30
+ANY = pl.ANY
+
+
+def spec(space):
+    return pl.BlockSpec(memory_space=space)
+
+
+def rotation_tables(first, rows, step, head_size):
+    column = jnp.arange(head_size, dtype=jnp.int32)
+    within = (column // 2 * 2).astype(F32)
+    inv_freq = jnp.exp(within * (-math.log(10000.0) / head_size))
+    sign = jnp.where(column % 2 == 0, -1.0, 1.0).astype(F32)
+    coarse = (first + step * jnp.arange(rows // step, dtype=jnp.int32)).astype(F32)
+    fine = jnp.arange(step, dtype=jnp.int32).astype(F32)
+    at = jnp.concatenate([coarse, fine])
+    angle = at[:, None] * inv_freq[None, :]
+    return jnp.cos(angle), jnp.sin(angle) * sign[None, :]
+
+
+def fill_rotation(cos_t, sin_t, cos_s, sin_s, step):
+    blocks = cos_s.shape[0] // step
+    cf = cos_t[blocks:, :]
+    sf = sin_t[blocks:, :]
+    for u in range(blocks):
+        cu = cos_t[u : u + 1, :]
+        su = sin_t[u : u + 1, :]
+        cos_s[u * step : (u + 1) * step, :] = cu * cf - su * sf
+        sin_s[u * step : (u + 1) * step, :] = su * cf + cu * sf
+
+
+def rotate(v, cos, sin, even):
+    width = v.shape[1]
+    swapped = jnp.where(even, pltpu.roll(v, width - 1, 1), pltpu.roll(v, 1, 1))
+    return v * cos + swapped * sin
+
+
+def project_kernel(head_size, step, tok, gain, wq, wkv, cos_t, sin_t, normed, q, kv, cos, sin):
+    rows = tok.shape[0]
+    tile = min(256, rows)
+    fill_rotation(cos_t, sin_t, cos, sin, step)
+    even = lax.broadcasted_iota(jnp.int32, (tile, head_size), 1) % 2 == 0
+    for i in range(rows // tile):
+        at = pl.ds(i * tile, tile)
+        xf = tok[at, :].astype(F32)
+        scale = lax.rsqrt(jnp.mean(xf * xf, axis=-1, keepdims=True) + 1e-06)
+        nb = (xf * scale * gain[...]).astype(BF16)
+        normed[at, :] = nb
+        c = cos[at, :]
+        s = sin[at, :]
+        both = jnp.dot(nb, wkv[...], preferred_element_type=F32)
+        kv[at, :head_size] = rotate(both[:, :head_size], c, s, even).astype(BF16)
+        kv[at, head_size:] = both[:, head_size:].astype(BF16)
+        for h in range(wq.shape[1] // head_size):
+            cols = slice(h * head_size, (h + 1) * head_size)
+            part = jnp.dot(nb, wq[:, cols], preferred_element_type=F32)
+            q[at, cols] = rotate(part, c, s, even).astype(BF16)
+
+
+def project(tok, gain, wq, wkv, cos_t, sin_t, head_size, step):
+    rows, width = tok.shape
+    qc, kc = wq.shape[1], wkv.shape[1]
+    return pl.pallas_call(
+        functools.partial(project_kernel, head_size, step),
+        out_shape=(
+            jax.ShapeDtypeStruct((rows, width), BF16),
+            jax.ShapeDtypeStruct((rows, qc), BF16),
+            jax.ShapeDtypeStruct((rows, kc), BF16),
+            jax.ShapeDtypeStruct((rows, head_size), F32),
+            jax.ShapeDtypeStruct((rows, head_size), F32),
+        ),
+        in_specs=[spec(pltpu.VMEM)] * 6,
+        out_specs=[spec(pltpu.VMEM)] * 5,
+        compiler_params=pltpu.CompilerParams(vmem_limit_bytes=48 * 2**20),
+        cost_estimate=pl.CostEstimate(
+            flops=2 * rows * width * (qc + kc), bytes_accessed=10 * 2**20, transcendentals=0
+        ),
+        name="project_own",
+    )(tok, gain.reshape(1, width), wq, wkv, cos_t, sin_t)
+
+
+def other_kernel(head_size, order, normed, w0, w1, w2, w3, cos, sin, q):
+    rows = normed.shape[0]
+    tile = min(256, rows)
+    deep = w0.shape[0]
+    even = lax.broadcasted_iota(jnp.int32, (tile, head_size), 1) % 2 == 0
+    for i in range(rows // tile):
+        at = pl.ds(i * tile, tile)
+        c = cos[at, :]
+        s = sin[at, :]
+        total = None
+        for n, w in enumerate((w0, w1, w2, w3)):
+            x = normed[at, pl.ds(pl.multiple_of(order[n] * deep, 128), deep)]
+            part = jnp.dot(x, w[...], preferred_element_type=F32)
+            total = part if total is None else total + part
+        for h in range(q.shape[1] // head_size):
+            cols = slice(h * head_size, (h + 1) * head_size)
+            q[at, cols] = rotate(total[:, cols], c, s, even).astype(BF16)
+
+
+def project_other(normed, pieces, order, cos, sin, head_size):
+    rows, width = normed.shape
+    qc = pieces[0].shape[1]
+    return pl.pallas_call(
+        functools.partial(other_kernel, head_size),
+        out_shape=jax.ShapeDtypeStruct((rows, qc), BF16),
+        in_specs=[spec(pltpu.SMEM)] + [spec(pltpu.VMEM)] * 7,
+        out_specs=spec(pltpu.VMEM),
+        compiler_params=pltpu.CompilerParams(vmem_limit_bytes=48 * 2**20),
+        cost_estimate=pl.CostEstimate(
+            flops=2 * rows * width * qc, bytes_accessed=6 * 2**20, transcendentals=0
+        ),
+        name="project_other",
+    )(order, normed, *pieces, cos, sin)
+
+
+def pick_kernel(idx, pool, out, sem):
+    copies = [
+        pltpu.make_async_copy(pool.at[idx[j]], out.at[j], sem.at[j]) for j in range(out.shape[0])
+    ]
+    for c in copies:
+        c.start()
+    for c in copies:
+        c.wait()
+
+
+def pick(pool, idx):
+    count = idx.shape[0]
+    return pl.pallas_call(
+        pick_kernel,
+        out_shape=jax.ShapeDtypeStruct((count,) + pool.shape[1:], pool.dtype),
+        in_specs=[spec(pltpu.SMEM), spec(ANY)],
+        out_specs=spec(ANY),
+        scratch_shapes=[pltpu.SemaphoreType.DMA((count,))],
+        cost_estimate=pl.CostEstimate(flops=0, bytes_accessed=2 * 2**20, transcendentals=0),
+        name="pick_pages",
+    )(idx, pool)
+
+
+def choose_kernel(home, idx, pool, came, out, sem):
+    count = out.shape[0]
+
+    @pl.when(home[0] == 1)
+    def _():
+        for j in range(count):
+            pltpu.make_async_copy(pool.at[idx[j]], out.at[j], sem.at[j]).start()
+
+    @pl.when(home[0] == 0)
+    def _():
+        for j in range(count):
+            pltpu.make_async_copy(came.at[j], out.at[j], sem.at[j]).start()
+
+    for j in range(count):
+        pltpu.make_async_copy(came.at[j], out.at[j], sem.at[j]).wait()
+
+
+def choose(pool, idx, home, came):
+    count = idx.shape[0]
+    return pl.pallas_call(
+        choose_kernel,
+        out_shape=jax.ShapeDtypeStruct(came.shape, came.dtype),
+        in_specs=[spec(pltpu.SMEM), spec(pltpu.SMEM), spec(ANY), spec(ANY)],
+        out_specs=spec(ANY),
+        scratch_shapes=[pltpu.SemaphoreType.DMA((count,))],
+        cost_estimate=pl.CostEstimate(flops=0, bytes_accessed=2 * 2**20, transcendentals=0),
+        name="choose_pages",
+    )(home, idx, pool, came)
+
+
+def attend_kernel(
+    head_size,
+    info,
+    qa,
+    qb,
+    mine,
+    peer,
+    kv_own,
+    kv_peer,
+    woa,
+    w0,
+    w1,
+    w2,
+    w3,
+    out,
+    keys,
+    vals,
+    wa,
+    wb,
+    mix,
+    ksem,
+    vsem,
+    wsem,
+):
+    part = info[0]
+    length = info[1]
+    rows, half = qa.shape
+    pages, prow, _ = mine.shape
+    page = 2 * prow
+    width = out.shape[1]
+    nheads = half // head_size
+    window = pages * page
+    wcols = w0.shape[1]
+
+    def move(which, dst, sem, lo):
+        cols = pl.ds(lo, head_size)
+        got = []
+        here = part == 0
+        for u in range(pages):
+            at0 = u * page
+            at1 = (u - rows // page) * page
+            for src, side in ((mine, part), (peer, 1 - part)):
+                row = pl.multiple_of(side * prow, prow)
+                got.append((True, src.at[u, :, cols], at0, row, prow))
+                if at1 >= 0:
+                    got.append((False, src.at[u, :, cols], at1, row, prow))
+        got.append((True, kv_own.at[:, cols], window, 0, rows))
+        got.append((False, kv_own.at[:, cols], window, 0, rows))
+        got.append((False, kv_peer.at[:, cols], window - rows, 0, rows))
+        return got
+
+    def start(dst, sem, lo):
+        moves = move(None, dst, sem, lo)
+        for case in (True, False):
+
+            @pl.when((part == 0) == case)
+            def _():
+                for which, src, at, row, count in moves:
+                    if which == case:
+                        pltpu.make_async_copy(src, dst.at[pl.ds(at + row, count), :], sem).start()
+
+    def finish(dst, sem, lo):
+        pltpu.make_async_copy(dst, dst, sem).wait()
+
+    start(keys, ksem, 0)
+    start(vals, vsem, head_size)
+    weights = [pltpu.make_async_copy(woa, wa, wsem.at[0])]
+    for n, w in enumerate((w0, w1, w2, w3)):
+        cols = pl.ds(pl.multiple_of(info[2 + n] * wcols, 128), wcols)
+        weights.append(pltpu.make_async_copy(w, wb.at[:, cols], wsem.at[1 + n]))
+    for c in weights:
+        c.start()
+
+    tile = min(256, rows)
+    span = window + tile
+    row_id = lax.broadcasted_iota(jnp.int32, (tile, tile), 0)
+    col_id = lax.broadcasted_iota(jnp.int32, (tile, tile), 1)
+    first_seen = col_id >= row_id + 1
+    last_seen = col_id <= row_id
+    factor = math.log2(math.e) / math.sqrt(head_size)
+    finish(keys, ksem, 0)
+    for i in range(rows // tile):
+        at = pl.ds(i * tile, tile)
+        for n, q in enumerate((qa, qb)):
+            for h in range(nheads):
+                cols = slice(h * head_size, (h + 1) * head_size)
+                kk = keys[pl.ds(i * tile, span), :]
+                s = lax.dot_general(
+                    q[at, cols], kk, (((1,), (1,)), ((), ())), preferred_element_type=F32
+                )
+                s = jnp.concatenate(
+                    [
+                        jnp.where(first_seen, s[:, :tile], MASKED),
+                        s[:, tile : span - tile],
+                        jnp.where(last_seen, s[:, span - tile :], MASKED),
+                    ],
+                    axis=1,
+                )
+                top = jnp.max(s, axis=-1, keepdims=True)
+                e = jnp.exp2((s - top) * factor)
+                total = jnp.sum(e, axis=-1, keepdims=True)
+                if i == 0 and n == 0 and h == 0:
+                    finish(vals, vsem, head_size)
+                vv = vals[pl.ds(i * tile, span), :]
+                m = jnp.dot(e.astype(BF16), vv, preferred_element_type=F32)
+                mix[n, at, cols] = (m / total).astype(BF16)
+    for c in weights:
+        c.wait()
+    for i in range(rows // tile):
+        at = pl.ds(i * tile, tile)
+        row = part * rows + i * tile + lax.broadcasted_iota(jnp.int32, (tile, 1), 0)
+        live = row < length
+        for j in range(width // wcols):
+            cols = slice(j * wcols, (j + 1) * wcols)
+            a = jnp.dot(mix[0, at, :], wa[:, cols], preferred_element_type=F32)
+            b = jnp.dot(mix[1, at, :], wb[:, cols], preferred_element_type=F32)
+            both = a.astype(BF16).astype(F32) + b.astype(BF16).astype(F32)
+            out[at, cols] = jnp.where(live, both, 0.0).astype(BF16)
+
+
+def attend_pages(info, qa, qb, mine, peer, kv_own, kv_peer, woa, pieces, head_size):
+    rows, half = qa.shape
+    width = woa.shape[1]
+    window = mine.shape[0] * mine.shape[1] * 2
+    return pl.pallas_call(
+        functools.partial(attend_kernel, head_size),
+        out_shape=jax.ShapeDtypeStruct((rows, width), BF16),
+        in_specs=[spec(pltpu.SMEM)] + [spec(pltpu.VMEM)] * 2 + [spec(ANY)] * 9,
+        out_specs=spec(pltpu.VMEM),
+        scratch_shapes=[
+            pltpu.VMEM((window + rows, head_size), BF16),
+            pltpu.VMEM((window + rows, head_size), BF16),
+            pltpu.VMEM(woa.shape, BF16),
+            pltpu.VMEM(woa.shape, BF16),
+            pltpu.VMEM((2, rows, half), BF16),
+            pltpu.SemaphoreType.DMA,
+            pltpu.SemaphoreType.DMA,
+            pltpu.SemaphoreType.DMA((5,)),
+        ],
+        compiler_params=pltpu.CompilerParams(vmem_limit_bytes=56 * 2**20),
+        cost_estimate=pl.CostEstimate(
+            flops=4 * rows * 2 * half * (window + 256) + 4 * rows * half * width,
+            bytes_accessed=12 * 2**20,
+            transcendentals=rows * 6 * (window + 256),
+        ),
+        name="attend_and_out",
+    )(info, qa, qb, mine, peer, kv_own, kv_peer, woa, *pieces)
+
+
+def pair_shards(tokens, norm_gain, w_query, w_keyval, w_out, kv_pages, page_table, lengths, starts):
+    head_size = w_keyval.shape[1] // 2
+    part = lax.axis_index("tensor")
+    rep = lax.axis_index("rep")
+    dp = lax.axis_index("dp")
+    ndp = lax.axis_size("dp")
+    core = dp % 2
+    rows = tokens.shape[1]
+    swap = [(0, 1), (1, 0)]
+    cores = [(i, i ^ 1) for i in range(ndp)]
+
+    quarter = rep * 2 + core
+    order = jnp.stack(
+        [quarter, (1 - rep) * 2 + core, rep * 2 + 1 - core, (1 - rep) * 2 + 1 - core]
+    ).astype(jnp.int32)
+
+    def spread(piece):
+        a = lax.ppermute(piece, "tensor", swap)
+        b = lax.ppermute(a, "rep", swap)
+        return a, b, lax.ppermute(a, "dp", cores), lax.ppermute(b, "dp", cores)
+
+    deep = w_query.shape[0] // 4
+    wide = w_out.shape[1] // 4
+    wq_pieces = spread(lax.dynamic_slice_in_dim(w_query, quarter * deep, deep, 0))
+    wo_pieces = spread(lax.dynamic_slice_in_dim(w_out, quarter * wide, wide, 1))
+
+    table = page_table[0]
+    peer_table = lax.ppermute(table, "rep", swap)
+    per_rep = kv_pages.shape[0] * ndp
+    pool = lax.all_gather(kv_pages, "dp", axis=0, tiled=True)
+    came = lax.ppermute(pick(pool, peer_table % per_rep), "rep", swap)
+    home = (table[:1] // per_rep == rep).astype(jnp.int32)
+    mine = choose(pool, table % per_rep, home, came)
+    peer = lax.ppermute(mine, "tensor", swap)
+
+    step = 32
+    cos_t, sin_t = rotation_tables(starts[0] + part * rows, rows, step, head_size)
+    normed, qa, kv_own, cos, sin = project(
+        tokens[0], norm_gain, w_query, w_keyval, cos_t, sin_t, head_size, step
+    )
+    kv_peer = lax.ppermute(kv_own, "tensor", swap)
+    qb = project_other(normed, wq_pieces, order, cos, sin, head_size)
+    info = jnp.concatenate([jnp.stack([part, lengths[0]]).astype(jnp.int32), order])
+    return attend_pages(info, qa, qb, mine, peer, kv_own, kv_peer, w_out, wo_pieces, head_size)[None]
 
 
 def rotate_pairs(values, positions, columns_from, head_size):
@@ -105,8 +473,9 @@
         P(("rep", "dp")),
         P(("rep", "dp")),
     )
+    body = pair_shards if mesh.shape["tensor"] == 2 and mesh.shape["rep"] == 2 else shards
     return jax.shard_map(
-        shards,
+        body,
         mesh=mesh,
         in_specs=placed,
         out_specs=P(("rep", "dp"), "tensor", None),

time: 300 us -> 144 us (0.48)
  waiting for transfers between devices: 133 us -> 47 us
  Pallas kernels: 0 us -> 57.3 us
  matrix products: 47.8 us -> 0 us
  local copies, waits for them, and re-layouts: 54.5 us -> 9.76 us
  blocking collectives: 22.7 us -> 0 us
  other arithmetic: 21.4 us -> 1.53 us
  starting transfers between devices: 4.82 us -> 13.2 us
    all_gather x3 -> x1, waiting for transfers between devices: 86.2 us -> 19 us  [pair_shards(): pool = lax.all_gather(kv_pages, 'dp', axis=0, tiled=True)]
    pallas_call x0 -> x5, Pallas kernels: none -> 57.3 us  [the longest x1 17.8 us: choose(): pl.pallas_call(choose_kernel, out_shape=jax.ShapeDtypeStruct(came.shape,...]
    reduce_scatter x1 -> x0, waiting for transfers between devices: 40.3 us -> none  [shards(): lax.psum_scatter(jnp.dot(mixed_cols, w_out, preferred_element_type=jnp.fl...]
    dot_general x5 -> x0, matrix products: 33.5 us -> none  [the longest x1 12.9 us: attend(): jnp.einsum('hrk,kd->rhd', probs, values, preferred_element_type=jnp.float32)]
    ppermute x0 -> x12, waiting for transfers between devices: none -> 27.3 us  [the longest x2 19.6 us: spread(): a = lax.ppermute(piece, 'tensor', swap)]
    all_to_all x1 -> x0, blocking collectives: 22.7 us -> none  [shards(): lax.all_to_all(mixed, 'tensor', split_axis=1, concat_axis=0, tiled=True)]
    sub x1 -> x0, matrix products: 14.3 us -> none  [attend(): expd = jnp.exp(scores - top)]
    ppermute x0 -> x12, starting transfers between devices: none -> 13.2 us  [the longest x2 3.74 us: spread(): b = lax.ppermute(a, 'rep', swap)]
  transfers between devices with their start and end apart: 5 -> 13, of which waited for: 4 -> 5; matrix products, arithmetic and copies ran while one was open for 23% -> 3% of each run, Pallas kernels for 0% -> 31%
where the time goes in v1:
time: 144 us
  Pallas kernels  57.3 us (40%)
  waiting for transfers between devices  47 us (33%)
  between operations  15 us (10%)
  starting transfers between devices  13.2 us (9%)
  local copies, waits for them, and re-layouts  9.76 us (7%)
  other arithmetic  1.53 us (1%)
    ppermute x2, waiting for transfers between devices, spread(): a = lax.ppermute(piece, 'tensor', swap)  19.6 us
    all_gather x1, waiting for transfers between devices, pair_shards(): pool = lax.all_gather(kv_pages, 'dp', axis=0, tiled=True)  19 us
    pallas_call x1, Pallas kernels, choose(): pl.pallas_call(choose_kernel, out_shape=jax.ShapeDtypeStruct(came.shape,...  17.8 us
    pallas_call x1, Pallas kernels, pick(): pl.pallas_call(pick_kernel, out_shape=jax.ShapeDtypeStruct((count,) + poo...  17.7 us
    pallas_call x1, Pallas kernels, attend_pages(): pl.pallas_call(functools.partial(attend_kernel, head_size), out_shape=jax...  13.4 us
    unnamed x18, local copies, waits for them, and re-layouts  6.85 us
    pallas_call x1, Pallas kernels, project(): pl.pallas_call(functools.partial(project_kernel, head_size, step), out_sh...  4.99 us
    ppermute x1, waiting for transfers between devices, pair_shards(): peer = lax.ppermute(mine, 'tensor', swap)  4.84 us
  transfers between devices with their start and end apart: 13, of which 5 were waited for; matrix products, arithmetic and copies ran while one was open for 3% of the time, Pallas kernels for 31%

profile of v1, /device:TPU:0, one launch (start us, length us, event | category | flops | bytes accessed | tf_op | source)
XLA Modules:
  0.0 143.8 jit_solution(3371769640392555234)
XLA Ops:
  6.5 0.0 copy-start.8
  6.5 0.0 copy-start.7
  6.5 0.0 all-gather.2.cloned.1.call-start
  6.5 0.7 all-gather.2.cloned.1.call-update
  7.3 1.1 constant_dynamic-slice_fusion.1
  8.4 3.0 %collective-permute-start = (bf16[384,768]{1,0:T(8,128)(2,1)S(1)}, bf16[384,768]{1,0:T(8,128)(2,1)S(1)}, u32[]{:S(2)}, u32[]{:S(2)}) collective-permute-start(bf16[384,768]{1,0:T(8,128)(2,1)S(1)} %constant_dynamic-slice_fusion.1), channel_id=1, source_target_pairs={{0,1},{1,0},{2,3},{3,2},{4,5},{5,4},{6,7},{7,6},{8,9},{9,8},{10,11... | collective-permute-start | bytes 1769480 | tf_op jit(solution)/shard_map/ppermute | solution.py:348
  11.4 1.1 constant_dynamic-slice_fusion
  12.6 0.1 collective-permute-start.8
  12.6 0.0 copy-done.8
  12.6 2.0 %collective-permute-start.4 = (s32[8]{0:T(128)S(1)}, s32[8]{0:T(128)S(1)}, u32[]{:S(2)}, u32[]{:S(2)}) collective-permute-start(s32[8]{0:T(128)S(1)} %bitcast.15), channel_id=1, source_target_pairs={{0,16},{16,0},{1,17},{17,1},{2,18},{18,2},{3,19},{19,3},{4,20},{20... | collective-permute-start | bytes 104 | tf_op jit(solution)/shard_map/ppermute | solution.py:358
  15.3 0.6 and_select_fusion.1.idx
  15.9 9.7 %collective-permute-done.w0 = bf16[384,768]{1,0:T(8,128)(2,1)S(1)} collective-permute-done((bf16[384,768]{1,0:T(8,128)(2,1)S(1)}, bf16[384,768]{1,0:T(8,128)(2,1)S(1)}, u32[]{:S(2)}, u32[]{:S(2)}) %collective-permute-start) | collective-permute-done | bytes 589856 | tf_op jit(solution)/shard_map/ppermute | solution.py:348
  25.6 2.0 %collective-permute-start.1 = (bf16[384,768]{1,0:T(8,128)(2,1)S(1)}, bf16[384,768]{1,0:T(8,128)(2,1)S(1)}, u32[]{:S(2)}, u32[]{:S(2)}) collective-permute-start(bf16[384,768]{1,0:T(8,128)(2,1)S(1)} %collective-permute-done.w0), channel_id=1, source_target_pairs={{0,16},{16,0},{1,17},{17,1},{2,18},{18,2},{3,19},{19,3},{4,20},{20... | collective-permute-start | bytes 1769480 | tf_op jit(solution)/shard_map/ppermute | solution.py:349
  27.6 9.9 %collective-permute-done.8.w0 = bf16[768,384]{1,0:T(8,128)(2,1)} collective-permute-done((bf16[768,384]{1,0:T(8,128)(2,1)S(1)}, bf16[768,384]{1,0:T(8,128)(2,1)}, u32[]{:S(2)}, u32[]{:S(2)}) %collective-permute-start.8) | collective-permute-done | bytes 589856 | tf_op jit(solution)/shard_map/ppermute | solution.py:348
  37.5 1.7 %collective-permute-start.9 = (bf16[768,384]{1,0:T(8,128)(2,1)}, bf16[768,384]{1,0:T(8,128)(2,1)}, u32[]{:S(2)}, u32[]{:S(2)}) collective-permute-start(bf16[768,384]{1,0:T(8,128)(2,1)} %collective-permute-done.8.w0), channel_id=1, source_target_pairs={{0,16},{16,0},{1,17},{17,1},{2,18},{18,2},{3,19},{19,3},{4,20},{20... | collective-permute-start | bytes 1769480 | tf_op jit(solution)/shard_map/ppermute | solution.py:349
  39.2 0.0 copy-done.7
  39.2 0.1 collective-permute-start.2
  39.3 0.0 collective-permute-done.4
  39.3 0.5 and_select_fusion.idx
  39.8 19.0 %all-gather.2.cloned.1.call-done.pool = bf16[64,64,512]{2,1,0:T(8,128)(2,1)} async-done(((bf16[8,64,512]{2,1,0:T(8,128)(2,1)}), bf16[64,64,512]{2,1,0:T(8,128)(2,1)}) %all-gather.2.cloned.1.call-update) | async-done | bytes 4194320 | tf_op jit(solution)/shard_map/all_gather | solution.py:360
  58.8 17.7 %pick_pages.1 = bf16[8,64,512]{2,1,0:T(8,128)(2,1)} custom-call(s32[8]{0:T(128)} %and_select_fusion.idx, bf16[64,64,512]{2,1,0:T(8,128)(2,1)} %all-gather.2.cloned.1.call-done.pool), custom_call_target="tpu_custom_call" | custom-call | bytes 2097152 | tf_op jit(solution)/shard_map/pick_pages/pallas_call | solution.py:141
  76.6 1.5 %collective-permute-start.5 = (bf16[8,64,512]{2,1,0:T(8,128)(2,1)}, bf16[8,64,512]{2,1,0:T(8,128)(2,1)}, u32[]{:S(2)}, u32[]{:S(2)}) collective-permute-start(bf16[8,64,512]{2,1,0:T(8,128)(2,1)} %pick_pages.1), channel_id=1, source_target_pairs={{0,16},{16,0},{1,17},{17,1},{2,18},{18,2},{3,19},{19,3},{4,20},{20... | collective-permute-start | bytes 1572872 | tf_op jit(solution)/shard_map/ppermute | solution.py:361
  78.1 0.1 pad_maximum_fusion
  78.2 0.3 fusion
  78.4 0.1 collective-permute-start.10
  78.5 0.0 collective-permute-done.1.w1
  78.5 0.5 collective-permute-start.3
  79.0 0.0 collective-permute-done.9.w1
  79.0 0.1 collective-permute-start.11
  79.1 0.0 copy-start.5
  79.1 1.4 copy-done.5
  80.5 5.0 %project_own.1 = (bf16[512,1536]{1,0:T(8,128)(2,1)S(1)}, bf16[512,768]{1,0:T(8,128)(2,1)S(1)}, bf16[512,512]{1,0:T(8,128)(2,1)}, f32[512,256]{1,0:T(8,128)S(1)}, f32[512,256]{1,0:T(8,128)S(1)}) custom-call(bf16[512,1536]{1,0:T(8,128)(2,1)S(1)} %bitcast.14, f32[1,1536]{1,0:T(1,128)S(1)} %reshape.37.gain, bf16[1536,768]{1,0:T(8,128)(2,1)} %wq.1, ...), custom_call_target="tpu_custom_call" | custom-call | flops 2013265920 | bytes 10485760 | tf_op jit(solution)/shard_map/project_own/pallas_call | solution.py:75
  85.5 0.0 copy-start.1
  85.5 0.8 copy-done.1
  86.3 0.0 copy-start.3
  86.3 0.8 copy-done.3
  87.1 0.0 copy-start.6
  87.1 0.9 copy-done.6
  88.1 2.9 %collective-permute-done.5.came = bf16[8,64,512]{2,1,0:T(8,128)(2,1)} collective-permute-done((bf16[8,64,512]{2,1,0:T(8,128)(2,1)}, bf16[8,64,512]{2,1,0:T(8,128)(2,1)}, u32[]{:S(2)}, u32[]{:S(2)}) %collective-permute-start.5) | collective-permute-done | bytes 524320 | tf_op jit(solution)/shard_map/ppermute | solution.py:361
  91.0 1.5 %collective-permute-start.7 = (bf16[512,512]{1,0:T(8,128)(2,1)}, bf16[512,512]{1,0:T(8,128)(2,1)}, u32[]{:S(2)}, u32[]{:S(2)}) collective-permute-start(bf16[512,512]{1,0:T(8,128)(2,1)} %get-tuple-element.14.kv_own), channel_id=1, source_target_pairs={{0,1},{1,0},{2,3},{3,2},{4,5},{5,4},{6,7},{7,6},{8,9},{9,8},{10,11... | collective-permute-start | bytes 1572872 | tf_op jit(solution)/shard_map/ppermute | solution.py:371
  92.5 17.8 %choose_pages.1.mine = bf16[8,64,512]{2,1,0:T(8,128)(2,1)} custom-call(s32[1]{0:T(128)S(6)} %convert_element_type.19.home, s32[8]{0:T(128)} %and_select_fusion.1.idx, bf16[64,64,512]{2,1,0:T(8,128)(2,1)} %all-gather.2.cloned.1.call-done.pool, bf16[8,64,512]{2,1,0:T(8,128)(2,1)} %collective-permute-done.5.came), custom_call_target="tpu_custom_call" | custom-call | bytes 2097152 | tf_op jit(solution)/shard_map/choose_pages/pallas_call | solution.py:171
  110.3 0.0 collective-permute-done.2.w2
  110.3 0.6 collective-permute-start.6
  111.5 0.7 concatenate.7.info
  112.2 0.1 pad_add_fusion.order
  112.3 0.0 collective-permute-done.3.w3
  112.3 0.0 copy-start.2
  112.3 1.0 copy-done.2
  113.3 0.0 copy-start.4
  113.3 1.0 copy-done.4
  114.4 3.5 %project_other.1.qb = bf16[512,768]{1,0:T(8,128)(2,1)S(1)} custom-call(s32[4]{0:T(128)S(1)} %pad_add_fusion.order, bf16[512,1536]{1,0:T(8,128)(2,1)S(1)} %get-tuple-element.11.normed, bf16[384,768]{1,0:T(8,128)(2,1)S(1)} %collective-permute-done.w0, bf16[384,768]{1,0:T(8,128)(2,1)S(1)} %collective-permute-done.1.w1, ...), custom_call_target="tpu_custom_call" | custom-call | flops 1207959552 | bytes 6291456 | tf_op jit(solution)/shard_map/project_other/pallas_call | solution.py:116
  117.8 0.0 copy-start
  117.8 0.9 copy-done
  118.7 0.0 collective-permute-done.7.kv_peer
  118.7 0.0 collective-permute-done.10.w2
  118.7 0.0 collective-permute-done.11.w3
  118.7 4.8 %collective-permute-done.6.peer = bf16[8,64,512]{2,1,0:T(8,128)(2,1)} collective-permute-done((bf16[8,64,512]{2,1,0:T(8,128)(2,1)}, bf16[8,64,512]{2,1,0:T(8,128)(2,1)}, u32[]{:S(2)}, u32[]{:S(2)}) %collective-permute-start.6) | collective-permute-done | bytes 524320 | tf_op jit(solution)/shard_map/ppermute | solution.py:364
  123.6 13.4 %attend_and_out.1 = bf16[512,1536]{1,0:T(8,128)(2,1)} custom-call(s32[6]{0:T(128)} %concatenate.7.info, bf16[512,768]{1,0:T(8,128)(2,1)} %copy-done.6, bf16[512,768]{1,0:T(8,128)(2,1)} %copy-done, bf16[8,64,512]{2,1,0:T(8,128)(2,1)} %choose_pages.1.mine, bf16[8,64,512]{2,1,0:T(8,128)(2,1)} %collective-permute-done.6.peer, ...), custom_call_target="tpu_custom_call" | custom-call | flops 6442450944 | bytes 12582912 | tf_op jit(solution)/shard_map/attend_and_out/pallas_call | solution.py:306
  (4 shorter events, 0.0 us)
Async XLA Ops:
  6.5 6.1 %copy-start.8 = (s32[1,8]{1,0:T(1,128)S(1)}, s32[1,8]{1,0:T(1,128)}, u32[]{:S(2)}) copy-start(s32[1,8]{1,0:T(1,128)} %param.15) | copy-start | bytes 100
  6.5 32.7 %copy-start.7 = (f32[1536]{0:T(1024)S(1)}, f32[1536]{0:T(1024)}, u32[]{:S(2)}) copy-start(f32[1536]{0:T(1024)} %param.10) | copy-start | bytes 18436
  6.5 52.3 %all-gather.2.cloned.1.call-start = ((), (), s32[]{:S(2)}) async-start(), calls=%async_computation | async-start | bytes 4718592 | tf_op jit(solution)/shard_map/all_gather | solution.py:360
  8.4 17.2 %collective-permute-start = (bf16[384,768]{1,0:T(8,128)(2,1)S(1)}, bf16[384,768]{1,0:T(8,128)(2,1)S(1)}, u32[]{:S(2)}, u32[]{:S(2)}) collective-permute-start(bf16[384,768]{1,0:T(8,128)(2,1)S(1)} %constant_dynamic-slice_fusion.1), channel_id=1, source_target_pairs={{0,1},{1,0},{2,3},{3,2},{4,5},{5,4},{6,7},{7,6},{8,9},{9,8},{10,11... | collective-permute-start | bytes 1769480 | tf_op jit(solution)/shard_map/ppermute | solution.py:348
  12.6 24.9 %collective-permute-start.8 = (bf16[768,384]{1,0:T(8,128)(2,1)S(1)}, bf16[768,384]{1,0:T(8,128)(2,1)}, u32[]{:S(2)}, u32[]{:S(2)}) collective-permute-start(bf16[768,384]{1,0:T(8,128)(2,1)S(1)} %constant_dynamic-slice_fusion), channel_id=1, source_target_pairs={{0,1},{1,0},{2,3},{3,2},{4,5},{5,4},{6,7},{7,6},{8,9},{9,8},{10,11... | collective-permute-start | bytes 1769480 | tf_op jit(solution)/shard_map/ppermute | solution.py:348
  12.6 26.7 %collective-permute-start.4 = (s32[8]{0:T(128)S(1)}, s32[8]{0:T(128)S(1)}, u32[]{:S(2)}, u32[]{:S(2)}) collective-permute-start(s32[8]{0:T(128)S(1)} %bitcast.15), channel_id=1, source_target_pairs={{0,16},{16,0},{1,17},{17,1},{2,18},{18,2},{3,19},{19,3},{4,20},{20... | collective-permute-start | bytes 104 | tf_op jit(solution)/shard_map/ppermute | solution.py:358
  25.6 52.9 %collective-permute-start.1 = (bf16[384,768]{1,0:T(8,128)(2,1)S(1)}, bf16[384,768]{1,0:T(8,128)(2,1)S(1)}, u32[]{:S(2)}, u32[]{:S(2)}) collective-permute-start(bf16[384,768]{1,0:T(8,128)(2,1)S(1)} %collective-permute-done.w0), channel_id=1, source_target_pairs={{0,16},{16,0},{1,17},{17,1},{2,18},{18,2},{3,19},{19,3},{4,20},{20... | collective-permute-start | bytes 1769480 | tf_op jit(solution)/shard_map/ppermute | solution.py:349
  37.5 41.5 %collective-permute-start.9 = (bf16[768,384]{1,0:T(8,128)(2,1)}, bf16[768,384]{1,0:T(8,128)(2,1)}, u32[]{:S(2)}, u32[]{:S(2)}) collective-permute-start(bf16[768,384]{1,0:T(8,128)(2,1)} %collective-permute-done.8.w0), channel_id=1, source_target_pairs={{0,16},{16,0},{1,17},{17,1},{2,18},{18,2},{3,19},{19,3},{4,20},{20... | collective-permute-start | bytes 1769480 | tf_op jit(solution)/shard_map/ppermute | solution.py:349
  39.2 71.0 %collective-permute-start.2 = (bf16[384,768]{1,0:T(8,128)(2,1)S(1)}, bf16[384,768]{1,0:T(8,128)(2,1)S(1)}, u32[]{:S(2)}, u32[]{:S(2)}) collective-permute-start(bf16[384,768]{1,0:T(8,128)(2,1)S(1)} %collective-permute-done.w0), channel_id=1, source_target_pairs={{0,2},{2,0},{4,6},{6,4},{8,10},{10,8},{12,14},{14,12},{1,3},{3,1},... | collective-permute-start | bytes 1769480 | tf_op jit(solution)/shard_map/ppermute | solution.py:350
  76.6 14.4 %collective-permute-start.5 = (bf16[8,64,512]{2,1,0:T(8,128)(2,1)}, bf16[8,64,512]{2,1,0:T(8,128)(2,1)}, u32[]{:S(2)}, u32[]{:S(2)}) collective-permute-start(bf16[8,64,512]{2,1,0:T(8,128)(2,1)} %pick_pages.1), channel_id=1, source_target_pairs={{0,16},{16,0},{1,17},{17,1},{2,18},{18,2},{3,19},{19,3},{4,20},{20... | collective-permute-start | bytes 1572872 | tf_op jit(solution)/shard_map/ppermute | solution.py:361
  78.4 40.3 %collective-permute-start.10 = (bf16[768,384]{1,0:T(8,128)(2,1)}, bf16[768,384]{1,0:T(8,128)(2,1)}, u32[]{:S(2)}, u32[]{:S(2)}) collective-permute-start(bf16[768,384]{1,0:T(8,128)(2,1)} %collective-permute-done.8.w0), channel_id=1, source_target_pairs={{0,2},{2,0},{4,6},{6,4},{8,10},{10,8},{12,14},{14,12},{1,3},{3,1},... | collective-permute-start | bytes 1769480 | tf_op jit(solution)/shard_map/ppermute | solution.py:350
  78.5 33.8 %collective-permute-start.3 = (bf16[384,768]{1,0:T(8,128)(2,1)S(1)}, bf16[384,768]{1,0:T(8,128)(2,1)}, u32[]{:S(2)}, u32[]{:S(2)}) collective-permute-start(bf16[384,768]{1,0:T(8,128)(2,1)S(1)} %collective-permute-done.1.w1), channel_id=1, source_target_pairs={{0,2},{2,0},{4,6},{6,4},{8,10},{10,8},{12,14},{14,12},{1,3},{3,1},... | collective-permute-start | bytes 1769480 | tf_op jit(solution)/shard_map/ppermute | solution.py:350
  79.0 39.7 %collective-permute-start.11 = (bf16[768,384]{1,0:T(8,128)(2,1)}, bf16[768,384]{1,0:T(8,128)(2,1)}, u32[]{:S(2)}, u32[]{:S(2)}) collective-permute-start(bf16[768,384]{1,0:T(8,128)(2,1)} %collective-permute-done.9.w1), channel_id=1, source_target_pairs={{0,2},{2,0},{4,6},{6,4},{8,10},{10,8},{12,14},{14,12},{1,3},{3,1},... | collective-permute-start | bytes 1769480 | tf_op jit(solution)/shard_map/ppermute | solution.py:350
  79.1 1.4 copy-start.5
  85.5 0.8 copy-start.1
  86.3 0.8 copy-start.3
  87.1 0.9 copy-start.6
  91.0 27.7 %collective-permute-start.7 = (bf16[512,512]{1,0:T(8,128)(2,1)}, bf16[512,512]{1,0:T(8,128)(2,1)}, u32[]{:S(2)}, u32[]{:S(2)}) collective-permute-start(bf16[512,512]{1,0:T(8,128)(2,1)} %get-tuple-element.14.kv_own), channel_id=1, source_target_pairs={{0,1},{1,0},{2,3},{3,2},{4,5},{5,4},{6,7},{7,6},{8,9},{9,8},{10,11... | collective-permute-start | bytes 1572872 | tf_op jit(solution)/shard_map/ppermute | solution.py:371
  110.3 13.3 %collective-permute-start.6 = (bf16[8,64,512]{2,1,0:T(8,128)(2,1)}, bf16[8,64,512]{2,1,0:T(8,128)(2,1)}, u32[]{:S(2)}, u32[]{:S(2)}) collective-permute-start(bf16[8,64,512]{2,1,0:T(8,128)(2,1)} %choose_pages.1.mine), channel_id=1, source_target_pairs={{0,1},{1,0},{2,3},{3,2},{4,5},{5,4},{6,7},{7,6},{8,9},{9,8},{10,11... | collective-permute-start | bytes 1572872 | tf_op jit(solution)/shard_map/ppermute | solution.py:364
  112.3 1.0 copy-start.2
  113.3 1.0 copy-start.4
  117.8 0.9 copy-start
Sparse Core Ops, SparseCore 0:
  9.0 49.8 all-gather.1

commit v2 on v1

--- a/solution.py
+++ b/solution.py
@@ -83,7 +83,7 @@
         ),
         in_specs=[spec(pltpu.VMEM)] * 6,
         out_specs=[spec(pltpu.VMEM)] * 5,
-        compiler_params=pltpu.CompilerParams(vmem_limit_bytes=48 * 2**20),
+        compiler_params=pltpu.CompilerParams(vmem_limit_bytes=20 * 2**20),
         cost_estimate=pl.CostEstimate(
             flops=2 * rows * width * (qc + kc), bytes_accessed=10 * 2**20, transcendentals=0
         ),
@@ -91,92 +91,63 @@
     )(tok, gain.reshape(1, width), wq, wkv, cos_t, sin_t)
 
 
-def other_kernel(head_size, order, normed, w0, w1, w2, w3, cos, sin, q):
+def other_kernel(head_size, normed, wq, cos, sin, q):
     rows = normed.shape[0]
     tile = min(256, rows)
-    deep = w0.shape[0]
     even = lax.broadcasted_iota(jnp.int32, (tile, head_size), 1) % 2 == 0
     for i in range(rows // tile):
         at = pl.ds(i * tile, tile)
         c = cos[at, :]
         s = sin[at, :]
-        total = None
-        for n, w in enumerate((w0, w1, w2, w3)):
-            x = normed[at, pl.ds(pl.multiple_of(order[n] * deep, 128), deep)]
-            part = jnp.dot(x, w[...], preferred_element_type=F32)
-            total = part if total is None else total + part
         for h in range(q.shape[1] // head_size):
             cols = slice(h * head_size, (h + 1) * head_size)
-            q[at, cols] = rotate(total[:, cols], c, s, even).astype(BF16)
-
-
-def project_other(normed, pieces, order, cos, sin, head_size):
+            part = jnp.dot(normed[at, :], wq[:, cols], preferred_element_type=F32)
+            q[at, cols] = rotate(part, c, s, even).astype(BF16)
+
+
+def project_other(normed, wq, cos, sin, head_size):
     rows, width = normed.shape
-    qc = pieces[0].shape[1]
+    qc = wq.shape[1]
     return pl.pallas_call(
         functools.partial(other_kernel, head_size),
         out_shape=jax.ShapeDtypeStruct((rows, qc), BF16),
-        in_specs=[spec(pltpu.SMEM)] + [spec(pltpu.VMEM)] * 7,
+        in_specs=[spec(pltpu.VMEM)] * 4,
         out_specs=spec(pltpu.VMEM),
-        compiler_params=pltpu.CompilerParams(vmem_limit_bytes=48 * 2**20),
+        compiler_params=pltpu.CompilerParams(vmem_limit_bytes=20 * 2**20),
         cost_estimate=pl.CostEstimate(
             flops=2 * rows * width * qc, bytes_accessed=6 * 2**20, transcendentals=0
         ),
         name="project_other",
-    )(order, normed, *pieces, cos, sin)
-
-
-def pick_kernel(idx, pool, out, sem):
-    copies = [
-        pltpu.make_async_copy(pool.at[idx[j]], out.at[j], sem.at[j]) for j in range(out.shape[0])
-    ]
-    for c in copies:
-        c.start()
-    for c in copies:
-        c.wait()
-
-
-def pick(pool, idx):
-    count = idx.shape[0]
+    )(normed, wq, cos, sin)
+
+
+def collect_kernel(where, *refs):
+    arrays, out = refs[:-1], refs[-1]
+
+    def one(j, _):
+        for n, array in enumerate(arrays):
+
+            @pl.when(where[0, j] == n)
+            def _():
+                out[j] = array[where[1, j]]
+
+        return 0
+
+    lax.fori_loop(0, out.shape[0], one, 0)
+
+
+def collect(where, arrays, name):
+    count = where.shape[1]
+    shape = (count,) + arrays[0].shape[1:]
     return pl.pallas_call(
-        pick_kernel,
-        out_shape=jax.ShapeDtypeStruct((count,) + pool.shape[1:], pool.dtype),
-        in_specs=[spec(pltpu.SMEM), spec(ANY)],
-        out_specs=spec(ANY),
-        scratch_shapes=[pltpu.SemaphoreType.DMA((count,))],
+        collect_kernel,
+        out_shape=jax.ShapeDtypeStruct(shape, arrays[0].dtype),
+        in_specs=[spec(pltpu.SMEM)] + [spec(pltpu.VMEM)] * len(arrays),
+        out_specs=spec(pltpu.VMEM),
+        compiler_params=pltpu.CompilerParams(vmem_limit_bytes=12 * 2**20),
         cost_estimate=pl.CostEstimate(flops=0, bytes_accessed=2 * 2**20, transcendentals=0),
-        name="pick_pages",
-    )(idx, pool)
-
-
-def choose_kernel(home, idx, pool, came, out, sem):
-    count = out.shape[0]
-
-    @pl.when(home[0] == 1)
-    def _():
-        for j in range(count):
-            pltpu.make_async_copy(pool.at[idx[j]], out.at[j], sem.at[j]).start()
-
-    @pl.when(home[0] == 0)
-    def _():
-        for j in range(count):
-            pltpu.make_async_copy(came.at[j], out.at[j], sem.at[j]).start()
-
-    for j in range(count):
-        pltpu.make_async_copy(came.at[j], out.at[j], sem.at[j]).wait()
-
-
-def choose(pool, idx, home, came):
-    count = idx.shape[0]
-    return pl.pallas_call(
-        choose_kernel,
-        out_shape=jax.ShapeDtypeStruct(came.shape, came.dtype),
-        in_specs=[spec(pltpu.SMEM), spec(pltpu.SMEM), spec(ANY), spec(ANY)],
-        out_specs=spec(ANY),
-        scratch_shapes=[pltpu.SemaphoreType.DMA((count,))],
-        cost_estimate=pl.CostEstimate(flops=0, bytes_accessed=2 * 2**20, transcendentals=0),
-        name="choose_pages",
-    )(home, idx, pool, came)
+        name=name,
+    )(where, *arrays)
 
 
 def attend_kernel(
@@ -184,15 +155,14 @@
     info,
     qa,
     qb,
-    mine,
-    peer,
+    k_mine,
+    k_peer,
+    v_mine,
+    v_peer,
     kv_own,
     kv_peer,
     woa,
-    w0,
-    w1,
-    w2,
-    w3,
+    wob,
     out,
     keys,
     vals,
@@ -206,49 +176,38 @@
     part = info[0]
     length = info[1]
     rows, half = qa.shape
-    pages, prow, _ = mine.shape
+    pages, prow, _ = k_mine.shape
     page = 2 * prow
     width = out.shape[1]
     nheads = half // head_size
     window = pages * page
-    wcols = w0.shape[1]
-
-    def move(which, dst, sem, lo):
+
+    def start(mine, peer, lo, dst, sem):
         cols = pl.ds(lo, head_size)
-        got = []
-        here = part == 0
-        for u in range(pages):
-            at0 = u * page
-            at1 = (u - rows // page) * page
-            for src, side in ((mine, part), (peer, 1 - part)):
-                row = pl.multiple_of(side * prow, prow)
-                got.append((True, src.at[u, :, cols], at0, row, prow))
-                if at1 >= 0:
-                    got.append((False, src.at[u, :, cols], at1, row, prow))
-        got.append((True, kv_own.at[:, cols], window, 0, rows))
-        got.append((False, kv_own.at[:, cols], window, 0, rows))
-        got.append((False, kv_peer.at[:, cols], window - rows, 0, rows))
-        return got
-
-    def start(dst, sem, lo):
-        moves = move(None, dst, sem, lo)
-        for case in (True, False):
-
-            @pl.when((part == 0) == case)
+        for case in (0, 1):
+
+            @pl.when(part == case)
             def _():
-                for which, src, at, row, count in moves:
-                    if which == case:
-                        pltpu.make_async_copy(src, dst.at[pl.ds(at + row, count), :], sem).start()
-
-    def finish(dst, sem, lo):
+                skip = case * rows // page
+                for u in range(skip, pages):
+                    for src, side in ((mine, case), (peer, 1 - case)):
+                        to = pl.ds((u - skip) * page + side * prow, prow)
+                        pltpu.make_async_copy(src.at[u], dst.at[to, :], sem).start()
+                if case == 1:
+                    to = pl.ds(window - rows, rows)
+                    pltpu.make_async_copy(kv_peer.at[:, cols], dst.at[to, :], sem).start()
+                to = pl.ds(window, rows)
+                pltpu.make_async_copy(kv_own.at[:, cols], dst.at[to, :], sem).start()
+
+    def finish(dst, sem):
         pltpu.make_async_copy(dst, dst, sem).wait()
 
-    start(keys, ksem, 0)
-    start(vals, vsem, head_size)
-    weights = [pltpu.make_async_copy(woa, wa, wsem.at[0])]
-    for n, w in enumerate((w0, w1, w2, w3)):
-        cols = pl.ds(pl.multiple_of(info[2 + n] * wcols, 128), wcols)
-        weights.append(pltpu.make_async_copy(w, wb.at[:, cols], wsem.at[1 + n]))
+    start(k_mine, k_peer, 0, keys, ksem)
+    start(v_mine, v_peer, head_size, vals, vsem)
+    weights = [
+        pltpu.make_async_copy(woa, wa, wsem.at[0]),
+        pltpu.make_async_copy(wob, wb, wsem.at[1]),
+    ]
     for c in weights:
         c.start()
 
@@ -259,7 +218,7 @@
     first_seen = col_id >= row_id + 1
     last_seen = col_id <= row_id
     factor = math.log2(math.e) / math.sqrt(head_size)
-    finish(keys, ksem, 0)
+    finish(keys, ksem)
     for i in range(rows // tile):
         at = pl.ds(i * tile, tile)
         for n, q in enumerate((qa, qb)):
@@ -281,7 +240,7 @@
                 e = jnp.exp2((s - top) * factor)
                 total = jnp.sum(e, axis=-1, keepdims=True)
                 if i == 0 and n == 0 and h == 0:
-                    finish(vals, vsem, head_size)
+                    finish(vals, vsem)
                 vv = vals[pl.ds(i * tile, span), :]
                 m = jnp.dot(e.astype(BF16), vv, preferred_element_type=F32)
                 mix[n, at, cols] = (m / total).astype(BF16)
@@ -291,41 +250,53 @@
         at = pl.ds(i * tile, tile)
         row = part * rows + i * tile + lax.broadcasted_iota(jnp.int32, (tile, 1), 0)
         live = row < length
-        for j in range(width // wcols):
-            cols = slice(j * wcols, (j + 1) * wcols)
+        for j in range(width // 512):
+            cols = slice(j * 512, (j + 1) * 512)
             a = jnp.dot(mix[0, at, :], wa[:, cols], preferred_element_type=F32)
             b = jnp.dot(mix[1, at, :], wb[:, cols], preferred_element_type=F32)
             both = a.astype(BF16).astype(F32) + b.astype(BF16).astype(F32)
             out[at, cols] = jnp.where(live, both, 0.0).astype(BF16)
 
 
-def attend_pages(info, qa, qb, mine, peer, kv_own, kv_peer, woa, pieces, head_size):
+def attend_pages(info, qa, qb, k_mine, k_peer, v_mine, v_peer, kv_own, kv_peer, woa, wob):
     rows, half = qa.shape
     width = woa.shape[1]
-    window = mine.shape[0] * mine.shape[1] * 2
+    head_size = k_mine.shape[2]
+    window = k_mine.shape[0] * k_mine.shape[1] * 2
     return pl.pallas_call(
         functools.partial(attend_kernel, head_size),
         out_shape=jax.ShapeDtypeStruct((rows, width), BF16),
-        in_specs=[spec(pltpu.SMEM)] + [spec(pltpu.VMEM)] * 2 + [spec(ANY)] * 9,
+        in_specs=[spec(pltpu.SMEM)] + [spec(pltpu.VMEM)] * 2 + [spec(ANY)] * 8,
         out_specs=spec(pltpu.VMEM),
         scratch_shapes=[
             pltpu.VMEM((window + rows, head_size), BF16),
             pltpu.VMEM((window + rows, head_size), BF16),
             pltpu.VMEM(woa.shape, BF16),
-            pltpu.VMEM(woa.shape, BF16),
+            pltpu.VMEM(wob.shape, BF16),
             pltpu.VMEM((2, rows, half), BF16),
             pltpu.SemaphoreType.DMA,
             pltpu.SemaphoreType.DMA,
-            pltpu.SemaphoreType.DMA((5,)),
+            pltpu.SemaphoreType.DMA((2,)),
         ],
-        compiler_params=pltpu.CompilerParams(vmem_limit_bytes=56 * 2**20),
+        compiler_params=pltpu.CompilerParams(vmem_limit_bytes=28 * 2**20),
         cost_estimate=pl.CostEstimate(
             flops=4 * rows * 2 * half * (window + 256) + 4 * rows * half * width,
             bytes_accessed=12 * 2**20,
             transcendentals=rows * 6 * (window + 256),
         ),
         name="attend_and_out",
-    )(info, qa, qb, mine, peer, kv_own, kv_peer, woa, *pieces)
+    )(info, qa, qb, k_mine, k_peer, v_mine, v_peer, kv_own, kv_peer, woa, wob)
+
+
+def line_gather(x, swap_at, after):
+    pairs = swap_at([(0, 1), (1, 0), (2, 3), (3, 2)])
+    middle = swap_at([(1, 2), (2, 1)])
+    outward = swap_at([(1, 0), (2, 3)])
+    first = lax.ppermute(x, "dp", pairs)
+    near = lax.ppermute(x, "dp", middle)
+    first, near, _ = lax.optimization_barrier((first, near, after))
+    far = lax.ppermute(first, "dp", middle)
+    return [x, first, near, lax.ppermute(near, "dp", outward), far, lax.ppermute(far, "dp", outward)]
 
 
 def pair_shards(tokens, norm_gain, w_query, w_keyval, w_out, kv_pages, page_table, lengths, starts):
@@ -334,34 +305,65 @@
     rep = lax.axis_index("rep")
     dp = lax.axis_index("dp")
     ndp = lax.axis_size("dp")
-    core = dp % 2
+    chip, core = dp // 2, dp % 2
     rows = tokens.shape[1]
+    held = kv_pages.shape[0]
+    count = page_table.shape[1]
     swap = [(0, 1), (1, 0)]
     cores = [(i, i ^ 1) for i in range(ndp)]
 
+    def both_cores(perm):
+        return [(2 * a + c, 2 * b + c) for a, b in perm for c in (0, 1)]
+
     quarter = rep * 2 + core
-    order = jnp.stack(
-        [quarter, (1 - rep) * 2 + core, rep * 2 + 1 - core, (1 - rep) * 2 + 1 - core]
-    ).astype(jnp.int32)
-
-    def spread(piece):
-        a = lax.ppermute(piece, "tensor", swap)
-        b = lax.ppermute(a, "rep", swap)
-        return a, b, lax.ppermute(a, "dp", cores), lax.ppermute(b, "dp", cores)
-
-    deep = w_query.shape[0] // 4
-    wide = w_out.shape[1] // 4
-    wq_pieces = spread(lax.dynamic_slice_in_dim(w_query, quarter * deep, deep, 0))
-    wo_pieces = spread(lax.dynamic_slice_in_dim(w_out, quarter * wide, wide, 1))
-
-    table = page_table[0]
-    peer_table = lax.ppermute(table, "rep", swap)
-    per_rep = kv_pages.shape[0] * ndp
-    pool = lax.all_gather(kv_pages, "dp", axis=0, tiled=True)
-    came = lax.ppermute(pick(pool, peer_table % per_rep), "rep", swap)
-    home = (table[:1] // per_rep == rep).astype(jnp.int32)
-    mine = choose(pool, table % per_rep, home, came)
-    peer = lax.ppermute(mine, "tensor", swap)
+    groups = [[r * ndp + 2 * z + c for r in (0, 1) for c in (0, 1)] for z in range(ndp // 2)]
+
+    def other_half(w):
+        deep = w.shape[0] // 4
+        piece = lax.dynamic_slice_in_dim(w, quarter * deep, deep, 0)
+        piece = lax.ppermute(piece, "tensor", swap)
+        return lax.all_gather(
+            piece, ("rep", "dp"), axis=0, tiled=True, axis_index_groups=groups
+        )
+
+    wq_other = other_half(w_query)
+    wo_other = other_half(w_out)
+
+    table = page_table
+    chip_tables = jnp.concatenate([table, lax.ppermute(table, "dp", cores)], axis=0)
+    peer_tables = lax.ppermute(chip_tables, "rep", swap)
+    per_rep = held * ndp
+    upper = chip >= 2
+    is_end = (chip == 0) | (chip == 3)
+    near_chip = jnp.where(upper, 1, 2)
+
+    def locate(pages):
+        page = pages % per_rep
+        holder = page // held
+        at = holder // 2
+        ends = is_end.astype(jnp.int32)
+        array = jnp.where(
+            at == chip, 0, jnp.where(at == chip ^ 1, 1, jnp.where(at == near_chip, 2, 4) + ends)
+        )
+        return array, page % held, holder % 2 == core
+
+    array_c, slot_c, line_c = locate(chip_tables)
+    array_p, slot_p, line_p = locate(peer_tables)
+    j = jnp.arange(count, dtype=jnp.int32)
+    where_core = jnp.stack(
+        [jnp.concatenate([array_c[1], array_p[1]]), jnp.concatenate([slot_c[1], slot_p[1]])]
+    )
+    lines = 6
+    where_peer = jnp.stack(
+        [jnp.where(line_p[0], array_p[0], lines), jnp.where(line_p[0], slot_p[0], count + j)]
+    )
+    home = chip_tables[0] // per_rep == rep
+    where_own = jnp.stack(
+        [
+            jnp.where(home, jnp.where(line_c[0], array_c[0], lines), lines + 1),
+            jnp.where(home & line_c[0], slot_c[0], j),
+        ]
+    )
 
     step = 32
     cos_t, sin_t = rotation_tables(starts[0] + part * rows, rows, step, head_size)
@@ -369,9 +371,22 @@
         tokens[0], norm_gain, w_query, w_keyval, cos_t, sin_t, head_size, step
     )
     kv_peer = lax.ppermute(kv_own, "tensor", swap)
-    qb = project_other(normed, wq_pieces, order, cos, sin, head_size)
-    info = jnp.concatenate([jnp.stack([part, lengths[0]]).astype(jnp.int32), order])
-    return attend_pages(info, qa, qb, mine, peer, kv_own, kv_peer, w_out, wo_pieces, head_size)[None]
+
+    def window_half(x):
+        line = line_gather(x, both_cores, kv_own)
+        given = lax.ppermute(collect(where_core, line, "pick_core"), "dp", cores)
+        came = lax.ppermute(collect(where_peer, line + [given], "pick_rep"), "rep", swap)
+        mine = collect(where_own, line + [given, came], "pick_own")
+        return mine, lax.ppermute(mine, "tensor", swap)
+
+    k_mine, k_peer = window_half(kv_pages[:, :, :head_size])
+    v_mine, v_peer = window_half(kv_pages[:, :, head_size:])
+
+    qb = project_other(normed, wq_other, cos, sin, head_size)
+    info = jnp.stack([part, lengths[0]]).astype(jnp.int32)
+    return attend_pages(
+        info, qa, qb, k_mine, k_peer, v_mine, v_peer, kv_own, kv_peer, w_out, wo_other
+    )[None]
 
 
 def rotate_pairs(values, positions, columns_from, head_size):
@@ -473,7 +488,8 @@
         P(("rep", "dp")),
         P(("rep", "dp")),
     )
-    body = pair_shards if mesh.shape["tensor"] == 2 and mesh.shape["rep"] == 2 else shards
+    line = mesh.shape["tensor"] == 2 and mesh.shape["rep"] == 2 and mesh.shape["dp"] == 8
+    body = pair_shards if line else shards
     return jax.shard_map(
         body,
         mesh=mesh,

time: 144 us -> 134 us (0.931)
  Pallas kernels: 57.3 us -> 24.1 us
  starting transfers between devices: 13.2 us -> 25.4 us
  local copies, waits for them, and re-layouts: 9.76 us -> 16.7 us
  waiting for transfers between devices: 47 us -> 51.8 us
    pallas_call x2 -> x6, Pallas kernels: 35.5 us -> 7.58 us  [collect(): pl.pallas_call(collect_kernel, out_shape=jax.ShapeDtypeStruct(shape, arra...]
    ppermute x11 -> x20, waiting for transfers between devices: 27.3 us -> 51.7 us  [the longest x2 17.9 us: other_half(): piece = lax.ppermute(piece, 'tensor', swap)]
    all_gather x1 -> x2, waiting for transfers between devices: 19 us -> 0.01 us  [other_half(): lax.all_gather(piece, ('rep', 'dp'), axis=0, tiled=True, axis_index_group...]
    ppermute x11 -> x20, starting transfers between devices: 11.7 us -> 23.7 us  [the longest x2 6.09 us: line_gather(): first = lax.ppermute(x, 'dp', pairs)]
    unnamed x18 -> x34, local copies, waits for them, and re-layouts: 6.85 us -> 14.4 us
    pallas_call x1, Pallas kernels: 4.99 us -> 3.04 us  [project(): pl.pallas_call(functools.partial(project_kernel, head_size, step), out_sh...]
    pallas_call x1, Pallas kernels: 3.45 us -> 1.66 us  [project_other(): pl.pallas_call(functools.partial(other_kernel, head_size), out_shape=jax....]
    pallas_call x1, Pallas kernels: 13.4 us -> 11.8 us  [attend_pages(): pl.pallas_call(functools.partial(attend_kernel, head_size), out_shape=jax...]
  transfers between devices with their start and end apart: 13 -> 23, of which waited for: 5 -> 9; matrix products, arithmetic and copies ran while one was open for 3% -> 1% of each run, Pallas kernels for 31% -> 9%
where the time goes in v2:
time: 134 us
  waiting for transfers between devices  51.8 us (39%)
  starting transfers between devices  25.4 us (19%)
  Pallas kernels  24.1 us (18%)
  local copies, waits for them, and re-layouts  16.7 us (12%)
  between operations  15.1 us (11%)
    ppermute x2, waiting for transfers between devices, other_half(): piece = lax.ppermute(piece, 'tensor', swap)  17.9 us
    unnamed x34, local copies, waits for them, and re-layouts  14.4 us
    ppermute x2, waiting for transfers between devices, line_gather(): lax.ppermute(far, 'dp', outward)  12.5 us
    pallas_call x1, Pallas kernels, attend_pages(): pl.pallas_call(functools.partial(attend_kernel, head_size), out_shape=jax...  11.8 us
    ppermute x2, waiting for transfers between devices, line_gather(): lax.ppermute(near, 'dp', outward)  9.09 us
    ppermute x2, waiting for transfers between devices, window_half(): lax.ppermute(collect(where_peer, line + [given], 'pick_rep'), 'rep', swap)  9.03 us
    pallas_call x6, Pallas kernels, collect(): pl.pallas_call(collect_kernel, out_shape=jax.ShapeDtypeStruct(shape, arra...  7.58 us
    ppermute x2, starting transfers between devices, line_gather(): first = lax.ppermute(x, 'dp', pairs)  6.09 us
  transfers between devices with their start and end apart: 23, of which 9 were waited for; matrix products, arithmetic and copies ran while one was open for 1% of the time, Pallas kernels for 9%

profile of v2, /device:TPU:0, one launch (start us, length us, event | category | flops | bytes accessed | tf_op | source)
XLA Modules:
  0.0 133.7 jit_solution(16645184983722239056)
XLA Ops:
  6.5 1.2 constant_dynamic-slice_fusion.1
  7.7 3.0 %collective-permute-start = (bf16[384,768]{1,0:T(8,128)(2,1)S(1)}, bf16[384,768]{1,0:T(8,128)(2,1)S(1)}, u32[]{:S(2)}, u32[]{:S(2)}) collective-permute-start(bf16[384,768]{1,0:T(8,128)(2,1)S(1)} %constant_dynamic-slice_fusion.1), channel_id=1, source_target_pairs={{0,1},{1,0},{2,3},{3,2},{4,5},{5,4},{6,7},{7,6},{8,9},{9,8},{10,11... | collective-permute-start | bytes 1769480 | tf_op jit(solution)/shard_map/ppermute | solution.py:324
  10.7 13.3 %collective-permute-done = bf16[384,768]{1,0:T(8,128)(2,1)S(1)} collective-permute-done((bf16[384,768]{1,0:T(8,128)(2,1)S(1)}, bf16[384,768]{1,0:T(8,128)(2,1)S(1)}, u32[]{:S(2)}, u32[]{:S(2)}) %collective-permute-start) | collective-permute-done | bytes 589856 | tf_op jit(solution)/shard_map/ppermute | solution.py:324
  24.1 0.8 copy-done.12
  24.9 0.0 all-gather.3.cloned.1.call-update
  24.9 0.0 all-gather.5.cloned.1.call-start
  25.0 1.1 constant_dynamic-slice_fusion
  26.1 1.8 %collective-permute-start.20 = (bf16[192,1536]{1,0:T(8,128)(2,1)S(1)}, bf16[192,1536]{1,0:T(8,128)(2,1)S(1)}, u32[]{:S(2)}, u32[]{:S(2)}) collective-permute-start(bf16[192,1536]{1,0:T(8,128)(2,1)S(1)} %constant_dynamic-slice_fusion), channel_id=1, source_target_pairs={{0,1},{1,0},{2,3},{3,2},{4,5},{5,4},{6,7},{7,6},{8,9},{9,8},{10,11... | collective-permute-start | bytes 1769480 | tf_op jit(solution)/shard_map/ppermute | solution.py:324
  27.9 1.6 %collective-permute-start.2 = (bf16[8,64,256]{2,1,0:T(8,128)(2,1)S(1)}, bf16[8,64,256]{2,1,0:T(8,128)(2,1)S(1)}, u32[]{:S(2)}, u32[]{:S(2)}) collective-permute-start(bf16[8,64,256]{2,1,0:T(8,128)(2,1)S(1)} %get-tuple-element.32.refs_0_), channel_id=1, source_target_pairs={{0,4},{2,6},{4,0},{6,2},{8,12},{10,14},{12,8},{14,10},{1,5},{3,7},... | collective-permute-start | bytes 786440 | tf_op jit(solution)/shard_map/ppermute | solution.py:295
  29.6 0.7 collective-permute-start.3
  30.3 4.4 %collective-permute-start.11 = (bf16[8,64,256]{2,1,0:T(8,128)(2,1)S(1)}, bf16[8,64,256]{2,1,0:T(8,128)(2,1)S(1)}, u32[]{:S(2)}, u32[]{:S(2)}) collective-permute-start(bf16[8,64,256]{2,1,0:T(8,128)(2,1)S(1)} %get-tuple-element.31.refs_0_), channel_id=1, source_target_pairs={{0,4},{2,6},{4,0},{6,2},{8,12},{10,14},{12,8},{14,10},{1,5},{3,7},... | collective-permute-start | bytes 786440 | tf_op jit(solution)/shard_map/ppermute | solution.py:295
  34.7 0.7 collective-permute-start.12
  36.1 4.6 %collective-permute-done.20 = bf16[192,1536]{1,0:T(8,128)(2,1)S(1)} collective-permute-done((bf16[192,1536]{1,0:T(8,128)(2,1)S(1)}, bf16[192,1536]{1,0:T(8,128)(2,1)S(1)}, u32[]{:S(2)}, u32[]{:S(2)}) %collective-permute-start.20) | collective-permute-done | bytes 589856 | tf_op jit(solution)/shard_map/ppermute | solution.py:324
  40.7 0.0 collective-permute-start.1
  40.7 0.8 copy-done.13
  41.5 0.0 all-gather.5.cloned.1.call-update
  41.5 0.1 pad_maximum_fusion
  41.6 0.3 fusion
  41.9 0.0 copy-start.5
  41.9 1.7 %copy-done.5 = bf16[1536,768]{1,0:T(8,128)(2,1)S(1)} copy-done((bf16[1536,768]{1,0:T(8,128)(2,1)S(1)}, bf16[1536,768]{1,0:T(8,128)(2,1)}, u32[]{:S(2)}) %copy-start.5) | copy-done | bytes 2359320
  43.5 1.4 %copy-done.8 = bf16[1,512,1536]{2,1,0:T(8,128)(2,1)S(1)} copy-done((bf16[1,512,1536]{2,1,0:T(8,128)(2,1)S(1)}, bf16[1,512,1536]{2,1,0:T(8,128)(2,1)}, u32[]{:S(2)}) %copy-start.8) | copy-done | bytes 1572888
  45.0 1.4 %copy-done.9 = bf16[1536,512]{1,0:T(8,128)(2,1)S(1)} copy-done((bf16[1536,512]{1,0:T(8,128)(2,1)S(1)}, bf16[1536,512]{1,0:T(8,128)(2,1)}, u32[]{:S(2)}) %copy-start.9) | copy-done | bytes 1572888
  46.4 3.0 %project_own.1 = (bf16[512,1536]{1,0:T(8,128)(2,1)S(1)}, bf16[512,768]{1,0:T(8,128)(2,1)S(1)}, bf16[512,512]{1,0:T(8,128)(2,1)}, f32[512,256]{1,0:T(8,128)S(1)}, f32[512,256]{1,0:T(8,128)S(1)}) custom-call(bf16[512,1536]{1,0:T(8,128)(2,1)S(1)} %bitcast.17, f32[1,1536]{1,0:T(1,128)S(1)} %reshape.40.gain, bf16[1536,768]{1,0:T(8,128)(2,1)S(1)} %copy-done.5, ...), custom_call_target="tpu_custom_call" | custom-call | flops 2013265920 | bytes 10485760 | tf_op jit(solution)/shard_map/project_own/pallas_call | solution.py:75
  49.5 1.5 %collective-permute-start.7 = (s32[2,8]{1,0:T(2,128)S(1)}, s32[2,8]{1,0:T(2,128)S(1)}, u32[]{:S(2)}, u32[]{:S(2)}) collective-permute-start(s32[2,8]{1,0:T(2,128)S(1)} %get-tuple-element.42), channel_id=1, source_target_pairs={{0,16},{16,0},{1,17},{17,1},{2,18},{18,2},{3,19},{19,3},{4,20},{20... | collective-permute-start | bytes 200 | tf_op jit(solution)/shard_map/ppermute | solution.py:334
  51.0 2.1 %collective-permute-done.7 = s32[2,8]{1,0:T(2,128)S(1)} collective-permute-done((s32[2,8]{1,0:T(2,128)S(1)}, s32[2,8]{1,0:T(2,128)S(1)}, u32[]{:S(2)}, u32[]{:S(2)}) %collective-permute-start.7) | collective-permute-done | bytes 96 | tf_op jit(solution)/shard_map/ppermute | solution.py:334
  53.2 0.7 collective-permute-start.5
  53.8 0.0 collective-permute-done.11.refs_1_
  53.9 0.7 collective-permute-start.14
  54.6 1.3 collective-permute-start.4
  55.9 1.3 collective-permute-start.13
  57.2 0.0 collective-permute-done.5.refs_4_
  57.2 1.3 collective-permute-start.6
  58.5 0.0 collective-permute-done.14.refs_4_
  58.5 1.3 collective-permute-start.15
  59.8 0.1 add_bitcast_fusion.1
  59.9 0.1 add_bitcast_fusion
  60.0 9.1 %collective-permute-done.4.refs_3_ = bf16[8,64,256]{2,1,0:T(8,128)(2,1)S(1)} collective-permute-done((bf16[8,64,256]{2,1,0:T(8,128)(2,1)S(1)}, bf16[8,64,256]{2,1,0:T(8,128)(2,1)S(1)}, u32[]{:S(2)}, u32[]{:S(2)}) %collective-permute-start.4) | collective-permute-done | bytes 262176 | tf_op jit(solution)/shard_map/ppermute | solution.py:299
  69.1 11.2 %collective-permute-done.6.refs_5_ = bf16[8,64,256]{2,1,0:T(8,128)(2,1)S(1)} collective-permute-done((bf16[8,64,256]{2,1,0:T(8,128)(2,1)S(1)}, bf16[8,64,256]{2,1,0:T(8,128)(2,1)S(1)}, u32[]{:S(2)}, u32[]{:S(2)}) %collective-permute-start.6) | collective-permute-done | bytes 262176 | tf_op jit(solution)/shard_map/ppermute | solution.py:299
  80.3 1.5 %pick_core.2 = bf16[16,64,256]{2,1,0:T(8,128)(2,1)S(1)} custom-call(s32[2,16]{1,0:T(2,128)S(1)} %pad_add_fusion.2.where, bf16[8,64,256]{2,1,0:T(8,128)(2,1)S(1)} %get-tuple-element.32.refs_0_, bf16[8,64,256]{2,1,0:T(8,128)(2,1)S(1)} %collective-permute-done.2.refs_1_, bf16[8,64,256]{2,1,0:T(8,128)(2,1)S(1)} %collective-permute-done.3.refs_2_, ...), custom_call_target="tpu_custom_call" | custom-call | bytes 2097152 | tf_op jit(solution)/shard_map/pick_core/pallas_call | solution.py:142
  81.8 0.1 collective-permute-start.8
  81.9 1.2 collective-permute-done.15.refs_5_
  83.1 1.5 %pick_core.3 = bf16[16,64,256]{2,1,0:T(8,128)(2,1)S(1)} custom-call(s32[2,16]{1,0:T(2,128)S(1)} %pad_add_fusion.2.where, bf16[8,64,256]{2,1,0:T(8,128)(2,1)S(1)} %get-tuple-element.31.refs_0_, bf16[8,64,256]{2,1,0:T(8,128)(2,1)S(1)} %collective-permute-done.11.refs_1_, bf16[8,64,256]{2,1,0:T(8,128)(2,1)S(1)} %collective-permute-done.12.refs_2_, ...), custom_call_target="tpu_custom_call" | custom-call | bytes 2097152 | tf_op jit(solution)/shard_map/pick_core/pallas_call | solution.py:142
  84.6 0.1 collective-permute-start.16
  84.7 1.6 %collective-permute-start.19 = (bf16[512,512]{1,0:T(8,128)(2,1)}, bf16[512,512]{1,0:T(8,128)(2,1)}, u32[]{:S(2)}, u32[]{:S(2)}) collective-permute-start(bf16[512,512]{1,0:T(8,128)(2,1)} %get-tuple-element.18.kv_own), channel_id=1, source_target_pairs={{0,1},{1,0},{2,3},{3,2},{4,5},{5,4},{6,7},{7,6},{8,9},{9,8},{10,11... | collective-permute-start | bytes 1572872 | tf_op jit(solution)/shard_map/ppermute | solution.py:373
  86.3 1.1 pick_rep.2
  87.5 1.6 %collective-permute-start.9 = (bf16[8,64,256]{2,1,0:T(8,128)(2,1)S(1)}, bf16[8,64,256]{2,1,0:T(8,128)(2,1)S(1)}, u32[]{:S(2)}, u32[]{:S(2)}) collective-permute-start(bf16[8,64,256]{2,1,0:T(8,128)(2,1)S(1)} %pick_rep.2), channel_id=1, source_target_pairs={{0,16},{16,0},{1,17},{17,1},{2,18},{18,2},{3,19},{19,3},{4,20},{20... | collective-permute-start | bytes 786440 | tf_op jit(solution)/shard_map/ppermute | solution.py:378
  89.1 1.1 pick_rep.3
  90.2 0.5 collective-permute-start.17
  90.7 5.9 %collective-permute-done.9.refs_7_ = bf16[8,64,256]{2,1,0:T(8,128)(2,1)S(1)} collective-permute-done((bf16[8,64,256]{2,1,0:T(8,128)(2,1)S(1)}, bf16[8,64,256]{2,1,0:T(8,128)(2,1)S(1)}, u32[]{:S(2)}, u32[]{:S(2)}) %collective-permute-start.9) | collective-permute-done | bytes 262176 | tf_op jit(solution)/shard_map/ppermute | solution.py:378
  96.7 1.2 pick_own.2.k_mine
  97.8 0.6 collective-permute-start.10
  98.4 3.1 %collective-permute-done.17.refs_7_ = bf16[8,64,256]{2,1,0:T(8,128)(2,1)S(1)} collective-permute-done((bf16[8,64,256]{2,1,0:T(8,128)(2,1)S(1)}, bf16[8,64,256]{2,1,0:T(8,128)(2,1)S(1)}, u32[]{:S(2)}, u32[]{:S(2)}) %collective-permute-start.17) | collective-permute-done | bytes 262176 | tf_op jit(solution)/shard_map/ppermute | solution.py:378
  101.5 1.2 pick_own.3.v_mine
  102.7 0.6 collective-permute-start.18
  103.9 0.1 pad_add_fusion.4.info
  104.0 1.7 %copy-done = bf16[1536,768]{1,0:T(8,128)(2,1)S(1)} copy-done((bf16[1536,768]{1,0:T(8,128)(2,1)S(1)}, bf16[1536,768]{1,0:T(8,128)(2,1)}, u32[]{:S(2)}) %copy-start) | copy-done | bytes 2359320
  105.7 1.0 copy-done.2
  106.7 1.0 copy-done.4
  107.8 1.7 %project_other.1.qb = bf16[512,768]{1,0:T(8,128)(2,1)S(1)} custom-call(bf16[512,1536]{1,0:T(8,128)(2,1)S(1)} %get-tuple-element.15.normed, bf16[1536,768]{1,0:T(8,128)(2,1)S(1)} %copy-done, f32[512,256]{1,0:T(8,128)S(1)} %copy-done.2, f32[512,256]{1,0:T(8,128)S(1)} %copy-done.4), custom_call_target="tpu_custom_call" | custom-call | flops 1207959552 | bytes 6291456 | tf_op jit(solution)/shard_map/project_other/pallas_call | solution.py:111
  109.4 1.2 collective-permute-done.18.v_peer
  110.6 1.7 %copy-done.6 = bf16[768,1536]{1,0:T(8,128)(2,1)S(1)} copy-done((bf16[768,1536]{1,0:T(8,128)(2,1)S(1)}, bf16[768,1536]{1,0:T(8,128)(2,1)}, u32[]{:S(2)}) %copy-start.6) | copy-done | bytes 2359320
  112.3 1.7 %copy-done.7 = bf16[768,1536]{1,0:T(8,128)(2,1)S(1)} copy-done((bf16[768,1536]{1,0:T(8,128)(2,1)S(1)}, bf16[768,1536]{1,0:T(8,128)(2,1)}, u32[]{:S(2)}) %copy-start.7) | copy-done | bytes 2359320
  114.0 1.1 copy-done.11
  115.1 11.8 %attend_and_out.1 = bf16[512,1536]{1,0:T(8,128)(2,1)} custom-call(s32[2]{0:T(128)S(1)} %pad_add_fusion.4.info, bf16[512,768]{1,0:T(8,128)(2,1)S(1)} %copy-done.11, bf16[512,768]{1,0:T(8,128)(2,1)S(1)} %project_other.1.qb, bf16[8,64,256]{2,1,0:T(8,128)(2,1)S(1)} %pick_own.2.k_mine, bf16[8,64,256]{2,1,0:T(8,128)(2,1)} %collective-permute-done.10.k_peer, ...), custom_call_target="tpu_custom_call" | custom-call | flops 6442450944 | bytes 12582912 | tf_op jit(solution)/shard_map/attend_and_out/pallas_call | solution.py:266
  (50 shorter events, 0.3 us)
Async XLA Ops:
  6.5 21.4 %copy-start.14 = (bf16[8,64,512]{2,1,0:T(8,128)(2,1)S(1)}, bf16[8,64,512]{2,1,0:T(8,128)(2,1)}, u32[]{:S(2)}) copy-start(bf16[8,64,512]{2,1,0:T(8,128)(2,1)} %param.14) | copy-start | bytes 1572868
  6.5 34.1 %copy-start.16 = (s32[1,8]{1,0:T(1,128)S(1)}, s32[1,8]{1,0:T(1,128)}, u32[]{:S(2)}) copy-start(s32[1,8]{1,0:T(1,128)} %param.15) | copy-start | bytes 100
  6.5 35.0 %copy-start.15 = (f32[1536]{0:T(1024)S(1)}, f32[1536]{0:T(1024)}, u32[]{:S(2)}) copy-start(f32[1536]{0:T(1024)} %param.10) | copy-start | bytes 18436
  6.5 97.5 %all-gather.3.cloned.1.call-start = ((), (), s32[]{:S(2)}) async-start(), calls=%async_computation | async-start | bytes 2949120 | tf_op jit(solution)/shard_map/all_gather | solution.py:325
  7.7 16.4 %collective-permute-start = (bf16[384,768]{1,0:T(8,128)(2,1)S(1)}, bf16[384,768]{1,0:T(8,128)(2,1)S(1)}, u32[]{:S(2)}, u32[]{:S(2)}) collective-permute-start(bf16[384,768]{1,0:T(8,128)(2,1)S(1)} %constant_dynamic-slice_fusion.1), channel_id=1, source_target_pairs={{0,1},{1,0},{2,3},{3,2},{4,5},{5,4},{6,7},{7,6},{8,9},{9,8},{10,11... | collective-permute-start | bytes 1769480 | tf_op jit(solution)/shard_map/ppermute | solution.py:324
  24.1 0.8 copy-start.12
  24.9 85.7 %all-gather.5.cloned.1.call-start = ((), (), s32[]{:S(2)}) async-start(), calls=%async_computation.1 | async-start | bytes 2949120 | tf_op jit(solution)/shard_map/all_gather | solution.py:325
  26.1 14.6 %collective-permute-start.20 = (bf16[192,1536]{1,0:T(8,128)(2,1)S(1)}, bf16[192,1536]{1,0:T(8,128)(2,1)S(1)}, u32[]{:S(2)}, u32[]{:S(2)}) collective-permute-start(bf16[192,1536]{1,0:T(8,128)(2,1)S(1)} %constant_dynamic-slice_fusion), channel_id=1, source_target_pairs={{0,1},{1,0},{2,3},{3,2},{4,5},{5,4},{6,7},{7,6},{8,9},{9,8},{10,11... | collective-permute-start | bytes 1769480 | tf_op jit(solution)/shard_map/ppermute | solution.py:324
  27.9 25.2 %collective-permute-start.2 = (bf16[8,64,256]{2,1,0:T(8,128)(2,1)S(1)}, bf16[8,64,256]{2,1,0:T(8,128)(2,1)S(1)}, u32[]{:S(2)}, u32[]{:S(2)}) collective-permute-start(bf16[8,64,256]{2,1,0:T(8,128)(2,1)S(1)} %get-tuple-element.32.refs_0_), channel_id=1, source_target_pairs={{0,4},{2,6},{4,0},{6,2},{8,12},{10,14},{12,8},{14,10},{1,5},{3,7},... | collective-permute-start | bytes 786440 | tf_op jit(solution)/shard_map/ppermute | solution.py:295
  29.6 23.6 %collective-permute-start.3 = (bf16[8,64,256]{2,1,0:T(8,128)(2,1)S(1)}, bf16[8,64,256]{2,1,0:T(8,128)(2,1)S(1)}, u32[]{:S(2)}, u32[]{:S(2)}) collective-permute-start(bf16[8,64,256]{2,1,0:T(8,128)(2,1)S(1)} %get-tuple-element.32.refs_0_), channel_id=1, source_target_pairs={{4,8},{6,10},{8,4},{10,6},{5,9},{7,11},{9,5},{11,7},{20,24},{22,26... | collective-permute-start | bytes 786440 | tf_op jit(solution)/shard_map/ppermute | solution.py:296
  30.3 23.6 %collective-permute-start.11 = (bf16[8,64,256]{2,1,0:T(8,128)(2,1)S(1)}, bf16[8,64,256]{2,1,0:T(8,128)(2,1)S(1)}, u32[]{:S(2)}, u32[]{:S(2)}) collective-permute-start(bf16[8,64,256]{2,1,0:T(8,128)(2,1)S(1)} %get-tuple-element.31.refs_0_), channel_id=1, source_target_pairs={{0,4},{2,6},{4,0},{6,2},{8,12},{10,14},{12,8},{14,10},{1,5},{3,7},... | collective-permute-start | bytes 786440 | tf_op jit(solution)/shard_map/ppermute | solution.py:295
  34.7 19.1 %collective-permute-start.12 = (bf16[8,64,256]{2,1,0:T(8,128)(2,1)S(1)}, bf16[8,64,256]{2,1,0:T(8,128)(2,1)S(1)}, u32[]{:S(2)}, u32[]{:S(2)}) collective-permute-start(bf16[8,64,256]{2,1,0:T(8,128)(2,1)S(1)} %get-tuple-element.31.refs_0_), channel_id=1, source_target_pairs={{4,8},{6,10},{8,4},{10,6},{5,9},{7,11},{9,5},{11,7},{20,24},{22,26... | collective-permute-start | bytes 786440 | tf_op jit(solution)/shard_map/ppermute | solution.py:296
  40.7 0.8 copy-start.13
  40.7 8.8 %collective-permute-start.1 = (s32[1,8]{1,0:T(1,128)S(1)}, s32[1,8]{1,0:T(1,128)S(1)}, u32[]{:S(2)}, u32[]{:S(2)}) collective-permute-start(s32[1,8]{1,0:T(1,128)S(1)} %copy-done.16), channel_id=1, source_target_pairs={{0,2},{2,0},{4,6},{6,4},{8,10},{10,8},{12,14},{14,12},{1,3},{3,1},... | collective-permute-start | bytes 104 | tf_op jit(solution)/shard_map/ppermute | solution.py:333
  41.9 1.7 %copy-start.5 = (bf16[1536,768]{1,0:T(8,128)(2,1)S(1)}, bf16[1536,768]{1,0:T(8,128)(2,1)}, u32[]{:S(2)}) copy-start(bf16[1536,768]{1,0:T(8,128)(2,1)} %wq.1) | copy-start | bytes 7077892
  43.5 1.4 %copy-start.8 = (bf16[1,512,1536]{2,1,0:T(8,128)(2,1)S(1)}, bf16[1,512,1536]{2,1,0:T(8,128)(2,1)}, u32[]{:S(2)}) copy-start(bf16[1,512,1536]{2,1,0:T(8,128)(2,1)} %param.9) | copy-start | bytes 4718596
  45.0 1.4 %copy-start.9 = (bf16[1536,512]{1,0:T(8,128)(2,1)S(1)}, bf16[1536,512]{1,0:T(8,128)(2,1)}, u32[]{:S(2)}) copy-start(bf16[1536,512]{1,0:T(8,128)(2,1)} %wkv.1) | copy-start | bytes 4718596
  49.4 36.9 %copy-start.10 = (bf16[512,768]{1,0:T(8,128)(2,1)}, bf16[512,768]{1,0:T(8,128)(2,1)S(1)}, u32[]{:S(2)}) copy-start(bf16[512,768]{1,0:T(8,128)(2,1)S(1)} %get-tuple-element.14.qa) | copy-start | bytes 2359300
  49.4 38.0 %copy-start.1 = (f32[512,256]{1,0:T(8,128)}, f32[512,256]{1,0:T(8,128)S(1)}, u32[]{:S(2)}) copy-start(f32[512,256]{1,0:T(8,128)S(1)} %get-tuple-element.16.cos) | copy-start | bytes 1572868
  49.4 38.0 %copy-start.3 = (f32[512,256]{1,0:T(8,128)}, f32[512,256]{1,0:T(8,128)S(1)}, u32[]{:S(2)}) copy-start(f32[512,256]{1,0:T(8,128)S(1)} %get-tuple-element.17.sin) | copy-start | bytes 1572868
  49.5 3.6 %collective-permute-start.7 = (s32[2,8]{1,0:T(2,128)S(1)}, s32[2,8]{1,0:T(2,128)S(1)}, u32[]{:S(2)}, u32[]{:S(2)}) collective-permute-start(s32[2,8]{1,0:T(2,128)S(1)} %get-tuple-element.42), channel_id=1, source_target_pairs={{0,16},{16,0},{1,17},{17,1},{2,18},{18,2},{3,19},{19,3},{4,20},{20... | collective-permute-start | bytes 200 | tf_op jit(solution)/shard_map/ppermute | solution.py:334
  53.2 4.0 %collective-permute-start.5 = (bf16[8,64,256]{2,1,0:T(8,128)(2,1)S(1)}, bf16[8,64,256]{2,1,0:T(8,128)(2,1)S(1)}, u32[]{:S(2)}, u32[]{:S(2)}) collective-permute-start(bf16[8,64,256]{2,1,0:T(8,128)(2,1)S(1)} %collective-permute-done.2.refs_1_), channel_id=1, source_target_pairs={{4,8},{6,10},{8,4},{10,6},{5,9},{7,11},{9,5},{11,7},{20,24},{22,26... | collective-permute-start | bytes 786440 | tf_op jit(solution)/shard_map/ppermute | solution.py:298
  53.9 4.6 %collective-permute-start.14 = (bf16[8,64,256]{2,1,0:T(8,128)(2,1)S(1)}, bf16[8,64,256]{2,1,0:T(8,128)(2,1)S(1)}, u32[]{:S(2)}, u32[]{:S(2)}) collective-permute-start(bf16[8,64,256]{2,1,0:T(8,128)(2,1)S(1)} %collective-permute-done.11.refs_1_), channel_id=1, source_target_pairs={{4,8},{6,10},{8,4},{10,6},{5,9},{7,11},{9,5},{11,7},{20,24},{22,26... | collective-permute-start | bytes 786440 | tf_op jit(solution)/shard_map/ppermute | solution.py:298
  54.6 14.5 %collective-permute-start.4 = (bf16[8,64,256]{2,1,0:T(8,128)(2,1)S(1)}, bf16[8,64,256]{2,1,0:T(8,128)(2,1)S(1)}, u32[]{:S(2)}, u32[]{:S(2)}) collective-permute-start(bf16[8,64,256]{2,1,0:T(8,128)(2,1)S(1)} %collective-permute-done.3.refs_2_), channel_id=1, source_target_pairs={{4,0},{6,2},{8,12},{10,14},{5,1},{7,3},{9,13},{11,15},{20,16},{22,... | collective-permute-start | bytes 786440 | tf_op jit(solution)/shard_map/ppermute | solution.py:299
  55.9 26.0 %collective-permute-start.13 = (bf16[8,64,256]{2,1,0:T(8,128)(2,1)S(1)}, bf16[8,64,256]{2,1,0:T(8,128)(2,1)S(1)}, u32[]{:S(2)}, u32[]{:S(2)}) collective-permute-start(bf16[8,64,256]{2,1,0:T(8,128)(2,1)S(1)} %collective-permute-done.12.refs_2_), channel_id=1, source_target_pairs={{4,0},{6,2},{8,12},{10,14},{5,1},{7,3},{9,13},{11,15},{20,16},{22,... | collective-permute-start | bytes 786440 | tf_op jit(solution)/shard_map/ppermute | solution.py:299
  57.2 23.1 %collective-permute-start.6 = (bf16[8,64,256]{2,1,0:T(8,128)(2,1)S(1)}, bf16[8,64,256]{2,1,0:T(8,128)(2,1)S(1)}, u32[]{:S(2)}, u32[]{:S(2)}) collective-permute-start(bf16[8,64,256]{2,1,0:T(8,128)(2,1)S(1)} %collective-permute-done.5.refs_4_), channel_id=1, source_target_pairs={{4,0},{6,2},{8,12},{10,14},{5,1},{7,3},{9,13},{11,15},{20,16},{22,... | collective-permute-start | bytes 786440 | tf_op jit(solution)/shard_map/ppermute | solution.py:299
  58.5 24.6 %collective-permute-start.15 = (bf16[8,64,256]{2,1,0:T(8,128)(2,1)S(1)}, bf16[8,64,256]{2,1,0:T(8,128)(2,1)S(1)}, u32[]{:S(2)}, u32[]{:S(2)}) collective-permute-start(bf16[8,64,256]{2,1,0:T(8,128)(2,1)S(1)} %collective-permute-done.14.refs_4_), channel_id=1, source_target_pairs={{4,0},{6,2},{8,12},{10,14},{5,1},{7,3},{9,13},{11,15},{20,16},{22,... | collective-permute-start | bytes 786440 | tf_op jit(solution)/shard_map/ppermute | solution.py:299
  81.8 4.5 %collective-permute-start.8 = (bf16[16,64,256]{2,1,0:T(8,128)(2,1)S(1)}, bf16[16,64,256]{2,1,0:T(8,128)(2,1)S(1)}, u32[]{:S(2)}, u32[]{:S(2)}) collective-permute-start(bf16[16,64,256]{2,1,0:T(8,128)(2,1)S(1)} %pick_core.2), channel_id=1, source_target_pairs={{0,2},{2,0},{4,6},{6,4},{8,10},{10,8},{12,14},{14,12},{1,3},{3,1},... | collective-permute-start | bytes 1572872 | tf_op jit(solution)/shard_map/ppermute | solution.py:377
  84.6 4.4 %collective-permute-start.16 = (bf16[16,64,256]{2,1,0:T(8,128)(2,1)S(1)}, bf16[16,64,256]{2,1,0:T(8,128)(2,1)S(1)}, u32[]{:S(2)}, u32[]{:S(2)}) collective-permute-start(bf16[16,64,256]{2,1,0:T(8,128)(2,1)S(1)} %pick_core.3), channel_id=1, source_target_pairs={{0,2},{2,0},{4,6},{6,4},{8,10},{10,8},{12,14},{14,12},{1,3},{3,1},... | collective-permute-start | bytes 1572872 | tf_op jit(solution)/shard_map/ppermute | solution.py:377
  84.7 24.7 %collective-permute-start.19 = (bf16[512,512]{1,0:T(8,128)(2,1)}, bf16[512,512]{1,0:T(8,128)(2,1)}, u32[]{:S(2)}, u32[]{:S(2)}) collective-permute-start(bf16[512,512]{1,0:T(8,128)(2,1)} %get-tuple-element.18.kv_own), channel_id=1, source_target_pairs={{0,1},{1,0},{2,3},{3,2},{4,5},{5,4},{6,7},{7,6},{8,9},{9,8},{10,11... | collective-permute-start | bytes 1572872 | tf_op jit(solution)/shard_map/ppermute | solution.py:373
  87.5 9.2 %collective-permute-start.9 = (bf16[8,64,256]{2,1,0:T(8,128)(2,1)S(1)}, bf16[8,64,256]{2,1,0:T(8,128)(2,1)S(1)}, u32[]{:S(2)}, u32[]{:S(2)}) collective-permute-start(bf16[8,64,256]{2,1,0:T(8,128)(2,1)S(1)} %pick_rep.2), channel_id=1, source_target_pairs={{0,16},{16,0},{1,17},{17,1},{2,18},{18,2},{3,19},{19,3},{4,20},{20... | collective-permute-start | bytes 786440 | tf_op jit(solution)/shard_map/ppermute | solution.py:378
  90.2 11.3 %collective-permute-start.17 = (bf16[8,64,256]{2,1,0:T(8,128)(2,1)S(1)}, bf16[8,64,256]{2,1,0:T(8,128)(2,1)S(1)}, u32[]{:S(2)}, u32[]{:S(2)}) collective-permute-start(bf16[8,64,256]{2,1,0:T(8,128)(2,1)S(1)} %pick_rep.3), channel_id=1, source_target_pairs={{0,16},{16,0},{1,17},{17,1},{2,18},{18,2},{3,19},{19,3},{4,20},{20... | collective-permute-start | bytes 786440 | tf_op jit(solution)/shard_map/ppermute | solution.py:378
  97.8 11.6 %collective-permute-start.10 = (bf16[8,64,256]{2,1,0:T(8,128)(2,1)S(1)}, bf16[8,64,256]{2,1,0:T(8,128)(2,1)}, u32[]{:S(2)}, u32[]{:S(2)}) collective-permute-start(bf16[8,64,256]{2,1,0:T(8,128)(2,1)S(1)} %pick_own.2.k_mine), channel_id=1, source_target_pairs={{0,1},{1,0},{2,3},{3,2},{4,5},{5,4},{6,7},{7,6},{8,9},{9,8},{10,11... | collective-permute-start | bytes 786440 | tf_op jit(solution)/shard_map/ppermute | solution.py:380
  102.7 7.9 %collective-permute-start.18 = (bf16[8,64,256]{2,1,0:T(8,128)(2,1)S(1)}, bf16[8,64,256]{2,1,0:T(8,128)(2,1)}, u32[]{:S(2)}, u32[]{:S(2)}) collective-permute-start(bf16[8,64,256]{2,1,0:T(8,128)(2,1)S(1)} %pick_own.3.v_mine), channel_id=1, source_target_pairs={{0,1},{1,0},{2,3},{3,2},{4,5},{5,4},{6,7},{7,6},{8,9},{9,8},{10,11... | collective-permute-start | bytes 786440 | tf_op jit(solution)/shard_map/ppermute | solution.py:380
  104.0 1.7 %copy-start = (bf16[1536,768]{1,0:T(8,128)(2,1)S(1)}, bf16[1536,768]{1,0:T(8,128)(2,1)}, u32[]{:S(2)}) copy-start(bf16[1536,768]{1,0:T(8,128)(2,1)} %all-gather.3.cloned.1.call-done.wq) | copy-start | bytes 7077892
  105.7 1.0 copy-start.2
  106.7 1.0 copy-start.4
  110.6 1.7 %copy-start.6 = (bf16[768,1536]{1,0:T(8,128)(2,1)S(1)}, bf16[768,1536]{1,0:T(8,128)(2,1)}, u32[]{:S(2)}) copy-start(bf16[768,1536]{1,0:T(8,128)(2,1)} %woa.1) | copy-start | bytes 7077892
  112.3 1.7 %copy-start.7 = (bf16[768,1536]{1,0:T(8,128)(2,1)S(1)}, bf16[768,1536]{1,0:T(8,128)(2,1)}, u32[]{:S(2)}) copy-start(bf16[768,1536]{1,0:T(8,128)(2,1)} %all-gather.5.cloned.1.call-done.wob) | copy-start | bytes 7077892
  113.9 1.1 copy-start.11
Sparse Core Ops, SparseCore 0:
  25.0 25.5 all-gather.2
  52.2 24.0 all-gather.4

commit v3 on v2

--- a/solution.py
+++ b/solution.py
@@ -145,88 +145,70 @@
         in_specs=[spec(pltpu.SMEM)] + [spec(pltpu.VMEM)] * len(arrays),
         out_specs=spec(pltpu.VMEM),
         compiler_params=pltpu.CompilerParams(vmem_limit_bytes=12 * 2**20),
-        cost_estimate=pl.CostEstimate(flops=0, bytes_accessed=2 * 2**20, transcendentals=0),
+        cost_estimate=pl.CostEstimate(flops=0, bytes_accessed=1024, transcendentals=0),
         name=name,
     )(where, *arrays)
 
 
-def attend_kernel(
-    head_size,
-    info,
-    qa,
-    qb,
-    k_mine,
-    k_peer,
-    v_mine,
-    v_peer,
-    kv_own,
-    kv_peer,
-    woa,
-    wob,
-    out,
-    keys,
-    vals,
-    wa,
-    wb,
-    mix,
-    ksem,
-    vsem,
-    wsem,
+def start_rows(part, mine, peer, kv_own, kv_peer, lo, dst, sem):
+    pages, prow, head_size = mine.shape
+    rows = kv_own.shape[0]
+    page = 2 * prow
+    window = pages * page
+    cols = pl.ds(lo, head_size)
+    for case in (0, 1):
+
+        @pl.when(part == case)
+        def _():
+            skip = case * rows // page
+            for u in range(skip, pages):
+                for src, side in ((mine, case), (peer, 1 - case)):
+                    to = pl.ds((u - skip) * page + side * prow, prow)
+                    pltpu.make_async_copy(src.at[u], dst.at[to, :], sem).start()
+            if case == 1:
+                to = pl.ds(window - rows, rows)
+                pltpu.make_async_copy(kv_peer.at[:, cols], dst.at[to, :], sem).start()
+            to = pl.ds(window, rows)
+            pltpu.make_async_copy(kv_own.at[:, cols], dst.at[to, :], sem).start()
+
+
+def finish_rows(dst, sem):
+    pltpu.make_async_copy(dst, dst, sem).wait()
+
+
+def weigh_kernel(
+    head_size, info, qa_hbm, qb_hbm, k_mine, k_peer, kv_own, kv_peer, probs, qa, qb, keys, done, ksem, qsem, psem
 ):
-    part = info[0]
-    length = info[1]
     rows, half = qa.shape
-    pages, prow, _ = k_mine.shape
-    page = 2 * prow
-    width = out.shape[1]
+    start_rows(info[0], k_mine, k_peer, kv_own, kv_peer, 0, keys, ksem)
+    loads = [
+        pltpu.make_async_copy(qa_hbm, qa, qsem.at[0]),
+        pltpu.make_async_copy(qb_hbm, qb, qsem.at[1]),
+    ]
+    for c in loads:
+        c.start()
     nheads = half // head_size
-    window = pages * page
-
-    def start(mine, peer, lo, dst, sem):
-        cols = pl.ds(lo, head_size)
-        for case in (0, 1):
-
-            @pl.when(part == case)
-            def _():
-                skip = case * rows // page
-                for u in range(skip, pages):
-                    for src, side in ((mine, case), (peer, 1 - case)):
-                        to = pl.ds((u - skip) * page + side * prow, prow)
-                        pltpu.make_async_copy(src.at[u], dst.at[to, :], sem).start()
-                if case == 1:
-                    to = pl.ds(window - rows, rows)
-                    pltpu.make_async_copy(kv_peer.at[:, cols], dst.at[to, :], sem).start()
-                to = pl.ds(window, rows)
-                pltpu.make_async_copy(kv_own.at[:, cols], dst.at[to, :], sem).start()
-
-    def finish(dst, sem):
-        pltpu.make_async_copy(dst, dst, sem).wait()
-
-    start(k_mine, k_peer, 0, keys, ksem)
-    start(v_mine, v_peer, head_size, vals, vsem)
-    weights = [
-        pltpu.make_async_copy(woa, wa, wsem.at[0]),
-        pltpu.make_async_copy(wob, wb, wsem.at[1]),
-    ]
-    for c in weights:
-        c.start()
-
-    tile = min(256, rows)
-    span = window + tile
+    span = probs.shape[2]
+    tile = span + rows - keys.shape[0]
     row_id = lax.broadcasted_iota(jnp.int32, (tile, tile), 0)
     col_id = lax.broadcasted_iota(jnp.int32, (tile, tile), 1)
     first_seen = col_id >= row_id + 1
     last_seen = col_id <= row_id
     factor = math.log2(math.e) / math.sqrt(head_size)
-    finish(keys, ksem)
+    for c in loads:
+        c.wait()
+    finish_rows(keys, ksem)
+    stores = []
     for i in range(rows // tile):
         at = pl.ds(i * tile, tile)
         for n, q in enumerate((qa, qb)):
             for h in range(nheads):
-                cols = slice(h * head_size, (h + 1) * head_size)
                 kk = keys[pl.ds(i * tile, span), :]
                 s = lax.dot_general(
-                    q[at, cols], kk, (((1,), (1,)), ((), ())), preferred_element_type=F32
+                    q[at, h * head_size : (h + 1) * head_size],
+                    kk,
+                    (((1,), (1,)), ((), ())),
+                    preferred_element_type=F32,
                 )
                 s = jnp.concatenate(
                     [
@@ -239,64 +221,127 @@
                 top = jnp.max(s, axis=-1, keepdims=True)
                 e = jnp.exp2((s - top) * factor)
                 total = jnp.sum(e, axis=-1, keepdims=True)
-                if i == 0 and n == 0 and h == 0:
-                    finish(vals, vsem)
-                vv = vals[pl.ds(i * tile, span), :]
-                m = jnp.dot(e.astype(BF16), vv, preferred_element_type=F32)
-                mix[n, at, cols] = (m / total).astype(BF16)
+                m = len(stores)
+                done[m] = (e * (1.0 / total)).astype(BF16)
+                stores.append(
+                    pltpu.make_async_copy(done.at[m], probs.at[n * nheads + h, at, :], psem.at[m])
+                )
+                stores[m].start()
+    for c in stores:
+        c.wait()
+
+
+def weigh(info, qa, qb, k_mine, k_peer, kv_own, kv_peer):
+    rows, half = qa.shape
+    head_size = k_mine.shape[2]
+    heads = 2 * half // head_size
+    window = k_mine.shape[0] * k_mine.shape[1] * 2
+    span = window + min(256, rows)
+    chunks = heads * rows // (span - window)
+    return pl.pallas_call(
+        functools.partial(weigh_kernel, head_size),
+        out_shape=jax.ShapeDtypeStruct((heads, rows, span), BF16),
+        in_specs=[spec(pltpu.SMEM)] + [spec(ANY)] * 6,
+        out_specs=spec(ANY),
+        scratch_shapes=[
+            pltpu.VMEM((rows, half), BF16),
+            pltpu.VMEM((rows, half), BF16),
+            pltpu.VMEM((window + rows, head_size), BF16),
+            pltpu.VMEM((chunks, span - window, span), BF16),
+            pltpu.SemaphoreType.DMA,
+            pltpu.SemaphoreType.DMA((2,)),
+            pltpu.SemaphoreType.DMA((chunks,)),
+        ],
+        compiler_params=pltpu.CompilerParams(vmem_limit_bytes=56 * 2**20),
+        cost_estimate=pl.CostEstimate(
+            flops=4 * rows * half * span,
+            bytes_accessed=12 * 2**20,
+            transcendentals=rows * heads * span,
+        ),
+        name="scores_softmax",
+    )(info, qa, qb, k_mine, k_peer, kv_own, kv_peer)
+
+
+def out_kernel(
+    info, probs, v_mine, v_peer, kv_own, kv_peer, woa, wob, out, vals, pv, wa, wb, mix, vsem, psem, wsem
+):
+    part = info[0]
+    length = info[1]
+    heads, rows, span = probs.shape
+    head_size = vals.shape[1]
+    width = out.shape[1]
+    nheads = heads // 2
+    tile = span + rows - vals.shape[0]
+    start_rows(part, v_mine, v_peer, kv_own, kv_peer, head_size, vals, vsem)
+    order = [(i, h) for i in range(rows // tile) for h in range(heads)]
+    loads = [
+        pltpu.make_async_copy(probs.at[h, pl.ds(i * tile, tile), :], pv.at[m], psem.at[m])
+        for m, (i, h) in enumerate(order)
+    ]
+    for c in loads:
+        c.start()
+    weights = [
+        pltpu.make_async_copy(woa, wa, wsem.at[0]),
+        pltpu.make_async_copy(wob, wb, wsem.at[1]),
+    ]
+    for c in weights:
+        c.start()
+    finish_rows(vals, vsem)
+    for m, (i, h) in enumerate(order):
+        vv = vals[pl.ds(i * tile, span), :]
+        loads[m].wait()
+        mixed = jnp.dot(pv[m], vv, preferred_element_type=F32).astype(BF16)
+        lo = h % nheads * head_size
+        mix[h // nheads, pl.ds(i * tile, tile), lo : lo + head_size] = mixed
     for c in weights:
         c.wait()
     for i in range(rows // tile):
         at = pl.ds(i * tile, tile)
         row = part * rows + i * tile + lax.broadcasted_iota(jnp.int32, (tile, 1), 0)
         live = row < length
-        for j in range(width // 512):
-            cols = slice(j * 512, (j + 1) * 512)
+        for lo in range(0, width, 512):
+            cols = slice(lo, lo + 512)
             a = jnp.dot(mix[0, at, :], wa[:, cols], preferred_element_type=F32)
             b = jnp.dot(mix[1, at, :], wb[:, cols], preferred_element_type=F32)
             both = a.astype(BF16).astype(F32) + b.astype(BF16).astype(F32)
             out[at, cols] = jnp.where(live, both, 0.0).astype(BF16)
 
 
-def attend_pages(info, qa, qb, k_mine, k_peer, v_mine, v_peer, kv_own, kv_peer, woa, wob):
-    rows, half = qa.shape
-    width = woa.shape[1]
-    head_size = k_mine.shape[2]
-    window = k_mine.shape[0] * k_mine.shape[1] * 2
+def mix_and_out(info, probs, v_mine, v_peer, kv_own, kv_peer, woa, wob):
+    heads, rows, span = probs.shape
+    half, width = woa.shape
+    head_size = v_mine.shape[2]
+    window = v_mine.shape[0] * v_mine.shape[1] * 2
+    chunks = heads * rows // (span - window)
     return pl.pallas_call(
-        functools.partial(attend_kernel, head_size),
+        out_kernel,
         out_shape=jax.ShapeDtypeStruct((rows, width), BF16),
-        in_specs=[spec(pltpu.SMEM)] + [spec(pltpu.VMEM)] * 2 + [spec(ANY)] * 8,
+        in_specs=[spec(pltpu.SMEM)] + [spec(ANY)] * 7,
         out_specs=spec(pltpu.VMEM),
         scratch_shapes=[
             pltpu.VMEM((window + rows, head_size), BF16),
-            pltpu.VMEM((window + rows, head_size), BF16),
+            pltpu.VMEM((chunks, span - window, span), BF16),
             pltpu.VMEM(woa.shape, BF16),
             pltpu.VMEM(wob.shape, BF16),
             pltpu.VMEM((2, rows, half), BF16),
             pltpu.SemaphoreType.DMA,
-            pltpu.SemaphoreType.DMA,
+            pltpu.SemaphoreType.DMA((chunks,)),
             pltpu.SemaphoreType.DMA((2,)),
         ],
-        compiler_params=pltpu.CompilerParams(vmem_limit_bytes=28 * 2**20),
+        compiler_params=pltpu.CompilerParams(vmem_limit_bytes=56 * 2**20),
         cost_estimate=pl.CostEstimate(
-            flops=4 * rows * 2 * half * (window + 256) + 4 * rows * half * width,
-            bytes_accessed=12 * 2**20,
-            transcendentals=rows * 6 * (window + 256),
+            flops=4 * rows * half * span + 4 * rows * half * width,
+            bytes_accessed=16 * 2**20,
+            transcendentals=0,
         ),
-        name="attend_and_out",
-    )(info, qa, qb, k_mine, k_peer, v_mine, v_peer, kv_own, kv_peer, woa, wob)
-
-
-def line_gather(x, swap_at, after):
+        name="mix_and_out",
+    )(info, probs, v_mine, v_peer, kv_own, kv_peer, woa, wob)
+
+
+def first_hop(x, swap_at):
     pairs = swap_at([(0, 1), (1, 0), (2, 3), (3, 2)])
     middle = swap_at([(1, 2), (2, 1)])
-    outward = swap_at([(1, 0), (2, 3)])
-    first = lax.ppermute(x, "dp", pairs)
-    near = lax.ppermute(x, "dp", middle)
-    first, near, _ = lax.optimization_barrier((first, near, after))
-    far = lax.ppermute(first, "dp", middle)
-    return [x, first, near, lax.ppermute(near, "dp", outward), far, lax.ppermute(far, "dp", outward)]
+    return lax.ppermute(x, "dp", pairs), lax.ppermute(x, "dp", middle)
 
 
 def pair_shards(tokens, norm_gain, w_query, w_keyval, w_out, kv_pages, page_table, lengths, starts):
@@ -315,21 +360,31 @@
     def both_cores(perm):
         return [(2 * a + c, 2 * b + c) for a, b in perm for c in (0, 1)]
 
+    k_pages = kv_pages[:, :, :head_size]
+    v_pages = kv_pages[:, :, head_size:]
+    k_first = first_hop(k_pages, both_cores)
+    v_first = first_hop(v_pages, both_cores)
+
     quarter = rep * 2 + core
     groups = [[r * ndp + 2 * z + c for r in (0, 1) for c in (0, 1)] for z in range(ndp // 2)]
 
-    def other_half(w):
+    def peer_quarter(w):
         deep = w.shape[0] // 4
-        piece = lax.dynamic_slice_in_dim(w, quarter * deep, deep, 0)
-        piece = lax.ppermute(piece, "tensor", swap)
-        return lax.all_gather(
-            piece, ("rep", "dp"), axis=0, tiled=True, axis_index_groups=groups
-        )
-
-    wq_other = other_half(w_query)
-    wo_other = other_half(w_out)
-
-    table = page_table
+        return lax.ppermute(lax.dynamic_slice_in_dim(w, quarter * deep, deep, 0), "tensor", swap)
+
+    def share(piece):
+        return lax.all_gather(piece, ("rep", "dp"), axis=0, tiled=True, axis_index_groups=groups)
+
+    wq_piece = peer_quarter(w_query)
+
+    step = 32
+    cos_t, sin_t = rotation_tables(starts[0] + part * rows, rows, step, head_size)
+    normed, qa, kv_own, cos, sin = project(
+        tokens[0], norm_gain, w_query, w_keyval, cos_t, sin_t, head_size, step
+    )
+    kv_peer = lax.ppermute(kv_own, "tensor", swap)
+
+    table, kv_own = lax.optimization_barrier((page_table, kv_own))
     chip_tables = jnp.concatenate([table, lax.ppermute(table, "dp", cores)], axis=0)
     peer_tables = lax.ppermute(chip_tables, "rep", swap)
     per_rep = held * ndp
@@ -365,28 +420,39 @@
         ]
     )
 
-    step = 32
-    cos_t, sin_t = rotation_tables(starts[0] + part * rows, rows, step, head_size)
-    normed, qa, kv_own, cos, sin = project(
-        tokens[0], norm_gain, w_query, w_keyval, cos_t, sin_t, head_size, step
-    )
-    kv_peer = lax.ppermute(kv_own, "tensor", swap)
-
-    def window_half(x):
-        line = line_gather(x, both_cores, kv_own)
-        given = lax.ppermute(collect(where_core, line, "pick_core"), "dp", cores)
-        came = lax.ppermute(collect(where_peer, line + [given], "pick_rep"), "rep", swap)
-        mine = collect(where_own, line + [given, came], "pick_own")
-        return mine, lax.ppermute(mine, "tensor", swap)
-
-    k_mine, k_peer = window_half(kv_pages[:, :, :head_size])
-    v_mine, v_peer = window_half(kv_pages[:, :, head_size:])
+    middle = both_cores([(1, 2), (2, 1)])
+    outward = both_cores([(1, 0), (2, 3)])
+    kf, kn, _ = lax.optimization_barrier((*k_first, kv_own))
+    k_near = lax.ppermute(kn, "dp", outward)
+    k_far = lax.ppermute(kf, "dp", middle)
+    wq_piece, w_out_late, _ = lax.optimization_barrier((wq_piece, w_out, kf))
+    vf, vn = v_first
+    v_far = lax.ppermute(vf, "dp", middle)
+    v_near = lax.ppermute(vn, "dp", outward)
+    wq_other = share(wq_piece)
+    wo_piece = peer_quarter(w_out_late)
+    k_far, k_near, v_far, v_near = lax.optimization_barrier((k_far, k_near, v_far, v_near))
+    k_end = lax.ppermute(k_far, "dp", outward)
+    v_end = lax.ppermute(v_far, "dp", outward)
+    k_end, wo_piece = lax.optimization_barrier((k_end, wo_piece))
+    wo_other = share(wo_piece)
+    k_line = [k_pages, kf, kn, k_near, k_far, k_end]
+    k_given = lax.ppermute(collect(where_core, k_line, "pick_core"), "dp", cores)
+    k_given, v_end, kv_peer = lax.optimization_barrier((k_given, v_end, kv_peer))
+    v_line = [v_pages, vf, vn, v_near, v_far, v_end]
+    v_given = lax.ppermute(collect(where_core, v_line, "pick_core"), "dp", cores)
+    k_came = lax.ppermute(collect(where_peer, k_line + [k_given], "pick_rep"), "rep", swap)
+    k_came, v_given = lax.optimization_barrier((k_came, v_given))
+    v_came = lax.ppermute(collect(where_peer, v_line + [v_given], "pick_rep"), "rep", swap)
+    k_mine = collect(where_own, k_line + [k_given, k_came], "pick_own")
+    k_peer = lax.ppermute(k_mine, "tensor", swap)
+    v_mine = collect(where_own, v_line + [v_given, v_came], "pick_own")
+    v_peer = lax.ppermute(v_mine, "tensor", swap)
 
     qb = project_other(normed, wq_other, cos, sin, head_size)
     info = jnp.stack([part, lengths[0]]).astype(jnp.int32)
-    return attend_pages(
-        info, qa, qb, k_mine, k_peer, v_mine, v_peer, kv_own, kv_peer, w_out, wo_other
-    )[None]
+    probs = weigh(info, qa, qb, k_mine, k_peer, kv_own, kv_peer)
+    return mix_and_out(info, probs, v_mine, v_peer, kv_own, kv_peer, w_out, wo_other)[None]
 
 
 def rotate_pairs(values, positions, columns_from, head_size):

time: 134 us -> 135 us (level)
  waiting for transfers between devices: 51.8 us -> 41 us
  Pallas kernels: 24.1 us -> 32.6 us
  local copies, waits for them, and re-layouts: 16.7 us -> 18.4 us
    ppermute x18, waiting for transfers between devices: 49.7 us -> 38.3 us  [the longest x1 9.37 us: pair_shards(): lax.ppermute(collect(where_peer, k_line + [k_given], 'pick_rep'), 'rep',...]
    pallas_call x1 -> x2, Pallas kernels: 11.8 us -> 20.4 us  [the longest x1 12.1 us: mix_and_out(): pl.pallas_call(out_kernel, out_shape=jax.ShapeDtypeStruct((rows, width),...]
    ppermute x1, waiting for transfers between devices: 2.06 us -> 0.01 us  [pair_shards(): peer_tables = lax.ppermute(chip_tables, 'rep', swap)]
    ppermute x1, waiting for transfers between devices: 0.01 us -> 1.48 us  [pair_shards(): kv_peer = lax.ppermute(kv_own, 'tensor', swap)]
    ppermute x18, starting transfers between devices: 22.2 us -> 23.6 us  [the longest x4 8.59 us: first_hop(): return (lax.ppermute(x, 'dp', pairs), lax.ppermute(x, 'dp', middle))]
    unnamed x34 -> x40, local copies, waits for them, and re-layouts: 14.4 us -> 14.3 us
  transfers between devices with their start and end apart: 23 -> 23, of which waited for: 9 -> 9; matrix products, arithmetic and copies ran while one was open for 1% -> 3% of each run, Pallas kernels for 9% -> 15%
where the time goes in v3:
time: 135 us; the launch traced here: 134 us
  waiting for transfers between devices  41 us (30%)
  Pallas kernels  32.6 us (24%)
  starting transfers between devices  25.8 us (19%)
  local copies, waits for them, and re-layouts  18.4 us (14%)
  between operations  15.2 us (11%)
    unnamed x40, local copies, waits for them, and re-layouts  14.3 us
    pallas_call x1, Pallas kernels, mix_and_out(): pl.pallas_call(out_kernel, out_shape=jax.ShapeDtypeStruct((rows, width),...  12.1 us
    ppermute x1, waiting for transfers between devices, pair_shards(): lax.ppermute(collect(where_peer, k_line + [k_given], 'pick_rep'), 'rep',...  9.37 us
    ppermute x1, waiting for transfers between devices, pair_shards(): k_near = lax.ppermute(kn, 'dp', outward)  9.34 us
    ppermute x4, starting transfers between devices, first_hop(): return (lax.ppermute(x, 'dp', pairs), lax.ppermute(x, 'dp', middle))  8.59 us
    pallas_call x1, Pallas kernels, weigh(): pl.pallas_call(functools.partial(weigh_kernel, head_size), out_shape=jax....  8.37 us
    ppermute x1, waiting for transfers between devices, pair_shards(): v_end = lax.ppermute(v_far, 'dp', outward)  7.81 us
    pallas_call x6, Pallas kernels, collect(): pl.pallas_call(collect_kernel, out_shape=jax.ShapeDtypeStruct(shape, arra...  7.76 us
  transfers between devices with their start and end apart: 23, of which 9 were waited for; matrix products, arithmetic and copies ran while one was open for 3% of the time, Pallas kernels for 15%

profile of v3, /device:TPU:0, one launch (start us, length us, event | category | flops | bytes accessed | tf_op | source)
XLA Modules:
  0.0 134.1 jit_solution(7518829787760131712)
XLA Ops:
  6.5 1.1 fusion.13
  7.6 3.1 %collective-permute-start.1 = (bf16[8,64,256]{2,1,0:T(8,128)(2,1)S(1)}, bf16[8,64,256]{2,1,0:T(8,128)(2,1)S(1)}, u32[]{:S(2)}, u32[]{:S(2)}) collective-permute-start(bf16[8,64,256]{2,1,0:T(8,128)(2,1)S(1)} %get-tuple-element.58.refs_0_), channel_id=1, source_target_pairs={{0,4},{2,6},{4,0},{6,2},{8,12},{10,14},{12,8},{14,10},{1,5},{3,7},... | collective-permute-start | bytes 786440 | tf_op jit(solution)/shard_map/ppermute | solution.py:344
  10.7 0.7 collective-permute-start.2
  11.4 1.1 constant_dynamic-slice_fusion.1
  12.5 1.6 %collective-permute-start = (bf16[384,768]{1,0:T(8,128)(2,1)S(1)}, bf16[384,768]{1,0:T(8,128)(2,1)S(1)}, u32[]{:S(2)}, u32[]{:S(2)}) collective-permute-start(bf16[384,768]{1,0:T(8,128)(2,1)S(1)} %constant_dynamic-slice_fusion.1), channel_id=1, source_target_pairs={{0,1},{1,0},{2,3},{3,2},{4,5},{5,4},{6,7},{7,6},{8,9},{9,8},{10,11... | collective-permute-start | bytes 1769480 | tf_op jit(solution)/shard_map/ppermute | solution.py:373
  14.8 0.1 pad_maximum_fusion
  14.9 0.3 fusion
  15.2 1.7 %copy-done.12 = bf16[1536,768]{1,0:T(8,128)(2,1)S(1)} copy-done((bf16[1536,768]{1,0:T(8,128)(2,1)S(1)}, bf16[1536,768]{1,0:T(8,128)(2,1)}, u32[]{:S(2)}) %copy-start.12) | copy-done | bytes 2359320
  16.8 1.4 %copy-done.13 = bf16[1,512,1536]{2,1,0:T(8,128)(2,1)S(1)} copy-done((bf16[1,512,1536]{2,1,0:T(8,128)(2,1)S(1)}, bf16[1,512,1536]{2,1,0:T(8,128)(2,1)}, u32[]{:S(2)}) %copy-start.13) | copy-done | bytes 1572888
  18.2 1.4 %copy-done.14 = bf16[1536,512]{1,0:T(8,128)(2,1)S(1)} copy-done((bf16[1536,512]{1,0:T(8,128)(2,1)S(1)}, bf16[1536,512]{1,0:T(8,128)(2,1)}, u32[]{:S(2)}) %copy-start.14) | copy-done | bytes 1572888
  19.6 2.7 %project_own.1 = (bf16[512,1536]{1,0:T(8,128)(2,1)S(1)}, bf16[512,768]{1,0:T(8,128)(2,1)S(1)}, bf16[512,512]{1,0:T(8,128)(2,1)S(1)}, f32[512,256]{1,0:T(8,128)S(1)}, f32[512,256]{1,0:T(8,128)S(1)}) custom-call(bf16[512,1536]{1,0:T(8,128)(2,1)S(1)} %bitcast.17, f32[1,1536]{1,0:T(1,128)S(1)} %reshape.40.gain, bf16[1536,768]{1,0:T(8,128)(2,1)S(1)} %copy-done.12, ...), custom_call_target="tpu_custom_call" | custom-call | flops 2013265920 | bytes 10485760 | tf_op jit(solution)/shard_map/project_own/pallas_call | solution.py:75
  22.4 1.1 copy-done.2
  23.5 0.9 copy-done.5
  24.4 0.8 copy-done.7
  25.2 0.8 copy-done.9
  26.0 1.4 %collective-permute-done = bf16[384,768]{1,0:T(8,128)(2,1)S(1)} collective-permute-done((bf16[384,768]{1,0:T(8,128)(2,1)S(1)}, bf16[384,768]{1,0:T(8,128)(2,1)S(1)}, u32[]{:S(2)}, u32[]{:S(2)}) %collective-permute-start) | collective-permute-done | bytes 589856 | tf_op jit(solution)/shard_map/ppermute | solution.py:373
  27.4 0.8 copy-done.15
  28.2 0.0 all-gather.3.cloned.1.call-update
  28.2 0.0 all-gather.5.cloned.1.call-start
  28.3 4.2 %collective-permute-start.6 = (bf16[8,64,256]{2,1,0:T(8,128)(2,1)S(1)}, bf16[8,64,256]{2,1,0:T(8,128)(2,1)S(1)}, u32[]{:S(2)}, u32[]{:S(2)}) collective-permute-start(bf16[8,64,256]{2,1,0:T(8,128)(2,1)S(1)} %get-tuple-element.57.refs_0_), channel_id=1, source_target_pairs={{0,4},{2,6},{4,0},{6,2},{8,12},{10,14},{12,8},{14,10},{1,5},{3,7},... | collective-permute-start | bytes 786440 | tf_op jit(solution)/shard_map/ppermute | solution.py:344
  32.5 0.7 collective-permute-start.8
  33.1 1.9 %constant_dynamic-slice_fusion = bf16[192,1536]{1,0:T(8,128)(2,1)} fusion(bf16[768,1536]{1,0:T(8,128)(2,1)} %woa.1, s32[]{:T(128)S(6)} %select_n.155), kind=kLoop, calls=%fused_computation.82 | loop fusion | bytes 1179652 | tf_op jit(solution)/shard_map/dynamic_slice | solution.py:373
  35.1 1.5 %collective-permute-start.11 = (bf16[192,1536]{1,0:T(8,128)(2,1)}, bf16[192,1536]{1,0:T(8,128)(2,1)}, u32[]{:S(2)}, u32[]{:S(2)}) collective-permute-start(bf16[192,1536]{1,0:T(8,128)(2,1)} %constant_dynamic-slice_fusion), channel_id=1, source_target_pairs={{0,1},{1,0},{2,3},{3,2},{4,5},{5,4},{6,7},{7,6},{8,9},{9,8},{10,11... | collective-permute-start | bytes 1769480 | tf_op jit(solution)/shard_map/ppermute | solution.py:373
  36.6 0.7 collective-permute-start.4
  37.3 1.3 collective-permute-start.5
  38.6 0.7 collective-permute-start.7
  39.3 1.3 collective-permute-start.9
  40.6 9.3 %collective-permute-done.5.refs_3_ = bf16[8,64,256]{2,1,0:T(8,128)(2,1)S(1)} collective-permute-done((bf16[8,64,256]{2,1,0:T(8,128)(2,1)S(1)}, bf16[8,64,256]{2,1,0:T(8,128)(2,1)S(1)}, u32[]{:S(2)}, u32[]{:S(2)}) %collective-permute-start.5) | collective-permute-done | bytes 262176 | tf_op jit(solution)/shard_map/ppermute | solution.py:426
  49.9 3.1 %collective-permute-done.9.refs_3_ = bf16[8,64,256]{2,1,0:T(8,128)(2,1)S(1)} collective-permute-done((bf16[8,64,256]{2,1,0:T(8,128)(2,1)S(1)}, bf16[8,64,256]{2,1,0:T(8,128)(2,1)S(1)}, u32[]{:S(2)}, u32[]{:S(2)}) %collective-permute-start.9) | collective-permute-done | bytes 262176 | tf_op jit(solution)/shard_map/ppermute | solution.py:431
  53.0 1.3 collective-permute-start.10
  54.3 0.6 collective-permute-start.15
  54.9 1.1 collective-permute-done.3
  56.0 1.6 %collective-permute-start.12 = (s32[2,8]{1,0:T(2,128)S(1)}, s32[2,8]{1,0:T(2,128)S(1)}, u32[]{:S(2)}, u32[]{:S(2)}) collective-permute-start(s32[2,8]{1,0:T(2,128)S(1)} %get-tuple-element.68), channel_id=1, source_target_pairs={{0,16},{16,0},{1,17},{17,1},{2,18},{18,2},{3,19},{19,3},{4,20},{20... | collective-permute-start | bytes 200 | tf_op jit(solution)/shard_map/ppermute | solution.py:389
  57.6 3.7 %collective-permute-done.10.refs_5_ = bf16[8,64,256]{2,1,0:T(8,128)(2,1)S(1)} collective-permute-done((bf16[8,64,256]{2,1,0:T(8,128)(2,1)S(1)}, bf16[8,64,256]{2,1,0:T(8,128)(2,1)S(1)}, u32[]{:S(2)}, u32[]{:S(2)}) %collective-permute-start.10) | collective-permute-done | bytes 262176 | tf_op jit(solution)/shard_map/ppermute | solution.py:435
  61.3 0.0 all-gather.5.cloned.1.call-update
  61.5 0.1 add_bitcast_fusion
  61.5 0.1 add_bitcast_fusion.1
  61.6 1.5 %pick_core.2 = bf16[16,64,256]{2,1,0:T(8,128)(2,1)S(1)} custom-call(s32[2,16]{1,0:T(2,128)S(1)} %pad_add_fusion.2.where, bf16[8,64,256]{2,1,0:T(8,128)(2,1)S(1)} %get-tuple-element.58.refs_0_, bf16[8,64,256]{2,1,0:T(8,128)(2,1)S(1)} %collective-permute-done.1.refs_1_, bf16[8,64,256]{2,1,0:T(8,128)(2,1)S(1)} %collective-permute-done.2.refs_2_, ...), custom_call_target="tpu_custom_call" | custom-call | bytes 1024 | tf_op jit(solution)/shard_map/pick_core/pallas_call | solution.py:142
  63.1 0.1 collective-permute-start.13
  63.2 1.3 collective-permute-start.14
  64.5 1.5 %collective-permute-done.15.kv_peer = bf16[512,512]{1,0:T(8,128)(2,1)} collective-permute-done((bf16[512,512]{1,0:T(8,128)(2,1)S(1)}, bf16[512,512]{1,0:T(8,128)(2,1)}, u32[]{:S(2)}, u32[]{:S(2)}) %collective-permute-start.15) | collective-permute-done | bytes 524320 | tf_op jit(solution)/shard_map/ppermute | solution.py:385
  66.0 7.8 %collective-permute-done.14.refs_5_ = bf16[8,64,256]{2,1,0:T(8,128)(2,1)S(1)} collective-permute-done((bf16[8,64,256]{2,1,0:T(8,128)(2,1)S(1)}, bf16[8,64,256]{2,1,0:T(8,128)(2,1)S(1)}, u32[]{:S(2)}, u32[]{:S(2)}) %collective-permute-start.14) | collective-permute-done | bytes 262176 | tf_op jit(solution)/shard_map/ppermute | solution.py:436
  73.8 1.5 %pick_core.3 = bf16[16,64,256]{2,1,0:T(8,128)(2,1)S(1)} custom-call(s32[2,16]{1,0:T(2,128)S(1)} %pad_add_fusion.2.where, bf16[8,64,256]{2,1,0:T(8,128)(2,1)S(1)} %get-tuple-element.57.refs_0_, bf16[8,64,256]{2,1,0:T(8,128)(2,1)S(1)} %collective-permute-done.6.refs_1_, bf16[8,64,256]{2,1,0:T(8,128)(2,1)S(1)} %collective-permute-done.8.refs_2_, ...), custom_call_target="tpu_custom_call" | custom-call | bytes 1024 | tf_op jit(solution)/shard_map/pick_core/pallas_call | solution.py:142
  75.4 0.1 collective-permute-start.17
  75.4 1.1 pick_rep.2
  76.6 1.6 %collective-permute-start.16 = (bf16[8,64,256]{2,1,0:T(8,128)(2,1)S(1)}, bf16[8,64,256]{2,1,0:T(8,128)(2,1)S(1)}, u32[]{:S(2)}, u32[]{:S(2)}) collective-permute-start(bf16[8,64,256]{2,1,0:T(8,128)(2,1)S(1)} %pick_rep.2), channel_id=1, source_target_pairs={{0,16},{16,0},{1,17},{17,1},{2,18},{18,2},{3,19},{19,3},{4,20},{20... | collective-permute-start | bytes 786440 | tf_op jit(solution)/shard_map/ppermute | solution.py:444
  78.1 9.4 %collective-permute-done.16.refs_7_ = bf16[8,64,256]{2,1,0:T(8,128)(2,1)S(1)} collective-permute-done((bf16[8,64,256]{2,1,0:T(8,128)(2,1)S(1)}, bf16[8,64,256]{2,1,0:T(8,128)(2,1)S(1)}, u32[]{:S(2)}, u32[]{:S(2)}) %collective-permute-start.16) | collective-permute-done | bytes 262176 | tf_op jit(solution)/shard_map/ppermute | solution.py:444
  87.5 1.1 pick_rep.3
  88.6 0.4 collective-permute-start.19
  89.0 1.2 pick_own.2.k_mine
  90.2 1.8 %collective-permute-start.18 = (bf16[8,64,256]{2,1,0:T(8,128)(2,1)S(1)}, bf16[8,64,256]{2,1,0:T(8,128)(2,1)S(1)}, u32[]{:S(2)}, u32[]{:S(2)}) collective-permute-start(bf16[8,64,256]{2,1,0:T(8,128)(2,1)S(1)} %pick_own.2.k_mine), channel_id=1, source_target_pairs={{0,1},{1,0},{2,3},{3,2},{4,5},{5,4},{6,7},{7,6},{8,9},{9,8},{10,11... | collective-permute-start | bytes 786440 | tf_op jit(solution)/shard_map/ppermute | solution.py:448
  92.6 0.6 pad_add_fusion.4.info
  93.2 3.6 %collective-permute-done.19.refs_7_ = bf16[8,64,256]{2,1,0:T(8,128)(2,1)S(1)} collective-permute-done((bf16[8,64,256]{2,1,0:T(8,128)(2,1)S(1)}, bf16[8,64,256]{2,1,0:T(8,128)(2,1)S(1)}, u32[]{:S(2)}, u32[]{:S(2)}) %collective-permute-start.19) | collective-permute-done | bytes 262176 | tf_op jit(solution)/shard_map/ppermute | solution.py:446
  96.8 1.3 %pick_own.3.v_mine = bf16[8,64,256]{2,1,0:T(8,128)(2,1)S(1)} custom-call(s32[2,8]{1,0:T(2,128)S(1)} %pad_add_fusion.1.where, bf16[8,64,256]{2,1,0:T(8,128)(2,1)S(1)} %get-tuple-element.57.refs_0_, bf16[8,64,256]{2,1,0:T(8,128)(2,1)S(1)} %collective-permute-done.6.refs_1_, bf16[8,64,256]{2,1,0:T(8,128)(2,1)S(1)} %collective-permute-done.8.refs_2_, ...), custom_call_target="tpu_custom_call" | custom-call | bytes 1024 | tf_op jit(solution)/shard_map/pick_own/pallas_call | solution.py:142
  98.2 1.5 %collective-permute-start.20 = (bf16[8,64,256]{2,1,0:T(8,128)(2,1)S(1)}, bf16[8,64,256]{2,1,0:T(8,128)(2,1)S(1)}, u32[]{:S(2)}, u32[]{:S(2)}) collective-permute-start(bf16[8,64,256]{2,1,0:T(8,128)(2,1)S(1)} %pick_own.3.v_mine), channel_id=1, source_target_pairs={{0,1},{1,0},{2,3},{3,2},{4,5},{5,4},{6,7},{7,6},{8,9},{9,8},{10,11... | collective-permute-start | bytes 786440 | tf_op jit(solution)/shard_map/ppermute | solution.py:450
  99.8 1.7 %copy-done.1 = bf16[1536,768]{1,0:T(8,128)(2,1)S(1)} copy-done((bf16[1536,768]{1,0:T(8,128)(2,1)S(1)}, bf16[1536,768]{1,0:T(8,128)(2,1)}, u32[]{:S(2)}) %copy-start.1) | copy-done | bytes 2359320
  101.4 1.4 %copy-done.3 = bf16[512,1536]{1,0:T(8,128)(2,1)S(1)} copy-done((bf16[512,1536]{1,0:T(8,128)(2,1)S(1)}, bf16[512,1536]{1,0:T(8,128)(2,1)}, u32[]{:S(2)}) %copy-start.3) | copy-done | bytes 1572888
  102.8 1.7 %project_other.1.qb_hbm = bf16[512,768]{1,0:T(8,128)(2,1)S(1)} custom-call(bf16[512,1536]{1,0:T(8,128)(2,1)S(1)} %copy-done.3, bf16[1536,768]{1,0:T(8,128)(2,1)S(1)} %copy-done.1, f32[512,256]{1,0:T(8,128)S(1)} %copy-done.8, f32[512,256]{1,0:T(8,128)S(1)} %copy-done.10), custom_call_target="tpu_custom_call" | custom-call | flops 1207959552 | bytes 6291456 | tf_op jit(solution)/shard_map/project_other/pallas_call | solution.py:111
  104.5 0.9 copy-done
  105.4 0.7 copy-done.16
  106.1 8.4 %scores_softmax.1.probs = bf16[6,512,1280]{2,1,0:T(8,128)(2,1)} custom-call(s32[2]{0:T(128)} %pad_add_fusion.4.info, bf16[512,768]{1,0:T(8,128)(2,1)} %copy-done.5, bf16[512,768]{1,0:T(8,128)(2,1)} %copy-done, bf16[8,64,256]{2,1,0:T(8,128)(2,1)} %copy-done.4, bf16[8,64,256]{2,1,0:T(8,128)(2,1)} %copy-done.16, bf16[512,512]{1,0:T(8,128)(2,1)} %copy-done.6, ...), custom_call_target="tpu_custom_call" | custom-call | flops 2013265920 | bytes 12582912 | tf_op jit(solution)/shard_map/scores_softmax/pallas_call | solution.py:241
  114.5 0.0 all-gather.5.cloned.1.call-done.wob
  114.5 0.7 copy-done.19
  115.2 12.1 %mix_and_out.1 = bf16[512,1536]{1,0:T(8,128)(2,1)} custom-call(s32[2]{0:T(128)} %pad_add_fusion.4.info, bf16[6,512,1280]{2,1,0:T(8,128)(2,1)} %scores_softmax.1.probs, bf16[8,64,256]{2,1,0:T(8,128)(2,1)} %copy-done.11, bf16[8,64,256]{2,1,0:T(8,128)(2,1)} %copy-done.19, bf16[512,512]{1,0:T(8,128)(2,1)} %copy-done.6, ...), custom_call_target="tpu_custom_call" | custom-call | flops 4429185024 | bytes 16777216 | tf_op jit(solution)/shard_map/mix_and_out/pallas_call | solution.py:316
  (58 shorter events, 0.3 us)
Async XLA Ops:
  6.5 8.6 %copy-start.17 = (f32[1536]{0:T(1024)S(1)}, f32[1536]{0:T(1024)}, u32[]{:S(2)}) copy-start(f32[1536]{0:T(1024)} %param.10) | copy-start | bytes 18436
  6.5 93.2 %all-gather.3.cloned.1.call-start = ((), (), s32[]{:S(2)}) async-start(), calls=%async_computation | async-start | bytes 2949120 | tf_op jit(solution)/shard_map/all_gather | solution.py:376
  7.6 18.4 %collective-permute-start.1 = (bf16[8,64,256]{2,1,0:T(8,128)(2,1)S(1)}, bf16[8,64,256]{2,1,0:T(8,128)(2,1)S(1)}, u32[]{:S(2)}, u32[]{:S(2)}) collective-permute-start(bf16[8,64,256]{2,1,0:T(8,128)(2,1)S(1)} %get-tuple-element.58.refs_0_), channel_id=1, source_target_pairs={{0,4},{2,6},{4,0},{6,2},{8,12},{10,14},{12,8},{14,10},{1,5},{3,7},... | collective-permute-start | bytes 786440 | tf_op jit(solution)/shard_map/ppermute | solution.py:344
  10.7 15.3 %collective-permute-start.2 = (bf16[8,64,256]{2,1,0:T(8,128)(2,1)S(1)}, bf16[8,64,256]{2,1,0:T(8,128)(2,1)S(1)}, u32[]{:S(2)}, u32[]{:S(2)}) collective-permute-start(bf16[8,64,256]{2,1,0:T(8,128)(2,1)S(1)} %get-tuple-element.58.refs_0_), channel_id=1, source_target_pairs={{4,8},{6,10},{8,4},{10,6},{5,9},{7,11},{9,5},{11,7},{20,24},{22,26... | collective-permute-start | bytes 786440 | tf_op jit(solution)/shard_map/ppermute | solution.py:344
  12.5 14.9 %collective-permute-start = (bf16[384,768]{1,0:T(8,128)(2,1)S(1)}, bf16[384,768]{1,0:T(8,128)(2,1)S(1)}, u32[]{:S(2)}, u32[]{:S(2)}) collective-permute-start(bf16[384,768]{1,0:T(8,128)(2,1)S(1)} %constant_dynamic-slice_fusion.1), channel_id=1, source_target_pairs={{0,1},{1,0},{2,3},{3,2},{4,5},{5,4},{6,7},{7,6},{8,9},{9,8},{10,11... | collective-permute-start | bytes 1769480 | tf_op jit(solution)/shard_map/ppermute | solution.py:373
  15.2 1.7 %copy-start.12 = (bf16[1536,768]{1,0:T(8,128)(2,1)S(1)}, bf16[1536,768]{1,0:T(8,128)(2,1)}, u32[]{:S(2)}) copy-start(bf16[1536,768]{1,0:T(8,128)(2,1)} %wq.1) | copy-start | bytes 7077892
  16.8 1.4 %copy-start.13 = (bf16[1,512,1536]{2,1,0:T(8,128)(2,1)S(1)}, bf16[1,512,1536]{2,1,0:T(8,128)(2,1)}, u32[]{:S(2)}) copy-start(bf16[1,512,1536]{2,1,0:T(8,128)(2,1)} %param.9) | copy-start | bytes 4718596
  18.2 1.4 %copy-start.14 = (bf16[1536,512]{1,0:T(8,128)(2,1)S(1)}, bf16[1536,512]{1,0:T(8,128)(2,1)}, u32[]{:S(2)}) copy-start(bf16[1536,512]{1,0:T(8,128)(2,1)} %wkv.1) | copy-start | bytes 4718596
  19.6 35.2 %copy-start.18 = (s32[1,8]{1,0:T(1,128)S(1)}, s32[1,8]{1,0:T(1,128)}, u32[]{:S(2)}) copy-start(s32[1,8]{1,0:T(1,128)} %param.15) | copy-start | bytes 100
  22.4 1.1 copy-start.2
  23.5 0.9 copy-start.5
  24.4 0.8 copy-start.7
  25.2 0.8 copy-start.9
  26.0 49.4 %copy-start.6 = (bf16[512,512]{1,0:T(8,128)(2,1)}, bf16[512,512]{1,0:T(8,128)(2,1)S(1)}, u32[]{:S(2)}) copy-start(bf16[512,512]{1,0:T(8,128)(2,1)S(1)} %get-tuple-element.30.kv_own) | copy-start | bytes 1572868
  27.4 0.8 copy-start.15
  28.2 86.3 %all-gather.5.cloned.1.call-start = ((), (), s32[]{:S(2)}) async-start(), calls=%async_computation.1 | async-start | bytes 2949120 | tf_op jit(solution)/shard_map/all_gather | solution.py:376
  28.3 10.3 %collective-permute-start.6 = (bf16[8,64,256]{2,1,0:T(8,128)(2,1)S(1)}, bf16[8,64,256]{2,1,0:T(8,128)(2,1)S(1)}, u32[]{:S(2)}, u32[]{:S(2)}) collective-permute-start(bf16[8,64,256]{2,1,0:T(8,128)(2,1)S(1)} %get-tuple-element.57.refs_0_), channel_id=1, source_target_pairs={{0,4},{2,6},{4,0},{6,2},{8,12},{10,14},{12,8},{14,10},{1,5},{3,7},... | collective-permute-start | bytes 786440 | tf_op jit(solution)/shard_map/ppermute | solution.py:344
  32.5 6.8 %collective-permute-start.8 = (bf16[8,64,256]{2,1,0:T(8,128)(2,1)S(1)}, bf16[8,64,256]{2,1,0:T(8,128)(2,1)S(1)}, u32[]{:S(2)}, u32[]{:S(2)}) collective-permute-start(bf16[8,64,256]{2,1,0:T(8,128)(2,1)S(1)} %get-tuple-element.57.refs_0_), channel_id=1, source_target_pairs={{4,8},{6,10},{8,4},{10,6},{5,9},{7,11},{9,5},{11,7},{20,24},{22,26... | collective-permute-start | bytes 786440 | tf_op jit(solution)/shard_map/ppermute | solution.py:344
  35.1 26.2 %collective-permute-start.11 = (bf16[192,1536]{1,0:T(8,128)(2,1)}, bf16[192,1536]{1,0:T(8,128)(2,1)}, u32[]{:S(2)}, u32[]{:S(2)}) collective-permute-start(bf16[192,1536]{1,0:T(8,128)(2,1)} %constant_dynamic-slice_fusion), channel_id=1, source_target_pairs={{0,1},{1,0},{2,3},{3,2},{4,5},{5,4},{6,7},{7,6},{8,9},{9,8},{10,11... | collective-permute-start | bytes 1769480 | tf_op jit(solution)/shard_map/ppermute | solution.py:373
  36.6 4.0 %collective-permute-start.4 = (bf16[8,64,256]{2,1,0:T(8,128)(2,1)S(1)}, bf16[8,64,256]{2,1,0:T(8,128)(2,1)S(1)}, u32[]{:S(2)}, u32[]{:S(2)}) collective-permute-start(bf16[8,64,256]{2,1,0:T(8,128)(2,1)S(1)} %collective-permute-done.1.refs_1_), channel_id=1, source_target_pairs={{4,8},{6,10},{8,4},{10,6},{5,9},{7,11},{9,5},{11,7},{20,24},{22,26... | collective-permute-start | bytes 786440 | tf_op jit(solution)/shard_map/ppermute | solution.py:427
  37.3 12.7 %collective-permute-start.5 = (bf16[8,64,256]{2,1,0:T(8,128)(2,1)S(1)}, bf16[8,64,256]{2,1,0:T(8,128)(2,1)S(1)}, u32[]{:S(2)}, u32[]{:S(2)}) collective-permute-start(bf16[8,64,256]{2,1,0:T(8,128)(2,1)S(1)} %collective-permute-done.2.refs_2_), channel_id=1, source_target_pairs={{4,0},{6,2},{8,12},{10,14},{5,1},{7,3},{9,13},{11,15},{20,16},{22,... | collective-permute-start | bytes 786440 | tf_op jit(solution)/shard_map/ppermute | solution.py:426
  38.6 11.3 %collective-permute-start.7 = (bf16[8,64,256]{2,1,0:T(8,128)(2,1)S(1)}, bf16[8,64,256]{2,1,0:T(8,128)(2,1)S(1)}, u32[]{:S(2)}, u32[]{:S(2)}) collective-permute-start(bf16[8,64,256]{2,1,0:T(8,128)(2,1)S(1)} %collective-permute-done.6.refs_1_), channel_id=1, source_target_pairs={{4,8},{6,10},{8,4},{10,6},{5,9},{7,11},{9,5},{11,7},{20,24},{22,26... | collective-permute-start | bytes 786440 | tf_op jit(solution)/shard_map/ppermute | solution.py:430
  39.3 13.8 %collective-permute-start.9 = (bf16[8,64,256]{2,1,0:T(8,128)(2,1)S(1)}, bf16[8,64,256]{2,1,0:T(8,128)(2,1)S(1)}, u32[]{:S(2)}, u32[]{:S(2)}) collective-permute-start(bf16[8,64,256]{2,1,0:T(8,128)(2,1)S(1)} %collective-permute-done.8.refs_2_), channel_id=1, source_target_pairs={{4,0},{6,2},{8,12},{10,14},{5,1},{7,3},{9,13},{11,15},{20,16},{22,... | collective-permute-start | bytes 786440 | tf_op jit(solution)/shard_map/ppermute | solution.py:431
  53.0 8.3 %collective-permute-start.10 = (bf16[8,64,256]{2,1,0:T(8,128)(2,1)S(1)}, bf16[8,64,256]{2,1,0:T(8,128)(2,1)S(1)}, u32[]{:S(2)}, u32[]{:S(2)}) collective-permute-start(bf16[8,64,256]{2,1,0:T(8,128)(2,1)S(1)} %collective-permute-done.4.refs_4_), channel_id=1, source_target_pairs={{4,0},{6,2},{8,12},{10,14},{5,1},{7,3},{9,13},{11,15},{20,16},{22,... | collective-permute-start | bytes 786440 | tf_op jit(solution)/shard_map/ppermute | solution.py:435
  54.3 11.7 %collective-permute-start.15 = (bf16[512,512]{1,0:T(8,128)(2,1)S(1)}, bf16[512,512]{1,0:T(8,128)(2,1)}, u32[]{:S(2)}, u32[]{:S(2)}) collective-permute-start(bf16[512,512]{1,0:T(8,128)(2,1)S(1)} %get-tuple-element.30.kv_own), channel_id=1, source_target_pairs={{0,1},{1,0},{2,3},{3,2},{4,5},{5,4},{6,7},{7,6},{8,9},{9,8},{10,11... | collective-permute-start | bytes 1572872 | tf_op jit(solution)/shard_map/ppermute | solution.py:385
  54.9 1.1 collective-permute-start.3
  56.0 5.3 %collective-permute-start.12 = (s32[2,8]{1,0:T(2,128)S(1)}, s32[2,8]{1,0:T(2,128)S(1)}, u32[]{:S(2)}, u32[]{:S(2)}) collective-permute-start(s32[2,8]{1,0:T(2,128)S(1)} %get-tuple-element.68), channel_id=1, source_target_pairs={{0,16},{16,0},{1,17},{17,1},{2,18},{18,2},{3,19},{19,3},{4,20},{20... | collective-permute-start | bytes 200 | tf_op jit(solution)/shard_map/ppermute | solution.py:389
  63.1 10.7 %collective-permute-start.13 = (bf16[16,64,256]{2,1,0:T(8,128)(2,1)S(1)}, bf16[16,64,256]{2,1,0:T(8,128)(2,1)S(1)}, u32[]{:S(2)}, u32[]{:S(2)}) collective-permute-start(bf16[16,64,256]{2,1,0:T(8,128)(2,1)S(1)} %pick_core.2), channel_id=1, source_target_pairs={{0,2},{2,0},{4,6},{6,4},{8,10},{10,8},{12,14},{14,12},{1,3},{3,1},... | collective-permute-start | bytes 1572872 | tf_op jit(solution)/shard_map/ppermute | solution.py:440
  63.2 10.6 %collective-permute-start.14 = (bf16[8,64,256]{2,1,0:T(8,128)(2,1)S(1)}, bf16[8,64,256]{2,1,0:T(8,128)(2,1)S(1)}, u32[]{:S(2)}, u32[]{:S(2)}) collective-permute-start(bf16[8,64,256]{2,1,0:T(8,128)(2,1)S(1)} %collective-permute-done.7.refs_4_), channel_id=1, source_target_pairs={{4,0},{6,2},{8,12},{10,14},{5,1},{7,3},{9,13},{11,15},{20,16},{22,... | collective-permute-start | bytes 786440 | tf_op jit(solution)/shard_map/ppermute | solution.py:436
  75.4 12.1 %collective-permute-start.17 = (bf16[16,64,256]{2,1,0:T(8,128)(2,1)S(1)}, bf16[16,64,256]{2,1,0:T(8,128)(2,1)S(1)}, u32[]{:S(2)}, u32[]{:S(2)}) collective-permute-start(bf16[16,64,256]{2,1,0:T(8,128)(2,1)S(1)} %pick_core.3), channel_id=1, source_target_pairs={{0,2},{2,0},{4,6},{6,4},{8,10},{10,8},{12,14},{14,12},{1,3},{3,1},... | collective-permute-start | bytes 1572872 | tf_op jit(solution)/shard_map/ppermute | solution.py:443
  76.6 10.9 %collective-permute-start.16 = (bf16[8,64,256]{2,1,0:T(8,128)(2,1)S(1)}, bf16[8,64,256]{2,1,0:T(8,128)(2,1)S(1)}, u32[]{:S(2)}, u32[]{:S(2)}) collective-permute-start(bf16[8,64,256]{2,1,0:T(8,128)(2,1)S(1)} %pick_rep.2), channel_id=1, source_target_pairs={{0,16},{16,0},{1,17},{17,1},{2,18},{18,2},{3,19},{19,3},{4,20},{20... | collective-permute-start | bytes 786440 | tf_op jit(solution)/shard_map/ppermute | solution.py:444
  88.6 8.2 %collective-permute-start.19 = (bf16[8,64,256]{2,1,0:T(8,128)(2,1)S(1)}, bf16[8,64,256]{2,1,0:T(8,128)(2,1)S(1)}, u32[]{:S(2)}, u32[]{:S(2)}) collective-permute-start(bf16[8,64,256]{2,1,0:T(8,128)(2,1)S(1)} %pick_rep.3), channel_id=1, source_target_pairs={{0,16},{16,0},{1,17},{17,1},{2,18},{18,2},{3,19},{19,3},{4,20},{20... | collective-permute-start | bytes 786440 | tf_op jit(solution)/shard_map/ppermute | solution.py:446
  90.2 14.3 %copy-start.4 = (bf16[8,64,256]{2,1,0:T(8,128)(2,1)}, bf16[8,64,256]{2,1,0:T(8,128)(2,1)S(1)}, u32[]{:S(2)}) copy-start(bf16[8,64,256]{2,1,0:T(8,128)(2,1)S(1)} %pick_own.2.k_mine) | copy-start | bytes 786436
  90.2 9.6 %copy-start.8 = (f32[512,256]{1,0:T(8,128)S(1)}, f32[512,256]{1,0:T(8,128)}, u32[]{:S(2)}) copy-start(f32[512,256]{1,0:T(8,128)} %copy-done.7) | copy-start | bytes 1572868
  90.2 9.6 %copy-start.10 = (f32[512,256]{1,0:T(8,128)S(1)}, f32[512,256]{1,0:T(8,128)}, u32[]{:S(2)}) copy-start(f32[512,256]{1,0:T(8,128)} %copy-done.9) | copy-start | bytes 1572868
  90.2 15.2 %collective-permute-start.18 = (bf16[8,64,256]{2,1,0:T(8,128)(2,1)S(1)}, bf16[8,64,256]{2,1,0:T(8,128)(2,1)S(1)}, u32[]{:S(2)}, u32[]{:S(2)}) collective-permute-start(bf16[8,64,256]{2,1,0:T(8,128)(2,1)S(1)} %pick_own.2.k_mine), channel_id=1, source_target_pairs={{0,1},{1,0},{2,3},{3,2},{4,5},{5,4},{6,7},{7,6},{8,9},{9,8},{10,11... | collective-permute-start | bytes 786440 | tf_op jit(solution)/shard_map/ppermute | solution.py:448
  98.2 6.3 %copy-start.11 = (bf16[8,64,256]{2,1,0:T(8,128)(2,1)}, bf16[8,64,256]{2,1,0:T(8,128)(2,1)S(1)}, u32[]{:S(2)}) copy-start(bf16[8,64,256]{2,1,0:T(8,128)(2,1)S(1)} %pick_own.3.v_mine) | copy-start | bytes 786436
  98.2 16.3 %collective-permute-start.20 = (bf16[8,64,256]{2,1,0:T(8,128)(2,1)S(1)}, bf16[8,64,256]{2,1,0:T(8,128)(2,1)S(1)}, u32[]{:S(2)}, u32[]{:S(2)}) collective-permute-start(bf16[8,64,256]{2,1,0:T(8,128)(2,1)S(1)} %pick_own.3.v_mine), channel_id=1, source_target_pairs={{0,1},{1,0},{2,3},{3,2},{4,5},{5,4},{6,7},{7,6},{8,9},{9,8},{10,11... | collective-permute-start | bytes 786440 | tf_op jit(solution)/shard_map/ppermute | solution.py:450
  99.7 1.7 %copy-start.1 = (bf16[1536,768]{1,0:T(8,128)(2,1)S(1)}, bf16[1536,768]{1,0:T(8,128)(2,1)}, u32[]{:S(2)}) copy-start(bf16[1536,768]{1,0:T(8,128)(2,1)} %all-gather.3.cloned.1.call-done.wq) | copy-start | bytes 7077892
  101.4 1.4 %copy-start.3 = (bf16[512,1536]{1,0:T(8,128)(2,1)S(1)}, bf16[512,1536]{1,0:T(8,128)(2,1)}, u32[]{:S(2)}) copy-start(bf16[512,1536]{1,0:T(8,128)(2,1)} %copy-done.2) | copy-start | bytes 4718596
  104.5 0.9 copy-start
  105.4 0.7 copy-start.16
  114.5 0.7 copy-start.19
Sparse Core Ops, SparseCore 0:
  28.4 25.8 all-gather.2
  61.4 24.1 all-gather.4

commit v4 on v3

--- a/solution.py
+++ b/solution.py
@@ -91,34 +91,56 @@
     )(tok, gain.reshape(1, width), wq, wkv, cos_t, sin_t)
 
 
-def other_kernel(head_size, normed, wq, cos, sin, q):
+def other_kernel(head_size, normed, wq_hbm, cos, sin, wo, q, wo_held, wq, sem):
     rows = normed.shape[0]
+    heads = q.shape[1] // head_size
+    loads = [
+        pltpu.make_async_copy(wq_hbm.at[:, pl.ds(h * head_size, head_size)], wq.at[h], sem.at[h])
+        for h in range(heads)
+    ]
+    loads.append(pltpu.make_async_copy(wo, wo_held, sem.at[heads]))
+    for c in loads:
+        c.start()
     tile = min(256, rows)
     even = lax.broadcasted_iota(jnp.int32, (tile, head_size), 1) % 2 == 0
-    for i in range(rows // tile):
-        at = pl.ds(i * tile, tile)
-        c = cos[at, :]
-        s = sin[at, :]
-        for h in range(q.shape[1] // head_size):
-            cols = slice(h * head_size, (h + 1) * head_size)
-            part = jnp.dot(normed[at, :], wq[:, cols], preferred_element_type=F32)
-            q[at, cols] = rotate(part, c, s, even).astype(BF16)
-
-
-def project_other(normed, wq, cos, sin, head_size):
+    for h in range(heads):
+        loads[h].wait()
+        for i in range(rows // tile):
+            at = pl.ds(i * tile, tile)
+            part = jnp.dot(normed[at, :], wq[h], preferred_element_type=F32)
+            turned = rotate(part, cos[at, :], sin[at, :], even)
+            q[at, h * head_size : (h + 1) * head_size] = turned.astype(BF16)
+    loads[heads].wait()
+
+
+def project_other(normed, wq, cos, sin, wo, head_size):
     rows, width = normed.shape
     qc = wq.shape[1]
+    heads = qc // head_size
     return pl.pallas_call(
         functools.partial(other_kernel, head_size),
-        out_shape=jax.ShapeDtypeStruct((rows, qc), BF16),
-        in_specs=[spec(pltpu.VMEM)] * 4,
-        out_specs=spec(pltpu.VMEM),
+        out_shape=(
+            jax.ShapeDtypeStruct((rows, qc), BF16),
+            jax.ShapeDtypeStruct(wo.shape, BF16),
+        ),
+        in_specs=[
+            spec(pltpu.VMEM),
+            spec(pltpu.HBM),
+            spec(pltpu.VMEM),
+            spec(pltpu.VMEM),
+            spec(pltpu.HBM),
+        ],
+        out_specs=[spec(pltpu.VMEM)] * 2,
+        scratch_shapes=[
+            pltpu.VMEM((heads, width, head_size), BF16),
+            pltpu.SemaphoreType.DMA((heads + 1,)),
+        ],
         compiler_params=pltpu.CompilerParams(vmem_limit_bytes=20 * 2**20),
         cost_estimate=pl.CostEstimate(
-            flops=2 * rows * width * qc, bytes_accessed=6 * 2**20, transcendentals=0
+            flops=2 * rows * width * qc, bytes_accessed=4 * 2**20, transcendentals=0
         ),
         name="project_other",
-    )(normed, wq, cos, sin)
+    )(normed, wq, cos, sin, wo)
 
 
 def collect_kernel(where, *refs):
@@ -150,12 +172,12 @@
     )(where, *arrays)
 
 
-def start_rows(part, mine, peer, kv_own, kv_peer, lo, dst, sem):
+def gather_rows(part, mine, peer, kv_own, kv_peer, lo, dst):
     pages, prow, head_size = mine.shape
     rows = kv_own.shape[0]
     page = 2 * prow
     window = pages * page
-    cols = pl.ds(lo, head_size)
+    cols = slice(lo, lo + head_size)
     for case in (0, 1):
 
         @pl.when(part == case)
@@ -163,30 +185,18 @@
             skip = case * rows // page
             for u in range(skip, pages):
                 for src, side in ((mine, case), (peer, 1 - case)):
-                    to = pl.ds((u - skip) * page + side * prow, prow)
-                    pltpu.make_async_copy(src.at[u], dst.at[to, :], sem).start()
+                    at = (u - skip) * page + side * prow
+                    dst[at : at + prow, :] = src[u]
             if case == 1:
-                to = pl.ds(window - rows, rows)
-                pltpu.make_async_copy(kv_peer.at[:, cols], dst.at[to, :], sem).start()
-            to = pl.ds(window, rows)
-            pltpu.make_async_copy(kv_own.at[:, cols], dst.at[to, :], sem).start()
-
-
-def finish_rows(dst, sem):
-    pltpu.make_async_copy(dst, dst, sem).wait()
+                dst[window - rows : window, :] = kv_peer[:, cols]
+            dst[window : window + rows, :] = kv_own[:, cols]
 
 
 def weigh_kernel(
-    head_size, info, qa_hbm, qb_hbm, k_mine, k_peer, kv_own, kv_peer, probs, qa, qb, keys, done, ksem, qsem, psem
+    head_size, info, qa, qb, k_mine, k_peer, kv_own, kv_peer, probs, keys
 ):
     rows, half = qa.shape
-    start_rows(info[0], k_mine, k_peer, kv_own, kv_peer, 0, keys, ksem)
-    loads = [
-        pltpu.make_async_copy(qa_hbm, qa, qsem.at[0]),
-        pltpu.make_async_copy(qb_hbm, qb, qsem.at[1]),
-    ]
-    for c in loads:
-        c.start()
+    gather_rows(info[0], k_mine, k_peer, kv_own, kv_peer, 0, keys)
     nheads = half // head_size
     span = probs.shape[2]
     tile = span + rows - keys.shape[0]
@@ -195,18 +205,13 @@
     first_seen = col_id >= row_id + 1
     last_seen = col_id <= row_id
     factor = math.log2(math.e) / math.sqrt(head_size)
-    for c in loads:
-        c.wait()
-    finish_rows(keys, ksem)
-    stores = []
     for i in range(rows // tile):
         at = pl.ds(i * tile, tile)
         for n, q in enumerate((qa, qb)):
             for h in range(nheads):
-                kk = keys[pl.ds(i * tile, span), :]
                 s = lax.dot_general(
                     q[at, h * head_size : (h + 1) * head_size],
-                    kk,
+                    keys[pl.ds(i * tile, span), :],
                     (((1,), (1,)), ((), ())),
                     preferred_element_type=F32,
                 )
@@ -221,14 +226,7 @@
                 top = jnp.max(s, axis=-1, keepdims=True)
                 e = jnp.exp2((s - top) * factor)
                 total = jnp.sum(e, axis=-1, keepdims=True)
-                m = len(stores)
-                done[m] = (e * (1.0 / total)).astype(BF16)
-                stores.append(
-                    pltpu.make_async_copy(done.at[m], probs.at[n * nheads + h, at, :], psem.at[m])
-                )
-                stores[m].start()
-    for c in stores:
-        c.wait()
+                probs[n * nheads + h, at, :] = (e * (1.0 / total)).astype(BF16)
 
 
 def weigh(info, qa, qb, k_mine, k_peer, kv_own, kv_peer):
@@ -237,34 +235,23 @@
     heads = 2 * half // head_size
     window = k_mine.shape[0] * k_mine.shape[1] * 2
     span = window + min(256, rows)
-    chunks = heads * rows // (span - window)
     return pl.pallas_call(
         functools.partial(weigh_kernel, head_size),
         out_shape=jax.ShapeDtypeStruct((heads, rows, span), BF16),
-        in_specs=[spec(pltpu.SMEM)] + [spec(ANY)] * 6,
-        out_specs=spec(ANY),
-        scratch_shapes=[
-            pltpu.VMEM((rows, half), BF16),
-            pltpu.VMEM((rows, half), BF16),
-            pltpu.VMEM((window + rows, head_size), BF16),
-            pltpu.VMEM((chunks, span - window, span), BF16),
-            pltpu.SemaphoreType.DMA,
-            pltpu.SemaphoreType.DMA((2,)),
-            pltpu.SemaphoreType.DMA((chunks,)),
-        ],
-        compiler_params=pltpu.CompilerParams(vmem_limit_bytes=56 * 2**20),
+        in_specs=[spec(pltpu.SMEM)] + [spec(pltpu.VMEM)] * 6,
+        out_specs=spec(pltpu.VMEM),
+        scratch_shapes=[pltpu.VMEM((window + rows, head_size), BF16)],
+        compiler_params=pltpu.CompilerParams(vmem_limit_bytes=28 * 2**20),
         cost_estimate=pl.CostEstimate(
             flops=4 * rows * half * span,
-            bytes_accessed=12 * 2**20,
+            bytes_accessed=6 * 2**20,
             transcendentals=rows * heads * span,
         ),
         name="scores_softmax",
     )(info, qa, qb, k_mine, k_peer, kv_own, kv_peer)
 
 
-def out_kernel(
-    info, probs, v_mine, v_peer, kv_own, kv_peer, woa, wob, out, vals, pv, wa, wb, mix, vsem, psem, wsem
-):
+def out_kernel(info, probs, v_mine, v_peer, kv_own, kv_peer, wa, wb, out, vals, mix):
     part = info[0]
     length = info[1]
     heads, rows, span = probs.shape
@@ -272,31 +259,14 @@
     width = out.shape[1]
     nheads = heads // 2
     tile = span + rows - vals.shape[0]
-    start_rows(part, v_mine, v_peer, kv_own, kv_peer, head_size, vals, vsem)
-    order = [(i, h) for i in range(rows // tile) for h in range(heads)]
-    loads = [
-        pltpu.make_async_copy(probs.at[h, pl.ds(i * tile, tile), :], pv.at[m], psem.at[m])
-        for m, (i, h) in enumerate(order)
-    ]
-    for c in loads:
-        c.start()
-    weights = [
-        pltpu.make_async_copy(woa, wa, wsem.at[0]),
-        pltpu.make_async_copy(wob, wb, wsem.at[1]),
-    ]
-    for c in weights:
-        c.start()
-    finish_rows(vals, vsem)
-    for m, (i, h) in enumerate(order):
-        vv = vals[pl.ds(i * tile, span), :]
-        loads[m].wait()
-        mixed = jnp.dot(pv[m], vv, preferred_element_type=F32).astype(BF16)
-        lo = h % nheads * head_size
-        mix[h // nheads, pl.ds(i * tile, tile), lo : lo + head_size] = mixed
-    for c in weights:
-        c.wait()
+    gather_rows(part, v_mine, v_peer, kv_own, kv_peer, head_size, vals)
     for i in range(rows // tile):
         at = pl.ds(i * tile, tile)
+        for h in range(heads):
+            vv = vals[pl.ds(i * tile, span), :]
+            mixed = jnp.dot(probs[h, at, :], vv, preferred_element_type=F32).astype(BF16)
+            lo = h % nheads * head_size
+            mix[h // nheads, at, lo : lo + head_size] = mixed
         row = part * rows + i * tile + lax.broadcasted_iota(jnp.int32, (tile, 1), 0)
         live = row < length
         for lo in range(0, width, 512):
@@ -307,35 +277,28 @@
             out[at, cols] = jnp.where(live, both, 0.0).astype(BF16)
 
 
-def mix_and_out(info, probs, v_mine, v_peer, kv_own, kv_peer, woa, wob):
+def mix_and_out(info, probs, v_mine, v_peer, kv_own, kv_peer, wa, wb):
     heads, rows, span = probs.shape
-    half, width = woa.shape
+    half, width = wa.shape
     head_size = v_mine.shape[2]
     window = v_mine.shape[0] * v_mine.shape[1] * 2
-    chunks = heads * rows // (span - window)
     return pl.pallas_call(
         out_kernel,
         out_shape=jax.ShapeDtypeStruct((rows, width), BF16),
-        in_specs=[spec(pltpu.SMEM)] + [spec(ANY)] * 7,
+        in_specs=[spec(pltpu.SMEM)] + [spec(pltpu.VMEM)] * 7,
         out_specs=spec(pltpu.VMEM),
         scratch_shapes=[
             pltpu.VMEM((window + rows, head_size), BF16),
-            pltpu.VMEM((chunks, span - window, span), BF16),
-            pltpu.VMEM(woa.shape, BF16),
-            pltpu.VMEM(wob.shape, BF16),
             pltpu.VMEM((2, rows, half), BF16),
-            pltpu.SemaphoreType.DMA,
-            pltpu.SemaphoreType.DMA((chunks,)),
-            pltpu.SemaphoreType.DMA((2,)),
         ],
-        compiler_params=pltpu.CompilerParams(vmem_limit_bytes=56 * 2**20),
+        compiler_params=pltpu.CompilerParams(vmem_limit_bytes=28 * 2**20),
         cost_estimate=pl.CostEstimate(
             flops=4 * rows * half * span + 4 * rows * half * width,
-            bytes_accessed=16 * 2**20,
+            bytes_accessed=4 * 2**20,
             transcendentals=0,
         ),
         name="mix_and_out",
-    )(info, probs, v_mine, v_peer, kv_own, kv_peer, woa, wob)
+    )(info, probs, v_mine, v_peer, kv_own, kv_peer, wa, wb)
 
 
 def first_hop(x, swap_at):
@@ -365,17 +328,20 @@
     k_first = first_hop(k_pages, both_cores)
     v_first = first_hop(v_pages, both_cores)
 
-    quarter = rep * 2 + core
-    groups = [[r * ndp + 2 * z + c for r in (0, 1) for c in (0, 1)] for z in range(ndp // 2)]
-
-    def peer_quarter(w):
-        deep = w.shape[0] // 4
-        return lax.ppermute(lax.dynamic_slice_in_dim(w, quarter * deep, deep, 0), "tensor", swap)
-
-    def share(piece):
-        return lax.all_gather(piece, ("rep", "dp"), axis=0, tiled=True, axis_index_groups=groups)
-
-    wq_piece = peer_quarter(w_query)
+    quads = [[r * ndp + 2 * z + c for r in (0, 1) for c in (0, 1)] for z in range(ndp // 2)]
+    chips = [[2 * z, 2 * z + 1] for z in range(ndp // 2)]
+
+    def peer_rows(w, at, parts):
+        deep = w.shape[0] // parts
+        return lax.ppermute(lax.dynamic_slice_in_dim(w, at * deep, deep, 0), "tensor", swap)
+
+    wq_piece = peer_rows(w_query, rep * 2 + core, 4)
+
+    kf, kn, vf, vn, wq_piece, tokens, w_out_late, table = lax.optimization_barrier(
+        (*k_first, *v_first, wq_piece, tokens, w_out, page_table)
+    )
+    wq_other = lax.all_gather(wq_piece, ("rep", "dp"), axis=0, tiled=True, axis_index_groups=quads)
+    wo_piece = peer_rows(w_out_late, core, 2)
 
     step = 32
     cos_t, sin_t = rotation_tables(starts[0] + part * rows, rows, step, head_size)
@@ -384,7 +350,6 @@
     )
     kv_peer = lax.ppermute(kv_own, "tensor", swap)
 
-    table, kv_own = lax.optimization_barrier((page_table, kv_own))
     chip_tables = jnp.concatenate([table, lax.ppermute(table, "dp", cores)], axis=0)
     peer_tables = lax.ppermute(chip_tables, "rep", swap)
     per_rep = held * ndp
@@ -422,37 +387,35 @@
 
     middle = both_cores([(1, 2), (2, 1)])
     outward = both_cores([(1, 0), (2, 3)])
-    kf, kn, _ = lax.optimization_barrier((*k_first, kv_own))
     k_near = lax.ppermute(kn, "dp", outward)
+    v_near = lax.ppermute(vn, "dp", outward)
     k_far = lax.ppermute(kf, "dp", middle)
-    wq_piece, w_out_late, _ = lax.optimization_barrier((wq_piece, w_out, kf))
-    vf, vn = v_first
     v_far = lax.ppermute(vf, "dp", middle)
-    v_near = lax.ppermute(vn, "dp", outward)
-    wq_other = share(wq_piece)
-    wo_piece = peer_quarter(w_out_late)
-    k_far, k_near, v_far, v_near = lax.optimization_barrier((k_far, k_near, v_far, v_near))
     k_end = lax.ppermute(k_far, "dp", outward)
     v_end = lax.ppermute(v_far, "dp", outward)
-    k_end, wo_piece = lax.optimization_barrier((k_end, wo_piece))
-    wo_other = share(wo_piece)
+    k_near, v_near, k_end, v_end, kv_own, where_core = lax.optimization_barrier(
+        (k_near, v_near, k_end, v_end, kv_own, where_core)
+    )
     k_line = [k_pages, kf, kn, k_near, k_far, k_end]
+    v_line = [v_pages, vf, vn, v_near, v_far, v_end]
     k_given = lax.ppermute(collect(where_core, k_line, "pick_core"), "dp", cores)
-    k_given, v_end, kv_peer = lax.optimization_barrier((k_given, v_end, kv_peer))
-    v_line = [v_pages, vf, vn, v_near, v_far, v_end]
     v_given = lax.ppermute(collect(where_core, v_line, "pick_core"), "dp", cores)
+    k_given, v_given = lax.optimization_barrier((k_given, v_given))
     k_came = lax.ppermute(collect(where_peer, k_line + [k_given], "pick_rep"), "rep", swap)
-    k_came, v_given = lax.optimization_barrier((k_came, v_given))
-    v_came = lax.ppermute(collect(where_peer, v_line + [v_given], "pick_rep"), "rep", swap)
+    v_sent = collect(where_peer, v_line + [v_given], "pick_rep")
+    v_sent, normed = lax.optimization_barrier((v_sent, normed))
+    v_came = lax.ppermute(v_sent, "rep", swap)
+    qb, wa = project_other(normed, wq_other, cos, sin, w_out, head_size)
+    k_came, qb, kv_peer, wo_piece = lax.optimization_barrier((k_came, qb, kv_peer, wo_piece))
+    wo_other = lax.all_gather(wo_piece, "dp", axis=0, tiled=True, axis_index_groups=chips)
     k_mine = collect(where_own, k_line + [k_given, k_came], "pick_own")
     k_peer = lax.ppermute(k_mine, "tensor", swap)
     v_mine = collect(where_own, v_line + [v_given, v_came], "pick_own")
     v_peer = lax.ppermute(v_mine, "tensor", swap)
 
-    qb = project_other(normed, wq_other, cos, sin, head_size)
     info = jnp.stack([part, lengths[0]]).astype(jnp.int32)
     probs = weigh(info, qa, qb, k_mine, k_peer, kv_own, kv_peer)
-    return mix_and_out(info, probs, v_mine, v_peer, kv_own, kv_peer, w_out, wo_other)[None]
+    return mix_and_out(info, probs, v_mine, v_peer, kv_own, kv_peer, wa, wo_other)[None]
 
 
 def rotate_pairs(values, positions, columns_from, head_size):

time: 135 us -> 135 us (level); the launches traced: 134 us -> 133 us
  local copies, waits for them, and re-layouts: 18.4 us -> 31.7 us
  waiting for transfers between devices: 41 us -> 29.5 us
  Pallas kernels: 32.6 us -> 29.5 us
    unnamed x40 -> x80, local copies, waits for them, and re-layouts: 14.3 us -> 28.3 us
    ppermute x1, waiting for transfers between devices: 9.37 us -> 0.01 us  [pair_shards(): lax.ppermute(collect(where_peer, k_line + [k_given], 'pick_rep'), 'rep',...]
    ppermute x1, waiting for transfers between devices: 9.34 us -> 0.01 us  [pair_shards(): k_near = lax.ppermute(kn, 'dp', outward)]
    ppermute x1, waiting for transfers between devices: 3.68 us -> 10.5 us  [pair_shards(): k_end = lax.ppermute(k_far, 'dp', outward)]
    ppermute x4, waiting for transfers between devices: 0.01 us -> 5.25 us  [first_hop(): return (lax.ppermute(x, 'dp', pairs), lax.ppermute(x, 'dp', middle))]
    ppermute x3, waiting for transfers between devices: 4.99 us -> 0.03 us  [the longest x1 0.03 us: pair_shards(): v_came = lax.ppermute(v_sent, 'rep', swap)]
    pallas_call x1, Pallas kernels: 12.1 us -> 7.18 us  [mix_and_out(): pl.pallas_call(out_kernel, out_shape=jax.ShapeDtypeStruct((rows, width),...]
    ppermute x1, waiting for transfers between devices: 7.81 us -> 3.84 us  [pair_shards(): v_end = lax.ppermute(v_far, 'dp', outward)]
  transfers between devices with their start and end apart: 23 -> 23, of which waited for: 9 -> 8; matrix products, arithmetic and copies ran while one was open for 3% -> 2% of each run, Pallas kernels for 15% -> 17%
where the time goes in v4:
time: 135 us; the launch traced here: 133 us
  local copies, waits for them, and re-layouts  31.7 us (23%)
  waiting for transfers between devices  29.5 us (22%)
  Pallas kernels  29.5 us (22%)
  starting transfers between devices  26.1 us (19%)
  between operations  15.2 us (11%)
    unnamed x80, local copies, waits for them, and re-layouts  28.3 us
    ppermute x1, waiting for transfers between devices, pair_shards(): k_end = lax.ppermute(k_far, 'dp', outward)  10.5 us
    pallas_call x6, Pallas kernels, collect(): pl.pallas_call(collect_kernel, out_shape=jax.ShapeDtypeStruct(shape, arra...  10.3 us
    ppermute x4, starting transfers between devices, first_hop(): return (lax.ppermute(x, 'dp', pairs), lax.ppermute(x, 'dp', middle))  7.43 us
    pallas_call x1, Pallas kernels, mix_and_out(): pl.pallas_call(out_kernel, out_shape=jax.ShapeDtypeStruct((rows, width),...  7.18 us
    pallas_call x1, Pallas kernels, weigh(): pl.pallas_call(functools.partial(weigh_kernel, head_size), out_shape=jax....  6.31 us
    ppermute x4, waiting for transfers between devices, first_hop(): return (lax.ppermute(x, 'dp', pairs), lax.ppermute(x, 'dp', middle))  5.25 us
    ppermute x1, waiting for transfers between devices, pair_shards(): v_near = lax.ppermute(vn, 'dp', outward)  4.33 us
  transfers between devices with their start and end apart: 23, of which 8 were waited for; matrix products, arithmetic and copies ran while one was open for 2% of the time, Pallas kernels for 17%

profile of v4, /device:TPU:0, one launch (start us, length us, event | category | flops | bytes accessed | tf_op | source)
XLA Modules:
  0.0 132.7 jit_solution(3056473448614270729)
XLA Ops:
  6.5 1.1 constant_dynamic-slice_fusion.1
  7.7 3.0 %collective-permute-start.4 = (bf16[384,768]{1,0:T(8,128)(2,1)S(1)}, bf16[384,768]{1,0:T(8,128)(2,1)S(1)}, u32[]{:S(2)}, u32[]{:S(2)}) collective-permute-start(bf16[384,768]{1,0:T(8,128)(2,1)S(1)} %constant_dynamic-slice_fusion.1), channel_id=1, source_target_pairs={{0,1},{1,0},{2,3},{3,2},{4,5},{5,4},{6,7},{7,6},{8,9},{9,8},{10,11... | collective-permute-start | bytes 1769480 | tf_op jit(solution)/shard_map/ppermute | solution.py:336
  10.7 1.1 fusion.13
  11.8 1.6 %collective-permute-start = (bf16[8,64,256]{2,1,0:T(8,128)(2,1)S(1)}, bf16[8,64,256]{2,1,0:T(8,128)(2,1)}, u32[]{:S(2)}, u32[]{:S(2)}) collective-permute-start(bf16[8,64,256]{2,1,0:T(8,128)(2,1)S(1)} %get-tuple-element.72.refs_0_), channel_id=1, source_target_pairs={{0,4},{2,6},{4,0},{6,2},{8,12},{10,14},{12,8},{14,10},{1,5},{3,7},... | collective-permute-start | bytes 786440 | tf_op jit(solution)/shard_map/ppermute | solution.py:307
  13.4 1.4 %collective-permute-start.1 = (bf16[8,64,256]{2,1,0:T(8,128)(2,1)S(1)}, bf16[8,64,256]{2,1,0:T(8,128)(2,1)}, u32[]{:S(2)}, u32[]{:S(2)}) collective-permute-start(bf16[8,64,256]{2,1,0:T(8,128)(2,1)S(1)} %get-tuple-element.72.refs_0_), channel_id=1, source_target_pairs={{4,8},{6,10},{8,4},{10,6},{5,9},{7,11},{9,5},{11,7},{20,24},{22,26... | collective-permute-start | bytes 786440 | tf_op jit(solution)/shard_map/ppermute | solution.py:307
  14.8 3.8 %collective-permute-start.2 = (bf16[8,64,256]{2,1,0:T(8,128)(2,1)S(1)}, bf16[8,64,256]{2,1,0:T(8,128)(2,1)S(1)}, u32[]{:S(2)}, u32[]{:S(2)}) collective-permute-start(bf16[8,64,256]{2,1,0:T(8,128)(2,1)S(1)} %get-tuple-element.71.refs_0_), channel_id=1, source_target_pairs={{0,4},{2,6},{4,0},{6,2},{8,12},{10,14},{12,8},{14,10},{1,5},{3,7},... | collective-permute-start | bytes 786440 | tf_op jit(solution)/shard_map/ppermute | solution.py:307
  18.5 0.7 collective-permute-start.3
  19.9 0.1 pad_maximum_fusion
  20.0 0.9 collective-permute-done.refs_1_
  20.9 4.4 %collective-permute-done.2.refs_1_ = bf16[8,64,256]{2,1,0:T(8,128)(2,1)S(1)} collective-permute-done((bf16[8,64,256]{2,1,0:T(8,128)(2,1)S(1)}, bf16[8,64,256]{2,1,0:T(8,128)(2,1)S(1)}, u32[]{:S(2)}, u32[]{:S(2)}) %collective-permute-start.2) | collective-permute-done | bytes 262176 | tf_op jit(solution)/shard_map/ppermute | solution.py:307
  25.2 0.8 copy-done.37
  26.2 0.3 fusion
  26.6 0.7 collective-permute-start.9
  27.2 0.7 collective-permute-start.11
  27.9 1.3 collective-permute-start.7
  29.2 1.3 collective-permute-start.8
  30.5 1.7 %copy-done.31 = bf16[1536,768]{1,0:T(8,128)(2,1)S(1)} copy-done((bf16[1536,768]{1,0:T(8,128)(2,1)S(1)}, bf16[1536,768]{1,0:T(8,128)(2,1)}, u32[]{:S(2)}) %copy-start.31) | copy-done | bytes 2359320
  32.2 1.4 %copy-done.35 = bf16[1,512,1536]{2,1,0:T(8,128)(2,1)S(1)} copy-done((bf16[1,512,1536]{2,1,0:T(8,128)(2,1)S(1)}, bf16[1,512,1536]{2,1,0:T(8,128)(2,1)}, u32[]{:S(2)}) %copy-start.35) | copy-done | bytes 1572888
  33.6 1.5 %copy-done.36 = bf16[1536,512]{1,0:T(8,128)(2,1)S(1)} copy-done((bf16[1536,512]{1,0:T(8,128)(2,1)S(1)}, bf16[1536,512]{1,0:T(8,128)(2,1)}, u32[]{:S(2)}) %copy-start.36) | copy-done | bytes 1572888
  35.1 2.8 %project_own.1 = (bf16[512,1536]{1,0:T(8,128)(2,1)S(1)}, bf16[512,768]{1,0:T(8,128)(2,1)S(1)}, bf16[512,512]{1,0:T(8,128)(2,1)}, f32[512,256]{1,0:T(8,128)S(1)}, f32[512,256]{1,0:T(8,128)S(1)}) custom-call(bf16[512,1536]{1,0:T(8,128)(2,1)S(1)} %bitcast.17, f32[1,1536]{1,0:T(1,128)S(1)} %reshape.40.gain, bf16[1536,768]{1,0:T(8,128)(2,1)S(1)} %copy-done.31, ...), custom_call_target="tpu_custom_call" | custom-call | flops 2013265920 | bytes 10485760 | tf_op jit(solution)/shard_map/project_own/pallas_call | solution.py:75
  38.0 1.2 constant_dynamic-slice_fusion
  39.2 1.5 %collective-permute-start.6 = (s32[2,8]{1,0:T(2,128)S(1)}, s32[2,8]{1,0:T(2,128)S(1)}, u32[]{:S(2)}, u32[]{:S(2)}) collective-permute-start(s32[2,8]{1,0:T(2,128)S(1)} %pad_add_fusion), channel_id=1, source_target_pairs={{0,16},{16,0},{1,17},{17,1},{2,18},{18,2},{3,19},{19,3},{4,20},{20... | collective-permute-start | bytes 200 | tf_op jit(solution)/shard_map/ppermute | solution.py:354
  40.7 2.1 %collective-permute-done.6 = s32[2,8]{1,0:T(2,128)S(1)} collective-permute-done((s32[2,8]{1,0:T(2,128)S(1)}, s32[2,8]{1,0:T(2,128)S(1)}, u32[]{:S(2)}, u32[]{:S(2)}) %collective-permute-start.6) | collective-permute-done | bytes 96 | tf_op jit(solution)/shard_map/ppermute | solution.py:354
  42.8 0.4 collective-permute-start.17
  43.4 1.3 collective-permute-start.10
  44.7 1.3 collective-permute-start.12
  46.0 0.1 add_bitcast_fusion
  46.1 0.1 add_bitcast_fusion.1
  46.2 4.3 %collective-permute-done.8.refs_3_ = bf16[8,64,256]{2,1,0:T(8,128)(2,1)S(1)} collective-permute-done((bf16[8,64,256]{2,1,0:T(8,128)(2,1)S(1)}, bf16[8,64,256]{2,1,0:T(8,128)(2,1)S(1)}, u32[]{:S(2)}, u32[]{:S(2)}) %collective-permute-start.8) | collective-permute-done | bytes 262176 | tf_op jit(solution)/shard_map/ppermute | solution.py:391
  50.5 10.5 %collective-permute-done.10.refs_5_ = bf16[8,64,256]{2,1,0:T(8,128)(2,1)S(1)} collective-permute-done((bf16[8,64,256]{2,1,0:T(8,128)(2,1)S(1)}, bf16[8,64,256]{2,1,0:T(8,128)(2,1)S(1)}, u32[]{:S(2)}, u32[]{:S(2)}) %collective-permute-start.10) | collective-permute-done | bytes 262176 | tf_op jit(solution)/shard_map/ppermute | solution.py:394
  61.0 3.8 %collective-permute-done.12.refs_5_ = bf16[8,64,256]{2,1,0:T(8,128)(2,1)S(1)} collective-permute-done((bf16[8,64,256]{2,1,0:T(8,128)(2,1)S(1)}, bf16[8,64,256]{2,1,0:T(8,128)(2,1)S(1)}, u32[]{:S(2)}, u32[]{:S(2)}) %collective-permute-start.12) | collective-permute-done | bytes 262176 | tf_op jit(solution)/shard_map/ppermute | solution.py:395
  64.8 1.5 %pick_core.3 = bf16[16,64,256]{2,1,0:T(8,128)(2,1)S(1)} custom-call(s32[2,16]{1,0:T(2,128)S(1)} %pad_add_fusion.2.where, bf16[8,64,256]{2,1,0:T(8,128)(2,1)S(1)} %get-tuple-element.71.refs_0_, bf16[8,64,256]{2,1,0:T(8,128)(2,1)S(1)} %collective-permute-done.2.refs_1_, bf16[8,64,256]{2,1,0:T(8,128)(2,1)S(1)} %collective-permute-done.3.refs_2_, ...), custom_call_target="tpu_custom_call" | custom-call | bytes 1024 | tf_op jit(solution)/shard_map/pick_core/pallas_call | solution.py:164
  66.4 2.0 %pick_core.2 = bf16[16,64,256]{2,1,0:T(8,128)(2,1)S(1)} custom-call(s32[2,16]{1,0:T(2,128)S(1)} %pad_add_fusion.2.where, bf16[8,64,256]{2,1,0:T(8,128)(2,1)S(1)} %get-tuple-element.72.refs_0_, bf16[8,64,256]{2,1,0:T(8,128)(2,1)} %collective-permute-done.refs_1_, bf16[8,64,256]{2,1,0:T(8,128)(2,1)} %collective-permute-done.1.refs_2_, ...), custom_call_target="tpu_custom_call" | custom-call | bytes 1024 | tf_op jit(solution)/shard_map/pick_core/pallas_call | solution.py:164
  68.5 0.6 collective-permute-start.13
  69.0 1.4 %collective-permute-start.16 = (bf16[512,512]{1,0:T(8,128)(2,1)}, bf16[512,512]{1,0:T(8,128)(2,1)}, u32[]{:S(2)}, u32[]{:S(2)}) collective-permute-start(bf16[512,512]{1,0:T(8,128)(2,1)} %get-tuple-element.58.kv_own), channel_id=1, source_target_pairs={{0,1},{1,0},{2,3},{3,2},{4,5},{5,4},{6,7},{7,6},{8,9},{9,8},{10,11... | collective-permute-start | bytes 1572872 | tf_op jit(solution)/shard_map/ppermute | solution.py:351
  70.5 0.1 collective-permute-done.13.refs_6_
  70.6 2.6 %pick_rep.2 = bf16[8,64,256]{2,1,0:T(8,128)(2,1)} custom-call(s32[2,8]{1,0:T(2,128)S(1)} %pad_add_fusion.1.where, bf16[8,64,256]{2,1,0:T(8,128)(2,1)S(1)} %get-tuple-element.72.refs_0_, bf16[8,64,256]{2,1,0:T(8,128)(2,1)} %collective-permute-done.refs_1_, bf16[8,64,256]{2,1,0:T(8,128)(2,1)} %collective-permute-done.1.refs_2_, ...), custom_call_target="tpu_custom_call" | custom-call | bytes 1024 | tf_op jit(solution)/shard_map/pick_rep/pallas_call | solution.py:164
  73.2 1.6 %collective-permute-start.15 = (bf16[8,64,256]{2,1,0:T(8,128)(2,1)}, bf16[8,64,256]{2,1,0:T(8,128)(2,1)}, u32[]{:S(2)}, u32[]{:S(2)}) collective-permute-start(bf16[8,64,256]{2,1,0:T(8,128)(2,1)} %pick_rep.2), channel_id=1, source_target_pairs={{0,16},{16,0},{1,17},{17,1},{2,18},{18,2},{3,19},{19,3},{4,20},{20... | collective-permute-start | bytes 786440 | tf_op jit(solution)/shard_map/ppermute | solution.py:404
  74.8 1.1 pick_rep.3
  75.9 0.7 copy-done.30
  76.6 1.7 %copy-done.3 = bf16[1536,768]{1,0:T(8,128)(2,1)S(1)} copy-done((bf16[1536,768]{1,0:T(8,128)(2,1)S(1)}, bf16[1536,768]{1,0:T(8,128)(2,1)}, u32[]{:S(2)}) %copy-start.3) | copy-done | bytes 2359320
  78.3 1.4 %copy-done.21 = bf16[512,1536]{1,0:T(8,128)(2,1)S(1)} copy-done((bf16[512,1536]{1,0:T(8,128)(2,1)S(1)}, bf16[512,1536]{1,0:T(8,128)(2,1)}, u32[]{:S(2)}) %copy-start.21) | copy-done | bytes 1572888
  79.7 1.0 copy-done.27
  80.7 1.0 copy-done.29
  81.8 2.9 %project_other.1 = (bf16[512,768]{1,0:T(8,128)(2,1)S(1)}, bf16[768,1536]{1,0:T(8,128)(2,1)S(1)}) custom-call(bf16[512,1536]{1,0:T(8,128)(2,1)S(1)} %copy-done.21, bf16[1536,768]{1,0:T(8,128)(2,1)S(1)} %copy-done.3, f32[512,256]{1,0:T(8,128)S(1)} %copy-done.27, f32[512,256]{1,0:T(8,128)S(1)} %copy-done.29, bf16[768,1536]{1,0:T(8,128)(2,1)S(1)} %copy-done.2), custom_call_target="tpu_custom_call" | custom-call | flops 1207959552 | bytes 4194304 | tf_op jit(solution)/shard_map/project_other/pallas_call | solution.py:120
  84.7 0.9 copy-done.24
  85.6 1.4 %copy-done.32 = bf16[768,1536]{1,0:T(8,128)(2,1)} copy-done((bf16[768,1536]{1,0:T(8,128)(2,1)}, bf16[768,1536]{1,0:T(8,128)(2,1)S(1)}, u32[]{:S(2)}) %copy-start.32) | copy-done | bytes 2359320
  87.0 0.6 collective-permute-start.19
  87.7 0.9 copy-done.9
  88.6 0.9 copy-done.11
  89.6 0.9 copy-done.15
  90.5 1.0 copy-done.19
  91.6 1.9 %pick_own.2.k_mine = bf16[8,64,256]{2,1,0:T(8,128)(2,1)S(1)} custom-call(s32[2,8]{1,0:T(2,128)S(1)} %pad_add_fusion.3.where, bf16[8,64,256]{2,1,0:T(8,128)(2,1)S(1)} %get-tuple-element.72.refs_0_, bf16[8,64,256]{2,1,0:T(8,128)(2,1)} %collective-permute-done.refs_1_, bf16[8,64,256]{2,1,0:T(8,128)(2,1)} %collective-permute-done.1.refs_2_, ...), custom_call_target="tpu_custom_call" | custom-call | bytes 1024 | tf_op jit(solution)/shard_map/pick_own/pallas_call | solution.py:164
  93.4 1.4 %collective-permute-start.18 = (bf16[8,64,256]{2,1,0:T(8,128)(2,1)S(1)}, bf16[8,64,256]{2,1,0:T(8,128)(2,1)S(1)}, u32[]{:S(2)}, u32[]{:S(2)}) collective-permute-start(bf16[8,64,256]{2,1,0:T(8,128)(2,1)S(1)} %pick_own.2.k_mine), channel_id=1, source_target_pairs={{0,1},{1,0},{2,3},{3,2},{4,5},{5,4},{6,7},{7,6},{8,9},{9,8},{10,11... | collective-permute-start | bytes 786440 | tf_op jit(solution)/shard_map/ppermute | solution.py:412
  95.5 1.1 copy-done.17
  96.6 1.2 pick_own.3.v_mine
  97.8 1.5 %collective-permute-start.20 = (bf16[8,64,256]{2,1,0:T(8,128)(2,1)S(1)}, bf16[8,64,256]{2,1,0:T(8,128)(2,1)S(1)}, u32[]{:S(2)}, u32[]{:S(2)}) collective-permute-start(bf16[8,64,256]{2,1,0:T(8,128)(2,1)S(1)} %pick_own.3.v_mine), channel_id=1, source_target_pairs={{0,1},{1,0},{2,3},{3,2},{4,5},{5,4},{6,7},{7,6},{8,9},{9,8},{10,11... | collective-permute-start | bytes 786440 | tf_op jit(solution)/shard_map/ppermute | solution.py:414
  99.4 3.3 %collective-permute-done.18.k_peer = bf16[8,64,256]{2,1,0:T(8,128)(2,1)S(1)} collective-permute-done((bf16[8,64,256]{2,1,0:T(8,128)(2,1)S(1)}, bf16[8,64,256]{2,1,0:T(8,128)(2,1)S(1)}, u32[]{:S(2)}, u32[]{:S(2)}) %collective-permute-start.18) | collective-permute-done | bytes 262176 | tf_op jit(solution)/shard_map/ppermute | solution.py:412
  102.7 6.3 %scores_softmax.1.probs = bf16[6,512,1280]{2,1,0:T(8,128)(2,1)S(1)} custom-call(s32[2]{0:T(128)S(1)} %pad_add_fusion.4.info, bf16[512,768]{1,0:T(8,128)(2,1)S(1)} %copy-done.23, bf16[512,768]{1,0:T(8,128)(2,1)S(1)} %copy-done.25, bf16[8,64,256]{2,1,0:T(8,128)(2,1)S(1)} %pick_own.2.k_mine, bf16[8,64,256]{2,1,0:T(8,128)(2,1)S(1)} %collective-permute-done.18.k_peer, ...), custom_call_target="tpu_custom_call" | custom-call | flops 2013265920 | bytes 6291456 | tf_op jit(solution)/shard_map/scores_softmax/pallas_call | solution.py:238
  109.0 3.1 %copy-done = bf16[6,512,1280]{2,1,0:T(8,128)(2,1)} copy-done((bf16[6,512,1280]{2,1,0:T(8,128)(2,1)}, bf16[6,512,1280]{2,1,0:T(8,128)(2,1)S(1)}, u32[]{:S(2)}) %copy-start) | copy-done | bytes 7864344
  112.1 3.2 %copy-done.1 = bf16[6,512,1280]{2,1,0:T(8,128)(2,1)S(1)} copy-done((bf16[6,512,1280]{2,1,0:T(8,128)(2,1)S(1)}, bf16[6,512,1280]{2,1,0:T(8,128)(2,1)}, u32[]{:S(2)}) %copy-start.1) | copy-done | bytes 7864344
  115.4 1.7 %copy-done.33 = bf16[768,1536]{1,0:T(8,128)(2,1)S(1)} copy-done((bf16[768,1536]{1,0:T(8,128)(2,1)S(1)}, bf16[768,1536]{1,0:T(8,128)(2,1)}, u32[]{:S(2)}) %copy-start.33) | copy-done | bytes 2359320
  117.0 1.7 %copy-done.34 = bf16[768,1536]{1,0:T(8,128)(2,1)S(1)} copy-done((bf16[768,1536]{1,0:T(8,128)(2,1)S(1)}, bf16[768,1536]{1,0:T(8,128)(2,1)}, u32[]{:S(2)}) %copy-start.34) | copy-done | bytes 2359320
  118.7 7.2 %mix_and_out.1 = bf16[512,1536]{1,0:T(8,128)(2,1)} custom-call(s32[2]{0:T(128)S(1)} %pad_add_fusion.4.info, bf16[6,512,1280]{2,1,0:T(8,128)(2,1)S(1)} %copy-done.1, bf16[8,64,256]{2,1,0:T(8,128)(2,1)S(1)} %pick_own.3.v_mine, bf16[8,64,256]{2,1,0:T(8,128)(2,1)S(1)} %collective-permute-done.20.v_peer, bf16[512,512]{1,0:T(8,128)(2,1)} %get-tuple-element.58.kv_own, ...), custom_call_target="tpu_custom_call" | custom-call | flops 4429185024 | bytes 4194304 | tf_op jit(solution)/shard_map/mix_and_out/pallas_call | solution.py:285
  (99 shorter events, 0.7 us)
Async XLA Ops:
  6.5 19.9 %copy-start.39 = (s32[1,8]{1,0:T(1,128)S(1)}, s32[1,8]{1,0:T(1,128)}, u32[]{:S(2)}) copy-start(s32[1,8]{1,0:T(1,128)} %param.15) | copy-start | bytes 100
  6.5 19.9 %copy-start.38 = (f32[1536]{0:T(1024)S(1)}, f32[1536]{0:T(1024)}, u32[]{:S(2)}) copy-start(f32[1536]{0:T(1024)} %param.10) | copy-start | bytes 18436
  6.5 70.1 %all-gather.3.cloned.1.call-start = ((), (), s32[]{:S(2)}) async-start(), calls=%async_computation | async-start | bytes 2949120 | tf_op jit(solution)/shard_map/all_gather | solution.py:343
  7.7 17.6 %collective-permute-start.4 = (bf16[384,768]{1,0:T(8,128)(2,1)S(1)}, bf16[384,768]{1,0:T(8,128)(2,1)S(1)}, u32[]{:S(2)}, u32[]{:S(2)}) collective-permute-start(bf16[384,768]{1,0:T(8,128)(2,1)S(1)} %constant_dynamic-slice_fusion.1), channel_id=1, source_target_pairs={{0,1},{1,0},{2,3},{3,2},{4,5},{5,4},{6,7},{7,6},{8,9},{9,8},{10,11... | collective-permute-start | bytes 1769480 | tf_op jit(solution)/shard_map/ppermute | solution.py:336
  11.8 9.1 %collective-permute-start = (bf16[8,64,256]{2,1,0:T(8,128)(2,1)S(1)}, bf16[8,64,256]{2,1,0:T(8,128)(2,1)}, u32[]{:S(2)}, u32[]{:S(2)}) collective-permute-start(bf16[8,64,256]{2,1,0:T(8,128)(2,1)S(1)} %get-tuple-element.72.refs_0_), channel_id=1, source_target_pairs={{0,4},{2,6},{4,0},{6,2},{8,12},{10,14},{12,8},{14,10},{1,5},{3,7},... | collective-permute-start | bytes 786440 | tf_op jit(solution)/shard_map/ppermute | solution.py:307
  13.4 7.4 %collective-permute-start.1 = (bf16[8,64,256]{2,1,0:T(8,128)(2,1)S(1)}, bf16[8,64,256]{2,1,0:T(8,128)(2,1)}, u32[]{:S(2)}, u32[]{:S(2)}) collective-permute-start(bf16[8,64,256]{2,1,0:T(8,128)(2,1)S(1)} %get-tuple-element.72.refs_0_), channel_id=1, source_target_pairs={{4,8},{6,10},{8,4},{10,6},{5,9},{7,11},{9,5},{11,7},{20,24},{22,26... | collective-permute-start | bytes 786440 | tf_op jit(solution)/shard_map/ppermute | solution.py:307
  14.8 10.4 %collective-permute-start.2 = (bf16[8,64,256]{2,1,0:T(8,128)(2,1)S(1)}, bf16[8,64,256]{2,1,0:T(8,128)(2,1)S(1)}, u32[]{:S(2)}, u32[]{:S(2)}) collective-permute-start(bf16[8,64,256]{2,1,0:T(8,128)(2,1)S(1)} %get-tuple-element.71.refs_0_), channel_id=1, source_target_pairs={{0,4},{2,6},{4,0},{6,2},{8,12},{10,14},{12,8},{14,10},{1,5},{3,7},... | collective-permute-start | bytes 786440 | tf_op jit(solution)/shard_map/ppermute | solution.py:307
  18.5 6.7 %collective-permute-start.3 = (bf16[8,64,256]{2,1,0:T(8,128)(2,1)S(1)}, bf16[8,64,256]{2,1,0:T(8,128)(2,1)S(1)}, u32[]{:S(2)}, u32[]{:S(2)}) collective-permute-start(bf16[8,64,256]{2,1,0:T(8,128)(2,1)S(1)} %get-tuple-element.71.refs_0_), channel_id=1, source_target_pairs={{4,8},{6,10},{8,4},{10,6},{5,9},{7,11},{9,5},{11,7},{20,24},{22,26... | collective-permute-start | bytes 786440 | tf_op jit(solution)/shard_map/ppermute | solution.py:307
  25.2 0.8 copy-start.37
  26.1 86.0 %all-gather.5.cloned.1.call-start = ((), (), s32[]{:S(2)}) async-start(), calls=%async_computation.1 | async-start | bytes 3538944 | tf_op jit(solution)/shard_map/all_gather | solution.py:410
  26.5 12.7 %collective-permute-start.5 = (s32[1,8]{1,0:T(1,128)S(1)}, s32[1,8]{1,0:T(1,128)S(1)}, u32[]{:S(2)}, u32[]{:S(2)}) collective-permute-start(s32[1,8]{1,0:T(1,128)S(1)} %copy-done.39), channel_id=1, source_target_pairs={{0,2},{2,0},{4,6},{6,4},{8,10},{10,8},{12,14},{14,12},{1,3},{3,1},... | collective-permute-start | bytes 104 | tf_op jit(solution)/shard_map/ppermute | solution.py:353
  26.6 16.8 %collective-permute-start.9 = (bf16[8,64,256]{2,1,0:T(8,128)(2,1)}, bf16[8,64,256]{2,1,0:T(8,128)(2,1)S(1)}, u32[]{:S(2)}, u32[]{:S(2)}) collective-permute-start(bf16[8,64,256]{2,1,0:T(8,128)(2,1)} %collective-permute-done.refs_1_), channel_id=1, source_target_pairs={{4,8},{6,10},{8,4},{10,6},{5,9},{7,11},{9,5},{11,7},{20,24},{22,26... | collective-permute-start | bytes 786440 | tf_op jit(solution)/shard_map/ppermute | solution.py:392
  27.2 17.4 %collective-permute-start.11 = (bf16[8,64,256]{2,1,0:T(8,128)(2,1)S(1)}, bf16[8,64,256]{2,1,0:T(8,128)(2,1)S(1)}, u32[]{:S(2)}, u32[]{:S(2)}) collective-permute-start(bf16[8,64,256]{2,1,0:T(8,128)(2,1)S(1)} %collective-permute-done.2.refs_1_), channel_id=1, source_target_pairs={{4,8},{6,10},{8,4},{10,6},{5,9},{7,11},{9,5},{11,7},{20,24},{22,26... | collective-permute-start | bytes 786440 | tf_op jit(solution)/shard_map/ppermute | solution.py:393
  27.9 18.2 %collective-permute-start.7 = (bf16[8,64,256]{2,1,0:T(8,128)(2,1)}, bf16[8,64,256]{2,1,0:T(8,128)(2,1)S(1)}, u32[]{:S(2)}, u32[]{:S(2)}) collective-permute-start(bf16[8,64,256]{2,1,0:T(8,128)(2,1)} %collective-permute-done.1.refs_2_), channel_id=1, source_target_pairs={{4,0},{6,2},{8,12},{10,14},{5,1},{7,3},{9,13},{11,15},{20,16},{22,... | collective-permute-start | bytes 786440 | tf_op jit(solution)/shard_map/ppermute | solution.py:390
  29.2 21.3 %collective-permute-start.8 = (bf16[8,64,256]{2,1,0:T(8,128)(2,1)S(1)}, bf16[8,64,256]{2,1,0:T(8,128)(2,1)S(1)}, u32[]{:S(2)}, u32[]{:S(2)}) collective-permute-start(bf16[8,64,256]{2,1,0:T(8,128)(2,1)S(1)} %collective-permute-done.3.refs_2_), channel_id=1, source_target_pairs={{4,0},{6,2},{8,12},{10,14},{5,1},{7,3},{9,13},{11,15},{20,16},{22,... | collective-permute-start | bytes 786440 | tf_op jit(solution)/shard_map/ppermute | solution.py:391
  30.5 1.7 %copy-start.31 = (bf16[1536,768]{1,0:T(8,128)(2,1)S(1)}, bf16[1536,768]{1,0:T(8,128)(2,1)}, u32[]{:S(2)}) copy-start(bf16[1536,768]{1,0:T(8,128)(2,1)} %wq.1) | copy-start | bytes 7077892
  32.2 1.4 %copy-start.35 = (bf16[1,512,1536]{2,1,0:T(8,128)(2,1)S(1)}, bf16[1,512,1536]{2,1,0:T(8,128)(2,1)}, u32[]{:S(2)}) copy-start(bf16[1,512,1536]{2,1,0:T(8,128)(2,1)} %param.9) | copy-start | bytes 4718596
  33.6 1.5 %copy-start.36 = (bf16[1536,512]{1,0:T(8,128)(2,1)S(1)}, bf16[1536,512]{1,0:T(8,128)(2,1)}, u32[]{:S(2)}) copy-start(bf16[1536,512]{1,0:T(8,128)(2,1)} %wkv.1) | copy-start | bytes 4718596
  35.1 2.8 %copy-start.2 = (bf16[768,1536]{1,0:T(8,128)(2,1)S(1)}, bf16[768,1536]{1,0:T(8,128)(2,1)}, u32[]{:S(2)}) copy-start(bf16[768,1536]{1,0:T(8,128)(2,1)} %wo.1) | copy-start | bytes 7077892
  37.9 30.5 %copy-start.20 = (bf16[512,1536]{1,0:T(8,128)(2,1)}, bf16[512,1536]{1,0:T(8,128)(2,1)S(1)}, u32[]{:S(2)}) copy-start(bf16[512,1536]{1,0:T(8,128)(2,1)S(1)} %get-tuple-element.50.normed) | copy-start | bytes 4718596
  38.0 30.5 %copy-start.22 = (bf16[512,768]{1,0:T(8,128)(2,1)}, bf16[512,768]{1,0:T(8,128)(2,1)S(1)}, u32[]{:S(2)}) copy-start(bf16[512,768]{1,0:T(8,128)(2,1)S(1)} %get-tuple-element.35.qa) | copy-start | bytes 2359300
  38.0 30.5 %copy-start.26 = (f32[512,256]{1,0:T(8,128)}, f32[512,256]{1,0:T(8,128)S(1)}, u32[]{:S(2)}) copy-start(f32[512,256]{1,0:T(8,128)S(1)} %get-tuple-element.52.cos) | copy-start | bytes 1572868
  38.0 30.5 %copy-start.28 = (f32[512,256]{1,0:T(8,128)}, f32[512,256]{1,0:T(8,128)S(1)}, u32[]{:S(2)}) copy-start(f32[512,256]{1,0:T(8,128)S(1)} %get-tuple-element.53.sin) | copy-start | bytes 1572868
  39.2 3.6 %collective-permute-start.6 = (s32[2,8]{1,0:T(2,128)S(1)}, s32[2,8]{1,0:T(2,128)S(1)}, u32[]{:S(2)}, u32[]{:S(2)}) collective-permute-start(s32[2,8]{1,0:T(2,128)S(1)} %pad_add_fusion), channel_id=1, source_target_pairs={{0,16},{16,0},{1,17},{17,1},{2,18},{18,2},{3,19},{19,3},{4,20},{20... | collective-permute-start | bytes 200 | tf_op jit(solution)/shard_map/ppermute | solution.py:354
  42.8 44.2 %collective-permute-start.17 = (bf16[384,1536]{1,0:T(8,128)(2,1)}, bf16[384,1536]{1,0:T(8,128)(2,1)}, u32[]{:S(2)}, u32[]{:S(2)}) collective-permute-start(bf16[384,1536]{1,0:T(8,128)(2,1)} %constant_dynamic-slice_fusion), channel_id=1, source_target_pairs={{0,1},{1,0},{2,3},{3,2},{4,5},{5,4},{6,7},{7,6},{8,9},{9,8},{10,11... | collective-permute-start | bytes 3538952 | tf_op jit(solution)/shard_map/ppermute | solution.py:336
  43.4 29.8 %copy-start.8 = (bf16[8,64,256]{2,1,0:T(8,128)(2,1)}, bf16[8,64,256]{2,1,0:T(8,128)(2,1)S(1)}, u32[]{:S(2)}) copy-start(bf16[8,64,256]{2,1,0:T(8,128)(2,1)S(1)} %collective-permute-done.9.refs_4_) | copy-start | bytes 786436
  43.4 17.6 %collective-permute-start.10 = (bf16[8,64,256]{2,1,0:T(8,128)(2,1)S(1)}, bf16[8,64,256]{2,1,0:T(8,128)(2,1)S(1)}, u32[]{:S(2)}, u32[]{:S(2)}) collective-permute-start(bf16[8,64,256]{2,1,0:T(8,128)(2,1)S(1)} %collective-permute-done.9.refs_4_), channel_id=1, source_target_pairs={{4,0},{6,2},{8,12},{10,14},{5,1},{7,3},{9,13},{11,15},{20,16},{22,... | collective-permute-start | bytes 786440 | tf_op jit(solution)/shard_map/ppermute | solution.py:394
  44.7 30.1 %copy-start.4 = (bf16[8,64,256]{2,1,0:T(8,128)(2,1)}, bf16[8,64,256]{2,1,0:T(8,128)(2,1)S(1)}, u32[]{:S(2)}) copy-start(bf16[8,64,256]{2,1,0:T(8,128)(2,1)S(1)} %collective-permute-done.11.refs_4_) | copy-start | bytes 786436
  44.7 20.1 %collective-permute-start.12 = (bf16[8,64,256]{2,1,0:T(8,128)(2,1)S(1)}, bf16[8,64,256]{2,1,0:T(8,128)(2,1)S(1)}, u32[]{:S(2)}, u32[]{:S(2)}) collective-permute-start(bf16[8,64,256]{2,1,0:T(8,128)(2,1)S(1)} %collective-permute-done.11.refs_4_), channel_id=1, source_target_pairs={{4,0},{6,2},{8,12},{10,14},{5,1},{7,3},{9,13},{11,15},{20,16},{22,... | collective-permute-start | bytes 786440 | tf_op jit(solution)/shard_map/ppermute | solution.py:395
  46.2 27.0 %copy-start.10 = (bf16[8,64,256]{2,1,0:T(8,128)(2,1)}, bf16[8,64,256]{2,1,0:T(8,128)(2,1)S(1)}, u32[]{:S(2)}) copy-start(bf16[8,64,256]{2,1,0:T(8,128)(2,1)S(1)} %collective-permute-done.7.refs_3_) | copy-start | bytes 786436
  50.5 24.3 %copy-start.6 = (bf16[8,64,256]{2,1,0:T(8,128)(2,1)}, bf16[8,64,256]{2,1,0:T(8,128)(2,1)S(1)}, u32[]{:S(2)}) copy-start(bf16[8,64,256]{2,1,0:T(8,128)(2,1)S(1)} %collective-permute-done.8.refs_3_) | copy-start | bytes 786436
  61.0 12.2 %copy-start.14 = (bf16[8,64,256]{2,1,0:T(8,128)(2,1)}, bf16[8,64,256]{2,1,0:T(8,128)(2,1)S(1)}, u32[]{:S(2)}) copy-start(bf16[8,64,256]{2,1,0:T(8,128)(2,1)S(1)} %collective-permute-done.10.refs_5_) | copy-start | bytes 786436
  64.8 9.9 %copy-start.12 = (bf16[8,64,256]{2,1,0:T(8,128)(2,1)}, bf16[8,64,256]{2,1,0:T(8,128)(2,1)S(1)}, u32[]{:S(2)}) copy-start(bf16[8,64,256]{2,1,0:T(8,128)(2,1)S(1)} %collective-permute-done.12.refs_5_) | copy-start | bytes 786436
  66.4 4.1 %collective-permute-start.14 = (bf16[16,64,256]{2,1,0:T(8,128)(2,1)S(1)}, bf16[16,64,256]{2,1,0:T(8,128)(2,1)S(1)}, u32[]{:S(2)}, u32[]{:S(2)}) collective-permute-start(bf16[16,64,256]{2,1,0:T(8,128)(2,1)S(1)} %pick_core.3), channel_id=1, source_target_pairs={{0,2},{2,0},{4,6},{6,4},{8,10},{10,8},{12,14},{14,12},{1,3},{3,1},... | collective-permute-start | bytes 1572872 | tf_op jit(solution)/shard_map/ppermute | solution.py:402
  68.5 2.1 %collective-permute-start.13 = (bf16[16,64,256]{2,1,0:T(8,128)(2,1)S(1)}, bf16[16,64,256]{2,1,0:T(8,128)(2,1)S(1)}, u32[]{:S(2)}, u32[]{:S(2)}) collective-permute-start(bf16[16,64,256]{2,1,0:T(8,128)(2,1)S(1)} %pick_core.2), channel_id=1, source_target_pairs={{0,2},{2,0},{4,6},{6,4},{8,10},{10,8},{12,14},{14,12},{1,3},{3,1},... | collective-permute-start | bytes 1572872 | tf_op jit(solution)/shard_map/ppermute | solution.py:401
  69.0 17.9 %collective-permute-start.16 = (bf16[512,512]{1,0:T(8,128)(2,1)}, bf16[512,512]{1,0:T(8,128)(2,1)}, u32[]{:S(2)}, u32[]{:S(2)}) collective-permute-start(bf16[512,512]{1,0:T(8,128)(2,1)} %get-tuple-element.58.kv_own), channel_id=1, source_target_pairs={{0,1},{1,0},{2,3},{3,2},{4,5},{5,4},{6,7},{7,6},{8,9},{9,8},{10,11... | collective-permute-start | bytes 1572872 | tf_op jit(solution)/shard_map/ppermute | solution.py:351
  70.5 5.4 %copy-start.16 = (bf16[16,64,256]{2,1,0:T(8,128)(2,1)}, bf16[16,64,256]{2,1,0:T(8,128)(2,1)S(1)}, u32[]{:S(2)}) copy-start(bf16[16,64,256]{2,1,0:T(8,128)(2,1)S(1)} %collective-permute-done.14.refs_6_) | copy-start | bytes 1572868
  70.6 5.3 %copy-start.18 = (bf16[16,64,256]{2,1,0:T(8,128)(2,1)}, bf16[16,64,256]{2,1,0:T(8,128)(2,1)S(1)}, u32[]{:S(2)}) copy-start(bf16[16,64,256]{2,1,0:T(8,128)(2,1)S(1)} %collective-permute-done.13.refs_6_) | copy-start | bytes 1572868
  73.2 13.8 %collective-permute-start.15 = (bf16[8,64,256]{2,1,0:T(8,128)(2,1)}, bf16[8,64,256]{2,1,0:T(8,128)(2,1)}, u32[]{:S(2)}, u32[]{:S(2)}) collective-permute-start(bf16[8,64,256]{2,1,0:T(8,128)(2,1)} %pick_rep.2), channel_id=1, source_target_pairs={{0,16},{16,0},{1,17},{17,1},{2,18},{18,2},{3,19},{19,3},{4,20},{20... | collective-permute-start | bytes 786440 | tf_op jit(solution)/shard_map/ppermute | solution.py:404
  75.9 0.7 copy-start.30
  76.6 1.7 %copy-start.3 = (bf16[1536,768]{1,0:T(8,128)(2,1)S(1)}, bf16[1536,768]{1,0:T(8,128)(2,1)}, u32[]{:S(2)}) copy-start(bf16[1536,768]{1,0:T(8,128)(2,1)} %all-gather.3.cloned.1.call-done.wq_hbm) | copy-start | bytes 7077892
  78.3 1.4 %copy-start.21 = (bf16[512,1536]{1,0:T(8,128)(2,1)S(1)}, bf16[512,1536]{1,0:T(8,128)(2,1)}, u32[]{:S(2)}) copy-start(bf16[512,1536]{1,0:T(8,128)(2,1)} %copy-done.20) | copy-start | bytes 4718596
  79.7 1.0 copy-start.27
  80.7 1.0 copy-start.29
  84.7 0.9 copy-start.24
  85.6 1.4 %copy-start.32 = (bf16[768,1536]{1,0:T(8,128)(2,1)}, bf16[768,1536]{1,0:T(8,128)(2,1)S(1)}, u32[]{:S(2)}) copy-start(bf16[768,1536]{1,0:T(8,128)(2,1)S(1)} %get-tuple-element.61.wa) | copy-start | bytes 7077892
  87.0 8.5 %copy-start.5 = (bf16[8,64,256]{2,1,0:T(8,128)(2,1)S(1)}, bf16[8,64,256]{2,1,0:T(8,128)(2,1)}, u32[]{:S(2)}) copy-start(bf16[8,64,256]{2,1,0:T(8,128)(2,1)} %copy-done.4) | copy-start | bytes 786436
  87.0 8.5 %copy-start.7 = (bf16[8,64,256]{2,1,0:T(8,128)(2,1)S(1)}, bf16[8,64,256]{2,1,0:T(8,128)(2,1)}, u32[]{:S(2)}) copy-start(bf16[8,64,256]{2,1,0:T(8,128)(2,1)} %copy-done.6) | copy-start | bytes 786436
  87.0 8.5 %copy-start.13 = (bf16[8,64,256]{2,1,0:T(8,128)(2,1)S(1)}, bf16[8,64,256]{2,1,0:T(8,128)(2,1)}, u32[]{:S(2)}) copy-start(bf16[8,64,256]{2,1,0:T(8,128)(2,1)} %copy-done.12) | copy-start | bytes 786436
  87.0 8.5 %collective-permute-start.19 = (bf16[8,64,256]{2,1,0:T(8,128)(2,1)}, bf16[8,64,256]{2,1,0:T(8,128)(2,1)S(1)}, u32[]{:S(2)}, u32[]{:S(2)}) collective-permute-start(bf16[8,64,256]{2,1,0:T(8,128)(2,1)} %copy-done.30), channel_id=1, source_target_pairs={{0,16},{16,0},{1,17},{17,1},{2,18},{18,2},{3,19},{19,3},{4,20},{20... | collective-permute-start | bytes 786440 | tf_op jit(solution)/shard_map/ppermute | solution.py:407
  87.7 0.9 copy-start.9
  88.6 0.9 copy-start.11
  89.6 0.9 copy-start.15
  90.5 1.0 copy-start.19
  91.5 11.1 %copy-start.23 = (bf16[512,768]{1,0:T(8,128)(2,1)S(1)}, bf16[512,768]{1,0:T(8,128)(2,1)}, u32[]{:S(2)}) copy-start(bf16[512,768]{1,0:T(8,128)(2,1)} %copy-done.22) | copy-start | bytes 2359300
  91.5 11.1 %copy-start.25 = (bf16[512,768]{1,0:T(8,128)(2,1)S(1)}, bf16[512,768]{1,0:T(8,128)(2,1)}, u32[]{:S(2)}) copy-start(bf16[512,768]{1,0:T(8,128)(2,1)} %copy-done.24) | copy-start | bytes 2359300
  93.4 9.3 %collective-permute-start.18 = (bf16[8,64,256]{2,1,0:T(8,128)(2,1)S(1)}, bf16[8,64,256]{2,1,0:T(8,128)(2,1)S(1)}, u32[]{:S(2)}, u32[]{:S(2)}) collective-permute-start(bf16[8,64,256]{2,1,0:T(8,128)(2,1)S(1)} %pick_own.2.k_mine), channel_id=1, source_target_pairs={{0,1},{1,0},{2,3},{3,2},{4,5},{5,4},{6,7},{7,6},{8,9},{9,8},{10,11... | collective-permute-start | bytes 786440 | tf_op jit(solution)/shard_map/ppermute | solution.py:412
  95.5 1.1 copy-start.17
  97.8 14.3 %collective-permute-start.20 = (bf16[8,64,256]{2,1,0:T(8,128)(2,1)S(1)}, bf16[8,64,256]{2,1,0:T(8,128)(2,1)S(1)}, u32[]{:S(2)}, u32[]{:S(2)}) collective-permute-start(bf16[8,64,256]{2,1,0:T(8,128)(2,1)S(1)} %pick_own.3.v_mine), channel_id=1, source_target_pairs={{0,1},{1,0},{2,3},{3,2},{4,5},{5,4},{6,7},{7,6},{8,9},{9,8},{10,11... | collective-permute-start | bytes 786440 | tf_op jit(solution)/shard_map/ppermute | solution.py:414
  109.0 3.1 %copy-start = (bf16[6,512,1280]{2,1,0:T(8,128)(2,1)}, bf16[6,512,1280]{2,1,0:T(8,128)(2,1)S(1)}, u32[]{:S(2)}) copy-start(bf16[6,512,1280]{2,1,0:T(8,128)(2,1)S(1)} %scores_softmax.1.probs) | copy-start | bytes 23592964
  112.1 3.2 %copy-start.1 = (bf16[6,512,1280]{2,1,0:T(8,128)(2,1)S(1)}, bf16[6,512,1280]{2,1,0:T(8,128)(2,1)}, u32[]{:S(2)}) copy-start(bf16[6,512,1280]{2,1,0:T(8,128)(2,1)} %copy-done) | copy-start | bytes 23592964
  115.4 1.7 %copy-start.33 = (bf16[768,1536]{1,0:T(8,128)(2,1)S(1)}, bf16[768,1536]{1,0:T(8,128)(2,1)}, u32[]{:S(2)}) copy-start(bf16[768,1536]{1,0:T(8,128)(2,1)} %copy-done.32) | copy-start | bytes 7077892
  117.0 1.7 %copy-start.34 = (bf16[768,1536]{1,0:T(8,128)(2,1)S(1)}, bf16[768,1536]{1,0:T(8,128)(2,1)}, u32[]{:S(2)}) copy-start(bf16[768,1536]{1,0:T(8,128)(2,1)} %all-gather.5.cloned.1.call-done.wb) | copy-start | bytes 7077892
Sparse Core Ops, SparseCore 0:
  26.2 26.5 all-gather.2
  87.2 12.2 all-gather.4

commit v5 on v1

--- a/solution.py
+++ b/solution.py
@@ -47,7 +47,11 @@
     return v * cos + swapped * sin
 
 
-def project_kernel(head_size, step, tok, gain, wq, wkv, cos_t, sin_t, normed, q, kv, cos, sin):
+def score_factor(head_size):
+    return math.log2(math.e) / math.sqrt(head_size)
+
+
+def project_kernel(head_size, step, factor, tok, gain, wq, wkv, cos_t, sin_t, normed, q, kv, cos, sin):
     rows = tok.shape[0]
     tile = min(256, rows)
     fill_rotation(cos_t, sin_t, cos, sin, step)
@@ -66,14 +70,14 @@
         for h in range(wq.shape[1] // head_size):
             cols = slice(h * head_size, (h + 1) * head_size)
             part = jnp.dot(nb, wq[:, cols], preferred_element_type=F32)
-            q[at, cols] = rotate(part, c, s, even).astype(BF16)
+            q[at, cols] = (rotate(part, c, s, even) * factor).astype(BF16)
 
 
 def project(tok, gain, wq, wkv, cos_t, sin_t, head_size, step):
     rows, width = tok.shape
     qc, kc = wq.shape[1], wkv.shape[1]
     return pl.pallas_call(
-        functools.partial(project_kernel, head_size, step),
+        functools.partial(project_kernel, head_size, step, score_factor(head_size)),
         out_shape=(
             jax.ShapeDtypeStruct((rows, width), BF16),
             jax.ShapeDtypeStruct((rows, qc), BF16),
@@ -83,7 +87,7 @@
         ),
         in_specs=[spec(pltpu.VMEM)] * 6,
         out_specs=[spec(pltpu.VMEM)] * 5,
-        compiler_params=pltpu.CompilerParams(vmem_limit_bytes=48 * 2**20),
+        compiler_params=pltpu.CompilerParams(vmem_limit_bytes=20 * 2**20),
         cost_estimate=pl.CostEstimate(
             flops=2 * rows * width * (qc + kc), bytes_accessed=10 * 2**20, transcendentals=0
         ),
@@ -91,7 +95,7 @@
     )(tok, gain.reshape(1, width), wq, wkv, cos_t, sin_t)
 
 
-def other_kernel(head_size, order, normed, w0, w1, w2, w3, cos, sin, q):
+def other_kernel(head_size, factor, order, normed, w0, w1, w2, w3, cos, sin, q):
     rows = normed.shape[0]
     tile = min(256, rows)
     deep = w0.shape[0]
@@ -100,25 +104,25 @@
         at = pl.ds(i * tile, tile)
         c = cos[at, :]
         s = sin[at, :]
-        total = None
-        for n, w in enumerate((w0, w1, w2, w3)):
-            x = normed[at, pl.ds(pl.multiple_of(order[n] * deep, 128), deep)]
-            part = jnp.dot(x, w[...], preferred_element_type=F32)
-            total = part if total is None else total + part
         for h in range(q.shape[1] // head_size):
             cols = slice(h * head_size, (h + 1) * head_size)
-            q[at, cols] = rotate(total[:, cols], c, s, even).astype(BF16)
+            total = None
+            for n, w in enumerate((w0, w1, w2, w3)):
+                x = normed[at, pl.ds(pl.multiple_of(order[n] * deep, 128), deep)]
+                part = jnp.dot(x, w[:, cols], preferred_element_type=F32)
+                total = part if total is None else total + part
+            q[at, cols] = (rotate(total, c, s, even) * factor).astype(BF16)
 
 
 def project_other(normed, pieces, order, cos, sin, head_size):
     rows, width = normed.shape
     qc = pieces[0].shape[1]
     return pl.pallas_call(
-        functools.partial(other_kernel, head_size),
+        functools.partial(other_kernel, head_size, score_factor(head_size)),
         out_shape=jax.ShapeDtypeStruct((rows, qc), BF16),
         in_specs=[spec(pltpu.SMEM)] + [spec(pltpu.VMEM)] * 7,
         out_specs=spec(pltpu.VMEM),
-        compiler_params=pltpu.CompilerParams(vmem_limit_bytes=48 * 2**20),
+        compiler_params=pltpu.CompilerParams(vmem_limit_bytes=20 * 2**20),
         cost_estimate=pl.CostEstimate(
             flops=2 * rows * width * qc, bytes_accessed=6 * 2**20, transcendentals=0
         ),
@@ -142,9 +146,10 @@
         pick_kernel,
         out_shape=jax.ShapeDtypeStruct((count,) + pool.shape[1:], pool.dtype),
         in_specs=[spec(pltpu.SMEM), spec(ANY)],
-        out_specs=spec(ANY),
+        out_specs=spec(pltpu.VMEM),
         scratch_shapes=[pltpu.SemaphoreType.DMA((count,))],
-        cost_estimate=pl.CostEstimate(flops=0, bytes_accessed=2 * 2**20, transcendentals=0),
+        compiler_params=pltpu.CompilerParams(vmem_limit_bytes=60 * 2**20),
+        cost_estimate=pl.CostEstimate(flops=0, bytes_accessed=2**20, transcendentals=0),
         name="pick_pages",
     )(idx, pool)
 
@@ -171,10 +176,11 @@
     return pl.pallas_call(
         choose_kernel,
         out_shape=jax.ShapeDtypeStruct(came.shape, came.dtype),
-        in_specs=[spec(pltpu.SMEM), spec(pltpu.SMEM), spec(ANY), spec(ANY)],
-        out_specs=spec(ANY),
+        in_specs=[spec(pltpu.SMEM), spec(pltpu.SMEM), spec(ANY), spec(pltpu.VMEM)],
+        out_specs=spec(pltpu.VMEM),
         scratch_shapes=[pltpu.SemaphoreType.DMA((count,))],
-        cost_estimate=pl.CostEstimate(flops=0, bytes_accessed=2 * 2**20, transcendentals=0),
+        compiler_params=pltpu.CompilerParams(vmem_limit_bytes=60 * 2**20),
+        cost_estimate=pl.CostEstimate(flops=0, bytes_accessed=2**20, transcendentals=0),
         name="choose_pages",
     )(home, idx, pool, came)
 
@@ -182,73 +188,75 @@
 def attend_kernel(
     head_size,
     info,
-    qa,
-    qb,
-    mine,
-    peer,
+    qa_hbm,
+    qb_hbm,
+    k_mine,
+    k_peer,
+    v_mine,
+    v_peer,
     kv_own,
     kv_peer,
     woa,
-    w0,
-    w1,
-    w2,
-    w3,
-    out,
+    wob0,
+    wob1,
+    out_hbm,
+    qa,
+    qb,
     keys,
     vals,
     wa,
     wb,
     mix,
+    out,
     ksem,
     vsem,
     wsem,
+    osem,
 ):
     part = info[0]
     length = info[1]
     rows, half = qa.shape
-    pages, prow, _ = mine.shape
+    pages, prow, _ = k_mine.shape
     page = 2 * prow
     width = out.shape[1]
+    core = info[2]
+    deep = wob0.shape[0]
     nheads = half // head_size
     window = pages * page
-    wcols = w0.shape[1]
-
-    def move(which, dst, sem, lo):
+
+    def start(mine, peer, lo, dst, sem):
         cols = pl.ds(lo, head_size)
-        got = []
-        here = part == 0
-        for u in range(pages):
-            at0 = u * page
-            at1 = (u - rows // page) * page
-            for src, side in ((mine, part), (peer, 1 - part)):
-                row = pl.multiple_of(side * prow, prow)
-                got.append((True, src.at[u, :, cols], at0, row, prow))
-                if at1 >= 0:
-                    got.append((False, src.at[u, :, cols], at1, row, prow))
-        got.append((True, kv_own.at[:, cols], window, 0, rows))
-        got.append((False, kv_own.at[:, cols], window, 0, rows))
-        got.append((False, kv_peer.at[:, cols], window - rows, 0, rows))
-        return got
-
-    def start(dst, sem, lo):
-        moves = move(None, dst, sem, lo)
-        for case in (True, False):
-
-            @pl.when((part == 0) == case)
+        for case in (0, 1):
+
+            @pl.when(part == case)
             def _():
-                for which, src, at, row, count in moves:
-                    if which == case:
-                        pltpu.make_async_copy(src, dst.at[pl.ds(at + row, count), :], sem).start()
-
-    def finish(dst, sem, lo):
+                skip = case * rows // page
+                for u in range(skip, pages):
+                    for src, side in ((mine, case), (peer, 1 - case)):
+                        to = pl.ds((u - skip) * page + side * prow, prow)
+                        pltpu.make_async_copy(src.at[u], dst.at[to, :], sem).start()
+                if case == 1:
+                    to = pl.ds(window - rows, rows)
+                    pltpu.make_async_copy(kv_peer.at[:, cols], dst.at[to, :], sem).start()
+                to = pl.ds(window, rows)
+                pltpu.make_async_copy(kv_own.at[:, cols], dst.at[to, :], sem).start()
+
+    def finish(dst, sem):
         pltpu.make_async_copy(dst, dst, sem).wait()
 
-    start(keys, ksem, 0)
-    start(vals, vsem, head_size)
-    weights = [pltpu.make_async_copy(woa, wa, wsem.at[0])]
-    for n, w in enumerate((w0, w1, w2, w3)):
-        cols = pl.ds(pl.multiple_of(info[2 + n] * wcols, 128), wcols)
-        weights.append(pltpu.make_async_copy(w, wb.at[:, cols], wsem.at[1 + n]))
+    queries = [
+        pltpu.make_async_copy(qa_hbm, qa, wsem.at[3]),
+        pltpu.make_async_copy(qb_hbm, qb, wsem.at[4]),
+    ]
+    queries[0].start()
+    start(k_mine, k_peer, 0, keys, ksem)
+    queries[1].start()
+    start(v_mine, v_peer, head_size, vals, vsem)
+    weights = [
+        pltpu.make_async_copy(woa, wa, wsem.at[0]),
+        pltpu.make_async_copy(wob0, wb.at[pl.ds(core * deep, deep), :], wsem.at[1]),
+        pltpu.make_async_copy(wob1, wb.at[pl.ds((1 - core) * deep, deep), :], wsem.at[2]),
+    ]
     for c in weights:
         c.start()
 
@@ -258,8 +266,9 @@
     col_id = lax.broadcasted_iota(jnp.int32, (tile, tile), 1)
     first_seen = col_id >= row_id + 1
     last_seen = col_id <= row_id
-    factor = math.log2(math.e) / math.sqrt(head_size)
-    finish(keys, ksem, 0)
+    queries[0].wait()
+    finish(keys, ksem)
+    stores = []
     for i in range(rows // tile):
         at = pl.ds(i * tile, tile)
         for n, q in enumerate((qa, qb)):
@@ -278,45 +287,57 @@
                     axis=1,
                 )
                 top = jnp.max(s, axis=-1, keepdims=True)
-                e = jnp.exp2((s - top) * factor)
+                e = jnp.exp2(s - top)
                 total = jnp.sum(e, axis=-1, keepdims=True)
                 if i == 0 and n == 0 and h == 0:
-                    finish(vals, vsem, head_size)
+                    finish(vals, vsem)
+                    queries[1].wait()
                 vv = vals[pl.ds(i * tile, span), :]
                 m = jnp.dot(e.astype(BF16), vv, preferred_element_type=F32)
                 mix[n, at, cols] = (m / total).astype(BF16)
-    for c in weights:
-        c.wait()
-    for i in range(rows // tile):
-        at = pl.ds(i * tile, tile)
+        if i == 0:
+            for c in weights:
+                c.wait()
         row = part * rows + i * tile + lax.broadcasted_iota(jnp.int32, (tile, 1), 0)
         live = row < length
-        for j in range(width // wcols):
-            cols = slice(j * wcols, (j + 1) * wcols)
+        for j in range(width // 512):
+            cols = slice(j * 512, (j + 1) * 512)
             a = jnp.dot(mix[0, at, :], wa[:, cols], preferred_element_type=F32)
             b = jnp.dot(mix[1, at, :], wb[:, cols], preferred_element_type=F32)
             both = a.astype(BF16).astype(F32) + b.astype(BF16).astype(F32)
             out[at, cols] = jnp.where(live, both, 0.0).astype(BF16)
-
-
-def attend_pages(info, qa, qb, mine, peer, kv_own, kv_peer, woa, pieces, head_size):
+        stores.append(pltpu.make_async_copy(out.at[at, :], out_hbm.at[at, :], osem.at[i]))
+        stores[i].start()
+    for c in stores:
+        c.wait()
+
+
+def attend_pages(info, qa, qb, k_mine, k_peer, v_mine, v_peer, kv_own, kv_peer, woa, wobs):
     rows, half = qa.shape
     width = woa.shape[1]
-    window = mine.shape[0] * mine.shape[1] * 2
+    head_size = k_mine.shape[2]
+    window = k_mine.shape[0] * k_mine.shape[1] * 2
     return pl.pallas_call(
         functools.partial(attend_kernel, head_size),
         out_shape=jax.ShapeDtypeStruct((rows, width), BF16),
-        in_specs=[spec(pltpu.SMEM)] + [spec(pltpu.VMEM)] * 2 + [spec(ANY)] * 9,
-        out_specs=spec(pltpu.VMEM),
+        in_specs=[spec(pltpu.SMEM)]
+        + [spec(ANY)] * 2
+        + [spec(pltpu.VMEM)] * 4
+        + [spec(ANY)] * 5,
+        out_specs=spec(ANY),
         scratch_shapes=[
+            pltpu.VMEM((rows, half), BF16),
+            pltpu.VMEM((rows, half), BF16),
             pltpu.VMEM((window + rows, head_size), BF16),
             pltpu.VMEM((window + rows, head_size), BF16),
             pltpu.VMEM(woa.shape, BF16),
             pltpu.VMEM(woa.shape, BF16),
             pltpu.VMEM((2, rows, half), BF16),
+            pltpu.VMEM((rows, width), BF16),
             pltpu.SemaphoreType.DMA,
             pltpu.SemaphoreType.DMA,
             pltpu.SemaphoreType.DMA((5,)),
+            pltpu.SemaphoreType.DMA((rows // min(256, rows),)),
         ],
         compiler_params=pltpu.CompilerParams(vmem_limit_bytes=56 * 2**20),
         cost_estimate=pl.CostEstimate(
@@ -325,7 +346,7 @@
             transcendentals=rows * 6 * (window + 256),
         ),
         name="attend_and_out",
-    )(info, qa, qb, mine, peer, kv_own, kv_peer, woa, *pieces)
+    )(info, qa, qb, k_mine, k_peer, v_mine, v_peer, kv_own, kv_peer, woa, *wobs)
 
 
 def pair_shards(tokens, norm_gain, w_query, w_keyval, w_out, kv_pages, page_table, lengths, starts):
@@ -339,29 +360,22 @@
     swap = [(0, 1), (1, 0)]
     cores = [(i, i ^ 1) for i in range(ndp)]
 
-    quarter = rep * 2 + core
+    k_pool = lax.all_gather(kv_pages[:, :, :head_size], "dp", axis=0, tiled=True)
+    v_pool = lax.all_gather(kv_pages[:, :, head_size:], "dp", axis=0, tiled=True)
+
+    def peer_rows(w, at, parts):
+        deep = w.shape[0] // parts
+        return lax.ppermute(lax.dynamic_slice_in_dim(w, at * deep, deep, 0), "tensor", swap)
+
+    a = peer_rows(w_query, rep * 2 + core, 4)
+    a, w_out_late = lax.optimization_barrier((a, w_out))
+    b = lax.ppermute(a, "rep", swap)
+    wq_pieces = (a, b, lax.ppermute(a, "dp", cores), lax.ppermute(b, "dp", cores))
     order = jnp.stack(
-        [quarter, (1 - rep) * 2 + core, rep * 2 + 1 - core, (1 - rep) * 2 + 1 - core]
+        [rep * 2 + core, (1 - rep) * 2 + core, rep * 2 + 1 - core, (1 - rep) * 2 + 1 - core]
     ).astype(jnp.int32)
-
-    def spread(piece):
-        a = lax.ppermute(piece, "tensor", swap)
-        b = lax.ppermute(a, "rep", swap)
-        return a, b, lax.ppermute(a, "dp", cores), lax.ppermute(b, "dp", cores)
-
-    deep = w_query.shape[0] // 4
-    wide = w_out.shape[1] // 4
-    wq_pieces = spread(lax.dynamic_slice_in_dim(w_query, quarter * deep, deep, 0))
-    wo_pieces = spread(lax.dynamic_slice_in_dim(w_out, quarter * wide, wide, 1))
-
-    table = page_table[0]
-    peer_table = lax.ppermute(table, "rep", swap)
-    per_rep = kv_pages.shape[0] * ndp
-    pool = lax.all_gather(kv_pages, "dp", axis=0, tiled=True)
-    came = lax.ppermute(pick(pool, peer_table % per_rep), "rep", swap)
-    home = (table[:1] // per_rep == rep).astype(jnp.int32)
-    mine = choose(pool, table % per_rep, home, came)
-    peer = lax.ppermute(mine, "tensor", swap)
+    c = peer_rows(w_out_late, core, 2)
+    wo_pieces = (c, lax.ppermute(c, "dp", cores))
 
     step = 32
     cos_t, sin_t = rotation_tables(starts[0] + part * rows, rows, step, head_size)
@@ -370,8 +384,27 @@
     )
     kv_peer = lax.ppermute(kv_own, "tensor", swap)
     qb = project_other(normed, wq_pieces, order, cos, sin, head_size)
-    info = jnp.concatenate([jnp.stack([part, lengths[0]]).astype(jnp.int32), order])
-    return attend_pages(info, qa, qb, mine, peer, kv_own, kv_peer, w_out, wo_pieces, head_size)[None]
+
+    table = page_table[0]
+    peer_table = lax.ppermute(table, "rep", swap)
+    per_rep = kv_pages.shape[0] * ndp
+    home = (table[:1] // per_rep == rep).astype(jnp.int32)
+    own_at, peer_at = table % per_rep, peer_table % per_rep
+
+    wo_pieces, qb, kv_peer, k_pool, own_at, peer_at = lax.optimization_barrier(
+        (wo_pieces, qb, kv_peer, k_pool, own_at, peer_at)
+    )
+    k_came = lax.ppermute(pick(k_pool, peer_at), "rep", swap)
+    v_came = lax.ppermute(pick(v_pool, peer_at), "rep", swap)
+    k_mine = choose(k_pool, own_at, home, k_came)
+    k_peer = lax.ppermute(k_mine, "tensor", swap)
+    v_mine = choose(v_pool, own_at, home, v_came)
+    v_peer = lax.ppermute(v_mine, "tensor", swap)
+
+    info = jnp.stack([part, lengths[0], core]).astype(jnp.int32)
+    return attend_pages(
+        info, qa, qb, k_mine, k_peer, v_mine, v_peer, kv_own, kv_peer, w_out, wo_pieces
+    )[None]
 
 
 def rotate_pairs(values, positions, columns_from, head_size):
@@ -473,7 +506,8 @@
         P(("rep", "dp")),
         P(("rep", "dp")),
     )
-    body = pair_shards if mesh.shape["tensor"] == 2 and mesh.shape["rep"] == 2 else shards
+    pair = mesh.shape["tensor"] == 2 and mesh.shape["rep"] == 2 and mesh.shape["dp"] % 2 == 0
+    body = pair_shards if pair else shards
     return jax.shard_map(
         body,
         mesh=mesh,

time: 144 us -> 129 us (0.90)
  Pallas kernels: 57.3 us -> 28.4 us
  local copies, waits for them, and re-layouts: 9.76 us -> 16.5 us
  waiting for transfers between devices: 47 us -> 51.7 us
    ppermute x10, waiting for transfers between devices: 27.3 us -> 46.8 us  [the longest x2 36.8 us: peer_rows(): lax.ppermute(lax.dynamic_slice_in_dim(w, at * deep, deep, 0), 'tensor', s...]
    all_gather x1 -> x2, waiting for transfers between devices: 19 us -> 0.01 us  [the longest x1 0.01 us: pair_shards(): lax.all_gather(kv_pages[:, :, :head_size], 'dp', axis=0, tiled=True)]
    pallas_call x1 -> x2, Pallas kernels: 17.7 us -> 4.62 us  [pick(): pl.pallas_call(pick_kernel, out_shape=jax.ShapeDtypeStruct((count,) + poo...]
    pallas_call x1 -> x2, Pallas kernels: 17.8 us -> 5.22 us  [choose(): pl.pallas_call(choose_kernel, out_shape=jax.ShapeDtypeStruct(came.shape,...]
    unnamed x18 -> x30, local copies, waits for them, and re-layouts: 6.85 us -> 12.1 us
    ppermute x1, waiting for transfers between devices: 0.01 us -> 2.8 us  [pair_shards(): kv_peer = lax.ppermute(kv_own, 'tensor', swap)]
    pallas_call x2, Pallas kernels: 8.45 us -> 6.11 us  [the longest x1 3.23 us: project_other(): pl.pallas_call(functools.partial(other_kernel, head_size, score_factor(he...]
    slice x0 -> x1, local copies, waits for them, and re-layouts: none -> 1.9 us  [pair_shards(): kv_pages[:, :, head_size:]]
  transfers between devices with their start and end apart: 13 -> 14, of which waited for: 5 -> 7; matrix products, arithmetic and copies ran while one was open for 3% -> 4% of each run, Pallas kernels for 31% -> 12%
where the time goes in v5:
time: 129 us; the launch traced here: 128 us
  waiting for transfers between devices  51.7 us (40%)
  Pallas kernels  28.4 us (22%)
  local copies, waits for them, and re-layouts  16.5 us (13%)
  between operations  15 us (12%)
  starting transfers between devices  14.6 us (11%)
  other arithmetic  2.15 us (2%)
    ppermute x2, waiting for transfers between devices, peer_rows(): lax.ppermute(lax.dynamic_slice_in_dim(w, at * deep, deep, 0), 'tensor', s...  36.8 us
    pallas_call x1, Pallas kernels, attend_pages(): pl.pallas_call(functools.partial(attend_kernel, head_size), out_shape=jax...  12.4 us
    unnamed x30, local copies, waits for them, and re-layouts  12.1 us
    pallas_call x2, Pallas kernels, choose(): pl.pallas_call(choose_kernel, out_shape=jax.ShapeDtypeStruct(came.shape,...  5.22 us
    ppermute x1, waiting for transfers between devices, pair_shards(): v_peer = lax.ppermute(v_mine, 'tensor', swap)  4.99 us
    ppermute x2, starting transfers between devices, peer_rows(): lax.ppermute(lax.dynamic_slice_in_dim(w, at * deep, deep, 0), 'tensor', s...  4.84 us
    ppermute x1, waiting for transfers between devices, pair_shards(): k_came = lax.ppermute(pick(k_pool, peer_at), 'rep', swap)  4.83 us
    pallas_call x2, Pallas kernels, pick(): pl.pallas_call(pick_kernel, out_shape=jax.ShapeDtypeStruct((count,) + poo...  4.62 us
  transfers between devices with their start and end apart: 14, of which 7 were waited for; matrix products, arithmetic and copies ran while one was open for 4% of the time, Pallas kernels for 12%

profile of v5, /device:TPU:0, one launch (start us, length us, event | category | flops | bytes accessed | tf_op | source)
XLA Modules:
  0.0 128.4 jit_solution(11486365310527317995)
XLA Ops:
  6.5 0.0 all-gather.3.cloned.1.call-start
  6.5 1.9 %fusion.9 = (bf16[8,64,256]{2,1,0:T(8,128)(2,1)}, bf16[8,64,256]{2,1,0:T(8,128)(2,1)}) fusion(bf16[8,64,512]{2,1,0:T(8,128)(2,1)} %param.14), kind=kLoop, calls=%fused_computation.30 | loop fusion | bytes 1048576 | tf_op jit(solution)/shard_map/slice | solution.py:364
  8.4 0.0 all-gather.3.cloned.1.call-update
  8.5 0.0 all-gather.5.cloned.1.call-start
  8.5 0.7 all-gather.5.cloned.1.call-update
  9.2 0.0 copy-start.11
  9.2 1.1 constant_dynamic-slice_fusion.1
  10.4 3.0 %collective-permute-start = (bf16[384,768]{1,0:T(8,128)(2,1)S(1)}, bf16[384,768]{1,0:T(8,128)(2,1)S(1)}, u32[]{:S(2)}, u32[]{:S(2)}) collective-permute-start(bf16[384,768]{1,0:T(8,128)(2,1)S(1)} %constant_dynamic-slice_fusion.1), channel_id=1, source_target_pairs={{0,1},{1,0},{2,3},{3,2},{4,5},{5,4},{6,7},{7,6},{8,9},{9,8},{10,11... | collective-permute-start | bytes 1769480 | tf_op jit(solution)/shard_map/ppermute | solution.py:368
  13.4 13.3 %collective-permute-done.w0 = bf16[384,768]{1,0:T(8,128)(2,1)S(1)} collective-permute-done((bf16[384,768]{1,0:T(8,128)(2,1)S(1)}, bf16[384,768]{1,0:T(8,128)(2,1)S(1)}, u32[]{:S(2)}, u32[]{:S(2)}) %collective-permute-start) | collective-permute-done | bytes 589856 | tf_op jit(solution)/shard_map/ppermute | solution.py:368
  26.7 1.3 %constant_dynamic-slice_fusion = bf16[384,1536]{1,0:T(8,128)(2,1)S(1)} fusion(bf16[768,1536]{1,0:T(8,128)(2,1)} %woa.1, s32[]{:T(128)S(6)} %select_n.60), kind=kLoop, calls=%fused_computation.28 | loop fusion | bytes 2359300 | tf_op jit(solution)/shard_map/dynamic_slice | solution.py:368
  28.1 1.8 %collective-permute-start.1 = (bf16[384,1536]{1,0:T(8,128)(2,1)S(1)}, bf16[384,1536]{1,0:T(8,128)(2,1)}, u32[]{:S(2)}, u32[]{:S(2)}) collective-permute-start(bf16[384,1536]{1,0:T(8,128)(2,1)S(1)} %constant_dynamic-slice_fusion), channel_id=1, source_target_pairs={{0,1},{1,0},{2,3},{3,2},{4,5},{5,4},{6,7},{7,6},{8,9},{9,8},{10,11... | collective-permute-start | bytes 3538952 | tf_op jit(solution)/shard_map/ppermute | solution.py:368
  29.9 1.5 %collective-permute-start.3 = (bf16[384,768]{1,0:T(8,128)(2,1)S(1)}, bf16[384,768]{1,0:T(8,128)(2,1)S(1)}, u32[]{:S(2)}, u32[]{:S(2)}) collective-permute-start(bf16[384,768]{1,0:T(8,128)(2,1)S(1)} %collective-permute-done.w0), channel_id=1, source_target_pairs={{0,16},{16,0},{1,17},{17,1},{2,18},{18,2},{3,19},{19,3},{4,20},{20... | collective-permute-start | bytes 1769480 | tf_op jit(solution)/shard_map/ppermute | solution.py:372
  31.4 0.0 copy-done.11
  32.1 23.4 %collective-permute-done.1.wob0 = bf16[384,1536]{1,0:T(8,128)(2,1)} collective-permute-done((bf16[384,1536]{1,0:T(8,128)(2,1)S(1)}, bf16[384,1536]{1,0:T(8,128)(2,1)}, u32[]{:S(2)}, u32[]{:S(2)}) %collective-permute-start.1) | collective-permute-done | bytes 1179680 | tf_op jit(solution)/shard_map/ppermute | solution.py:368
  55.5 0.0 collective-permute-start.2
  55.5 0.1 pad_maximum_fusion
  55.6 0.3 fusion
  55.8 0.6 collective-permute-start.4
  56.4 0.0 collective-permute-done.3.w1
  56.4 0.1 collective-permute-start.5
  56.5 0.0 copy-start.5
  56.5 1.7 %copy-done.5 = bf16[1536,768]{1,0:T(8,128)(2,1)S(1)} copy-done((bf16[1536,768]{1,0:T(8,128)(2,1)S(1)}, bf16[1536,768]{1,0:T(8,128)(2,1)}, u32[]{:S(2)}) %copy-start.5) | copy-done | bytes 2359320
  58.2 0.0 copy-start.6
  58.2 1.4 %copy-done.6 = bf16[1,512,1536]{2,1,0:T(8,128)(2,1)S(1)} copy-done((bf16[1,512,1536]{2,1,0:T(8,128)(2,1)S(1)}, bf16[1,512,1536]{2,1,0:T(8,128)(2,1)}, u32[]{:S(2)}) %copy-start.6) | copy-done | bytes 1572888
  59.6 0.0 copy-start.7
  59.6 1.4 %copy-done.7 = bf16[1536,512]{1,0:T(8,128)(2,1)S(1)} copy-done((bf16[1536,512]{1,0:T(8,128)(2,1)S(1)}, bf16[1536,512]{1,0:T(8,128)(2,1)}, u32[]{:S(2)}) %copy-start.7) | copy-done | bytes 1572888
  61.0 2.9 %project_own.1 = (bf16[512,1536]{1,0:T(8,128)(2,1)S(1)}, bf16[512,768]{1,0:T(8,128)(2,1)S(1)}, bf16[512,512]{1,0:T(8,128)(2,1)}, f32[512,256]{1,0:T(8,128)S(1)}, f32[512,256]{1,0:T(8,128)S(1)}) custom-call(bf16[512,1536]{1,0:T(8,128)(2,1)S(1)} %bitcast.15, f32[1,1536]{1,0:T(1,128)S(1)} %reshape.37.gain, bf16[1536,768]{1,0:T(8,128)(2,1)S(1)} %copy-done.5, ...), custom_call_target="tpu_custom_call" | custom-call | flops 2013265920 | bytes 10485760 | tf_op jit(solution)/shard_map/project_own/pallas_call | solution.py:79
  63.9 0.8 copy-done.1
  64.7 0.8 copy-done.3
  65.5 0.9 copy-done.8
  66.4 1.4 %collective-permute-start.6 = (bf16[512,512]{1,0:T(8,128)(2,1)}, bf16[512,512]{1,0:T(8,128)(2,1)}, u32[]{:S(2)}, u32[]{:S(2)}) collective-permute-start(bf16[512,512]{1,0:T(8,128)(2,1)} %get-tuple-element.25.kv_own), channel_id=1, source_target_pairs={{0,1},{1,0},{2,3},{3,2},{4,5},{5,4},{6,7},{7,6},{8,9},{9,8},{10,11... | collective-permute-start | bytes 1572872 | tf_op jit(solution)/shard_map/ppermute | solution.py:385
  67.8 0.0 copy-done.12
  67.8 1.5 %collective-permute-start.7 = (s32[8]{0:T(128)S(1)}, s32[8]{0:T(128)S(1)}, u32[]{:S(2)}, u32[]{:S(2)}) collective-permute-start(s32[8]{0:T(128)S(1)} %bitcast.16), channel_id=1, source_target_pairs={{0,16},{16,0},{1,17},{17,1},{2,18},{18,2},{3,19},{19,3},{4,20},{20... | collective-permute-start | bytes 104 | tf_op jit(solution)/shard_map/ppermute | solution.py:389
  69.3 0.1 pad_add_fusion.1.order
  69.4 0.5 and_select_fusion.1.idx
  69.9 1.5 %collective-permute-done.7 = s32[8]{0:T(128)S(1)} collective-permute-done((s32[8]{0:T(128)S(1)}, s32[8]{0:T(128)S(1)}, u32[]{:S(2)}, u32[]{:S(2)}) %collective-permute-start.7) | collective-permute-done | bytes 64 | tf_op jit(solution)/shard_map/ppermute | solution.py:389
  71.4 0.5 and_select_fusion.idx
  71.9 0.0 collective-permute-done.4.w2
  71.9 0.0 collective-permute-done.5.w3
  71.9 1.0 copy-done.2
  73.0 1.0 copy-done.4
  74.0 3.2 %project_other.1.qb_hbm = bf16[512,768]{1,0:T(8,128)(2,1)S(1)} custom-call(s32[4]{0:T(128)S(1)} %pad_add_fusion.1.order, bf16[512,1536]{1,0:T(8,128)(2,1)S(1)} %get-tuple-element.21.normed, bf16[384,768]{1,0:T(8,128)(2,1)S(1)} %collective-permute-done.w0, bf16[384,768]{1,0:T(8,128)(2,1)S(1)} %collective-permute-done.3.w1, ...), custom_call_target="tpu_custom_call" | custom-call | flops 1207959552 | bytes 6291456 | tf_op jit(solution)/shard_map/project_other/pallas_call | solution.py:120
  77.2 0.0 copy-start
  77.2 1.0 copy-done
  78.2 2.8 %collective-permute-done.6.kv_peer = bf16[512,512]{1,0:T(8,128)(2,1)} collective-permute-done((bf16[512,512]{1,0:T(8,128)(2,1)}, bf16[512,512]{1,0:T(8,128)(2,1)}, u32[]{:S(2)}, u32[]{:S(2)}) %collective-permute-start.6) | collective-permute-done | bytes 524320 | tf_op jit(solution)/shard_map/ppermute | solution.py:385
  81.0 0.0 collective-permute-done.2.wob1
  81.0 2.3 %pick_pages.2 = bf16[8,64,256]{2,1,0:T(8,128)(2,1)} custom-call(s32[8]{0:T(128)} %and_select_fusion.idx, bf16[64,64,256]{2,1,0:T(8,128)(2,1)} %all-gather.3.cloned.1.call-done.pool), custom_call_target="tpu_custom_call" | custom-call | bytes 1048576 | tf_op jit(solution)/shard_map/pick_pages/pallas_call | solution.py:145
  83.3 1.5 %collective-permute-start.8 = (bf16[8,64,256]{2,1,0:T(8,128)(2,1)}, bf16[8,64,256]{2,1,0:T(8,128)(2,1)S(1)}, u32[]{:S(2)}, u32[]{:S(2)}) collective-permute-start(bf16[8,64,256]{2,1,0:T(8,128)(2,1)} %pick_pages.2), channel_id=1, source_target_pairs={{0,16},{16,0},{1,17},{17,1},{2,18},{18,2},{3,19},{19,3},{4,20},{20... | collective-permute-start | bytes 786440 | tf_op jit(solution)/shard_map/ppermute | solution.py:397
  84.8 2.3 %pick_pages.3 = bf16[8,64,256]{2,1,0:T(8,128)(2,1)} custom-call(s32[8]{0:T(128)} %and_select_fusion.idx, bf16[64,64,256]{2,1,0:T(8,128)(2,1)} %all-gather.5.cloned.1.call-done.pool), custom_call_target="tpu_custom_call" | custom-call | bytes 1048576 | tf_op jit(solution)/shard_map/pick_pages/pallas_call | solution.py:145
  87.1 0.7 collective-permute-start.10
  88.0 4.8 %collective-permute-done.8.came = bf16[8,64,256]{2,1,0:T(8,128)(2,1)S(1)} collective-permute-done((bf16[8,64,256]{2,1,0:T(8,128)(2,1)}, bf16[8,64,256]{2,1,0:T(8,128)(2,1)S(1)}, u32[]{:S(2)}, u32[]{:S(2)}) %collective-permute-start.8) | collective-permute-done | bytes 262176 | tf_op jit(solution)/shard_map/ppermute | solution.py:397
  92.8 0.7 copy-done.10
  93.5 2.6 %choose_pages.2.k_mine = bf16[8,64,256]{2,1,0:T(8,128)(2,1)} custom-call(s32[1]{0:T(128)S(6)} %convert_element_type.19.home, s32[8]{0:T(128)} %and_select_fusion.1.idx, bf16[64,64,256]{2,1,0:T(8,128)(2,1)} %all-gather.3.cloned.1.call-done.pool, bf16[8,64,256]{2,1,0:T(8,128)(2,1)} %copy-done.10), custom_call_target="tpu_custom_call" | custom-call | bytes 1048576 | tf_op jit(solution)/shard_map/choose_pages/pallas_call | solution.py:176
  96.1 1.5 %collective-permute-start.9 = (bf16[8,64,256]{2,1,0:T(8,128)(2,1)}, bf16[8,64,256]{2,1,0:T(8,128)(2,1)S(1)}, u32[]{:S(2)}, u32[]{:S(2)}) collective-permute-start(bf16[8,64,256]{2,1,0:T(8,128)(2,1)} %choose_pages.2.k_mine), channel_id=1, source_target_pairs={{0,1},{1,0},{2,3},{3,2},{4,5},{5,4},{6,7},{7,6},{8,9},{9,8},{10,11... | collective-permute-start | bytes 786440 | tf_op jit(solution)/shard_map/ppermute | solution.py:400
  97.6 0.0 collective-permute-done.10.came
  97.6 0.7 copy-done.9
  98.3 2.6 %choose_pages.3.v_mine = bf16[8,64,256]{2,1,0:T(8,128)(2,1)} custom-call(s32[1]{0:T(128)S(6)} %convert_element_type.19.home, s32[8]{0:T(128)} %and_select_fusion.1.idx, bf16[64,64,256]{2,1,0:T(8,128)(2,1)} %all-gather.5.cloned.1.call-done.pool, bf16[8,64,256]{2,1,0:T(8,128)(2,1)} %copy-done.9), custom_call_target="tpu_custom_call" | custom-call | bytes 1048576 | tf_op jit(solution)/shard_map/choose_pages/pallas_call | solution.py:176
  100.9 1.0 collective-permute-start.11
  102.6 0.7 pad_add_fusion.info
  103.2 0.2 collective-permute-done.9.k_peer
  103.4 5.0 %collective-permute-done.11.v_peer = bf16[8,64,256]{2,1,0:T(8,128)(2,1)S(1)} collective-permute-done((bf16[8,64,256]{2,1,0:T(8,128)(2,1)}, bf16[8,64,256]{2,1,0:T(8,128)(2,1)S(1)}, u32[]{:S(2)}, u32[]{:S(2)}) %collective-permute-start.11) | collective-permute-done | bytes 262176 | tf_op jit(solution)/shard_map/ppermute | solution.py:402
  108.4 0.0 copy-done.13
  108.4 0.7 copy-done.14
  109.1 12.4 %attend_and_out.1 = bf16[512,1536]{1,0:T(8,128)(2,1)} custom-call(s32[3]{0:T(128)} %pad_add_fusion.info, bf16[512,768]{1,0:T(8,128)(2,1)} %copy-done.8, bf16[512,768]{1,0:T(8,128)(2,1)} %copy-done, bf16[8,64,256]{2,1,0:T(8,128)(2,1)} %choose_pages.2.k_mine, bf16[8,64,256]{2,1,0:T(8,128)(2,1)} %copy-done.13, bf16[8,64,256]{2,1,0:T(8,128)(2,1)} %choose_pages.3.v_mine, ...), custom_call_target="tpu_custom_call" | custom-call | flops 6442450944 | bytes 12582912 | tf_op jit(solution)/shard_map/attend_and_out/pallas_call | solution.py:320
  (16 shorter events, 0.0 us)
Async XLA Ops:
  6.5 74.5 %all-gather.3.cloned.1.call-start = ((), (), s32[]{:S(2)}) async-start(), calls=%async_computation | async-start | bytes 2359296 | tf_op jit(solution)/shard_map/all_gather | solution.py:363
  8.5 76.3 %all-gather.5.cloned.1.call-start = ((), (), s32[]{:S(2)}) async-start(), calls=%async_computation.1 | async-start | bytes 2359296 | tf_op jit(solution)/shard_map/all_gather | solution.py:364
  9.2 22.1 %copy-start.11 = (f32[1536]{0:T(1024)S(1)}, f32[1536]{0:T(1024)}, u32[]{:S(2)}) copy-start(f32[1536]{0:T(1024)} %param.10) | copy-start | bytes 18436
  10.4 16.4 %collective-permute-start = (bf16[384,768]{1,0:T(8,128)(2,1)S(1)}, bf16[384,768]{1,0:T(8,128)(2,1)S(1)}, u32[]{:S(2)}, u32[]{:S(2)}) collective-permute-start(bf16[384,768]{1,0:T(8,128)(2,1)S(1)} %constant_dynamic-slice_fusion.1), channel_id=1, source_target_pairs={{0,1},{1,0},{2,3},{3,2},{4,5},{5,4},{6,7},{7,6},{8,9},{9,8},{10,11... | collective-permute-start | bytes 1769480 | tf_op jit(solution)/shard_map/ppermute | solution.py:368
  28.1 27.4 %collective-permute-start.1 = (bf16[384,1536]{1,0:T(8,128)(2,1)S(1)}, bf16[384,1536]{1,0:T(8,128)(2,1)}, u32[]{:S(2)}, u32[]{:S(2)}) collective-permute-start(bf16[384,1536]{1,0:T(8,128)(2,1)S(1)} %constant_dynamic-slice_fusion), channel_id=1, source_target_pairs={{0,1},{1,0},{2,3},{3,2},{4,5},{5,4},{6,7},{7,6},{8,9},{9,8},{10,11... | collective-permute-start | bytes 3538952 | tf_op jit(solution)/shard_map/ppermute | solution.py:368
  29.9 26.5 %collective-permute-start.3 = (bf16[384,768]{1,0:T(8,128)(2,1)S(1)}, bf16[384,768]{1,0:T(8,128)(2,1)S(1)}, u32[]{:S(2)}, u32[]{:S(2)}) collective-permute-start(bf16[384,768]{1,0:T(8,128)(2,1)S(1)} %collective-permute-done.w0), channel_id=1, source_target_pairs={{0,16},{16,0},{1,17},{17,1},{2,18},{18,2},{3,19},{19,3},{4,20},{20... | collective-permute-start | bytes 1769480 | tf_op jit(solution)/shard_map/ppermute | solution.py:372
  55.5 25.5 %collective-permute-start.2 = (bf16[384,1536]{1,0:T(8,128)(2,1)}, bf16[384,1536]{1,0:T(8,128)(2,1)}, u32[]{:S(2)}, u32[]{:S(2)}) collective-permute-start(bf16[384,1536]{1,0:T(8,128)(2,1)} %collective-permute-done.1.wob0), channel_id=1, source_target_pairs={{0,2},{2,0},{4,6},{6,4},{8,10},{10,8},{12,14},{14,12},{1,3},{3,1},... | collective-permute-start | bytes 3538952 | tf_op jit(solution)/shard_map/ppermute | solution.py:378
  55.8 16.1 %collective-permute-start.4 = (bf16[384,768]{1,0:T(8,128)(2,1)S(1)}, bf16[384,768]{1,0:T(8,128)(2,1)S(1)}, u32[]{:S(2)}, u32[]{:S(2)}) collective-permute-start(bf16[384,768]{1,0:T(8,128)(2,1)S(1)} %collective-permute-done.w0), channel_id=1, source_target_pairs={{0,2},{2,0},{4,6},{6,4},{8,10},{10,8},{12,14},{14,12},{1,3},{3,1},... | collective-permute-start | bytes 1769480 | tf_op jit(solution)/shard_map/ppermute | solution.py:373
  56.4 15.5 %collective-permute-start.5 = (bf16[384,768]{1,0:T(8,128)(2,1)S(1)}, bf16[384,768]{1,0:T(8,128)(2,1)}, u32[]{:S(2)}, u32[]{:S(2)}) collective-permute-start(bf16[384,768]{1,0:T(8,128)(2,1)S(1)} %collective-permute-done.3.w1), channel_id=1, source_target_pairs={{0,2},{2,0},{4,6},{6,4},{8,10},{10,8},{12,14},{14,12},{1,3},{3,1},... | collective-permute-start | bytes 1769480 | tf_op jit(solution)/shard_map/ppermute | solution.py:373
  56.5 1.7 %copy-start.5 = (bf16[1536,768]{1,0:T(8,128)(2,1)S(1)}, bf16[1536,768]{1,0:T(8,128)(2,1)}, u32[]{:S(2)}) copy-start(bf16[1536,768]{1,0:T(8,128)(2,1)} %wq.1) | copy-start | bytes 7077892
  58.2 1.4 %copy-start.6 = (bf16[1,512,1536]{2,1,0:T(8,128)(2,1)S(1)}, bf16[1,512,1536]{2,1,0:T(8,128)(2,1)}, u32[]{:S(2)}) copy-start(bf16[1,512,1536]{2,1,0:T(8,128)(2,1)} %param.9) | copy-start | bytes 4718596
  59.6 1.4 %copy-start.7 = (bf16[1536,512]{1,0:T(8,128)(2,1)S(1)}, bf16[1536,512]{1,0:T(8,128)(2,1)}, u32[]{:S(2)}) copy-start(bf16[1536,512]{1,0:T(8,128)(2,1)} %wkv.1) | copy-start | bytes 4718596
  61.0 6.8 %copy-start.12 = (s32[1,8]{1,0:T(1,128)S(1)}, s32[1,8]{1,0:T(1,128)}, u32[]{:S(2)}) copy-start(s32[1,8]{1,0:T(1,128)} %param.15) | copy-start | bytes 100
  63.9 0.8 copy-start.1
  64.7 0.8 copy-start.3
  65.5 0.9 copy-start.8
  66.4 14.6 %collective-permute-start.6 = (bf16[512,512]{1,0:T(8,128)(2,1)}, bf16[512,512]{1,0:T(8,128)(2,1)}, u32[]{:S(2)}, u32[]{:S(2)}) collective-permute-start(bf16[512,512]{1,0:T(8,128)(2,1)} %get-tuple-element.25.kv_own), channel_id=1, source_target_pairs={{0,1},{1,0},{2,3},{3,2},{4,5},{5,4},{6,7},{7,6},{8,9},{9,8},{10,11... | collective-permute-start | bytes 1572872 | tf_op jit(solution)/shard_map/ppermute | solution.py:385
  67.8 3.5 %collective-permute-start.7 = (s32[8]{0:T(128)S(1)}, s32[8]{0:T(128)S(1)}, u32[]{:S(2)}, u32[]{:S(2)}) collective-permute-start(s32[8]{0:T(128)S(1)} %bitcast.16), channel_id=1, source_target_pairs={{0,16},{16,0},{1,17},{17,1},{2,18},{18,2},{3,19},{19,3},{4,20},{20... | collective-permute-start | bytes 104 | tf_op jit(solution)/shard_map/ppermute | solution.py:389
  71.9 1.0 copy-start.2
  73.0 1.0 copy-start.4
  77.2 1.0 copy-start
  83.3 9.5 %collective-permute-start.8 = (bf16[8,64,256]{2,1,0:T(8,128)(2,1)}, bf16[8,64,256]{2,1,0:T(8,128)(2,1)S(1)}, u32[]{:S(2)}, u32[]{:S(2)}) collective-permute-start(bf16[8,64,256]{2,1,0:T(8,128)(2,1)} %pick_pages.2), channel_id=1, source_target_pairs={{0,16},{16,0},{1,17},{17,1},{2,18},{18,2},{3,19},{19,3},{4,20},{20... | collective-permute-start | bytes 786440 | tf_op jit(solution)/shard_map/ppermute | solution.py:397
  87.1 10.5 %collective-permute-start.10 = (bf16[8,64,256]{2,1,0:T(8,128)(2,1)}, bf16[8,64,256]{2,1,0:T(8,128)(2,1)S(1)}, u32[]{:S(2)}, u32[]{:S(2)}) collective-permute-start(bf16[8,64,256]{2,1,0:T(8,128)(2,1)} %pick_pages.3), channel_id=1, source_target_pairs={{0,16},{16,0},{1,17},{17,1},{2,18},{18,2},{3,19},{19,3},{4,20},{20... | collective-permute-start | bytes 786440 | tf_op jit(solution)/shard_map/ppermute | solution.py:398
  92.8 0.7 copy-start.10
  96.1 7.3 %collective-permute-start.9 = (bf16[8,64,256]{2,1,0:T(8,128)(2,1)}, bf16[8,64,256]{2,1,0:T(8,128)(2,1)S(1)}, u32[]{:S(2)}, u32[]{:S(2)}) collective-permute-start(bf16[8,64,256]{2,1,0:T(8,128)(2,1)} %choose_pages.2.k_mine), channel_id=1, source_target_pairs={{0,1},{1,0},{2,3},{3,2},{4,5},{5,4},{6,7},{7,6},{8,9},{9,8},{10,11... | collective-permute-start | bytes 786440 | tf_op jit(solution)/shard_map/ppermute | solution.py:400
  97.6 0.7 copy-start.9
  100.9 7.4 %collective-permute-start.11 = (bf16[8,64,256]{2,1,0:T(8,128)(2,1)}, bf16[8,64,256]{2,1,0:T(8,128)(2,1)S(1)}, u32[]{:S(2)}, u32[]{:S(2)}) collective-permute-start(bf16[8,64,256]{2,1,0:T(8,128)(2,1)} %choose_pages.3.v_mine), channel_id=1, source_target_pairs={{0,1},{1,0},{2,3},{3,2},{4,5},{5,4},{6,7},{7,6},{8,9},{9,8},{10,11... | collective-permute-start | bytes 786440 | tf_op jit(solution)/shard_map/ppermute | solution.py:402
  103.4 5.0 %copy-start.13 = (bf16[8,64,256]{2,1,0:T(8,128)(2,1)}, bf16[8,64,256]{2,1,0:T(8,128)(2,1)S(1)}, u32[]{:S(2)}) copy-start(bf16[8,64,256]{2,1,0:T(8,128)(2,1)S(1)} %collective-permute-done.9.k_peer) | copy-start | bytes 786436
  108.4 0.7 copy-start.14
Sparse Core Ops, SparseCore 0:
  9.0 31.7 all-gather.2
  42.4 28.5 all-gather.4

commit v6 on v5

--- a/solution.py
+++ b/solution.py
@@ -130,10 +130,14 @@
     )(order, normed, *pieces, cos, sin)
 
 
-def pick_kernel(idx, pool, out, sem):
-    copies = [
-        pltpu.make_async_copy(pool.at[idx[j]], out.at[j], sem.at[j]) for j in range(out.shape[0])
-    ]
+def pick_kernel(idx, pool, keys, vals, sem):
+    count, _, head_size = keys.shape
+    copies = []
+    for n, out in enumerate((keys, vals)):
+        cols = pl.ds(n * head_size, head_size)
+        for j in range(count):
+            page = pool.at[idx[j], :, cols]
+            copies.append(pltpu.make_async_copy(page, out.at[j], sem.at[n * count + j]))
     for c in copies:
         c.start()
     for c in copies:
@@ -142,47 +146,17 @@
 
 def pick(pool, idx):
     count = idx.shape[0]
+    half = jax.ShapeDtypeStruct((count, pool.shape[1], pool.shape[2] // 2), pool.dtype)
     return pl.pallas_call(
         pick_kernel,
-        out_shape=jax.ShapeDtypeStruct((count,) + pool.shape[1:], pool.dtype),
+        out_shape=(half, half),
         in_specs=[spec(pltpu.SMEM), spec(ANY)],
-        out_specs=spec(pltpu.VMEM),
-        scratch_shapes=[pltpu.SemaphoreType.DMA((count,))],
+        out_specs=[spec(pltpu.VMEM)] * 2,
+        scratch_shapes=[pltpu.SemaphoreType.DMA((2 * count,))],
         compiler_params=pltpu.CompilerParams(vmem_limit_bytes=60 * 2**20),
         cost_estimate=pl.CostEstimate(flops=0, bytes_accessed=2**20, transcendentals=0),
         name="pick_pages",
     )(idx, pool)
-
-
-def choose_kernel(home, idx, pool, came, out, sem):
-    count = out.shape[0]
-
-    @pl.when(home[0] == 1)
-    def _():
-        for j in range(count):
-            pltpu.make_async_copy(pool.at[idx[j]], out.at[j], sem.at[j]).start()
-
-    @pl.when(home[0] == 0)
-    def _():
-        for j in range(count):
-            pltpu.make_async_copy(came.at[j], out.at[j], sem.at[j]).start()
-
-    for j in range(count):
-        pltpu.make_async_copy(came.at[j], out.at[j], sem.at[j]).wait()
-
-
-def choose(pool, idx, home, came):
-    count = idx.shape[0]
-    return pl.pallas_call(
-        choose_kernel,
-        out_shape=jax.ShapeDtypeStruct(came.shape, came.dtype),
-        in_specs=[spec(pltpu.SMEM), spec(pltpu.SMEM), spec(ANY), spec(pltpu.VMEM)],
-        out_specs=spec(pltpu.VMEM),
-        scratch_shapes=[pltpu.SemaphoreType.DMA((count,))],
-        compiler_params=pltpu.CompilerParams(vmem_limit_bytes=60 * 2**20),
-        cost_estimate=pl.CostEstimate(flops=0, bytes_accessed=2**20, transcendentals=0),
-        name="choose_pages",
-    )(home, idx, pool, came)
 
 
 def attend_kernel(
@@ -360,45 +334,47 @@
     swap = [(0, 1), (1, 0)]
     cores = [(i, i ^ 1) for i in range(ndp)]
 
-    k_pool = lax.all_gather(kv_pages[:, :, :head_size], "dp", axis=0, tiled=True)
-    v_pool = lax.all_gather(kv_pages[:, :, head_size:], "dp", axis=0, tiled=True)
+    pool = lax.all_gather(kv_pages, "dp", axis=0, tiled=True)
 
     def peer_rows(w, at, parts):
         deep = w.shape[0] // parts
         return lax.ppermute(lax.dynamic_slice_in_dim(w, at * deep, deep, 0), "tensor", swap)
 
+    step = 32
+    cos_t, sin_t = rotation_tables(starts[0] + part * rows, rows, step, head_size)
+    normed, qa, kv_own, cos, sin = project(
+        tokens[0], norm_gain, w_query, w_keyval, cos_t, sin_t, head_size, step
+    )
+
     a = peer_rows(w_query, rep * 2 + core, 4)
-    a, w_out_late = lax.optimization_barrier((a, w_out))
+    a, kv_own, w_out_late, page_table = lax.optimization_barrier((a, kv_own, w_out, page_table))
     b = lax.ppermute(a, "rep", swap)
+    c = peer_rows(w_out_late, core, 2)
+    table = page_table[0]
+    peer_table = lax.ppermute(table, "rep", swap)
     wq_pieces = (a, b, lax.ppermute(a, "dp", cores), lax.ppermute(b, "dp", cores))
     order = jnp.stack(
         [rep * 2 + core, (1 - rep) * 2 + core, rep * 2 + 1 - core, (1 - rep) * 2 + 1 - core]
     ).astype(jnp.int32)
-    c = peer_rows(w_out_late, core, 2)
+    qb = project_other(normed, wq_pieces, order, cos, sin, head_size)
+    c, qb, kv_own = lax.optimization_barrier((c, qb, kv_own))
     wo_pieces = (c, lax.ppermute(c, "dp", cores))
-
-    step = 32
-    cos_t, sin_t = rotation_tables(starts[0] + part * rows, rows, step, head_size)
-    normed, qa, kv_own, cos, sin = project(
-        tokens[0], norm_gain, w_query, w_keyval, cos_t, sin_t, head_size, step
-    )
     kv_peer = lax.ppermute(kv_own, "tensor", swap)
-    qb = project_other(normed, wq_pieces, order, cos, sin, head_size)
-
-    table = page_table[0]
-    peer_table = lax.ppermute(table, "rep", swap)
+
     per_rep = kv_pages.shape[0] * ndp
-    home = (table[:1] // per_rep == rep).astype(jnp.int32)
+    home = table[0] // per_rep == rep
     own_at, peer_at = table % per_rep, peer_table % per_rep
-
-    wo_pieces, qb, kv_peer, k_pool, own_at, peer_at = lax.optimization_barrier(
-        (wo_pieces, qb, kv_peer, k_pool, own_at, peer_at)
-    )
-    k_came = lax.ppermute(pick(k_pool, peer_at), "rep", swap)
-    v_came = lax.ppermute(pick(v_pool, peer_at), "rep", swap)
-    k_mine = choose(k_pool, own_at, home, k_came)
+    wo_pieces, pool, own_at, peer_at = lax.optimization_barrier(
+        (wo_pieces, pool, own_at, peer_at)
+    )
+    k_sent, v_sent = pick(pool, peer_at)
+    k_came = lax.ppermute(k_sent, "rep", swap)
+    v_came = lax.ppermute(v_sent, "rep", swap)
+    k_held, v_held = pick(pool, own_at)
+    k_came, kv_peer, k_held = lax.optimization_barrier((k_came, kv_peer, k_held))
+    k_mine = jnp.where(home, k_held, k_came)
     k_peer = lax.ppermute(k_mine, "tensor", swap)
-    v_mine = choose(v_pool, own_at, home, v_came)
+    v_mine = jnp.where(home, v_held, v_came)
     v_peer = lax.ppermute(v_mine, "tensor", swap)
 
     info = jnp.stack([part, lengths[0], core]).astype(jnp.int32)

time: 129 us -> 105 us (0.81)
  waiting for transfers between devices: 51.7 us -> 39.3 us
  local copies, waits for them, and re-layouts: 16.5 us -> 10.5 us
  Pallas kernels: 28.4 us -> 23.9 us
    ppermute x2, waiting for transfers between devices: 36.8 us -> 11.3 us  [peer_rows(): lax.ppermute(lax.dynamic_slice_in_dim(w, at * deep, deep, 0), 'tensor', s...]
    ppermute x1, waiting for transfers between devices: 0.01 us -> 10.3 us  [pair_shards(): b = lax.ppermute(a, 'rep', swap)]
    ppermute x1, waiting for transfers between devices: 0.18 us -> 5.62 us  [pair_shards(): k_peer = lax.ppermute(k_mine, 'tensor', swap)]
    ppermute x1, waiting for transfers between devices: 4.99 us -> 0.15 us  [pair_shards(): v_peer = lax.ppermute(v_mine, 'tensor', swap)]
    pallas_call x4 -> x2, Pallas kernels: 9.84 us -> 5.21 us  [pick(): pl.pallas_call(pick_kernel, out_shape=(half, half), in_specs=[spec(pltpu....]
    unnamed x30 -> x36, local copies, waits for them, and re-layouts: 12.1 us -> 8.26 us
    ppermute x2, waiting for transfers between devices: 4.83 us -> 7.9 us  [the longest x1 4.57 us: pair_shards(): v_came = lax.ppermute(v_sent, 'rep', swap)]
    ppermute x1, waiting for transfers between devices: 2.8 us -> 0.01 us  [pair_shards(): kv_peer = lax.ppermute(kv_own, 'tensor', swap)]
  transfers between devices with their start and end apart: 14 -> 13, of which waited for: 7 -> 10; matrix products, arithmetic and copies ran while one was open for 4% -> 4% of each run, Pallas kernels for 12% -> 11%
where the time goes in v6:
time: 105 us; the launch traced here: 104 us
  waiting for transfers between devices  39.3 us (37%)
  Pallas kernels  23.9 us (23%)
  between operations  15.1 us (14%)
  starting transfers between devices  13.6 us (13%)
  local copies, waits for them, and re-layouts  10.5 us (10%)
  other arithmetic  2.17 us (2%)
    pallas_call x1, Pallas kernels, attend_pages(): pl.pallas_call(functools.partial(attend_kernel, head_size), out_shape=jax...  12.4 us
    ppermute x2, waiting for transfers between devices, peer_rows(): lax.ppermute(lax.dynamic_slice_in_dim(w, at * deep, deep, 0), 'tensor', s...  11.3 us
    ppermute x1, waiting for transfers between devices, pair_shards(): b = lax.ppermute(a, 'rep', swap)  10.3 us
    unnamed x36, local copies, waits for them, and re-layouts  8.26 us
    ppermute x1, waiting for transfers between devices, pair_shards(): k_peer = lax.ppermute(k_mine, 'tensor', swap)  5.62 us
    pallas_call x2, Pallas kernels, pick(): pl.pallas_call(pick_kernel, out_shape=(half, half), in_specs=[spec(pltpu....  5.21 us
    ppermute x1, waiting for transfers between devices, pair_shards(): v_came = lax.ppermute(v_sent, 'rep', swap)  4.57 us
    ppermute x2, starting transfers between devices, peer_rows(): lax.ppermute(lax.dynamic_slice_in_dim(w, at * deep, deep, 0), 'tensor', s...  4.55 us
  transfers between devices with their start and end apart: 13, of which 10 were waited for; matrix products, arithmetic and copies ran while one was open for 4% of the time, Pallas kernels for 11%

profile of v6, /device:TPU:0, one launch (start us, length us, event | category | flops | bytes accessed | tf_op | source)
XLA Modules:
  0.0 104.5 jit_solution(3160867369831080709)
XLA Ops:
  6.5 0.0 copy-start.12
  6.5 0.0 all-gather.2.cloned.1.call-start
  6.5 0.7 all-gather.2.cloned.1.call-update
  7.3 1.1 %constant_dynamic-slice_fusion.1 = bf16[384,768]{1,0:T(8,128)(2,1)S(1)} fusion(bf16[1536,768]{1,0:T(8,128)(2,1)} %wq.1, s32[]{:T(128)S(6)} %select_n.70), kind=kLoop, calls=%fused_computation.31 | loop fusion | bytes 1179652 | tf_op jit(solution)/shard_map/dynamic_slice | solution.py:341
  8.4 3.0 %collective-permute-start = (bf16[384,768]{1,0:T(8,128)(2,1)S(1)}, bf16[384,768]{1,0:T(8,128)(2,1)S(1)}, u32[]{:S(2)}, u32[]{:S(2)}) collective-permute-start(bf16[384,768]{1,0:T(8,128)(2,1)S(1)} %constant_dynamic-slice_fusion.1), channel_id=1, source_target_pairs={{0,1},{1,0},{2,3},{3,2},{4,5},{5,4},{6,7},{7,6},{8,9},{9,8},{10,11... | collective-permute-start | bytes 1769480 | tf_op jit(solution)/shard_map/ppermute | solution.py:341
  12.1 0.0 copy-done.12
  12.1 0.1 pad_maximum_fusion
  12.2 0.3 fusion
  12.5 0.0 copy-start.5
  12.5 1.7 %copy-done.5 = bf16[1536,768]{1,0:T(8,128)(2,1)S(1)} copy-done((bf16[1536,768]{1,0:T(8,128)(2,1)S(1)}, bf16[1536,768]{1,0:T(8,128)(2,1)}, u32[]{:S(2)}) %copy-start.5) | copy-done | bytes 2359320
  14.2 0.0 copy-start.6
  14.2 1.4 %copy-done.6 = bf16[1,512,1536]{2,1,0:T(8,128)(2,1)S(1)} copy-done((bf16[1,512,1536]{2,1,0:T(8,128)(2,1)S(1)}, bf16[1,512,1536]{2,1,0:T(8,128)(2,1)}, u32[]{:S(2)}) %copy-start.6) | copy-done | bytes 1572888
  15.6 1.4 %copy-done.7 = bf16[1536,512]{1,0:T(8,128)(2,1)S(1)} copy-done((bf16[1536,512]{1,0:T(8,128)(2,1)S(1)}, bf16[1536,512]{1,0:T(8,128)(2,1)}, u32[]{:S(2)}) %copy-start.7) | copy-done | bytes 1572888
  17.0 3.1 %project_own.1 = (bf16[512,1536]{1,0:T(8,128)(2,1)S(1)}, bf16[512,768]{1,0:T(8,128)(2,1)S(1)}, bf16[512,512]{1,0:T(8,128)(2,1)}, f32[512,256]{1,0:T(8,128)S(1)}, f32[512,256]{1,0:T(8,128)S(1)}) custom-call(bf16[512,1536]{1,0:T(8,128)(2,1)S(1)} %bitcast.14, f32[1,1536]{1,0:T(1,128)S(1)} %reshape.34.gain, bf16[1536,768]{1,0:T(8,128)(2,1)S(1)} %copy-done.5, ...), custom_call_target="tpu_custom_call" | custom-call | flops 2013265920 | bytes 10485760 | tf_op jit(solution)/shard_map/project_own/pallas_call | solution.py:79
  20.1 4.7 %collective-permute-done.w0 = bf16[384,768]{1,0:T(8,128)(2,1)S(1)} collective-permute-done((bf16[384,768]{1,0:T(8,128)(2,1)S(1)}, bf16[384,768]{1,0:T(8,128)(2,1)S(1)}, u32[]{:S(2)}, u32[]{:S(2)}) %collective-permute-start) | collective-permute-done | bytes 589856 | tf_op jit(solution)/shard_map/ppermute | solution.py:341
  24.8 1.7 %collective-permute-start.2 = (bf16[384,768]{1,0:T(8,128)(2,1)S(1)}, bf16[384,768]{1,0:T(8,128)(2,1)S(1)}, u32[]{:S(2)}, u32[]{:S(2)}) collective-permute-start(bf16[384,768]{1,0:T(8,128)(2,1)S(1)} %collective-permute-done.w0), channel_id=1, source_target_pairs={{0,16},{16,0},{1,17},{17,1},{2,18},{18,2},{3,19},{19,3},{4,20},{20... | collective-permute-start | bytes 1769480 | tf_op jit(solution)/shard_map/ppermute | solution.py:351
  26.5 0.0 copy-done.9
  26.5 1.1 %constant_dynamic-slice_fusion = bf16[384,1536]{1,0:T(8,128)(2,1)} fusion(bf16[768,1536]{1,0:T(8,128)(2,1)S(1)} %copy-done.9, s32[]{:T(128)S(6)} %select_n.71), kind=kLoop, calls=%fused_computation.30 | loop fusion | bytes 2359300 | tf_op jit(solution)/shard_map/dynamic_slice | solution.py:341
  27.6 1.5 %collective-permute-start.1 = (bf16[384,1536]{1,0:T(8,128)(2,1)}, bf16[384,1536]{1,0:T(8,128)(2,1)}, u32[]{:S(2)}, u32[]{:S(2)}) collective-permute-start(bf16[384,1536]{1,0:T(8,128)(2,1)} %constant_dynamic-slice_fusion), channel_id=1, source_target_pairs={{0,1},{1,0},{2,3},{3,2},{4,5},{5,4},{6,7},{7,6},{8,9},{9,8},{10,11... | collective-permute-start | bytes 3538952 | tf_op jit(solution)/shard_map/ppermute | solution.py:341
  29.1 0.0 collective-permute-start.3
  29.1 10.3 %collective-permute-done.2.w1 = bf16[384,768]{1,0:T(8,128)(2,1)S(1)} collective-permute-done((bf16[384,768]{1,0:T(8,128)(2,1)S(1)}, bf16[384,768]{1,0:T(8,128)(2,1)S(1)}, u32[]{:S(2)}, u32[]{:S(2)}) %collective-permute-start.2) | collective-permute-done | bytes 589856 | tf_op jit(solution)/shard_map/ppermute | solution.py:351
  39.4 0.0 copy-done.1
  39.4 0.0 copy-done.3
  39.4 0.0 copy-done.8
  39.4 0.1 collective-permute-start.4
  39.5 0.1 pad_add_fusion.1.order
  39.6 0.0 collective-permute-done.3.w2
  39.6 2.0 %collective-permute-done.4.w3 = bf16[384,768]{1,0:T(8,128)(2,1)} collective-permute-done((bf16[384,768]{1,0:T(8,128)(2,1)S(1)}, bf16[384,768]{1,0:T(8,128)(2,1)}, u32[]{:S(2)}, u32[]{:S(2)}) %collective-permute-start.4) | collective-permute-done | bytes 589856 | tf_op jit(solution)/shard_map/ppermute | solution.py:355
  41.6 1.1 %copy-done.2 = f32[512,256]{1,0:T(8,128)S(1)} copy-done((f32[512,256]{1,0:T(8,128)S(1)}, f32[512,256]{1,0:T(8,128)}, u32[]{:S(2)}) %copy-start.2) | copy-done | bytes 524312
  42.7 1.0 copy-done.4
  43.7 3.2 %project_other.1.qb_hbm = bf16[512,768]{1,0:T(8,128)(2,1)S(1)} custom-call(s32[4]{0:T(128)S(1)} %pad_add_fusion.1.order, bf16[512,1536]{1,0:T(8,128)(2,1)S(1)} %get-tuple-element.32.normed, bf16[384,768]{1,0:T(8,128)(2,1)S(1)} %collective-permute-done.w0, bf16[384,768]{1,0:T(8,128)(2,1)S(1)} %collective-permute-done.2.w1, ...), custom_call_target="tpu_custom_call" | custom-call | flops 1207959552 | bytes 6291456 | tf_op jit(solution)/shard_map/project_other/pallas_call | solution.py:120
  46.9 0.0 copy-start
  46.9 1.0 copy-done
  47.9 6.6 %collective-permute-done.1.wob0 = bf16[384,1536]{1,0:T(8,128)(2,1)} collective-permute-done((bf16[384,1536]{1,0:T(8,128)(2,1)}, bf16[384,1536]{1,0:T(8,128)(2,1)}, u32[]{:S(2)}, u32[]{:S(2)}) %collective-permute-start.1) | collective-permute-done | bytes 1179680 | tf_op jit(solution)/shard_map/ppermute | solution.py:341
  54.5 0.0 collective-permute-start.5
  54.5 0.0 copy-done.13
  54.5 0.6 collective-permute-start.6
  55.2 0.5 and_select_fusion.1.idx
  55.7 1.4 %collective-permute-start.8 = (bf16[512,512]{1,0:T(8,128)(2,1)}, bf16[512,512]{1,0:T(8,128)(2,1)S(1)}, u32[]{:S(2)}, u32[]{:S(2)}) collective-permute-start(bf16[512,512]{1,0:T(8,128)(2,1)} %get-tuple-element.43.kv_own), channel_id=1, source_target_pairs={{0,1},{1,0},{2,3},{3,2},{4,5},{5,4},{6,7},{7,6},{8,9},{9,8},{10,11... | collective-permute-start | bytes 1572872 | tf_op jit(solution)/shard_map/ppermute | solution.py:362
  57.1 1.0 collective-permute-done.6
  58.1 0.5 and_select_fusion.idx
  58.6 0.0 collective-permute-done.5.wob1
  58.6 0.2 all-gather.2.cloned.1.call-done.pool
  58.8 2.6 %pick_pages.2 = (bf16[8,64,256]{2,1,0:T(8,128)(2,1)}, bf16[8,64,256]{2,1,0:T(8,128)(2,1)}) custom-call(s32[8]{0:T(128)} %and_select_fusion.idx, bf16[64,64,512]{2,1,0:T(8,128)(2,1)} %all-gather.2.cloned.1.call-done.pool), custom_call_target="tpu_custom_call" | custom-call | bytes 1048576 | tf_op jit(solution)/shard_map/pick_pages/pallas_call | solution.py:150
  61.5 0.0 copy-done.14
  61.5 1.5 %collective-permute-start.10 = (bf16[8,64,256]{2,1,0:T(8,128)(2,1)}, bf16[8,64,256]{2,1,0:T(8,128)(2,1)S(1)}, u32[]{:S(2)}, u32[]{:S(2)}) collective-permute-start(bf16[8,64,256]{2,1,0:T(8,128)(2,1)} %get-tuple-element.49), channel_id=1, source_target_pairs={{0,16},{16,0},{1,17},{17,1},{2,18},{18,2},{3,19},{19,3},{4,20},{20... | collective-permute-start | bytes 786440 | tf_op jit(solution)/shard_map/ppermute | solution.py:372
  63.0 0.6 collective-permute-start.7
  63.7 2.6 %pick_pages.3 = (bf16[8,64,256]{2,1,0:T(8,128)(2,1)}, bf16[8,64,256]{2,1,0:T(8,128)(2,1)}) custom-call(s32[8]{0:T(128)} %and_select_fusion.1.idx, bf16[64,64,512]{2,1,0:T(8,128)(2,1)} %all-gather.2.cloned.1.call-done.pool), custom_call_target="tpu_custom_call" | custom-call | bytes 1048576 | tf_op jit(solution)/shard_map/pick_pages/pallas_call | solution.py:150
  66.3 4.6 %collective-permute-done.10 = bf16[8,64,256]{2,1,0:T(8,128)(2,1)S(1)} collective-permute-done((bf16[8,64,256]{2,1,0:T(8,128)(2,1)}, bf16[8,64,256]{2,1,0:T(8,128)(2,1)S(1)}, u32[]{:S(2)}, u32[]{:S(2)}) %collective-permute-start.10) | collective-permute-done | bytes 262176 | tf_op jit(solution)/shard_map/ppermute | solution.py:372
  70.9 0.0 copy-start.10
  70.9 1.5 %collective-permute-start.11 = (bf16[8,64,256]{2,1,0:T(8,128)(2,1)S(1)}, bf16[8,64,256]{2,1,0:T(8,128)(2,1)S(1)}, u32[]{:S(2)}, u32[]{:S(2)}) collective-permute-start(bf16[8,64,256]{2,1,0:T(8,128)(2,1)S(1)} %broadcast_select_fusion.v_mine), channel_id=1, source_target_pairs={{0,1},{1,0},{2,3},{3,2},{4,5},{5,4},{6,7},{7,6},{8,9},{9,8},{10,11... | collective-permute-start | bytes 786440 | tf_op jit(solution)/shard_map/ppermute | solution.py:378
  72.5 0.0 collective-permute-done.8.kv_peer
  72.5 3.3 %collective-permute-done.7 = bf16[8,64,256]{2,1,0:T(8,128)(2,1)S(1)} collective-permute-done((bf16[8,64,256]{2,1,0:T(8,128)(2,1)}, bf16[8,64,256]{2,1,0:T(8,128)(2,1)S(1)}, u32[]{:S(2)}, u32[]{:S(2)}) %collective-permute-start.7) | collective-permute-done | bytes 262176 | tf_op jit(solution)/shard_map/ppermute | solution.py:371
  75.9 0.0 copy-start.11
  75.9 1.6 %collective-permute-start.9 = (bf16[8,64,256]{2,1,0:T(8,128)(2,1)S(1)}, bf16[8,64,256]{2,1,0:T(8,128)(2,1)S(1)}, u32[]{:S(2)}, u32[]{:S(2)}) collective-permute-start(bf16[8,64,256]{2,1,0:T(8,128)(2,1)S(1)} %broadcast_select_fusion.1.k_mine), channel_id=1, source_target_pairs={{0,1},{1,0},{2,3},{3,2},{4,5},{5,4},{6,7},{7,6},{8,9},{9,8},{10,11... | collective-permute-start | bytes 786440 | tf_op jit(solution)/shard_map/ppermute | solution.py:376
  78.1 0.7 pad_add_fusion.info
  78.7 0.1 collective-permute-done.11.v_peer
  78.9 5.6 %collective-permute-done.9.k_peer = bf16[8,64,256]{2,1,0:T(8,128)(2,1)S(1)} collective-permute-done((bf16[8,64,256]{2,1,0:T(8,128)(2,1)S(1)}, bf16[8,64,256]{2,1,0:T(8,128)(2,1)S(1)}, u32[]{:S(2)}, u32[]{:S(2)}) %collective-permute-start.9) | collective-permute-done | bytes 262176 | tf_op jit(solution)/shard_map/ppermute | solution.py:376
  84.5 0.0 copy-done.10
  84.5 0.0 copy-done.15
  84.5 0.0 copy-done.11
  84.5 0.0 copy-done.16
  84.5 0.7 copy-done.17
  85.2 12.4 %attend_and_out.1 = bf16[512,1536]{1,0:T(8,128)(2,1)} custom-call(s32[3]{0:T(128)} %pad_add_fusion.info, bf16[512,768]{1,0:T(8,128)(2,1)} %copy-done.8, bf16[512,768]{1,0:T(8,128)(2,1)} %copy-done, bf16[8,64,256]{2,1,0:T(8,128)(2,1)} %copy-done.11, bf16[8,64,256]{2,1,0:T(8,128)(2,1)} %copy-done.17, bf16[8,64,256]{2,1,0:T(8,128)(2,1)} %copy-done.10, ...), custom_call_target="tpu_custom_call" | custom-call | flops 6442450944 | bytes 12582912 | tf_op jit(solution)/shard_map/attend_and_out/pallas_call | solution.py:294
  (18 shorter events, 0.1 us)
Async XLA Ops:
  6.5 5.5 %copy-start.12 = (f32[1536]{0:T(1024)S(1)}, f32[1536]{0:T(1024)}, u32[]{:S(2)}) copy-start(f32[1536]{0:T(1024)} %param.10) | copy-start | bytes 18436
  6.5 52.3 %all-gather.2.cloned.1.call-start = ((), (), s32[]{:S(2)}) async-start(), calls=%async_computation | async-start | bytes 4718592 | tf_op jit(solution)/shard_map/all_gather | solution.py:337
  8.4 16.4 %collective-permute-start = (bf16[384,768]{1,0:T(8,128)(2,1)S(1)}, bf16[384,768]{1,0:T(8,128)(2,1)S(1)}, u32[]{:S(2)}, u32[]{:S(2)}) collective-permute-start(bf16[384,768]{1,0:T(8,128)(2,1)S(1)} %constant_dynamic-slice_fusion.1), channel_id=1, source_target_pairs={{0,1},{1,0},{2,3},{3,2},{4,5},{5,4},{6,7},{7,6},{8,9},{9,8},{10,11... | collective-permute-start | bytes 1769480 | tf_op jit(solution)/shard_map/ppermute | solution.py:341
  12.5 1.7 %copy-start.5 = (bf16[1536,768]{1,0:T(8,128)(2,1)S(1)}, bf16[1536,768]{1,0:T(8,128)(2,1)}, u32[]{:S(2)}) copy-start(bf16[1536,768]{1,0:T(8,128)(2,1)} %wq.1) | copy-start | bytes 7077892
  14.2 1.4 %copy-start.6 = (bf16[1,512,1536]{2,1,0:T(8,128)(2,1)S(1)}, bf16[1,512,1536]{2,1,0:T(8,128)(2,1)}, u32[]{:S(2)}) copy-start(bf16[1,512,1536]{2,1,0:T(8,128)(2,1)} %param.9) | copy-start | bytes 4718596
  15.6 1.4 %copy-start.7 = (bf16[1536,512]{1,0:T(8,128)(2,1)S(1)}, bf16[1536,512]{1,0:T(8,128)(2,1)}, u32[]{:S(2)}) copy-start(bf16[1536,512]{1,0:T(8,128)(2,1)} %wkv.1) | copy-start | bytes 4718596
  17.0 9.5 %copy-start.9 = (bf16[768,1536]{1,0:T(8,128)(2,1)S(1)}, bf16[768,1536]{1,0:T(8,128)(2,1)}, u32[]{:S(2)}) copy-start(bf16[768,1536]{1,0:T(8,128)(2,1)} %woa.1) | copy-start | bytes 7077892
  20.1 19.3 %copy-start.1 = (f32[512,256]{1,0:T(8,128)}, f32[512,256]{1,0:T(8,128)S(1)}, u32[]{:S(2)}) copy-start(f32[512,256]{1,0:T(8,128)S(1)} %get-tuple-element.34.cos) | copy-start | bytes 1572868
  20.1 19.3 %copy-start.3 = (f32[512,256]{1,0:T(8,128)}, f32[512,256]{1,0:T(8,128)S(1)}, u32[]{:S(2)}) copy-start(f32[512,256]{1,0:T(8,128)S(1)} %get-tuple-element.35.sin) | copy-start | bytes 1572868
  20.1 19.3 %copy-start.8 = (bf16[512,768]{1,0:T(8,128)(2,1)}, bf16[512,768]{1,0:T(8,128)(2,1)S(1)}, u32[]{:S(2)}) copy-start(bf16[512,768]{1,0:T(8,128)(2,1)S(1)} %get-tuple-element.29.qa_hbm) | copy-start | bytes 2359300
  24.8 14.6 %collective-permute-start.2 = (bf16[384,768]{1,0:T(8,128)(2,1)S(1)}, bf16[384,768]{1,0:T(8,128)(2,1)S(1)}, u32[]{:S(2)}, u32[]{:S(2)}) collective-permute-start(bf16[384,768]{1,0:T(8,128)(2,1)S(1)} %collective-permute-done.w0), channel_id=1, source_target_pairs={{0,16},{16,0},{1,17},{17,1},{2,18},{18,2},{3,19},{19,3},{4,20},{20... | collective-permute-start | bytes 1769480 | tf_op jit(solution)/shard_map/ppermute | solution.py:351
  27.6 27.0 %collective-permute-start.1 = (bf16[384,1536]{1,0:T(8,128)(2,1)}, bf16[384,1536]{1,0:T(8,128)(2,1)}, u32[]{:S(2)}, u32[]{:S(2)}) collective-permute-start(bf16[384,1536]{1,0:T(8,128)(2,1)} %constant_dynamic-slice_fusion), channel_id=1, source_target_pairs={{0,1},{1,0},{2,3},{3,2},{4,5},{5,4},{6,7},{7,6},{8,9},{9,8},{10,11... | collective-permute-start | bytes 3538952 | tf_op jit(solution)/shard_map/ppermute | solution.py:341
  29.1 10.5 %collective-permute-start.3 = (bf16[384,768]{1,0:T(8,128)(2,1)S(1)}, bf16[384,768]{1,0:T(8,128)(2,1)S(1)}, u32[]{:S(2)}, u32[]{:S(2)}) collective-permute-start(bf16[384,768]{1,0:T(8,128)(2,1)S(1)} %collective-permute-done.w0), channel_id=1, source_target_pairs={{0,2},{2,0},{4,6},{6,4},{8,10},{10,8},{12,14},{14,12},{1,3},{3,1},... | collective-permute-start | bytes 1769480 | tf_op jit(solution)/shard_map/ppermute | solution.py:355
  39.4 2.2 %collective-permute-start.4 = (bf16[384,768]{1,0:T(8,128)(2,1)S(1)}, bf16[384,768]{1,0:T(8,128)(2,1)}, u32[]{:S(2)}, u32[]{:S(2)}) collective-permute-start(bf16[384,768]{1,0:T(8,128)(2,1)S(1)} %collective-permute-done.2.w1), channel_id=1, source_target_pairs={{0,2},{2,0},{4,6},{6,4},{8,10},{10,8},{12,14},{14,12},{1,3},{3,1},... | collective-permute-start | bytes 1769480 | tf_op jit(solution)/shard_map/ppermute | solution.py:355
  41.6 1.1 %copy-start.2 = (f32[512,256]{1,0:T(8,128)S(1)}, f32[512,256]{1,0:T(8,128)}, u32[]{:S(2)}) copy-start(f32[512,256]{1,0:T(8,128)} %copy-done.1) | copy-start | bytes 1572868
  42.6 1.0 copy-start.4
  43.7 10.8 %copy-start.13 = (s32[1,8]{1,0:T(1,128)S(1)}, s32[1,8]{1,0:T(1,128)}, u32[]{:S(2)}) copy-start(s32[1,8]{1,0:T(1,128)} %param.15) | copy-start | bytes 100
  46.9 1.0 copy-start
  54.5 4.1 %collective-permute-start.5 = (bf16[384,1536]{1,0:T(8,128)(2,1)}, bf16[384,1536]{1,0:T(8,128)(2,1)S(1)}, u32[]{:S(2)}, u32[]{:S(2)}) collective-permute-start(bf16[384,1536]{1,0:T(8,128)(2,1)} %collective-permute-done.1.wob0), channel_id=1, source_target_pairs={{0,2},{2,0},{4,6},{6,4},{8,10},{10,8},{12,14},{14,12},{1,3},{3,1},... | collective-permute-start | bytes 3538952 | tf_op jit(solution)/shard_map/ppermute | solution.py:361
  54.5 3.5 %collective-permute-start.6 = (s32[8]{0:T(128)S(1)}, s32[8]{0:T(128)S(1)}, u32[]{:S(2)}, u32[]{:S(2)}) collective-permute-start(s32[8]{0:T(128)S(1)} %bitcast.15), channel_id=1, source_target_pairs={{0,16},{16,0},{1,17},{17,1},{2,18},{18,2},{3,19},{19,3},{4,20},{20... | collective-permute-start | bytes 104 | tf_op jit(solution)/shard_map/ppermute | solution.py:354
  55.7 16.8 %collective-permute-start.8 = (bf16[512,512]{1,0:T(8,128)(2,1)}, bf16[512,512]{1,0:T(8,128)(2,1)S(1)}, u32[]{:S(2)}, u32[]{:S(2)}) collective-permute-start(bf16[512,512]{1,0:T(8,128)(2,1)} %get-tuple-element.43.kv_own), channel_id=1, source_target_pairs={{0,1},{1,0},{2,3},{3,2},{4,5},{5,4},{6,7},{7,6},{8,9},{9,8},{10,11... | collective-permute-start | bytes 1572872 | tf_op jit(solution)/shard_map/ppermute | solution.py:362
  58.6 2.9 %copy-start.14 = (bf16[384,1536]{1,0:T(8,128)(2,1)}, bf16[384,1536]{1,0:T(8,128)(2,1)S(1)}, u32[]{:S(2)}) copy-start(bf16[384,1536]{1,0:T(8,128)(2,1)S(1)} %collective-permute-done.5.wob1) | copy-start | bytes 3538948
  61.5 9.4 %collective-permute-start.10 = (bf16[8,64,256]{2,1,0:T(8,128)(2,1)}, bf16[8,64,256]{2,1,0:T(8,128)(2,1)S(1)}, u32[]{:S(2)}, u32[]{:S(2)}) collective-permute-start(bf16[8,64,256]{2,1,0:T(8,128)(2,1)} %get-tuple-element.49), channel_id=1, source_target_pairs={{0,16},{16,0},{1,17},{17,1},{2,18},{18,2},{3,19},{19,3},{4,20},{20... | collective-permute-start | bytes 786440 | tf_op jit(solution)/shard_map/ppermute | solution.py:372
  63.0 12.8 %collective-permute-start.7 = (bf16[8,64,256]{2,1,0:T(8,128)(2,1)}, bf16[8,64,256]{2,1,0:T(8,128)(2,1)S(1)}, u32[]{:S(2)}, u32[]{:S(2)}) collective-permute-start(bf16[8,64,256]{2,1,0:T(8,128)(2,1)} %get-tuple-element.42), channel_id=1, source_target_pairs={{0,16},{16,0},{1,17},{17,1},{2,18},{18,2},{3,19},{19,3},{4,20},{20... | collective-permute-start | bytes 786440 | tf_op jit(solution)/shard_map/ppermute | solution.py:371
  70.9 13.6 %copy-start.10 = (bf16[8,64,256]{2,1,0:T(8,128)(2,1)}, bf16[8,64,256]{2,1,0:T(8,128)(2,1)S(1)}, u32[]{:S(2)}) copy-start(bf16[8,64,256]{2,1,0:T(8,128)(2,1)S(1)} %broadcast_select_fusion.v_mine) | copy-start | bytes 786436
  70.9 8.0 %collective-permute-start.11 = (bf16[8,64,256]{2,1,0:T(8,128)(2,1)S(1)}, bf16[8,64,256]{2,1,0:T(8,128)(2,1)S(1)}, u32[]{:S(2)}, u32[]{:S(2)}) collective-permute-start(bf16[8,64,256]{2,1,0:T(8,128)(2,1)S(1)} %broadcast_select_fusion.v_mine), channel_id=1, source_target_pairs={{0,1},{1,0},{2,3},{3,2},{4,5},{5,4},{6,7},{7,6},{8,9},{9,8},{10,11... | collective-permute-start | bytes 786440 | tf_op jit(solution)/shard_map/ppermute | solution.py:378
  72.5 12.0 %copy-start.15 = (bf16[512,512]{1,0:T(8,128)(2,1)}, bf16[512,512]{1,0:T(8,128)(2,1)S(1)}, u32[]{:S(2)}) copy-start(bf16[512,512]{1,0:T(8,128)(2,1)S(1)} %collective-permute-done.8.kv_peer) | copy-start | bytes 1572868
  75.9 8.7 %copy-start.11 = (bf16[8,64,256]{2,1,0:T(8,128)(2,1)}, bf16[8,64,256]{2,1,0:T(8,128)(2,1)S(1)}, u32[]{:S(2)}) copy-start(bf16[8,64,256]{2,1,0:T(8,128)(2,1)S(1)} %broadcast_select_fusion.1.k_mine) | copy-start | bytes 786436
  75.9 8.6 %collective-permute-start.9 = (bf16[8,64,256]{2,1,0:T(8,128)(2,1)S(1)}, bf16[8,64,256]{2,1,0:T(8,128)(2,1)S(1)}, u32[]{:S(2)}, u32[]{:S(2)}) collective-permute-start(bf16[8,64,256]{2,1,0:T(8,128)(2,1)S(1)} %broadcast_select_fusion.1.k_mine), channel_id=1, source_target_pairs={{0,1},{1,0},{2,3},{3,2},{4,5},{5,4},{6,7},{7,6},{8,9},{9,8},{10,11... | collective-permute-start | bytes 786440 | tf_op jit(solution)/shard_map/ppermute | solution.py:376
  78.9 5.6 %copy-start.16 = (bf16[8,64,256]{2,1,0:T(8,128)(2,1)}, bf16[8,64,256]{2,1,0:T(8,128)(2,1)S(1)}, u32[]{:S(2)}) copy-start(bf16[8,64,256]{2,1,0:T(8,128)(2,1)S(1)} %collective-permute-done.11.v_peer) | copy-start | bytes 786436
  84.5 0.7 copy-start.17
Sparse Core Ops, SparseCore 0:
  9.0 49.8 all-gather.1

commit v7 on v6

--- a/solution.py
+++ b/solution.py
@@ -182,6 +182,9 @@
     wb,
     mix,
     out,
+    sbuf,
+    pbuf,
+    sums,
     ksem,
     vsem,
     wsem,
@@ -236,58 +239,106 @@
 
     tile = min(256, rows)
     span = window + tile
-    row_id = lax.broadcasted_iota(jnp.int32, (tile, tile), 0)
-    col_id = lax.broadcasted_iota(jnp.int32, (tile, tile), 1)
-    first_seen = col_id >= row_id + 1
-    last_seen = col_id <= row_id
+    band = min(32, tile)
+    gap = lax.broadcasted_iota(jnp.int32, (band, tile), 1) - lax.broadcasted_iota(
+        jnp.int32, (band, tile), 0
+    )
+    order = [(i, n, h) for i in range(rows // tile) for n in range(2) for h in range(nheads)]
+
+    def score(m):
+        i, n, h = order[m]
+        q = (qa, qb)[n][pl.ds(i * tile, tile), h * head_size : (h + 1) * head_size]
+        for lo in range(0, span, tile):
+            sbuf[m % 2, :, lo : lo + tile] = lax.dot_general(
+                q,
+                keys[pl.ds(i * tile + lo, tile), :],
+                (((1,), (1,)), ((), ())),
+                preferred_element_type=F32,
+            )
+
+    def soften(m):
+        for lo in range(0, tile, band):
+            at = pl.ds(lo, band)
+            s = jnp.concatenate(
+                [
+                    jnp.where(gap >= lo + 1, sbuf[m % 2, at, :tile], MASKED),
+                    sbuf[m % 2, at, tile : span - tile],
+                    jnp.where(gap <= lo, sbuf[m % 2, at, span - tile :], MASKED),
+                ],
+                axis=1,
+            )
+            e = jnp.exp2(s - jnp.max(s, axis=-1, keepdims=True))
+            total = jnp.sum(e, axis=-1, keepdims=True)
+            pbuf[m % 2, at, :] = e.astype(BF16)
+            sums[m % 2, at, :] = jnp.broadcast_to(1.0 / total, (band, 128))
+
+    def combine(m):
+        i, n, h = order[m]
+        mixed = jnp.dot(
+            pbuf[m % 2], vals[pl.ds(i * tile, span), :], preferred_element_type=F32
+        )
+        mixed = mixed * sums[m % 2, :, :1]
+        at = pl.ds(i * tile, tile)
+        mix[n, at, h * head_size : (h + 1) * head_size] = mixed.astype(BF16)
+
+    block = 512
+
+    def project_out(i, lo):
+        at = pl.ds(i * tile, tile)
+        row = part * rows + i * tile + lax.broadcasted_iota(jnp.int32, (tile, 1), 0)
+        cols = slice(lo, lo + block)
+        a = jnp.dot(mix[0, at, :], wa[:, cols], preferred_element_type=F32)
+        b = jnp.dot(mix[1, at, :], wb[:, cols], preferred_element_type=F32)
+        both = a.astype(BF16).astype(F32) + b.astype(BF16).astype(F32)
+        out[at, cols] = jnp.where(row < length, both, 0.0).astype(BF16)
+
+    stores = []
+
+    def send_out(i):
+        at = pl.ds(i * tile, tile)
+        stores.append(pltpu.make_async_copy(out.at[at, :], out_hbm.at[at, :], osem.at[i]))
+        stores[i].start()
+
     queries[0].wait()
     finish(keys, ksem)
-    stores = []
-    for i in range(rows // tile):
-        at = pl.ds(i * tile, tile)
-        for n, q in enumerate((qa, qb)):
-            for h in range(nheads):
-                cols = slice(h * head_size, (h + 1) * head_size)
-                kk = keys[pl.ds(i * tile, span), :]
-                s = lax.dot_general(
-                    q[at, cols], kk, (((1,), (1,)), ((), ())), preferred_element_type=F32
-                )
-                s = jnp.concatenate(
-                    [
-                        jnp.where(first_seen, s[:, :tile], MASKED),
-                        s[:, tile : span - tile],
-                        jnp.where(last_seen, s[:, span - tile :], MASKED),
-                    ],
-                    axis=1,
-                )
-                top = jnp.max(s, axis=-1, keepdims=True)
-                e = jnp.exp2(s - top)
-                total = jnp.sum(e, axis=-1, keepdims=True)
-                if i == 0 and n == 0 and h == 0:
-                    finish(vals, vsem)
-                    queries[1].wait()
-                vv = vals[pl.ds(i * tile, span), :]
-                m = jnp.dot(e.astype(BF16), vv, preferred_element_type=F32)
-                mix[n, at, cols] = (m / total).astype(BF16)
-        if i == 0:
-            for c in weights:
-                c.wait()
-        row = part * rows + i * tile + lax.broadcasted_iota(jnp.int32, (tile, 1), 0)
-        live = row < length
-        for j in range(width // 512):
-            cols = slice(j * 512, (j + 1) * 512)
-            a = jnp.dot(mix[0, at, :], wa[:, cols], preferred_element_type=F32)
-            b = jnp.dot(mix[1, at, :], wb[:, cols], preferred_element_type=F32)
-            both = a.astype(BF16).astype(F32) + b.astype(BF16).astype(F32)
-            out[at, cols] = jnp.where(live, both, 0.0).astype(BF16)
-        stores.append(pltpu.make_async_copy(out.at[at, :], out_hbm.at[at, :], osem.at[i]))
-        stores[i].start()
+    queries[1].wait()
+    score(0)
+    ready = []
+    for m in range(len(order)):
+        if m + 1 < len(order):
+            score(m + 1)
+        if m == 1:
+            finish(vals, vsem)
+        if m >= 1:
+            combine(m - 1)
+            i, n, h = order[m - 1]
+            if (n, h) == (1, nheads - 1):
+                if i == 0:
+                    for c in weights:
+                        c.wait()
+                ready += [(i, lo) for lo in range(0, width, block)]
+        if m >= 1 and ready and order[m - 1][1:] != (1, nheads - 1):
+            i, lo = ready.pop(0)
+            project_out(i, lo)
+            if lo + block == width:
+                send_out(i)
+        soften(m)
+    combine(len(order) - 1)
+    if rows == tile:
+        for c in weights:
+            c.wait()
+    ready += [(rows // tile - 1, lo) for lo in range(0, width, block)]
+    for i, lo in ready:
+        project_out(i, lo)
+        if lo + block == width:
+            send_out(i)
     for c in stores:
         c.wait()
 
 
 def attend_pages(info, qa, qb, k_mine, k_peer, v_mine, v_peer, kv_own, kv_peer, woa, wobs):
     rows, half = qa.shape
+    tile = min(256, rows)
     width = woa.shape[1]
     head_size = k_mine.shape[2]
     window = k_mine.shape[0] * k_mine.shape[1] * 2
@@ -308,10 +359,13 @@
             pltpu.VMEM(woa.shape, BF16),
             pltpu.VMEM((2, rows, half), BF16),
             pltpu.VMEM((rows, width), BF16),
+            pltpu.VMEM((2, tile, window + tile), F32),
+            pltpu.VMEM((2, tile, window + tile), BF16),
+            pltpu.VMEM((2, tile, 128), F32),
             pltpu.SemaphoreType.DMA,
             pltpu.SemaphoreType.DMA,
             pltpu.SemaphoreType.DMA((5,)),
-            pltpu.SemaphoreType.DMA((rows // min(256, rows),)),
+            pltpu.SemaphoreType.DMA((rows // tile,)),
         ],
         compiler_params=pltpu.CompilerParams(vmem_limit_bytes=56 * 2**20),
         cost_estimate=pl.CostEstimate(

time: 105 us -> 105 us (level)
  other arithmetic: 2.17 us -> 4.07 us
  waiting for transfers between devices: 39.3 us -> 37.4 us
  transfers between devices with their start and end apart: 13 -> 13, of which waited for: 10 -> 9; matrix products, arithmetic and copies ran while one was open for 4% -> 6% of each run, Pallas kernels for 11% -> 11%
where the time goes in v7:
time: 105 us
  waiting for transfers between devices  37.4 us (36%)
  Pallas kernels  24 us (23%)
  between operations  15.1 us (14%)
  starting transfers between devices  13.6 us (13%)
  local copies, waits for them, and re-layouts  10.5 us (10%)
  other arithmetic  4.07 us (4%)
    pallas_call x1, Pallas kernels, attend_pages(): pl.pallas_call(functools.partial(attend_kernel, head_size), out_shape=jax...  12.5 us
    ppermute x2, waiting for transfers between devices, peer_rows(): lax.ppermute(lax.dynamic_slice_in_dim(w, at * deep, deep, 0), 'tensor', s...  11.3 us
    ppermute x1, waiting for transfers between devices, pair_shards(): b = lax.ppermute(a, 'rep', swap)  10.3 us
    unnamed x36, local copies, waits for them, and re-layouts  8.26 us
    pallas_call x2, Pallas kernels, pick(): pl.pallas_call(pick_kernel, out_shape=(half, half), in_specs=[spec(pltpu....  5.21 us
    ppermute x1, waiting for transfers between devices, pair_shards(): k_peer = lax.ppermute(k_mine, 'tensor', swap)  4.83 us
    ppermute x1, waiting for transfers between devices, pair_shards(): v_came = lax.ppermute(v_sent, 'rep', swap)  4.57 us
    ppermute x2, starting transfers between devices, peer_rows(): lax.ppermute(lax.dynamic_slice_in_dim(w, at * deep, deep, 0), 'tensor', s...  4.55 us
  transfers between devices with their start and end apart: 13, of which 9 were waited for; matrix products, arithmetic and copies ran while one was open for 6% of the time, Pallas kernels for 11%

profile of v7, /device:TPU:0, one launch (start us, length us, event | category | flops | bytes accessed | tf_op | source)
XLA Modules:
  0.0 104.5 jit_solution(9382897796675124677)
XLA Ops:
  6.5 0.0 all-gather.2.cloned.1.call-start
  6.5 0.7 all-gather.2.cloned.1.call-update
  7.3 1.1 %constant_dynamic-slice_fusion.1 = bf16[384,768]{1,0:T(8,128)(2,1)S(1)} fusion(bf16[1536,768]{1,0:T(8,128)(2,1)} %wq.1, s32[]{:T(128)S(6)} %select_n.70), kind=kLoop, calls=%fused_computation.31 | loop fusion | bytes 1179652 | tf_op jit(solution)/shard_map/dynamic_slice | solution.py:395
  8.4 3.0 %collective-permute-start = (bf16[384,768]{1,0:T(8,128)(2,1)S(1)}, bf16[384,768]{1,0:T(8,128)(2,1)S(1)}, u32[]{:S(2)}, u32[]{:S(2)}) collective-permute-start(bf16[384,768]{1,0:T(8,128)(2,1)S(1)} %constant_dynamic-slice_fusion.1), channel_id=1, source_target_pairs={{0,1},{1,0},{2,3},{3,2},{4,5},{5,4},{6,7},{7,6},{8,9},{9,8},{10,11... | collective-permute-start | bytes 1769480 | tf_op jit(solution)/shard_map/ppermute | solution.py:395
  12.1 0.0 copy-done.12
  12.1 0.1 pad_maximum_fusion
  12.2 0.3 fusion
  12.5 0.0 copy-start.5
  12.5 1.7 %copy-done.5 = bf16[1536,768]{1,0:T(8,128)(2,1)S(1)} copy-done((bf16[1536,768]{1,0:T(8,128)(2,1)S(1)}, bf16[1536,768]{1,0:T(8,128)(2,1)}, u32[]{:S(2)}) %copy-start.5) | copy-done | bytes 2359320
  14.2 1.4 %copy-done.6 = bf16[1,512,1536]{2,1,0:T(8,128)(2,1)S(1)} copy-done((bf16[1,512,1536]{2,1,0:T(8,128)(2,1)S(1)}, bf16[1,512,1536]{2,1,0:T(8,128)(2,1)}, u32[]{:S(2)}) %copy-start.6) | copy-done | bytes 1572888
  15.6 1.4 %copy-done.7 = bf16[1536,512]{1,0:T(8,128)(2,1)S(1)} copy-done((bf16[1536,512]{1,0:T(8,128)(2,1)S(1)}, bf16[1536,512]{1,0:T(8,128)(2,1)}, u32[]{:S(2)}) %copy-start.7) | copy-done | bytes 1572888
  17.0 3.1 %project_own.1 = (bf16[512,1536]{1,0:T(8,128)(2,1)S(1)}, bf16[512,768]{1,0:T(8,128)(2,1)S(1)}, bf16[512,512]{1,0:T(8,128)(2,1)}, f32[512,256]{1,0:T(8,128)S(1)}, f32[512,256]{1,0:T(8,128)S(1)}) custom-call(bf16[512,1536]{1,0:T(8,128)(2,1)S(1)} %bitcast.14, f32[1,1536]{1,0:T(1,128)S(1)} %reshape.34.gain, bf16[1536,768]{1,0:T(8,128)(2,1)S(1)} %copy-done.5, ...), custom_call_target="tpu_custom_call" | custom-call | flops 2013265920 | bytes 10485760 | tf_op jit(solution)/shard_map/project_own/pallas_call | solution.py:79
  20.1 4.7 %collective-permute-done.w0 = bf16[384,768]{1,0:T(8,128)(2,1)S(1)} collective-permute-done((bf16[384,768]{1,0:T(8,128)(2,1)S(1)}, bf16[384,768]{1,0:T(8,128)(2,1)S(1)}, u32[]{:S(2)}, u32[]{:S(2)}) %collective-permute-start) | collective-permute-done | bytes 589856 | tf_op jit(solution)/shard_map/ppermute | solution.py:395
  24.8 1.7 %collective-permute-start.2 = (bf16[384,768]{1,0:T(8,128)(2,1)S(1)}, bf16[384,768]{1,0:T(8,128)(2,1)S(1)}, u32[]{:S(2)}, u32[]{:S(2)}) collective-permute-start(bf16[384,768]{1,0:T(8,128)(2,1)S(1)} %collective-permute-done.w0), channel_id=1, source_target_pairs={{0,16},{16,0},{1,17},{17,1},{2,18},{18,2},{3,19},{19,3},{4,20},{20... | collective-permute-start | bytes 1769480 | tf_op jit(solution)/shard_map/ppermute | solution.py:405
  26.5 0.0 copy-done.9
  26.5 1.1 %constant_dynamic-slice_fusion = bf16[384,1536]{1,0:T(8,128)(2,1)} fusion(bf16[768,1536]{1,0:T(8,128)(2,1)S(1)} %copy-done.9, s32[]{:T(128)S(6)} %select_n.71), kind=kLoop, calls=%fused_computation.30 | loop fusion | bytes 2359300 | tf_op jit(solution)/shard_map/dynamic_slice | solution.py:395
  27.6 1.5 %collective-permute-start.1 = (bf16[384,1536]{1,0:T(8,128)(2,1)}, bf16[384,1536]{1,0:T(8,128)(2,1)}, u32[]{:S(2)}, u32[]{:S(2)}) collective-permute-start(bf16[384,1536]{1,0:T(8,128)(2,1)} %constant_dynamic-slice_fusion), channel_id=1, source_target_pairs={{0,1},{1,0},{2,3},{3,2},{4,5},{5,4},{6,7},{7,6},{8,9},{9,8},{10,11... | collective-permute-start | bytes 3538952 | tf_op jit(solution)/shard_map/ppermute | solution.py:395
  29.1 0.0 collective-permute-start.3
  29.1 10.3 %collective-permute-done.2.w1 = bf16[384,768]{1,0:T(8,128)(2,1)S(1)} collective-permute-done((bf16[384,768]{1,0:T(8,128)(2,1)S(1)}, bf16[384,768]{1,0:T(8,128)(2,1)S(1)}, u32[]{:S(2)}, u32[]{:S(2)}) %collective-permute-start.2) | collective-permute-done | bytes 589856 | tf_op jit(solution)/shard_map/ppermute | solution.py:405
  39.4 0.0 copy-done.1
  39.4 0.0 copy-done.3
  39.4 0.0 copy-done.8
  39.4 0.1 collective-permute-start.4
  39.5 0.1 pad_add_fusion.1.order
  39.6 0.0 collective-permute-done.3.w2
  39.6 2.0 %collective-permute-done.4.w3 = bf16[384,768]{1,0:T(8,128)(2,1)} collective-permute-done((bf16[384,768]{1,0:T(8,128)(2,1)S(1)}, bf16[384,768]{1,0:T(8,128)(2,1)}, u32[]{:S(2)}, u32[]{:S(2)}) %collective-permute-start.4) | collective-permute-done | bytes 589856 | tf_op jit(solution)/shard_map/ppermute | solution.py:409
  41.6 1.1 %copy-done.2 = f32[512,256]{1,0:T(8,128)S(1)} copy-done((f32[512,256]{1,0:T(8,128)S(1)}, f32[512,256]{1,0:T(8,128)}, u32[]{:S(2)}) %copy-start.2) | copy-done | bytes 524312
  42.7 1.0 copy-done.4
  43.7 3.2 %project_other.1.qb_hbm = bf16[512,768]{1,0:T(8,128)(2,1)S(1)} custom-call(s32[4]{0:T(128)S(1)} %pad_add_fusion.1.order, bf16[512,1536]{1,0:T(8,128)(2,1)S(1)} %get-tuple-element.32.normed, bf16[384,768]{1,0:T(8,128)(2,1)S(1)} %collective-permute-done.w0, bf16[384,768]{1,0:T(8,128)(2,1)S(1)} %collective-permute-done.2.w1, ...), custom_call_target="tpu_custom_call" | custom-call | flops 1207959552 | bytes 6291456 | tf_op jit(solution)/shard_map/project_other/pallas_call | solution.py:120
  46.9 0.0 copy-start
  46.9 1.0 copy-done
  47.9 6.6 %collective-permute-done.1.wob0 = bf16[384,1536]{1,0:T(8,128)(2,1)} collective-permute-done((bf16[384,1536]{1,0:T(8,128)(2,1)}, bf16[384,1536]{1,0:T(8,128)(2,1)}, u32[]{:S(2)}, u32[]{:S(2)}) %collective-permute-start.1) | collective-permute-done | bytes 1179680 | tf_op jit(solution)/shard_map/ppermute | solution.py:395
  54.5 0.0 collective-permute-start.5
  54.5 0.0 copy-done.13
  54.5 0.6 collective-permute-start.6
  55.2 0.5 and_select_fusion.1.idx
  55.7 1.4 %collective-permute-start.8 = (bf16[512,512]{1,0:T(8,128)(2,1)}, bf16[512,512]{1,0:T(8,128)(2,1)S(1)}, u32[]{:S(2)}, u32[]{:S(2)}) collective-permute-start(bf16[512,512]{1,0:T(8,128)(2,1)} %get-tuple-element.43.kv_own), channel_id=1, source_target_pairs={{0,1},{1,0},{2,3},{3,2},{4,5},{5,4},{6,7},{7,6},{8,9},{9,8},{10,11... | collective-permute-start | bytes 1572872 | tf_op jit(solution)/shard_map/ppermute | solution.py:416
  57.1 1.0 collective-permute-done.6
  58.1 0.5 and_select_fusion.idx
  58.6 0.0 collective-permute-done.5.wob1
  58.6 0.2 all-gather.2.cloned.1.call-done.pool
  58.8 2.6 %pick_pages.2 = (bf16[8,64,256]{2,1,0:T(8,128)(2,1)}, bf16[8,64,256]{2,1,0:T(8,128)(2,1)}) custom-call(s32[8]{0:T(128)} %and_select_fusion.idx, bf16[64,64,512]{2,1,0:T(8,128)(2,1)} %all-gather.2.cloned.1.call-done.pool), custom_call_target="tpu_custom_call" | custom-call | bytes 1048576 | tf_op jit(solution)/shard_map/pick_pages/pallas_call | solution.py:150
  61.5 0.0 copy-done.14
  61.5 1.5 %collective-permute-start.10 = (bf16[8,64,256]{2,1,0:T(8,128)(2,1)}, bf16[8,64,256]{2,1,0:T(8,128)(2,1)S(1)}, u32[]{:S(2)}, u32[]{:S(2)}) collective-permute-start(bf16[8,64,256]{2,1,0:T(8,128)(2,1)} %get-tuple-element.49), channel_id=1, source_target_pairs={{0,16},{16,0},{1,17},{17,1},{2,18},{18,2},{3,19},{19,3},{4,20},{20... | collective-permute-start | bytes 786440 | tf_op jit(solution)/shard_map/ppermute | solution.py:426
  63.0 0.6 collective-permute-start.7
  63.7 2.6 %pick_pages.3 = (bf16[8,64,256]{2,1,0:T(8,128)(2,1)}, bf16[8,64,256]{2,1,0:T(8,128)(2,1)}) custom-call(s32[8]{0:T(128)} %and_select_fusion.1.idx, bf16[64,64,512]{2,1,0:T(8,128)(2,1)} %all-gather.2.cloned.1.call-done.pool), custom_call_target="tpu_custom_call" | custom-call | bytes 1048576 | tf_op jit(solution)/shard_map/pick_pages/pallas_call | solution.py:150
  66.3 4.6 %collective-permute-done.10 = bf16[8,64,256]{2,1,0:T(8,128)(2,1)S(1)} collective-permute-done((bf16[8,64,256]{2,1,0:T(8,128)(2,1)}, bf16[8,64,256]{2,1,0:T(8,128)(2,1)S(1)}, u32[]{:S(2)}, u32[]{:S(2)}) %collective-permute-start.10) | collective-permute-done | bytes 262176 | tf_op jit(solution)/shard_map/ppermute | solution.py:426
  70.9 1.0 broadcast_select_fusion.v_mine
  71.9 0.0 copy-start.10
  71.9 1.5 %collective-permute-start.11 = (bf16[8,64,256]{2,1,0:T(8,128)(2,1)S(1)}, bf16[8,64,256]{2,1,0:T(8,128)(2,1)S(1)}, u32[]{:S(2)}, u32[]{:S(2)}) collective-permute-start(bf16[8,64,256]{2,1,0:T(8,128)(2,1)S(1)} %broadcast_select_fusion.v_mine), channel_id=1, source_target_pairs={{0,1},{1,0},{2,3},{3,2},{4,5},{5,4},{6,7},{7,6},{8,9},{9,8},{10,11... | collective-permute-start | bytes 786440 | tf_op jit(solution)/shard_map/ppermute | solution.py:432
  73.4 0.0 collective-permute-done.8.kv_peer
  73.4 2.4 %collective-permute-done.7 = bf16[8,64,256]{2,1,0:T(8,128)(2,1)S(1)} collective-permute-done((bf16[8,64,256]{2,1,0:T(8,128)(2,1)}, bf16[8,64,256]{2,1,0:T(8,128)(2,1)S(1)}, u32[]{:S(2)}, u32[]{:S(2)}) %collective-permute-start.7) | collective-permute-done | bytes 262176 | tf_op jit(solution)/shard_map/ppermute | solution.py:425
  75.8 1.0 broadcast_select_fusion.1.k_mine
  76.8 0.0 copy-start.11
  76.8 1.5 %collective-permute-start.9 = (bf16[8,64,256]{2,1,0:T(8,128)(2,1)S(1)}, bf16[8,64,256]{2,1,0:T(8,128)(2,1)S(1)}, u32[]{:S(2)}, u32[]{:S(2)}) collective-permute-start(bf16[8,64,256]{2,1,0:T(8,128)(2,1)S(1)} %broadcast_select_fusion.1.k_mine), channel_id=1, source_target_pairs={{0,1},{1,0},{2,3},{3,2},{4,5},{5,4},{6,7},{7,6},{8,9},{9,8},{10,11... | collective-permute-start | bytes 786440 | tf_op jit(solution)/shard_map/ppermute | solution.py:430
  79.0 0.7 pad_add_fusion.info
  79.7 0.0 collective-permute-done.11.v_peer
  79.7 4.8 %collective-permute-done.9.k_peer = bf16[8,64,256]{2,1,0:T(8,128)(2,1)S(1)} collective-permute-done((bf16[8,64,256]{2,1,0:T(8,128)(2,1)S(1)}, bf16[8,64,256]{2,1,0:T(8,128)(2,1)S(1)}, u32[]{:S(2)}, u32[]{:S(2)}) %collective-permute-start.9) | collective-permute-done | bytes 262176 | tf_op jit(solution)/shard_map/ppermute | solution.py:430
  84.5 0.0 copy-done.10
  84.5 0.0 copy-done.15
  84.5 0.0 copy-done.11
  84.5 0.0 copy-done.16
  84.5 0.7 copy-done.17
  85.2 12.5 %attend_and_out.1 = bf16[512,1536]{1,0:T(8,128)(2,1)} custom-call(s32[3]{0:T(128)} %pad_add_fusion.info, bf16[512,768]{1,0:T(8,128)(2,1)} %copy-done.8, bf16[512,768]{1,0:T(8,128)(2,1)} %copy-done, bf16[8,64,256]{2,1,0:T(8,128)(2,1)} %copy-done.11, bf16[8,64,256]{2,1,0:T(8,128)(2,1)} %copy-done.17, bf16[8,64,256]{2,1,0:T(8,128)(2,1)} %copy-done.10, ...), custom_call_target="tpu_custom_call" | custom-call | flops 6442450944 | bytes 12582912 | tf_op jit(solution)/shard_map/attend_and_out/pallas_call | solution.py:345
  (18 shorter events, 0.0 us)
Async XLA Ops:
  6.5 5.5 %copy-start.12 = (f32[1536]{0:T(1024)S(1)}, f32[1536]{0:T(1024)}, u32[]{:S(2)}) copy-start(f32[1536]{0:T(1024)} %param.10) | copy-start | bytes 18436
  6.5 52.3 %all-gather.2.cloned.1.call-start = ((), (), s32[]{:S(2)}) async-start(), calls=%async_computation | async-start | bytes 4718592 | tf_op jit(solution)/shard_map/all_gather | solution.py:391
  8.4 16.4 %collective-permute-start = (bf16[384,768]{1,0:T(8,128)(2,1)S(1)}, bf16[384,768]{1,0:T(8,128)(2,1)S(1)}, u32[]{:S(2)}, u32[]{:S(2)}) collective-permute-start(bf16[384,768]{1,0:T(8,128)(2,1)S(1)} %constant_dynamic-slice_fusion.1), channel_id=1, source_target_pairs={{0,1},{1,0},{2,3},{3,2},{4,5},{5,4},{6,7},{7,6},{8,9},{9,8},{10,11... | collective-permute-start | bytes 1769480 | tf_op jit(solution)/shard_map/ppermute | solution.py:395
  12.5 1.7 %copy-start.5 = (bf16[1536,768]{1,0:T(8,128)(2,1)S(1)}, bf16[1536,768]{1,0:T(8,128)(2,1)}, u32[]{:S(2)}) copy-start(bf16[1536,768]{1,0:T(8,128)(2,1)} %wq.1) | copy-start | bytes 7077892
  14.2 1.4 %copy-start.6 = (bf16[1,512,1536]{2,1,0:T(8,128)(2,1)S(1)}, bf16[1,512,1536]{2,1,0:T(8,128)(2,1)}, u32[]{:S(2)}) copy-start(bf16[1,512,1536]{2,1,0:T(8,128)(2,1)} %param.9) | copy-start | bytes 4718596
  15.6 1.4 %copy-start.7 = (bf16[1536,512]{1,0:T(8,128)(2,1)S(1)}, bf16[1536,512]{1,0:T(8,128)(2,1)}, u32[]{:S(2)}) copy-start(bf16[1536,512]{1,0:T(8,128)(2,1)} %wkv.1) | copy-start | bytes 4718596
  17.0 9.5 %copy-start.9 = (bf16[768,1536]{1,0:T(8,128)(2,1)S(1)}, bf16[768,1536]{1,0:T(8,128)(2,1)}, u32[]{:S(2)}) copy-start(bf16[768,1536]{1,0:T(8,128)(2,1)} %woa.1) | copy-start | bytes 7077892
  20.1 19.3 %copy-start.1 = (f32[512,256]{1,0:T(8,128)}, f32[512,256]{1,0:T(8,128)S(1)}, u32[]{:S(2)}) copy-start(f32[512,256]{1,0:T(8,128)S(1)} %get-tuple-element.34.cos) | copy-start | bytes 1572868
  20.1 19.3 %copy-start.3 = (f32[512,256]{1,0:T(8,128)}, f32[512,256]{1,0:T(8,128)S(1)}, u32[]{:S(2)}) copy-start(f32[512,256]{1,0:T(8,128)S(1)} %get-tuple-element.35.sin) | copy-start | bytes 1572868
  20.1 19.3 %copy-start.8 = (bf16[512,768]{1,0:T(8,128)(2,1)}, bf16[512,768]{1,0:T(8,128)(2,1)S(1)}, u32[]{:S(2)}) copy-start(bf16[512,768]{1,0:T(8,128)(2,1)S(1)} %get-tuple-element.29.qa_hbm) | copy-start | bytes 2359300
  24.8 14.6 %collective-permute-start.2 = (bf16[384,768]{1,0:T(8,128)(2,1)S(1)}, bf16[384,768]{1,0:T(8,128)(2,1)S(1)}, u32[]{:S(2)}, u32[]{:S(2)}) collective-permute-start(bf16[384,768]{1,0:T(8,128)(2,1)S(1)} %collective-permute-done.w0), channel_id=1, source_target_pairs={{0,16},{16,0},{1,17},{17,1},{2,18},{18,2},{3,19},{19,3},{4,20},{20... | collective-permute-start | bytes 1769480 | tf_op jit(solution)/shard_map/ppermute | solution.py:405
  27.6 27.0 %collective-permute-start.1 = (bf16[384,1536]{1,0:T(8,128)(2,1)}, bf16[384,1536]{1,0:T(8,128)(2,1)}, u32[]{:S(2)}, u32[]{:S(2)}) collective-permute-start(bf16[384,1536]{1,0:T(8,128)(2,1)} %constant_dynamic-slice_fusion), channel_id=1, source_target_pairs={{0,1},{1,0},{2,3},{3,2},{4,5},{5,4},{6,7},{7,6},{8,9},{9,8},{10,11... | collective-permute-start | bytes 3538952 | tf_op jit(solution)/shard_map/ppermute | solution.py:395
  29.1 10.5 %collective-permute-start.3 = (bf16[384,768]{1,0:T(8,128)(2,1)S(1)}, bf16[384,768]{1,0:T(8,128)(2,1)S(1)}, u32[]{:S(2)}, u32[]{:S(2)}) collective-permute-start(bf16[384,768]{1,0:T(8,128)(2,1)S(1)} %collective-permute-done.w0), channel_id=1, source_target_pairs={{0,2},{2,0},{4,6},{6,4},{8,10},{10,8},{12,14},{14,12},{1,3},{3,1},... | collective-permute-start | bytes 1769480 | tf_op jit(solution)/shard_map/ppermute | solution.py:409
  39.4 2.2 %collective-permute-start.4 = (bf16[384,768]{1,0:T(8,128)(2,1)S(1)}, bf16[384,768]{1,0:T(8,128)(2,1)}, u32[]{:S(2)}, u32[]{:S(2)}) collective-permute-start(bf16[384,768]{1,0:T(8,128)(2,1)S(1)} %collective-permute-done.2.w1), channel_id=1, source_target_pairs={{0,2},{2,0},{4,6},{6,4},{8,10},{10,8},{12,14},{14,12},{1,3},{3,1},... | collective-permute-start | bytes 1769480 | tf_op jit(solution)/shard_map/ppermute | solution.py:409
  41.6 1.1 %copy-start.2 = (f32[512,256]{1,0:T(8,128)S(1)}, f32[512,256]{1,0:T(8,128)}, u32[]{:S(2)}) copy-start(f32[512,256]{1,0:T(8,128)} %copy-done.1) | copy-start | bytes 1572868
  42.6 1.0 copy-start.4
  43.7 10.8 %copy-start.13 = (s32[1,8]{1,0:T(1,128)S(1)}, s32[1,8]{1,0:T(1,128)}, u32[]{:S(2)}) copy-start(s32[1,8]{1,0:T(1,128)} %param.15) | copy-start | bytes 100
  46.9 1.0 copy-start
  54.5 4.1 %collective-permute-start.5 = (bf16[384,1536]{1,0:T(8,128)(2,1)}, bf16[384,1536]{1,0:T(8,128)(2,1)S(1)}, u32[]{:S(2)}, u32[]{:S(2)}) collective-permute-start(bf16[384,1536]{1,0:T(8,128)(2,1)} %collective-permute-done.1.wob0), channel_id=1, source_target_pairs={{0,2},{2,0},{4,6},{6,4},{8,10},{10,8},{12,14},{14,12},{1,3},{3,1},... | collective-permute-start | bytes 3538952 | tf_op jit(solution)/shard_map/ppermute | solution.py:415
  54.5 3.5 %collective-permute-start.6 = (s32[8]{0:T(128)S(1)}, s32[8]{0:T(128)S(1)}, u32[]{:S(2)}, u32[]{:S(2)}) collective-permute-start(s32[8]{0:T(128)S(1)} %bitcast.15), channel_id=1, source_target_pairs={{0,16},{16,0},{1,17},{17,1},{2,18},{18,2},{3,19},{19,3},{4,20},{20... | collective-permute-start | bytes 104 | tf_op jit(solution)/shard_map/ppermute | solution.py:408
  55.7 17.8 %collective-permute-start.8 = (bf16[512,512]{1,0:T(8,128)(2,1)}, bf16[512,512]{1,0:T(8,128)(2,1)S(1)}, u32[]{:S(2)}, u32[]{:S(2)}) collective-permute-start(bf16[512,512]{1,0:T(8,128)(2,1)} %get-tuple-element.43.kv_own), channel_id=1, source_target_pairs={{0,1},{1,0},{2,3},{3,2},{4,5},{5,4},{6,7},{7,6},{8,9},{9,8},{10,11... | collective-permute-start | bytes 1572872 | tf_op jit(solution)/shard_map/ppermute | solution.py:416
  58.6 2.9 %copy-start.14 = (bf16[384,1536]{1,0:T(8,128)(2,1)}, bf16[384,1536]{1,0:T(8,128)(2,1)S(1)}, u32[]{:S(2)}) copy-start(bf16[384,1536]{1,0:T(8,128)(2,1)S(1)} %collective-permute-done.5.wob1) | copy-start | bytes 3538948
  61.5 9.4 %collective-permute-start.10 = (bf16[8,64,256]{2,1,0:T(8,128)(2,1)}, bf16[8,64,256]{2,1,0:T(8,128)(2,1)S(1)}, u32[]{:S(2)}, u32[]{:S(2)}) collective-permute-start(bf16[8,64,256]{2,1,0:T(8,128)(2,1)} %get-tuple-element.49), channel_id=1, source_target_pairs={{0,16},{16,0},{1,17},{17,1},{2,18},{18,2},{3,19},{19,3},{4,20},{20... | collective-permute-start | bytes 786440 | tf_op jit(solution)/shard_map/ppermute | solution.py:426
  63.0 12.8 %collective-permute-start.7 = (bf16[8,64,256]{2,1,0:T(8,128)(2,1)}, bf16[8,64,256]{2,1,0:T(8,128)(2,1)S(1)}, u32[]{:S(2)}, u32[]{:S(2)}) collective-permute-start(bf16[8,64,256]{2,1,0:T(8,128)(2,1)} %get-tuple-element.42), channel_id=1, source_target_pairs={{0,16},{16,0},{1,17},{17,1},{2,18},{18,2},{3,19},{19,3},{4,20},{20... | collective-permute-start | bytes 786440 | tf_op jit(solution)/shard_map/ppermute | solution.py:425
  71.9 12.6 %copy-start.10 = (bf16[8,64,256]{2,1,0:T(8,128)(2,1)}, bf16[8,64,256]{2,1,0:T(8,128)(2,1)S(1)}, u32[]{:S(2)}) copy-start(bf16[8,64,256]{2,1,0:T(8,128)(2,1)S(1)} %broadcast_select_fusion.v_mine) | copy-start | bytes 786436
  71.9 7.8 %collective-permute-start.11 = (bf16[8,64,256]{2,1,0:T(8,128)(2,1)S(1)}, bf16[8,64,256]{2,1,0:T(8,128)(2,1)S(1)}, u32[]{:S(2)}, u32[]{:S(2)}) collective-permute-start(bf16[8,64,256]{2,1,0:T(8,128)(2,1)S(1)} %broadcast_select_fusion.v_mine), channel_id=1, source_target_pairs={{0,1},{1,0},{2,3},{3,2},{4,5},{5,4},{6,7},{7,6},{8,9},{9,8},{10,11... | collective-permute-start | bytes 786440 | tf_op jit(solution)/shard_map/ppermute | solution.py:432
  73.4 11.1 %copy-start.15 = (bf16[512,512]{1,0:T(8,128)(2,1)}, bf16[512,512]{1,0:T(8,128)(2,1)S(1)}, u32[]{:S(2)}) copy-start(bf16[512,512]{1,0:T(8,128)(2,1)S(1)} %collective-permute-done.8.kv_peer) | copy-start | bytes 1572868
  76.8 7.7 %copy-start.11 = (bf16[8,64,256]{2,1,0:T(8,128)(2,1)}, bf16[8,64,256]{2,1,0:T(8,128)(2,1)S(1)}, u32[]{:S(2)}) copy-start(bf16[8,64,256]{2,1,0:T(8,128)(2,1)S(1)} %broadcast_select_fusion.1.k_mine) | copy-start | bytes 786436
  76.8 7.7 %collective-permute-start.9 = (bf16[8,64,256]{2,1,0:T(8,128)(2,1)S(1)}, bf16[8,64,256]{2,1,0:T(8,128)(2,1)S(1)}, u32[]{:S(2)}, u32[]{:S(2)}) collective-permute-start(bf16[8,64,256]{2,1,0:T(8,128)(2,1)S(1)} %broadcast_select_fusion.1.k_mine), channel_id=1, source_target_pairs={{0,1},{1,0},{2,3},{3,2},{4,5},{5,4},{6,7},{7,6},{8,9},{9,8},{10,11... | collective-permute-start | bytes 786440 | tf_op jit(solution)/shard_map/ppermute | solution.py:430
  79.7 4.8 %copy-start.16 = (bf16[8,64,256]{2,1,0:T(8,128)(2,1)}, bf16[8,64,256]{2,1,0:T(8,128)(2,1)S(1)}, u32[]{:S(2)}) copy-start(bf16[8,64,256]{2,1,0:T(8,128)(2,1)S(1)} %collective-permute-done.11.v_peer) | copy-start | bytes 786436
  84.5 0.7 copy-start.17
Sparse Core Ops, SparseCore 0:
  9.0 49.8 all-gather.1

commit v8 on v7

--- a/solution.py
+++ b/solution.py
@@ -70,7 +70,7 @@
         for h in range(wq.shape[1] // head_size):
             cols = slice(h * head_size, (h + 1) * head_size)
             part = jnp.dot(nb, wq[:, cols], preferred_element_type=F32)
-            q[at, cols] = (rotate(part, c, s, even) * factor).astype(BF16)
+            q[h, at, :] = (rotate(part, c, s, even) * factor).astype(BF16)
 
 
 def project(tok, gain, wq, wkv, cos_t, sin_t, head_size, step):
@@ -80,7 +80,7 @@
         functools.partial(project_kernel, head_size, step, score_factor(head_size)),
         out_shape=(
             jax.ShapeDtypeStruct((rows, width), BF16),
-            jax.ShapeDtypeStruct((rows, qc), BF16),
+            jax.ShapeDtypeStruct((qc // head_size, rows, head_size), BF16),
             jax.ShapeDtypeStruct((rows, kc), BF16),
             jax.ShapeDtypeStruct((rows, head_size), F32),
             jax.ShapeDtypeStruct((rows, head_size), F32),
@@ -97,21 +97,16 @@
 
 def other_kernel(head_size, factor, order, normed, w0, w1, w2, w3, cos, sin, q):
     rows = normed.shape[0]
-    tile = min(256, rows)
     deep = w0.shape[0]
-    even = lax.broadcasted_iota(jnp.int32, (tile, head_size), 1) % 2 == 0
-    for i in range(rows // tile):
-        at = pl.ds(i * tile, tile)
-        c = cos[at, :]
-        s = sin[at, :]
-        for h in range(q.shape[1] // head_size):
-            cols = slice(h * head_size, (h + 1) * head_size)
-            total = None
-            for n, w in enumerate((w0, w1, w2, w3)):
-                x = normed[at, pl.ds(pl.multiple_of(order[n] * deep, 128), deep)]
-                part = jnp.dot(x, w[:, cols], preferred_element_type=F32)
-                total = part if total is None else total + part
-            q[at, cols] = (rotate(total, c, s, even) * factor).astype(BF16)
+    even = lax.broadcasted_iota(jnp.int32, (rows, head_size), 1) % 2 == 0
+    for h in range(q.shape[0]):
+        cols = slice(h * head_size, (h + 1) * head_size)
+        total = None
+        for n, w in enumerate((w0, w1, w2, w3)):
+            x = normed[:, pl.ds(pl.multiple_of(order[n] * deep, 128), deep)]
+            part = jnp.dot(x, w[:, cols], preferred_element_type=F32)
+            total = part if total is None else total + part
+        q[h] = (rotate(total, cos[...], sin[...], even) * factor).astype(BF16)
 
 
 def project_other(normed, pieces, order, cos, sin, head_size):
@@ -119,7 +114,7 @@
     qc = pieces[0].shape[1]
     return pl.pallas_call(
         functools.partial(other_kernel, head_size, score_factor(head_size)),
-        out_shape=jax.ShapeDtypeStruct((rows, qc), BF16),
+        out_shape=jax.ShapeDtypeStruct((qc // head_size, rows, head_size), BF16),
         in_specs=[spec(pltpu.SMEM)] + [spec(pltpu.VMEM)] * 7,
         out_specs=spec(pltpu.VMEM),
         compiler_params=pltpu.CompilerParams(vmem_limit_bytes=20 * 2**20),
@@ -192,13 +187,12 @@
 ):
     part = info[0]
     length = info[1]
-    rows, half = qa.shape
+    nheads, rows, _ = qa.shape
     pages, prow, _ = k_mine.shape
     page = 2 * prow
     width = out.shape[1]
     core = info[2]
     deep = wob0.shape[0]
-    nheads = half // head_size
     window = pages * page
 
     def start(mine, peer, lo, dst, sem):
@@ -243,102 +237,86 @@
     gap = lax.broadcasted_iota(jnp.int32, (band, tile), 1) - lax.broadcasted_iota(
         jnp.int32, (band, tile), 0
     )
-    order = [(i, n, h) for i in range(rows // tile) for n in range(2) for h in range(nheads)]
-
-    def score(m):
-        i, n, h = order[m]
-        q = (qa, qb)[n][pl.ds(i * tile, tile), h * head_size : (h + 1) * head_size]
+    groups = [(i, n) for i in range(rows // tile) for n in range(2)]
+    tall = nheads * tile
+
+    def score(g):
+        i, n = groups[g]
+        q = (qa, qb)[n][:, pl.ds(i * tile, tile), :].reshape(tall, head_size)
         for lo in range(0, span, tile):
-            sbuf[m % 2, :, lo : lo + tile] = lax.dot_general(
+            sbuf[g % 2, :, lo : lo + tile] = lax.dot_general(
                 q,
                 keys[pl.ds(i * tile + lo, tile), :],
                 (((1,), (1,)), ((), ())),
                 preferred_element_type=F32,
             )
 
-    def soften(m):
-        for lo in range(0, tile, band):
-            at = pl.ds(lo, band)
+    def soften(g):
+        for top in range(0, tall, band):
+            at = pl.ds(top, band)
+            lo = top % tile
             s = jnp.concatenate(
                 [
-                    jnp.where(gap >= lo + 1, sbuf[m % 2, at, :tile], MASKED),
-                    sbuf[m % 2, at, tile : span - tile],
-                    jnp.where(gap <= lo, sbuf[m % 2, at, span - tile :], MASKED),
+                    jnp.where(gap >= lo + 1, sbuf[g % 2, at, :tile], MASKED),
+                    sbuf[g % 2, at, tile : span - tile],
+                    jnp.where(gap <= lo, sbuf[g % 2, at, span - tile :], MASKED),
                 ],
                 axis=1,
             )
             e = jnp.exp2(s - jnp.max(s, axis=-1, keepdims=True))
             total = jnp.sum(e, axis=-1, keepdims=True)
-            pbuf[m % 2, at, :] = e.astype(BF16)
-            sums[m % 2, at, :] = jnp.broadcast_to(1.0 / total, (band, 128))
-
-    def combine(m):
-        i, n, h = order[m]
+            pbuf[g % 2, at, :] = e.astype(BF16)
+            sums[g % 2, at, :] = jnp.broadcast_to(1.0 / total, (band, 128))
+
+    def combine(g):
+        i, n = groups[g]
         mixed = jnp.dot(
-            pbuf[m % 2], vals[pl.ds(i * tile, span), :], preferred_element_type=F32
+            pbuf[g % 2], vals[pl.ds(i * tile, span), :], preferred_element_type=F32
         )
-        mixed = mixed * sums[m % 2, :, :1]
-        at = pl.ds(i * tile, tile)
-        mix[n, at, h * head_size : (h + 1) * head_size] = mixed.astype(BF16)
-
-    block = 512
-
-    def project_out(i, lo):
-        at = pl.ds(i * tile, tile)
-        row = part * rows + i * tile + lax.broadcasted_iota(jnp.int32, (tile, 1), 0)
-        cols = slice(lo, lo + block)
-        a = jnp.dot(mix[0, at, :], wa[:, cols], preferred_element_type=F32)
-        b = jnp.dot(mix[1, at, :], wb[:, cols], preferred_element_type=F32)
-        both = a.astype(BF16).astype(F32) + b.astype(BF16).astype(F32)
-        out[at, cols] = jnp.where(row < length, both, 0.0).astype(BF16)
-
-    stores = []
-
-    def send_out(i):
-        at = pl.ds(i * tile, tile)
-        stores.append(pltpu.make_async_copy(out.at[at, :], out_hbm.at[at, :], osem.at[i]))
-        stores[i].start()
+        mixed = (mixed * sums[g % 2, :, :1]).astype(BF16)
+        for h in range(nheads):
+            part_h = mixed[h * tile : (h + 1) * tile, :]
+            mix[n, pl.ds(i * tile, tile), h * head_size : (h + 1) * head_size] = part_h
 
     queries[0].wait()
     finish(keys, ksem)
+    score(0)
     queries[1].wait()
-    score(0)
-    ready = []
-    for m in range(len(order)):
-        if m + 1 < len(order):
-            score(m + 1)
-        if m == 1:
+    for g in range(len(groups)):
+        if g + 1 < len(groups):
+            score(g + 1)
+        if g == 1:
             finish(vals, vsem)
-        if m >= 1:
-            combine(m - 1)
-            i, n, h = order[m - 1]
-            if (n, h) == (1, nheads - 1):
-                if i == 0:
-                    for c in weights:
-                        c.wait()
-                ready += [(i, lo) for lo in range(0, width, block)]
-        if m >= 1 and ready and order[m - 1][1:] != (1, nheads - 1):
-            i, lo = ready.pop(0)
-            project_out(i, lo)
-            if lo + block == width:
-                send_out(i)
-        soften(m)
-    combine(len(order) - 1)
-    if rows == tile:
-        for c in weights:
-            c.wait()
-    ready += [(rows // tile - 1, lo) for lo in range(0, width, block)]
-    for i, lo in ready:
-        project_out(i, lo)
-        if lo + block == width:
-            send_out(i)
+        if g >= 1:
+            combine(g - 1)
+        soften(g)
+    if len(groups) == 1:
+        finish(vals, vsem)
+    combine(len(groups) - 1)
+    for c in weights:
+        c.wait()
+    row = part * rows + lax.broadcasted_iota(jnp.int32, (rows, 1), 0)
+    live = row < length
+    block = 256
+    stores = []
+    for lo in range(0, width, block):
+        cols = slice(lo, lo + block)
+        a = jnp.dot(mix[0], wa[:, cols], preferred_element_type=F32)
+        b = jnp.dot(mix[1], wb[:, cols], preferred_element_type=F32)
+        both = a.astype(BF16).astype(F32) + b.astype(BF16).astype(F32)
+        out[:, cols] = jnp.where(live, both, 0.0).astype(BF16)
+        m = len(stores)
+        stores.append(pltpu.make_async_copy(out.at[:, cols], out_hbm.at[:, cols], osem.at[m]))
+        stores[m].start()
     for c in stores:
         c.wait()
 
 
 def attend_pages(info, qa, qb, k_mine, k_peer, v_mine, v_peer, kv_own, kv_peer, woa, wobs):
-    rows, half = qa.shape
+    nheads, rows, _ = qa.shape
+    half = woa.shape[0]
     tile = min(256, rows)
+    tall = nheads * tile
     width = woa.shape[1]
     head_size = k_mine.shape[2]
     window = k_mine.shape[0] * k_mine.shape[1] * 2
@@ -351,21 +329,21 @@
         + [spec(ANY)] * 5,
         out_specs=spec(ANY),
         scratch_shapes=[
-            pltpu.VMEM((rows, half), BF16),
-            pltpu.VMEM((rows, half), BF16),
+            pltpu.VMEM(qa.shape, BF16),
+            pltpu.VMEM(qa.shape, BF16),
             pltpu.VMEM((window + rows, head_size), BF16),
             pltpu.VMEM((window + rows, head_size), BF16),
             pltpu.VMEM(woa.shape, BF16),
             pltpu.VMEM(woa.shape, BF16),
             pltpu.VMEM((2, rows, half), BF16),
             pltpu.VMEM((rows, width), BF16),
-            pltpu.VMEM((2, tile, window + tile), F32),
-            pltpu.VMEM((2, tile, window + tile), BF16),
-            pltpu.VMEM((2, tile, 128), F32),
+            pltpu.VMEM((2, tall, window + tile), F32),
+            pltpu.VMEM((2, tall, window + tile), BF16),
+            pltpu.VMEM((2, tall, 128), F32),
             pltpu.SemaphoreType.DMA,
             pltpu.SemaphoreType.DMA,
             pltpu.SemaphoreType.DMA((5,)),
-            pltpu.SemaphoreType.DMA((rows // tile,)),
+            pltpu.SemaphoreType.DMA((width // 256,)),
         ],
         compiler_params=pltpu.CompilerParams(vmem_limit_bytes=56 * 2**20),
         cost_estimate=pl.CostEstimate(

time: 105 us -> 106 us (level)
  other arithmetic: 4.07 us -> 2.17 us
  Pallas kernels: 24 us -> 25.1 us
    pallas_call x1, Pallas kernels: 12.5 us -> 13.5 us  [attend_pages(): pl.pallas_call(functools.partial(attend_kernel, head_size), out_shape=jax...]
  transfers between devices with their start and end apart: 13 -> 13, of which waited for: 9 -> 9; matrix products, arithmetic and copies ran while one was open for 6% -> 4% of each run, Pallas kernels for 11% -> 11%
where the time goes in v8:
time: 106 us; the launch traced here: 105 us
  waiting for transfers between devices  38.3 us (36%)
  Pallas kernels  25.1 us (24%)
  between operations  15.1 us (14%)
  starting transfers between devices  13.6 us (13%)
  local copies, waits for them, and re-layouts  10.5 us (10%)
  other arithmetic  2.17 us (2%)
    pallas_call x1, Pallas kernels, attend_pages(): pl.pallas_call(functools.partial(attend_kernel, head_size), out_shape=jax...  13.5 us
    ppermute x2, waiting for transfers between devices, peer_rows(): lax.ppermute(lax.dynamic_slice_in_dim(w, at * deep, deep, 0), 'tensor', s...  11.3 us
    ppermute x1, waiting for transfers between devices, pair_shards(): b = lax.ppermute(a, 'rep', swap)  10.3 us
    unnamed x36, local copies, waits for them, and re-layouts  8.26 us
    pallas_call x2, Pallas kernels, pick(): pl.pallas_call(pick_kernel, out_shape=(half, half), in_specs=[spec(pltpu....  5.21 us
    ppermute x1, waiting for transfers between devices, pair_shards(): k_peer = lax.ppermute(k_mine, 'tensor', swap)  4.83 us
    ppermute x1, waiting for transfers between devices, pair_shards(): v_came = lax.ppermute(v_sent, 'rep', swap)  4.57 us
    ppermute x2, starting transfers between devices, peer_rows(): lax.ppermute(lax.dynamic_slice_in_dim(w, at * deep, deep, 0), 'tensor', s...  4.55 us
  transfers between devices with their start and end apart: 13, of which 9 were waited for; matrix products, arithmetic and copies ran while one was open for 4% of the time, Pallas kernels for 11%

profile of v8, /device:TPU:0, one launch (start us, length us, event | category | flops | bytes accessed | tf_op | source)
XLA Modules:
  0.0 104.7 jit_solution(11747835602575015665)
XLA Ops:
  6.5 0.0 copy-start.12
  6.5 0.0 all-gather.2.cloned.1.call-start
  6.5 0.7 all-gather.2.cloned.1.call-update
  7.3 1.1 %constant_dynamic-slice_fusion.1 = bf16[384,768]{1,0:T(8,128)(2,1)S(1)} fusion(bf16[1536,768]{1,0:T(8,128)(2,1)} %wq.1, s32[]{:T(128)S(6)} %select_n.70), kind=kLoop, calls=%fused_computation.31 | loop fusion | bytes 1179652 | tf_op jit(solution)/shard_map/dynamic_slice | solution.py:373
  8.4 3.0 %collective-permute-start = (bf16[384,768]{1,0:T(8,128)(2,1)S(1)}, bf16[384,768]{1,0:T(8,128)(2,1)S(1)}, u32[]{:S(2)}, u32[]{:S(2)}) collective-permute-start(bf16[384,768]{1,0:T(8,128)(2,1)S(1)} %constant_dynamic-slice_fusion.1), channel_id=1, source_target_pairs={{0,1},{1,0},{2,3},{3,2},{4,5},{5,4},{6,7},{7,6},{8,9},{9,8},{10,11... | collective-permute-start | bytes 1769480 | tf_op jit(solution)/shard_map/ppermute | solution.py:373
  12.1 0.0 copy-done.12
  12.1 0.1 pad_maximum_fusion
  12.2 0.3 fusion
  12.5 0.0 copy-start.5
  12.5 1.7 %copy-done.5 = bf16[1536,768]{1,0:T(8,128)(2,1)S(1)} copy-done((bf16[1536,768]{1,0:T(8,128)(2,1)S(1)}, bf16[1536,768]{1,0:T(8,128)(2,1)}, u32[]{:S(2)}) %copy-start.5) | copy-done | bytes 2359320
  14.2 0.0 copy-start.6
  14.2 1.4 %copy-done.6 = bf16[1,512,1536]{2,1,0:T(8,128)(2,1)S(1)} copy-done((bf16[1,512,1536]{2,1,0:T(8,128)(2,1)S(1)}, bf16[1,512,1536]{2,1,0:T(8,128)(2,1)}, u32[]{:S(2)}) %copy-start.6) | copy-done | bytes 1572888
  15.6 1.4 %copy-done.7 = bf16[1536,512]{1,0:T(8,128)(2,1)S(1)} copy-done((bf16[1536,512]{1,0:T(8,128)(2,1)S(1)}, bf16[1536,512]{1,0:T(8,128)(2,1)}, u32[]{:S(2)}) %copy-start.7) | copy-done | bytes 1572888
  17.0 3.1 %project_own.1 = (bf16[512,1536]{1,0:T(8,128)(2,1)S(1)}, bf16[3,512,256]{2,1,0:T(8,128)(2,1)S(1)}, bf16[512,512]{1,0:T(8,128)(2,1)}, f32[512,256]{1,0:T(8,128)S(1)}, f32[512,256]{1,0:T(8,128)S(1)}) custom-call(bf16[512,1536]{1,0:T(8,128)(2,1)S(1)} %bitcast.14, f32[1,1536]{1,0:T(1,128)S(1)} %reshape.34.gain, bf16[1536,768]{1,0:T(8,128)(2,1)S(1)} %copy-done.5, ...), custom_call_target="tpu_custom_call" | custom-call | flops 2013265920 | bytes 10485760 | tf_op jit(solution)/shard_map/project_own/pallas_call | solution.py:79
  20.1 4.7 %collective-permute-done.w0 = bf16[384,768]{1,0:T(8,128)(2,1)S(1)} collective-permute-done((bf16[384,768]{1,0:T(8,128)(2,1)S(1)}, bf16[384,768]{1,0:T(8,128)(2,1)S(1)}, u32[]{:S(2)}, u32[]{:S(2)}) %collective-permute-start) | collective-permute-done | bytes 589856 | tf_op jit(solution)/shard_map/ppermute | solution.py:373
  24.8 1.7 %collective-permute-start.2 = (bf16[384,768]{1,0:T(8,128)(2,1)S(1)}, bf16[384,768]{1,0:T(8,128)(2,1)S(1)}, u32[]{:S(2)}, u32[]{:S(2)}) collective-permute-start(bf16[384,768]{1,0:T(8,128)(2,1)S(1)} %collective-permute-done.w0), channel_id=1, source_target_pairs={{0,16},{16,0},{1,17},{17,1},{2,18},{18,2},{3,19},{19,3},{4,20},{20... | collective-permute-start | bytes 1769480 | tf_op jit(solution)/shard_map/ppermute | solution.py:383
  26.5 0.0 copy-done.9
  26.5 1.1 %constant_dynamic-slice_fusion = bf16[384,1536]{1,0:T(8,128)(2,1)} fusion(bf16[768,1536]{1,0:T(8,128)(2,1)S(1)} %copy-done.9, s32[]{:T(128)S(6)} %select_n.71), kind=kLoop, calls=%fused_computation.30 | loop fusion | bytes 2359300 | tf_op jit(solution)/shard_map/dynamic_slice | solution.py:373
  27.6 1.5 %collective-permute-start.1 = (bf16[384,1536]{1,0:T(8,128)(2,1)}, bf16[384,1536]{1,0:T(8,128)(2,1)}, u32[]{:S(2)}, u32[]{:S(2)}) collective-permute-start(bf16[384,1536]{1,0:T(8,128)(2,1)} %constant_dynamic-slice_fusion), channel_id=1, source_target_pairs={{0,1},{1,0},{2,3},{3,2},{4,5},{5,4},{6,7},{7,6},{8,9},{9,8},{10,11... | collective-permute-start | bytes 3538952 | tf_op jit(solution)/shard_map/ppermute | solution.py:373
  29.1 0.0 collective-permute-start.3
  29.1 10.3 %collective-permute-done.2.w1 = bf16[384,768]{1,0:T(8,128)(2,1)S(1)} collective-permute-done((bf16[384,768]{1,0:T(8,128)(2,1)S(1)}, bf16[384,768]{1,0:T(8,128)(2,1)S(1)}, u32[]{:S(2)}, u32[]{:S(2)}) %collective-permute-start.2) | collective-permute-done | bytes 589856 | tf_op jit(solution)/shard_map/ppermute | solution.py:383
  39.4 0.0 copy-done.1
  39.4 0.0 copy-done.3
  39.4 0.0 copy-done.8
  39.4 0.1 collective-permute-start.4
  39.5 0.1 pad_add_fusion.1.order
  39.6 0.0 collective-permute-done.3.w2
  39.6 2.0 %collective-permute-done.4.w3 = bf16[384,768]{1,0:T(8,128)(2,1)} collective-permute-done((bf16[384,768]{1,0:T(8,128)(2,1)S(1)}, bf16[384,768]{1,0:T(8,128)(2,1)}, u32[]{:S(2)}, u32[]{:S(2)}) %collective-permute-start.4) | collective-permute-done | bytes 589856 | tf_op jit(solution)/shard_map/ppermute | solution.py:387
  41.6 1.1 %copy-done.2 = f32[512,256]{1,0:T(8,128)S(1)} copy-done((f32[512,256]{1,0:T(8,128)S(1)}, f32[512,256]{1,0:T(8,128)}, u32[]{:S(2)}) %copy-start.2) | copy-done | bytes 524312
  42.7 1.0 copy-done.4
  43.7 3.2 %project_other.1.qb_hbm = bf16[3,512,256]{2,1,0:T(8,128)(2,1)S(1)} custom-call(s32[4]{0:T(128)S(1)} %pad_add_fusion.1.order, bf16[512,1536]{1,0:T(8,128)(2,1)S(1)} %get-tuple-element.32.normed, bf16[384,768]{1,0:T(8,128)(2,1)S(1)} %collective-permute-done.w0, bf16[384,768]{1,0:T(8,128)(2,1)S(1)} %collective-permute-done.2.w1, ...), custom_call_target="tpu_custom_call" | custom-call | flops 1207959552 | bytes 6291456 | tf_op jit(solution)/shard_map/project_other/pallas_call | solution.py:115
  46.9 0.0 copy-start
  47.0 1.0 copy-done
  47.9 6.6 %collective-permute-done.1.wob0 = bf16[384,1536]{1,0:T(8,128)(2,1)} collective-permute-done((bf16[384,1536]{1,0:T(8,128)(2,1)}, bf16[384,1536]{1,0:T(8,128)(2,1)}, u32[]{:S(2)}, u32[]{:S(2)}) %collective-permute-start.1) | collective-permute-done | bytes 1179680 | tf_op jit(solution)/shard_map/ppermute | solution.py:373
  54.5 0.0 collective-permute-start.5
  54.5 0.0 copy-done.13
  54.5 0.6 collective-permute-start.6
  55.2 0.5 and_select_fusion.1.idx
  55.7 1.4 %collective-permute-start.8 = (bf16[512,512]{1,0:T(8,128)(2,1)}, bf16[512,512]{1,0:T(8,128)(2,1)S(1)}, u32[]{:S(2)}, u32[]{:S(2)}) collective-permute-start(bf16[512,512]{1,0:T(8,128)(2,1)} %get-tuple-element.43.kv_own), channel_id=1, source_target_pairs={{0,1},{1,0},{2,3},{3,2},{4,5},{5,4},{6,7},{7,6},{8,9},{9,8},{10,11... | collective-permute-start | bytes 1572872 | tf_op jit(solution)/shard_map/ppermute | solution.py:394
  57.1 1.0 collective-permute-done.6
  58.1 0.5 and_select_fusion.idx
  58.6 0.0 collective-permute-done.5.wob1
  58.6 0.2 all-gather.2.cloned.1.call-done.pool
  58.8 2.6 %pick_pages.2 = (bf16[8,64,256]{2,1,0:T(8,128)(2,1)}, bf16[8,64,256]{2,1,0:T(8,128)(2,1)}) custom-call(s32[8]{0:T(128)} %and_select_fusion.idx, bf16[64,64,512]{2,1,0:T(8,128)(2,1)} %all-gather.2.cloned.1.call-done.pool), custom_call_target="tpu_custom_call" | custom-call | bytes 1048576 | tf_op jit(solution)/shard_map/pick_pages/pallas_call | solution.py:145
  61.5 0.0 copy-done.14
  61.5 1.5 %collective-permute-start.10 = (bf16[8,64,256]{2,1,0:T(8,128)(2,1)}, bf16[8,64,256]{2,1,0:T(8,128)(2,1)S(1)}, u32[]{:S(2)}, u32[]{:S(2)}) collective-permute-start(bf16[8,64,256]{2,1,0:T(8,128)(2,1)} %get-tuple-element.49), channel_id=1, source_target_pairs={{0,16},{16,0},{1,17},{17,1},{2,18},{18,2},{3,19},{19,3},{4,20},{20... | collective-permute-start | bytes 786440 | tf_op jit(solution)/shard_map/ppermute | solution.py:404
  63.0 0.6 collective-permute-start.7
  63.7 2.6 %pick_pages.3 = (bf16[8,64,256]{2,1,0:T(8,128)(2,1)}, bf16[8,64,256]{2,1,0:T(8,128)(2,1)}) custom-call(s32[8]{0:T(128)} %and_select_fusion.1.idx, bf16[64,64,512]{2,1,0:T(8,128)(2,1)} %all-gather.2.cloned.1.call-done.pool), custom_call_target="tpu_custom_call" | custom-call | bytes 1048576 | tf_op jit(solution)/shard_map/pick_pages/pallas_call | solution.py:145
  66.3 4.6 %collective-permute-done.10 = bf16[8,64,256]{2,1,0:T(8,128)(2,1)S(1)} collective-permute-done((bf16[8,64,256]{2,1,0:T(8,128)(2,1)}, bf16[8,64,256]{2,1,0:T(8,128)(2,1)S(1)}, u32[]{:S(2)}, u32[]{:S(2)}) %collective-permute-start.10) | collective-permute-done | bytes 262176 | tf_op jit(solution)/shard_map/ppermute | solution.py:404
  70.9 0.0 copy-start.10
  70.9 1.5 %collective-permute-start.11 = (bf16[8,64,256]{2,1,0:T(8,128)(2,1)S(1)}, bf16[8,64,256]{2,1,0:T(8,128)(2,1)S(1)}, u32[]{:S(2)}, u32[]{:S(2)}) collective-permute-start(bf16[8,64,256]{2,1,0:T(8,128)(2,1)S(1)} %broadcast_select_fusion.v_mine), channel_id=1, source_target_pairs={{0,1},{1,0},{2,3},{3,2},{4,5},{5,4},{6,7},{7,6},{8,9},{9,8},{10,11... | collective-permute-start | bytes 786440 | tf_op jit(solution)/shard_map/ppermute | solution.py:410
  72.5 0.0 collective-permute-done.8.kv_peer
  72.5 3.3 %collective-permute-done.7 = bf16[8,64,256]{2,1,0:T(8,128)(2,1)S(1)} collective-permute-done((bf16[8,64,256]{2,1,0:T(8,128)(2,1)}, bf16[8,64,256]{2,1,0:T(8,128)(2,1)S(1)}, u32[]{:S(2)}, u32[]{:S(2)}) %collective-permute-start.7) | collective-permute-done | bytes 262176 | tf_op jit(solution)/shard_map/ppermute | solution.py:403
  75.9 0.0 copy-start.11
  75.9 1.5 %collective-permute-start.9 = (bf16[8,64,256]{2,1,0:T(8,128)(2,1)S(1)}, bf16[8,64,256]{2,1,0:T(8,128)(2,1)S(1)}, u32[]{:S(2)}, u32[]{:S(2)}) collective-permute-start(bf16[8,64,256]{2,1,0:T(8,128)(2,1)S(1)} %broadcast_select_fusion.1.k_mine), channel_id=1, source_target_pairs={{0,1},{1,0},{2,3},{3,2},{4,5},{5,4},{6,7},{7,6},{8,9},{9,8},{10,11... | collective-permute-start | bytes 786440 | tf_op jit(solution)/shard_map/ppermute | solution.py:408
  78.1 0.7 pad_add_fusion.info
  78.7 0.0 collective-permute-done.11.v_peer
  78.7 4.8 %collective-permute-done.9.k_peer = bf16[8,64,256]{2,1,0:T(8,128)(2,1)S(1)} collective-permute-done((bf16[8,64,256]{2,1,0:T(8,128)(2,1)S(1)}, bf16[8,64,256]{2,1,0:T(8,128)(2,1)S(1)}, u32[]{:S(2)}, u32[]{:S(2)}) %collective-permute-start.9) | collective-permute-done | bytes 262176 | tf_op jit(solution)/shard_map/ppermute | solution.py:408
  83.6 0.0 copy-done.10
  83.6 0.0 copy-done.15
  83.6 0.0 copy-done.11
  83.6 0.0 copy-done.16
  83.6 0.7 copy-done.17
  84.3 13.5 %attend_and_out.1 = bf16[512,1536]{1,0:T(8,128)(2,1)} custom-call(s32[3]{0:T(128)} %pad_add_fusion.info, bf16[3,512,256]{2,1,0:T(8,128)(2,1)} %copy-done.8, bf16[3,512,256]{2,1,0:T(8,128)(2,1)} %copy-done, bf16[8,64,256]{2,1,0:T(8,128)(2,1)} %copy-done.11, bf16[8,64,256]{2,1,0:T(8,128)(2,1)} %copy-done.17, bf16[8,64,256]{2,1,0:T(8,128)(2,1)} %copy-done.10, ...), custom_call_target="tpu_custom_call" | custom-call | flops 6442450944 | bytes 12582912 | tf_op jit(solution)/shard_map/attend_and_out/pallas_call | solution.py:323
  (18 shorter events, 0.1 us)
Async XLA Ops:
  6.5 5.5 %copy-start.12 = (f32[1536]{0:T(1024)S(1)}, f32[1536]{0:T(1024)}, u32[]{:S(2)}) copy-start(f32[1536]{0:T(1024)} %param.10) | copy-start | bytes 18436
  6.5 52.3 %all-gather.2.cloned.1.call-start = ((), (), s32[]{:S(2)}) async-start(), calls=%async_computation | async-start | bytes 4718592 | tf_op jit(solution)/shard_map/all_gather | solution.py:369
  8.4 16.4 %collective-permute-start = (bf16[384,768]{1,0:T(8,128)(2,1)S(1)}, bf16[384,768]{1,0:T(8,128)(2,1)S(1)}, u32[]{:S(2)}, u32[]{:S(2)}) collective-permute-start(bf16[384,768]{1,0:T(8,128)(2,1)S(1)} %constant_dynamic-slice_fusion.1), channel_id=1, source_target_pairs={{0,1},{1,0},{2,3},{3,2},{4,5},{5,4},{6,7},{7,6},{8,9},{9,8},{10,11... | collective-permute-start | bytes 1769480 | tf_op jit(solution)/shard_map/ppermute | solution.py:373
  12.5 1.7 %copy-start.5 = (bf16[1536,768]{1,0:T(8,128)(2,1)S(1)}, bf16[1536,768]{1,0:T(8,128)(2,1)}, u32[]{:S(2)}) copy-start(bf16[1536,768]{1,0:T(8,128)(2,1)} %wq.1) | copy-start | bytes 7077892
  14.2 1.4 %copy-start.6 = (bf16[1,512,1536]{2,1,0:T(8,128)(2,1)S(1)}, bf16[1,512,1536]{2,1,0:T(8,128)(2,1)}, u32[]{:S(2)}) copy-start(bf16[1,512,1536]{2,1,0:T(8,128)(2,1)} %param.9) | copy-start | bytes 4718596
  15.6 1.4 %copy-start.7 = (bf16[1536,512]{1,0:T(8,128)(2,1)S(1)}, bf16[1536,512]{1,0:T(8,128)(2,1)}, u32[]{:S(2)}) copy-start(bf16[1536,512]{1,0:T(8,128)(2,1)} %wkv.1) | copy-start | bytes 4718596
  17.0 9.5 %copy-start.9 = (bf16[768,1536]{1,0:T(8,128)(2,1)S(1)}, bf16[768,1536]{1,0:T(8,128)(2,1)}, u32[]{:S(2)}) copy-start(bf16[768,1536]{1,0:T(8,128)(2,1)} %woa.1) | copy-start | bytes 7077892
  20.1 19.3 %copy-start.1 = (f32[512,256]{1,0:T(8,128)}, f32[512,256]{1,0:T(8,128)S(1)}, u32[]{:S(2)}) copy-start(f32[512,256]{1,0:T(8,128)S(1)} %get-tuple-element.34.cos) | copy-start | bytes 1572868
  20.1 19.3 %copy-start.3 = (f32[512,256]{1,0:T(8,128)}, f32[512,256]{1,0:T(8,128)S(1)}, u32[]{:S(2)}) copy-start(f32[512,256]{1,0:T(8,128)S(1)} %get-tuple-element.35.sin) | copy-start | bytes 1572868
  20.1 19.3 %copy-start.8 = (bf16[3,512,256]{2,1,0:T(8,128)(2,1)}, bf16[3,512,256]{2,1,0:T(8,128)(2,1)S(1)}, u32[]{:S(2)}) copy-start(bf16[3,512,256]{2,1,0:T(8,128)(2,1)S(1)} %get-tuple-element.29.qa_hbm) | copy-start | bytes 2359300
  24.8 14.6 %collective-permute-start.2 = (bf16[384,768]{1,0:T(8,128)(2,1)S(1)}, bf16[384,768]{1,0:T(8,128)(2,1)S(1)}, u32[]{:S(2)}, u32[]{:S(2)}) collective-permute-start(bf16[384,768]{1,0:T(8,128)(2,1)S(1)} %collective-permute-done.w0), channel_id=1, source_target_pairs={{0,16},{16,0},{1,17},{17,1},{2,18},{18,2},{3,19},{19,3},{4,20},{20... | collective-permute-start | bytes 1769480 | tf_op jit(solution)/shard_map/ppermute | solution.py:383
  27.6 27.0 %collective-permute-start.1 = (bf16[384,1536]{1,0:T(8,128)(2,1)}, bf16[384,1536]{1,0:T(8,128)(2,1)}, u32[]{:S(2)}, u32[]{:S(2)}) collective-permute-start(bf16[384,1536]{1,0:T(8,128)(2,1)} %constant_dynamic-slice_fusion), channel_id=1, source_target_pairs={{0,1},{1,0},{2,3},{3,2},{4,5},{5,4},{6,7},{7,6},{8,9},{9,8},{10,11... | collective-permute-start | bytes 3538952 | tf_op jit(solution)/shard_map/ppermute | solution.py:373
  29.1 10.5 %collective-permute-start.3 = (bf16[384,768]{1,0:T(8,128)(2,1)S(1)}, bf16[384,768]{1,0:T(8,128)(2,1)S(1)}, u32[]{:S(2)}, u32[]{:S(2)}) collective-permute-start(bf16[384,768]{1,0:T(8,128)(2,1)S(1)} %collective-permute-done.w0), channel_id=1, source_target_pairs={{0,2},{2,0},{4,6},{6,4},{8,10},{10,8},{12,14},{14,12},{1,3},{3,1},... | collective-permute-start | bytes 1769480 | tf_op jit(solution)/shard_map/ppermute | solution.py:387
  39.4 2.2 %collective-permute-start.4 = (bf16[384,768]{1,0:T(8,128)(2,1)S(1)}, bf16[384,768]{1,0:T(8,128)(2,1)}, u32[]{:S(2)}, u32[]{:S(2)}) collective-permute-start(bf16[384,768]{1,0:T(8,128)(2,1)S(1)} %collective-permute-done.2.w1), channel_id=1, source_target_pairs={{0,2},{2,0},{4,6},{6,4},{8,10},{10,8},{12,14},{14,12},{1,3},{3,1},... | collective-permute-start | bytes 1769480 | tf_op jit(solution)/shard_map/ppermute | solution.py:387
  41.6 1.1 %copy-start.2 = (f32[512,256]{1,0:T(8,128)S(1)}, f32[512,256]{1,0:T(8,128)}, u32[]{:S(2)}) copy-start(f32[512,256]{1,0:T(8,128)} %copy-done.1) | copy-start | bytes 1572868
  42.6 1.0 copy-start.4
  43.7 10.8 %copy-start.13 = (s32[1,8]{1,0:T(1,128)S(1)}, s32[1,8]{1,0:T(1,128)}, u32[]{:S(2)}) copy-start(s32[1,8]{1,0:T(1,128)} %param.15) | copy-start | bytes 100
  46.9 1.0 copy-start
  54.5 4.1 %collective-permute-start.5 = (bf16[384,1536]{1,0:T(8,128)(2,1)}, bf16[384,1536]{1,0:T(8,128)(2,1)S(1)}, u32[]{:S(2)}, u32[]{:S(2)}) collective-permute-start(bf16[384,1536]{1,0:T(8,128)(2,1)} %collective-permute-done.1.wob0), channel_id=1, source_target_pairs={{0,2},{2,0},{4,6},{6,4},{8,10},{10,8},{12,14},{14,12},{1,3},{3,1},... | collective-permute-start | bytes 3538952 | tf_op jit(solution)/shard_map/ppermute | solution.py:393
  54.5 3.5 %collective-permute-start.6 = (s32[8]{0:T(128)S(1)}, s32[8]{0:T(128)S(1)}, u32[]{:S(2)}, u32[]{:S(2)}) collective-permute-start(s32[8]{0:T(128)S(1)} %bitcast.15), channel_id=1, source_target_pairs={{0,16},{16,0},{1,17},{17,1},{2,18},{18,2},{3,19},{19,3},{4,20},{20... | collective-permute-start | bytes 104 | tf_op jit(solution)/shard_map/ppermute | solution.py:386
  55.7 16.8 %collective-permute-start.8 = (bf16[512,512]{1,0:T(8,128)(2,1)}, bf16[512,512]{1,0:T(8,128)(2,1)S(1)}, u32[]{:S(2)}, u32[]{:S(2)}) collective-permute-start(bf16[512,512]{1,0:T(8,128)(2,1)} %get-tuple-element.43.kv_own), channel_id=1, source_target_pairs={{0,1},{1,0},{2,3},{3,2},{4,5},{5,4},{6,7},{7,6},{8,9},{9,8},{10,11... | collective-permute-start | bytes 1572872 | tf_op jit(solution)/shard_map/ppermute | solution.py:394
  58.6 2.9 %copy-start.14 = (bf16[384,1536]{1,0:T(8,128)(2,1)}, bf16[384,1536]{1,0:T(8,128)(2,1)S(1)}, u32[]{:S(2)}) copy-start(bf16[384,1536]{1,0:T(8,128)(2,1)S(1)} %collective-permute-done.5.wob1) | copy-start | bytes 3538948
  61.5 9.4 %collective-permute-start.10 = (bf16[8,64,256]{2,1,0:T(8,128)(2,1)}, bf16[8,64,256]{2,1,0:T(8,128)(2,1)S(1)}, u32[]{:S(2)}, u32[]{:S(2)}) collective-permute-start(bf16[8,64,256]{2,1,0:T(8,128)(2,1)} %get-tuple-element.49), channel_id=1, source_target_pairs={{0,16},{16,0},{1,17},{17,1},{2,18},{18,2},{3,19},{19,3},{4,20},{20... | collective-permute-start | bytes 786440 | tf_op jit(solution)/shard_map/ppermute | solution.py:404
  63.0 12.8 %collective-permute-start.7 = (bf16[8,64,256]{2,1,0:T(8,128)(2,1)}, bf16[8,64,256]{2,1,0:T(8,128)(2,1)S(1)}, u32[]{:S(2)}, u32[]{:S(2)}) collective-permute-start(bf16[8,64,256]{2,1,0:T(8,128)(2,1)} %get-tuple-element.42), channel_id=1, source_target_pairs={{0,16},{16,0},{1,17},{17,1},{2,18},{18,2},{3,19},{19,3},{4,20},{20... | collective-permute-start | bytes 786440 | tf_op jit(solution)/shard_map/ppermute | solution.py:403
  70.9 12.6 %copy-start.10 = (bf16[8,64,256]{2,1,0:T(8,128)(2,1)}, bf16[8,64,256]{2,1,0:T(8,128)(2,1)S(1)}, u32[]{:S(2)}) copy-start(bf16[8,64,256]{2,1,0:T(8,128)(2,1)S(1)} %broadcast_select_fusion.v_mine) | copy-start | bytes 786436
  70.9 7.8 %collective-permute-start.11 = (bf16[8,64,256]{2,1,0:T(8,128)(2,1)S(1)}, bf16[8,64,256]{2,1,0:T(8,128)(2,1)S(1)}, u32[]{:S(2)}, u32[]{:S(2)}) collective-permute-start(bf16[8,64,256]{2,1,0:T(8,128)(2,1)S(1)} %broadcast_select_fusion.v_mine), channel_id=1, source_target_pairs={{0,1},{1,0},{2,3},{3,2},{4,5},{5,4},{6,7},{7,6},{8,9},{9,8},{10,11... | collective-permute-start | bytes 786440 | tf_op jit(solution)/shard_map/ppermute | solution.py:410
  72.5 11.1 %copy-start.15 = (bf16[512,512]{1,0:T(8,128)(2,1)}, bf16[512,512]{1,0:T(8,128)(2,1)S(1)}, u32[]{:S(2)}) copy-start(bf16[512,512]{1,0:T(8,128)(2,1)S(1)} %collective-permute-done.8.kv_peer) | copy-start | bytes 1572868
  75.9 7.7 %copy-start.11 = (bf16[8,64,256]{2,1,0:T(8,128)(2,1)}, bf16[8,64,256]{2,1,0:T(8,128)(2,1)S(1)}, u32[]{:S(2)}) copy-start(bf16[8,64,256]{2,1,0:T(8,128)(2,1)S(1)} %broadcast_select_fusion.1.k_mine) | copy-start | bytes 786436
  75.9 7.7 %collective-permute-start.9 = (bf16[8,64,256]{2,1,0:T(8,128)(2,1)S(1)}, bf16[8,64,256]{2,1,0:T(8,128)(2,1)S(1)}, u32[]{:S(2)}, u32[]{:S(2)}) collective-permute-start(bf16[8,64,256]{2,1,0:T(8,128)(2,1)S(1)} %broadcast_select_fusion.1.k_mine), channel_id=1, source_target_pairs={{0,1},{1,0},{2,3},{3,2},{4,5},{5,4},{6,7},{7,6},{8,9},{9,8},{10,11... | collective-permute-start | bytes 786440 | tf_op jit(solution)/shard_map/ppermute | solution.py:408
  78.7 4.8 %copy-start.16 = (bf16[8,64,256]{2,1,0:T(8,128)(2,1)}, bf16[8,64,256]{2,1,0:T(8,128)(2,1)S(1)}, u32[]{:S(2)}) copy-start(bf16[8,64,256]{2,1,0:T(8,128)(2,1)S(1)} %collective-permute-done.11.v_peer) | copy-start | bytes 786436
  83.6 0.7 copy-start.17
Sparse Core Ops, SparseCore 0:
  9.0 49.8 all-gather.1

commit v9 on v7

--- a/solution.py
+++ b/solution.py
@@ -185,6 +185,7 @@
     sbuf,
     pbuf,
     sums,
+    tops,
     ksem,
     vsem,
     wsem,
@@ -234,43 +235,44 @@
         pltpu.make_async_copy(wob0, wb.at[pl.ds(core * deep, deep), :], wsem.at[1]),
         pltpu.make_async_copy(wob1, wb.at[pl.ds((1 - core) * deep, deep), :], wsem.at[2]),
     ]
-    for c in weights:
-        c.start()
-
     tile = min(256, rows)
     span = window + tile
-    band = min(32, tile)
-    gap = lax.broadcasted_iota(jnp.int32, (band, tile), 1) - lax.broadcasted_iota(
-        jnp.int32, (band, tile), 0
+    lanes = 128
+    gap = lax.broadcasted_iota(jnp.int32, (tile, tile), 1) - lax.broadcasted_iota(
+        jnp.int32, (tile, tile), 0
     )
     order = [(i, n, h) for i in range(rows // tile) for n in range(2) for h in range(nheads)]
 
     def score(m):
         i, n, h = order[m]
         q = (qa, qb)[n][pl.ds(i * tile, tile), h * head_size : (h + 1) * head_size]
+        top = None
         for lo in range(0, span, tile):
-            sbuf[m % 2, :, lo : lo + tile] = lax.dot_general(
+            s = lax.dot_general(
                 q,
                 keys[pl.ds(i * tile + lo, tile), :],
                 (((1,), (1,)), ((), ())),
                 preferred_element_type=F32,
             )
+            if lo == 0:
+                s = jnp.where(gap >= 1, s, MASKED)
+            if lo + tile == span:
+                s = jnp.where(gap <= 0, s, MASKED)
+            sbuf[m % 2, :, lo : lo + tile] = s
+            for at in range(0, tile, lanes):
+                piece = s[:, at : at + lanes]
+                top = piece if top is None else jnp.maximum(top, piece)
+        top = jnp.max(top, axis=-1, keepdims=True)
+        tops[m % 2] = jnp.broadcast_to(top, (tile, lanes))
 
     def soften(m):
-        for lo in range(0, tile, band):
-            at = pl.ds(lo, band)
-            s = jnp.concatenate(
-                [
-                    jnp.where(gap >= lo + 1, sbuf[m % 2, at, :tile], MASKED),
-                    sbuf[m % 2, at, tile : span - tile],
-                    jnp.where(gap <= lo, sbuf[m % 2, at, span - tile :], MASKED),
-                ],
-                axis=1,
-            )
-            e = jnp.exp2(s - jnp.max(s, axis=-1, keepdims=True))
-            total = jnp.sum(e, axis=-1, keepdims=True)
-            pbuf[m % 2, at, :] = e.astype(BF16)
-            sums[m % 2, at, :] = jnp.broadcast_to(1.0 / total, (band, 128))
+        total = None
+        for lo in range(0, span, lanes):
+            e = jnp.exp2(sbuf[m % 2, :, lo : lo + lanes] - tops[m % 2])
+            pbuf[m % 2, :, lo : lo + lanes] = e.astype(BF16)
+            total = e if total is None else total + e
+        total = jnp.sum(total, axis=-1, keepdims=True)
+        sums[m % 2] = jnp.broadcast_to(1.0 / total, (tile, lanes))
 
     def combine(m):
         i, n, h = order[m]
@@ -302,6 +304,8 @@
     queries[0].wait()
     finish(keys, ksem)
     queries[1].wait()
+    for c in weights:
+        c.start()
     score(0)
     ready = []
     for m in range(len(order)):
@@ -362,6 +366,7 @@
             pltpu.VMEM((2, tile, window + tile), F32),
             pltpu.VMEM((2, tile, window + tile), BF16),
             pltpu.VMEM((2, tile, 128), F32),
+            pltpu.VMEM((2, tile, 128), F32),
             pltpu.SemaphoreType.DMA,
             pltpu.SemaphoreType.DMA,
             pltpu.SemaphoreType.DMA((5,)),

time: 105 us -> 106 us (level)
  other arithmetic: 4.07 us -> 2.17 us
  waiting for transfers between devices: 37.4 us -> 39.3 us
  transfers between devices with their start and end apart: 13 -> 13, of which waited for: 9 -> 10; matrix products, arithmetic and copies ran while one was open for 6% -> 4% of each run, Pallas kernels for 11% -> 11%
where the time goes in v9:
time: 106 us; the launch traced here: 105 us
  waiting for transfers between devices  39.3 us (37%)
  Pallas kernels  24.3 us (23%)
  between operations  15.1 us (14%)
  starting transfers between devices  13.6 us (13%)
  local copies, waits for them, and re-layouts  10.5 us (10%)
  other arithmetic  2.17 us (2%)
    pallas_call x1, Pallas kernels, attend_pages(): pl.pallas_call(functools.partial(attend_kernel, head_size), out_shape=jax...  12.8 us
    ppermute x2, waiting for transfers between devices, peer_rows(): lax.ppermute(lax.dynamic_slice_in_dim(w, at * deep, deep, 0), 'tensor', s...  11.3 us
    ppermute x1, waiting for transfers between devices, pair_shards(): b = lax.ppermute(a, 'rep', swap)  10.3 us
    unnamed x36, local copies, waits for them, and re-layouts  8.26 us
    ppermute x1, waiting for transfers between devices, pair_shards(): k_peer = lax.ppermute(k_mine, 'tensor', swap)  5.62 us
    pallas_call x2, Pallas kernels, pick(): pl.pallas_call(pick_kernel, out_shape=(half, half), in_specs=[spec(pltpu....  5.21 us
    ppermute x1, waiting for transfers between devices, pair_shards(): v_came = lax.ppermute(v_sent, 'rep', swap)  4.57 us
    ppermute x2, starting transfers between devices, peer_rows(): lax.ppermute(lax.dynamic_slice_in_dim(w, at * deep, deep, 0), 'tensor', s...  4.55 us
  transfers between devices with their start and end apart: 13, of which 10 were waited for; matrix products, arithmetic and copies ran while one was open for 4% of the time, Pallas kernels for 11%

profile of v9, /device:TPU:0, one launch (start us, length us, event | category | flops | bytes accessed | tf_op | source)
XLA Modules:
  0.0 104.9 jit_solution(12272169347691603481)
XLA Ops:
  6.5 0.0 all-gather.2.cloned.1.call-start
  6.5 0.7 all-gather.2.cloned.1.call-update
  7.3 1.1 %constant_dynamic-slice_fusion.1 = bf16[384,768]{1,0:T(8,128)(2,1)S(1)} fusion(bf16[1536,768]{1,0:T(8,128)(2,1)} %wq.1, s32[]{:T(128)S(6)} %select_n.70), kind=kLoop, calls=%fused_computation.31 | loop fusion | bytes 1179652 | tf_op jit(solution)/shard_map/dynamic_slice | solution.py:400
  8.4 3.0 %collective-permute-start = (bf16[384,768]{1,0:T(8,128)(2,1)S(1)}, bf16[384,768]{1,0:T(8,128)(2,1)S(1)}, u32[]{:S(2)}, u32[]{:S(2)}) collective-permute-start(bf16[384,768]{1,0:T(8,128)(2,1)S(1)} %constant_dynamic-slice_fusion.1), channel_id=1, source_target_pairs={{0,1},{1,0},{2,3},{3,2},{4,5},{5,4},{6,7},{7,6},{8,9},{9,8},{10,11... | collective-permute-start | bytes 1769480 | tf_op jit(solution)/shard_map/ppermute | solution.py:400
  12.1 0.0 copy-done.12
  12.1 0.1 pad_maximum_fusion
  12.2 0.3 fusion
  12.5 0.0 copy-start.5
  12.5 1.7 %copy-done.5 = bf16[1536,768]{1,0:T(8,128)(2,1)S(1)} copy-done((bf16[1536,768]{1,0:T(8,128)(2,1)S(1)}, bf16[1536,768]{1,0:T(8,128)(2,1)}, u32[]{:S(2)}) %copy-start.5) | copy-done | bytes 2359320
  14.2 0.0 copy-start.6
  14.2 1.4 %copy-done.6 = bf16[1,512,1536]{2,1,0:T(8,128)(2,1)S(1)} copy-done((bf16[1,512,1536]{2,1,0:T(8,128)(2,1)S(1)}, bf16[1,512,1536]{2,1,0:T(8,128)(2,1)}, u32[]{:S(2)}) %copy-start.6) | copy-done | bytes 1572888
  15.6 0.0 copy-start.7
  15.6 1.4 %copy-done.7 = bf16[1536,512]{1,0:T(8,128)(2,1)S(1)} copy-done((bf16[1536,512]{1,0:T(8,128)(2,1)S(1)}, bf16[1536,512]{1,0:T(8,128)(2,1)}, u32[]{:S(2)}) %copy-start.7) | copy-done | bytes 1572888
  17.0 3.1 %project_own.1 = (bf16[512,1536]{1,0:T(8,128)(2,1)S(1)}, bf16[512,768]{1,0:T(8,128)(2,1)S(1)}, bf16[512,512]{1,0:T(8,128)(2,1)}, f32[512,256]{1,0:T(8,128)S(1)}, f32[512,256]{1,0:T(8,128)S(1)}) custom-call(bf16[512,1536]{1,0:T(8,128)(2,1)S(1)} %bitcast.14, f32[1,1536]{1,0:T(1,128)S(1)} %reshape.34.gain, bf16[1536,768]{1,0:T(8,128)(2,1)S(1)} %copy-done.5, ...), custom_call_target="tpu_custom_call" | custom-call | flops 2013265920 | bytes 10485760 | tf_op jit(solution)/shard_map/project_own/pallas_call | solution.py:79
  20.1 4.7 %collective-permute-done.w0 = bf16[384,768]{1,0:T(8,128)(2,1)S(1)} collective-permute-done((bf16[384,768]{1,0:T(8,128)(2,1)S(1)}, bf16[384,768]{1,0:T(8,128)(2,1)S(1)}, u32[]{:S(2)}, u32[]{:S(2)}) %collective-permute-start) | collective-permute-done | bytes 589856 | tf_op jit(solution)/shard_map/ppermute | solution.py:400
  24.8 1.7 %collective-permute-start.2 = (bf16[384,768]{1,0:T(8,128)(2,1)S(1)}, bf16[384,768]{1,0:T(8,128)(2,1)S(1)}, u32[]{:S(2)}, u32[]{:S(2)}) collective-permute-start(bf16[384,768]{1,0:T(8,128)(2,1)S(1)} %collective-permute-done.w0), channel_id=1, source_target_pairs={{0,16},{16,0},{1,17},{17,1},{2,18},{18,2},{3,19},{19,3},{4,20},{20... | collective-permute-start | bytes 1769480 | tf_op jit(solution)/shard_map/ppermute | solution.py:410
  26.5 0.0 copy-done.9
  26.5 1.1 %constant_dynamic-slice_fusion = bf16[384,1536]{1,0:T(8,128)(2,1)} fusion(bf16[768,1536]{1,0:T(8,128)(2,1)S(1)} %copy-done.9, s32[]{:T(128)S(6)} %select_n.71), kind=kLoop, calls=%fused_computation.30 | loop fusion | bytes 2359300 | tf_op jit(solution)/shard_map/dynamic_slice | solution.py:400
  27.6 1.5 %collective-permute-start.1 = (bf16[384,1536]{1,0:T(8,128)(2,1)}, bf16[384,1536]{1,0:T(8,128)(2,1)}, u32[]{:S(2)}, u32[]{:S(2)}) collective-permute-start(bf16[384,1536]{1,0:T(8,128)(2,1)} %constant_dynamic-slice_fusion), channel_id=1, source_target_pairs={{0,1},{1,0},{2,3},{3,2},{4,5},{5,4},{6,7},{7,6},{8,9},{9,8},{10,11... | collective-permute-start | bytes 3538952 | tf_op jit(solution)/shard_map/ppermute | solution.py:400
  29.1 0.0 collective-permute-start.3
  29.1 10.3 %collective-permute-done.2.w1 = bf16[384,768]{1,0:T(8,128)(2,1)S(1)} collective-permute-done((bf16[384,768]{1,0:T(8,128)(2,1)S(1)}, bf16[384,768]{1,0:T(8,128)(2,1)S(1)}, u32[]{:S(2)}, u32[]{:S(2)}) %collective-permute-start.2) | collective-permute-done | bytes 589856 | tf_op jit(solution)/shard_map/ppermute | solution.py:410
  39.4 0.0 copy-done.1
  39.4 0.0 copy-done.3
  39.4 0.0 copy-done.8
  39.4 0.1 collective-permute-start.4
  39.5 0.1 pad_add_fusion.1.order
  39.6 0.0 collective-permute-done.3.w2
  39.6 2.0 %collective-permute-done.4.w3 = bf16[384,768]{1,0:T(8,128)(2,1)} collective-permute-done((bf16[384,768]{1,0:T(8,128)(2,1)S(1)}, bf16[384,768]{1,0:T(8,128)(2,1)}, u32[]{:S(2)}, u32[]{:S(2)}) %collective-permute-start.4) | collective-permute-done | bytes 589856 | tf_op jit(solution)/shard_map/ppermute | solution.py:414
  41.6 1.1 %copy-done.2 = f32[512,256]{1,0:T(8,128)S(1)} copy-done((f32[512,256]{1,0:T(8,128)S(1)}, f32[512,256]{1,0:T(8,128)}, u32[]{:S(2)}) %copy-start.2) | copy-done | bytes 524312
  42.7 1.0 copy-done.4
  43.7 3.2 %project_other.1.qb_hbm = bf16[512,768]{1,0:T(8,128)(2,1)S(1)} custom-call(s32[4]{0:T(128)S(1)} %pad_add_fusion.1.order, bf16[512,1536]{1,0:T(8,128)(2,1)S(1)} %get-tuple-element.32.normed, bf16[384,768]{1,0:T(8,128)(2,1)S(1)} %collective-permute-done.w0, bf16[384,768]{1,0:T(8,128)(2,1)S(1)} %collective-permute-done.2.w1, ...), custom_call_target="tpu_custom_call" | custom-call | flops 1207959552 | bytes 6291456 | tf_op jit(solution)/shard_map/project_other/pallas_call | solution.py:120
  46.9 0.0 copy-start
  46.9 1.0 copy-done
  47.9 6.6 %collective-permute-done.1.wob0 = bf16[384,1536]{1,0:T(8,128)(2,1)} collective-permute-done((bf16[384,1536]{1,0:T(8,128)(2,1)}, bf16[384,1536]{1,0:T(8,128)(2,1)}, u32[]{:S(2)}, u32[]{:S(2)}) %collective-permute-start.1) | collective-permute-done | bytes 1179680 | tf_op jit(solution)/shard_map/ppermute | solution.py:400
  54.5 0.0 collective-permute-start.5
  54.5 0.0 copy-done.13
  54.5 0.6 collective-permute-start.6
  55.2 0.5 and_select_fusion.1.idx
  55.7 1.4 %collective-permute-start.8 = (bf16[512,512]{1,0:T(8,128)(2,1)}, bf16[512,512]{1,0:T(8,128)(2,1)S(1)}, u32[]{:S(2)}, u32[]{:S(2)}) collective-permute-start(bf16[512,512]{1,0:T(8,128)(2,1)} %get-tuple-element.43.kv_own), channel_id=1, source_target_pairs={{0,1},{1,0},{2,3},{3,2},{4,5},{5,4},{6,7},{7,6},{8,9},{9,8},{10,11... | collective-permute-start | bytes 1572872 | tf_op jit(solution)/shard_map/ppermute | solution.py:421
  57.1 1.0 collective-permute-done.6
  58.1 0.5 and_select_fusion.idx
  58.6 0.0 collective-permute-done.5.wob1
  58.6 0.2 all-gather.2.cloned.1.call-done.pool
  58.8 2.6 %pick_pages.2 = (bf16[8,64,256]{2,1,0:T(8,128)(2,1)}, bf16[8,64,256]{2,1,0:T(8,128)(2,1)}) custom-call(s32[8]{0:T(128)} %and_select_fusion.idx, bf16[64,64,512]{2,1,0:T(8,128)(2,1)} %all-gather.2.cloned.1.call-done.pool), custom_call_target="tpu_custom_call" | custom-call | bytes 1048576 | tf_op jit(solution)/shard_map/pick_pages/pallas_call | solution.py:150
  61.5 0.0 copy-done.14
  61.5 1.5 %collective-permute-start.10 = (bf16[8,64,256]{2,1,0:T(8,128)(2,1)}, bf16[8,64,256]{2,1,0:T(8,128)(2,1)S(1)}, u32[]{:S(2)}, u32[]{:S(2)}) collective-permute-start(bf16[8,64,256]{2,1,0:T(8,128)(2,1)} %get-tuple-element.49), channel_id=1, source_target_pairs={{0,16},{16,0},{1,17},{17,1},{2,18},{18,2},{3,19},{19,3},{4,20},{20... | collective-permute-start | bytes 786440 | tf_op jit(solution)/shard_map/ppermute | solution.py:431
  63.0 0.6 collective-permute-start.7
  63.7 2.6 %pick_pages.3 = (bf16[8,64,256]{2,1,0:T(8,128)(2,1)}, bf16[8,64,256]{2,1,0:T(8,128)(2,1)}) custom-call(s32[8]{0:T(128)} %and_select_fusion.1.idx, bf16[64,64,512]{2,1,0:T(8,128)(2,1)} %all-gather.2.cloned.1.call-done.pool), custom_call_target="tpu_custom_call" | custom-call | bytes 1048576 | tf_op jit(solution)/shard_map/pick_pages/pallas_call | solution.py:150
  66.3 4.6 %collective-permute-done.10 = bf16[8,64,256]{2,1,0:T(8,128)(2,1)S(1)} collective-permute-done((bf16[8,64,256]{2,1,0:T(8,128)(2,1)}, bf16[8,64,256]{2,1,0:T(8,128)(2,1)S(1)}, u32[]{:S(2)}, u32[]{:S(2)}) %collective-permute-start.10) | collective-permute-done | bytes 262176 | tf_op jit(solution)/shard_map/ppermute | solution.py:431
  70.9 0.0 copy-start.10
  70.9 1.5 %collective-permute-start.11 = (bf16[8,64,256]{2,1,0:T(8,128)(2,1)S(1)}, bf16[8,64,256]{2,1,0:T(8,128)(2,1)S(1)}, u32[]{:S(2)}, u32[]{:S(2)}) collective-permute-start(bf16[8,64,256]{2,1,0:T(8,128)(2,1)S(1)} %broadcast_select_fusion.v_mine), channel_id=1, source_target_pairs={{0,1},{1,0},{2,3},{3,2},{4,5},{5,4},{6,7},{7,6},{8,9},{9,8},{10,11... | collective-permute-start | bytes 786440 | tf_op jit(solution)/shard_map/ppermute | solution.py:437
  72.5 0.0 collective-permute-done.8.kv_peer
  72.5 3.3 %collective-permute-done.7 = bf16[8,64,256]{2,1,0:T(8,128)(2,1)S(1)} collective-permute-done((bf16[8,64,256]{2,1,0:T(8,128)(2,1)}, bf16[8,64,256]{2,1,0:T(8,128)(2,1)S(1)}, u32[]{:S(2)}, u32[]{:S(2)}) %collective-permute-start.7) | collective-permute-done | bytes 262176 | tf_op jit(solution)/shard_map/ppermute | solution.py:430
  75.9 0.0 copy-start.11
  75.9 1.6 %collective-permute-start.9 = (bf16[8,64,256]{2,1,0:T(8,128)(2,1)S(1)}, bf16[8,64,256]{2,1,0:T(8,128)(2,1)S(1)}, u32[]{:S(2)}, u32[]{:S(2)}) collective-permute-start(bf16[8,64,256]{2,1,0:T(8,128)(2,1)S(1)} %broadcast_select_fusion.1.k_mine), channel_id=1, source_target_pairs={{0,1},{1,0},{2,3},{3,2},{4,5},{5,4},{6,7},{7,6},{8,9},{9,8},{10,11... | collective-permute-start | bytes 786440 | tf_op jit(solution)/shard_map/ppermute | solution.py:435
  78.1 0.7 pad_add_fusion.info
  78.7 0.1 collective-permute-done.11.v_peer
  78.9 5.6 %collective-permute-done.9.k_peer = bf16[8,64,256]{2,1,0:T(8,128)(2,1)S(1)} collective-permute-done((bf16[8,64,256]{2,1,0:T(8,128)(2,1)S(1)}, bf16[8,64,256]{2,1,0:T(8,128)(2,1)S(1)}, u32[]{:S(2)}, u32[]{:S(2)}) %collective-permute-start.9) | collective-permute-done | bytes 262176 | tf_op jit(solution)/shard_map/ppermute | solution.py:435
  84.5 0.0 copy-done.10
  84.5 0.0 copy-done.15
  84.5 0.0 copy-done.11
  84.5 0.0 copy-done.16
  84.5 0.7 copy-done.17
  85.2 12.8 %attend_and_out.1 = bf16[512,1536]{1,0:T(8,128)(2,1)} custom-call(s32[3]{0:T(128)} %pad_add_fusion.info, bf16[512,768]{1,0:T(8,128)(2,1)} %copy-done.8, bf16[512,768]{1,0:T(8,128)(2,1)} %copy-done, bf16[8,64,256]{2,1,0:T(8,128)(2,1)} %copy-done.11, bf16[8,64,256]{2,1,0:T(8,128)(2,1)} %copy-done.17, bf16[8,64,256]{2,1,0:T(8,128)(2,1)} %copy-done.10, ...), custom_call_target="tpu_custom_call" | custom-call | flops 6442450944 | bytes 12582912 | tf_op jit(solution)/shard_map/attend_and_out/pallas_call | solution.py:349
  (18 shorter events, 0.1 us)
Async XLA Ops:
  6.5 5.5 %copy-start.12 = (f32[1536]{0:T(1024)S(1)}, f32[1536]{0:T(1024)}, u32[]{:S(2)}) copy-start(f32[1536]{0:T(1024)} %param.10) | copy-start | bytes 18436
  6.5 52.3 %all-gather.2.cloned.1.call-start = ((), (), s32[]{:S(2)}) async-start(), calls=%async_computation | async-start | bytes 4718592 | tf_op jit(solution)/shard_map/all_gather | solution.py:396
  8.4 16.4 %collective-permute-start = (bf16[384,768]{1,0:T(8,128)(2,1)S(1)}, bf16[384,768]{1,0:T(8,128)(2,1)S(1)}, u32[]{:S(2)}, u32[]{:S(2)}) collective-permute-start(bf16[384,768]{1,0:T(8,128)(2,1)S(1)} %constant_dynamic-slice_fusion.1), channel_id=1, source_target_pairs={{0,1},{1,0},{2,3},{3,2},{4,5},{5,4},{6,7},{7,6},{8,9},{9,8},{10,11... | collective-permute-start | bytes 1769480 | tf_op jit(solution)/shard_map/ppermute | solution.py:400
  12.5 1.7 %copy-start.5 = (bf16[1536,768]{1,0:T(8,128)(2,1)S(1)}, bf16[1536,768]{1,0:T(8,128)(2,1)}, u32[]{:S(2)}) copy-start(bf16[1536,768]{1,0:T(8,128)(2,1)} %wq.1) | copy-start | bytes 7077892
  14.2 1.4 %copy-start.6 = (bf16[1,512,1536]{2,1,0:T(8,128)(2,1)S(1)}, bf16[1,512,1536]{2,1,0:T(8,128)(2,1)}, u32[]{:S(2)}) copy-start(bf16[1,512,1536]{2,1,0:T(8,128)(2,1)} %param.9) | copy-start | bytes 4718596
  15.6 1.4 %copy-start.7 = (bf16[1536,512]{1,0:T(8,128)(2,1)S(1)}, bf16[1536,512]{1,0:T(8,128)(2,1)}, u32[]{:S(2)}) copy-start(bf16[1536,512]{1,0:T(8,128)(2,1)} %wkv.1) | copy-start | bytes 4718596
  17.0 9.5 %copy-start.9 = (bf16[768,1536]{1,0:T(8,128)(2,1)S(1)}, bf16[768,1536]{1,0:T(8,128)(2,1)}, u32[]{:S(2)}) copy-start(bf16[768,1536]{1,0:T(8,128)(2,1)} %woa.1) | copy-start | bytes 7077892
  20.1 19.3 %copy-start.1 = (f32[512,256]{1,0:T(8,128)}, f32[512,256]{1,0:T(8,128)S(1)}, u32[]{:S(2)}) copy-start(f32[512,256]{1,0:T(8,128)S(1)} %get-tuple-element.34.cos) | copy-start | bytes 1572868
  20.1 19.3 %copy-start.3 = (f32[512,256]{1,0:T(8,128)}, f32[512,256]{1,0:T(8,128)S(1)}, u32[]{:S(2)}) copy-start(f32[512,256]{1,0:T(8,128)S(1)} %get-tuple-element.35.sin) | copy-start | bytes 1572868
  20.1 19.3 %copy-start.8 = (bf16[512,768]{1,0:T(8,128)(2,1)}, bf16[512,768]{1,0:T(8,128)(2,1)S(1)}, u32[]{:S(2)}) copy-start(bf16[512,768]{1,0:T(8,128)(2,1)S(1)} %get-tuple-element.29.qa_hbm) | copy-start | bytes 2359300
  24.8 14.6 %collective-permute-start.2 = (bf16[384,768]{1,0:T(8,128)(2,1)S(1)}, bf16[384,768]{1,0:T(8,128)(2,1)S(1)}, u32[]{:S(2)}, u32[]{:S(2)}) collective-permute-start(bf16[384,768]{1,0:T(8,128)(2,1)S(1)} %collective-permute-done.w0), channel_id=1, source_target_pairs={{0,16},{16,0},{1,17},{17,1},{2,18},{18,2},{3,19},{19,3},{4,20},{20... | collective-permute-start | bytes 1769480 | tf_op jit(solution)/shard_map/ppermute | solution.py:410
  27.6 27.0 %collective-permute-start.1 = (bf16[384,1536]{1,0:T(8,128)(2,1)}, bf16[384,1536]{1,0:T(8,128)(2,1)}, u32[]{:S(2)}, u32[]{:S(2)}) collective-permute-start(bf16[384,1536]{1,0:T(8,128)(2,1)} %constant_dynamic-slice_fusion), channel_id=1, source_target_pairs={{0,1},{1,0},{2,3},{3,2},{4,5},{5,4},{6,7},{7,6},{8,9},{9,8},{10,11... | collective-permute-start | bytes 3538952 | tf_op jit(solution)/shard_map/ppermute | solution.py:400
  29.1 10.5 %collective-permute-start.3 = (bf16[384,768]{1,0:T(8,128)(2,1)S(1)}, bf16[384,768]{1,0:T(8,128)(2,1)S(1)}, u32[]{:S(2)}, u32[]{:S(2)}) collective-permute-start(bf16[384,768]{1,0:T(8,128)(2,1)S(1)} %collective-permute-done.w0), channel_id=1, source_target_pairs={{0,2},{2,0},{4,6},{6,4},{8,10},{10,8},{12,14},{14,12},{1,3},{3,1},... | collective-permute-start | bytes 1769480 | tf_op jit(solution)/shard_map/ppermute | solution.py:414
  39.4 2.2 %collective-permute-start.4 = (bf16[384,768]{1,0:T(8,128)(2,1)S(1)}, bf16[384,768]{1,0:T(8,128)(2,1)}, u32[]{:S(2)}, u32[]{:S(2)}) collective-permute-start(bf16[384,768]{1,0:T(8,128)(2,1)S(1)} %collective-permute-done.2.w1), channel_id=1, source_target_pairs={{0,2},{2,0},{4,6},{6,4},{8,10},{10,8},{12,14},{14,12},{1,3},{3,1},... | collective-permute-start | bytes 1769480 | tf_op jit(solution)/shard_map/ppermute | solution.py:414
  41.6 1.1 %copy-start.2 = (f32[512,256]{1,0:T(8,128)S(1)}, f32[512,256]{1,0:T(8,128)}, u32[]{:S(2)}) copy-start(f32[512,256]{1,0:T(8,128)} %copy-done.1) | copy-start | bytes 1572868
  42.6 1.0 copy-start.4
  43.7 10.8 %copy-start.13 = (s32[1,8]{1,0:T(1,128)S(1)}, s32[1,8]{1,0:T(1,128)}, u32[]{:S(2)}) copy-start(s32[1,8]{1,0:T(1,128)} %param.15) | copy-start | bytes 100
  46.9 1.0 copy-start
  54.5 4.1 %collective-permute-start.5 = (bf16[384,1536]{1,0:T(8,128)(2,1)}, bf16[384,1536]{1,0:T(8,128)(2,1)S(1)}, u32[]{:S(2)}, u32[]{:S(2)}) collective-permute-start(bf16[384,1536]{1,0:T(8,128)(2,1)} %collective-permute-done.1.wob0), channel_id=1, source_target_pairs={{0,2},{2,0},{4,6},{6,4},{8,10},{10,8},{12,14},{14,12},{1,3},{3,1},... | collective-permute-start | bytes 3538952 | tf_op jit(solution)/shard_map/ppermute | solution.py:420
  54.5 3.5 %collective-permute-start.6 = (s32[8]{0:T(128)S(1)}, s32[8]{0:T(128)S(1)}, u32[]{:S(2)}, u32[]{:S(2)}) collective-permute-start(s32[8]{0:T(128)S(1)} %bitcast.15), channel_id=1, source_target_pairs={{0,16},{16,0},{1,17},{17,1},{2,18},{18,2},{3,19},{19,3},{4,20},{20... | collective-permute-start | bytes 104 | tf_op jit(solution)/shard_map/ppermute | solution.py:413
  55.7 16.8 %collective-permute-start.8 = (bf16[512,512]{1,0:T(8,128)(2,1)}, bf16[512,512]{1,0:T(8,128)(2,1)S(1)}, u32[]{:S(2)}, u32[]{:S(2)}) collective-permute-start(bf16[512,512]{1,0:T(8,128)(2,1)} %get-tuple-element.43.kv_own), channel_id=1, source_target_pairs={{0,1},{1,0},{2,3},{3,2},{4,5},{5,4},{6,7},{7,6},{8,9},{9,8},{10,11... | collective-permute-start | bytes 1572872 | tf_op jit(solution)/shard_map/ppermute | solution.py:421
  58.6 2.9 %copy-start.14 = (bf16[384,1536]{1,0:T(8,128)(2,1)}, bf16[384,1536]{1,0:T(8,128)(2,1)S(1)}, u32[]{:S(2)}) copy-start(bf16[384,1536]{1,0:T(8,128)(2,1)S(1)} %collective-permute-done.5.wob1) | copy-start | bytes 3538948
  61.5 9.4 %collective-permute-start.10 = (bf16[8,64,256]{2,1,0:T(8,128)(2,1)}, bf16[8,64,256]{2,1,0:T(8,128)(2,1)S(1)}, u32[]{:S(2)}, u32[]{:S(2)}) collective-permute-start(bf16[8,64,256]{2,1,0:T(8,128)(2,1)} %get-tuple-element.49), channel_id=1, source_target_pairs={{0,16},{16,0},{1,17},{17,1},{2,18},{18,2},{3,19},{19,3},{4,20},{20... | collective-permute-start | bytes 786440 | tf_op jit(solution)/shard_map/ppermute | solution.py:431
  63.0 12.8 %collective-permute-start.7 = (bf16[8,64,256]{2,1,0:T(8,128)(2,1)}, bf16[8,64,256]{2,1,0:T(8,128)(2,1)S(1)}, u32[]{:S(2)}, u32[]{:S(2)}) collective-permute-start(bf16[8,64,256]{2,1,0:T(8,128)(2,1)} %get-tuple-element.42), channel_id=1, source_target_pairs={{0,16},{16,0},{1,17},{17,1},{2,18},{18,2},{3,19},{19,3},{4,20},{20... | collective-permute-start | bytes 786440 | tf_op jit(solution)/shard_map/ppermute | solution.py:430
  70.9 13.6 %copy-start.10 = (bf16[8,64,256]{2,1,0:T(8,128)(2,1)}, bf16[8,64,256]{2,1,0:T(8,128)(2,1)S(1)}, u32[]{:S(2)}) copy-start(bf16[8,64,256]{2,1,0:T(8,128)(2,1)S(1)} %broadcast_select_fusion.v_mine) | copy-start | bytes 786436
  70.9 8.0 %collective-permute-start.11 = (bf16[8,64,256]{2,1,0:T(8,128)(2,1)S(1)}, bf16[8,64,256]{2,1,0:T(8,128)(2,1)S(1)}, u32[]{:S(2)}, u32[]{:S(2)}) collective-permute-start(bf16[8,64,256]{2,1,0:T(8,128)(2,1)S(1)} %broadcast_select_fusion.v_mine), channel_id=1, source_target_pairs={{0,1},{1,0},{2,3},{3,2},{4,5},{5,4},{6,7},{7,6},{8,9},{9,8},{10,11... | collective-permute-start | bytes 786440 | tf_op jit(solution)/shard_map/ppermute | solution.py:437
  72.5 12.0 %copy-start.15 = (bf16[512,512]{1,0:T(8,128)(2,1)}, bf16[512,512]{1,0:T(8,128)(2,1)S(1)}, u32[]{:S(2)}) copy-start(bf16[512,512]{1,0:T(8,128)(2,1)S(1)} %collective-permute-done.8.kv_peer) | copy-start | bytes 1572868
  75.9 8.7 %copy-start.11 = (bf16[8,64,256]{2,1,0:T(8,128)(2,1)}, bf16[8,64,256]{2,1,0:T(8,128)(2,1)S(1)}, u32[]{:S(2)}) copy-start(bf16[8,64,256]{2,1,0:T(8,128)(2,1)S(1)} %broadcast_select_fusion.1.k_mine) | copy-start | bytes 786436
  75.9 8.6 %collective-permute-start.9 = (bf16[8,64,256]{2,1,0:T(8,128)(2,1)S(1)}, bf16[8,64,256]{2,1,0:T(8,128)(2,1)S(1)}, u32[]{:S(2)}, u32[]{:S(2)}) collective-permute-start(bf16[8,64,256]{2,1,0:T(8,128)(2,1)S(1)} %broadcast_select_fusion.1.k_mine), channel_id=1, source_target_pairs={{0,1},{1,0},{2,3},{3,2},{4,5},{5,4},{6,7},{7,6},{8,9},{9,8},{10,11... | collective-permute-start | bytes 786440 | tf_op jit(solution)/shard_map/ppermute | solution.py:435
  78.9 5.6 %copy-start.16 = (bf16[8,64,256]{2,1,0:T(8,128)(2,1)}, bf16[8,64,256]{2,1,0:T(8,128)(2,1)S(1)}, u32[]{:S(2)}) copy-start(bf16[8,64,256]{2,1,0:T(8,128)(2,1)S(1)} %collective-permute-done.11.v_peer) | copy-start | bytes 786436
  84.5 0.7 copy-start.17
Sparse Core Ops, SparseCore 0:
  9.0 49.8 all-gather.1

commit v10 on v9

--- a/solution.py
+++ b/solution.py
@@ -159,27 +159,55 @@
     )(idx, pool)
 
 
+def hold_kernel(info, qa, qb, own, peer, woa, wob0, wob1, qa_v, qb_v, own_v, peer_v, wa, wb, sem):
+    core = info[2]
+    deep = wob0.shape[0]
+    moves = [
+        (woa, wa),
+        (wob0, wb.at[pl.ds(core * deep, deep), :]),
+        (wob1, wb.at[pl.ds((1 - core) * deep, deep), :]),
+        (qa, qa_v),
+        (qb, qb_v),
+        (own, own_v),
+        (peer, peer_v),
+    ]
+    copies = [pltpu.make_async_copy(a, b, sem.at[n]) for n, (a, b) in enumerate(moves)]
+    for c in copies:
+        c.start()
+    for c in copies:
+        c.wait()
+
+
+def hold(info, qa, qb, kv_own, kv_peer, woa, wobs):
+    kept = (qa, qb, kv_own, kv_peer, woa, woa)
+    return pl.pallas_call(
+        hold_kernel,
+        out_shape=[jax.ShapeDtypeStruct(x.shape, x.dtype) for x in kept],
+        in_specs=[spec(pltpu.SMEM)] + [spec(ANY)] * 7,
+        out_specs=[spec(pltpu.VMEM)] * 6,
+        scratch_shapes=[pltpu.SemaphoreType.DMA((7,))],
+        compiler_params=pltpu.CompilerParams(vmem_limit_bytes=16 * 2**20),
+        cost_estimate=pl.CostEstimate(flops=0, bytes_accessed=8 * 2**20, transcendentals=0),
+        name="hold",
+    )(info, qa, qb, kv_own, kv_peer, woa, *wobs)
+
+
 def attend_kernel(
     head_size,
     info,
-    qa_hbm,
-    qb_hbm,
+    qa,
+    qb,
     k_mine,
     k_peer,
     v_mine,
     v_peer,
     kv_own,
     kv_peer,
-    woa,
-    wob0,
-    wob1,
+    wa,
+    wb,
     out_hbm,
-    qa,
-    qb,
     keys,
     vals,
-    wa,
-    wb,
     mix,
     out,
     sbuf,
@@ -188,7 +216,6 @@
     tops,
     ksem,
     vsem,
-    wsem,
     osem,
 ):
     part = info[0]
@@ -197,8 +224,6 @@
     pages, prow, _ = k_mine.shape
     page = 2 * prow
     width = out.shape[1]
-    core = info[2]
-    deep = wob0.shape[0]
     nheads = half // head_size
     window = pages * page
 
@@ -222,19 +247,8 @@
     def finish(dst, sem):
         pltpu.make_async_copy(dst, dst, sem).wait()
 
-    queries = [
-        pltpu.make_async_copy(qa_hbm, qa, wsem.at[3]),
-        pltpu.make_async_copy(qb_hbm, qb, wsem.at[4]),
-    ]
-    queries[0].start()
     start(k_mine, k_peer, 0, keys, ksem)
-    queries[1].start()
     start(v_mine, v_peer, head_size, vals, vsem)
-    weights = [
-        pltpu.make_async_copy(woa, wa, wsem.at[0]),
-        pltpu.make_async_copy(wob0, wb.at[pl.ds(core * deep, deep), :], wsem.at[1]),
-        pltpu.make_async_copy(wob1, wb.at[pl.ds((1 - core) * deep, deep), :], wsem.at[2]),
-    ]
     tile = min(256, rows)
     span = window + tile
     lanes = 128
@@ -301,11 +315,7 @@
         stores.append(pltpu.make_async_copy(out.at[at, :], out_hbm.at[at, :], osem.at[i]))
         stores[i].start()
 
-    queries[0].wait()
     finish(keys, ksem)
-    queries[1].wait()
-    for c in weights:
-        c.start()
     score(0)
     ready = []
     for m in range(len(order)):
@@ -317,9 +327,6 @@
             combine(m - 1)
             i, n, h = order[m - 1]
             if (n, h) == (1, nheads - 1):
-                if i == 0:
-                    for c in weights:
-                        c.wait()
                 ready += [(i, lo) for lo in range(0, width, block)]
         if m >= 1 and ready and order[m - 1][1:] != (1, nheads - 1):
             i, lo = ready.pop(0)
@@ -328,9 +335,6 @@
                 send_out(i)
         soften(m)
     combine(len(order) - 1)
-    if rows == tile:
-        for c in weights:
-            c.wait()
     ready += [(rows // tile - 1, lo) for lo in range(0, width, block)]
     for i, lo in ready:
         project_out(i, lo)
@@ -340,27 +344,20 @@
         c.wait()
 
 
-def attend_pages(info, qa, qb, k_mine, k_peer, v_mine, v_peer, kv_own, kv_peer, woa, wobs):
+def attend_pages(info, qa, qb, k_mine, k_peer, v_mine, v_peer, kv_own, kv_peer, wa, wb):
     rows, half = qa.shape
     tile = min(256, rows)
-    width = woa.shape[1]
+    width = wa.shape[1]
     head_size = k_mine.shape[2]
     window = k_mine.shape[0] * k_mine.shape[1] * 2
     return pl.pallas_call(
         functools.partial(attend_kernel, head_size),
         out_shape=jax.ShapeDtypeStruct((rows, width), BF16),
-        in_specs=[spec(pltpu.SMEM)]
-        + [spec(ANY)] * 2
-        + [spec(pltpu.VMEM)] * 4
-        + [spec(ANY)] * 5,
+        in_specs=[spec(pltpu.SMEM)] + [spec(pltpu.VMEM)] * 10,
         out_specs=spec(ANY),
         scratch_shapes=[
-            pltpu.VMEM((rows, half), BF16),
-            pltpu.VMEM((rows, half), BF16),
             pltpu.VMEM((window + rows, head_size), BF16),
             pltpu.VMEM((window + rows, head_size), BF16),
-            pltpu.VMEM(woa.shape, BF16),
-            pltpu.VMEM(woa.shape, BF16),
             pltpu.VMEM((2, rows, half), BF16),
             pltpu.VMEM((rows, width), BF16),
             pltpu.VMEM((2, tile, window + tile), F32),
@@ -369,17 +366,16 @@
             pltpu.VMEM((2, tile, 128), F32),
             pltpu.SemaphoreType.DMA,
             pltpu.SemaphoreType.DMA,
-            pltpu.SemaphoreType.DMA((5,)),
             pltpu.SemaphoreType.DMA((rows // tile,)),
         ],
-        compiler_params=pltpu.CompilerParams(vmem_limit_bytes=56 * 2**20),
+        compiler_params=pltpu.CompilerParams(vmem_limit_bytes=30 * 2**20),
         cost_estimate=pl.CostEstimate(
             flops=4 * rows * 2 * half * (window + 256) + 4 * rows * half * width,
             bytes_accessed=12 * 2**20,
             transcendentals=rows * 6 * (window + 256),
         ),
         name="attend_and_out",
-    )(info, qa, qb, k_mine, k_peer, v_mine, v_peer, kv_own, kv_peer, woa, *wobs)
+    )(info, qa, qb, k_mine, k_peer, v_mine, v_peer, kv_own, kv_peer, wa, wb)
 
 
 def pair_shards(tokens, norm_gain, w_query, w_keyval, w_out, kv_pages, page_table, lengths, starts):
@@ -437,8 +433,10 @@
     v_peer = lax.ppermute(v_mine, "tensor", swap)
 
     info = jnp.stack([part, lengths[0], core]).astype(jnp.int32)
+    info, k_mine = lax.optimization_barrier((info, k_mine))
+    qa, qb, kv_own, kv_peer, wa, wb = hold(info, qa, qb, kv_own, kv_peer, w_out, wo_pieces)
     return attend_pages(
-        info, qa, qb, k_mine, k_peer, v_mine, v_peer, kv_own, kv_peer, w_out, wo_pieces
+        info, qa, qb, k_mine, k_peer, v_mine, v_peer, kv_own, kv_peer, wa, wb
     )[None]
 
 

time: 106 us -> 104 us (0.981)
  waiting for transfers between devices: 39.3 us -> 28.2 us
  local copies, waits for them, and re-layouts: 10.5 us -> 17.4 us
  Pallas kernels: 24.3 us -> 26 us
  other arithmetic: 2.17 us -> 3.55 us
    unnamed x36 -> x40, local copies, waits for them, and re-layouts: 8.26 us -> 15.1 us
    ppermute x2, waiting for transfers between devices: 11.3 us -> 6.65 us  [peer_rows(): lax.ppermute(lax.dynamic_slice_in_dim(w, at * deep, deep, 0), 'tensor', s...]
    ppermute x1, waiting for transfers between devices: 5.62 us -> 2.29 us  [pair_shards(): k_peer = lax.ppermute(k_mine, 'tensor', swap)]
    pallas_call x0 -> x1, Pallas kernels: none -> 2.4 us  [hold(): pl.pallas_call(hold_kernel, out_shape=[jax.ShapeDtypeStruct(x.shape, x.dt...]
    ppermute x1, waiting for transfers between devices: 3.33 us -> 1.36 us  [pair_shards(): k_came = lax.ppermute(k_sent, 'rep', swap)]
  transfers between devices with their start and end apart: 13 -> 13, of which waited for: 10 -> 8; matrix products, arithmetic and copies ran while one was open for 4% -> 6% of each run, Pallas kernels for 11% -> 14%
where the time goes in v10:
time: 104 us
  waiting for transfers between devices  28.2 us (27%)
  Pallas kernels  26 us (25%)
  local copies, waits for them, and re-layouts  17.4 us (17%)
  between operations  15.1 us (15%)
  starting transfers between devices  13.5 us (13%)
  other arithmetic  3.55 us (3%)
    unnamed x40, local copies, waits for them, and re-layouts  15.1 us
    pallas_call x1, Pallas kernels, attend_pages(): pl.pallas_call(functools.partial(attend_kernel, head_size), out_shape=jax...  11.9 us
    ppermute x1, waiting for transfers between devices, pair_shards(): b = lax.ppermute(a, 'rep', swap)  10.3 us
    ppermute x2, waiting for transfers between devices, peer_rows(): lax.ppermute(lax.dynamic_slice_in_dim(w, at * deep, deep, 0), 'tensor', s...  6.65 us
    pallas_call x2, Pallas kernels, pick(): pl.pallas_call(pick_kernel, out_shape=(half, half), in_specs=[spec(pltpu....  5.27 us
    ppermute x1, waiting for transfers between devices, pair_shards(): v_came = lax.ppermute(v_sent, 'rep', swap)  4.69 us
    ppermute x2, starting transfers between devices, peer_rows(): lax.ppermute(lax.dynamic_slice_in_dim(w, at * deep, deep, 0), 'tensor', s...  4.55 us
    pallas_call x1, Pallas kernels, project_other(): pl.pallas_call(functools.partial(other_kernel, head_size, score_factor(he...  3.4 us
  transfers between devices with their start and end apart: 13, of which 8 were waited for; matrix products, arithmetic and copies ran while one was open for 6% of the time, Pallas kernels for 14%

profile of v10, /device:TPU:0, one launch (start us, length us, event | category | flops | bytes accessed | tf_op | source)
XLA Modules:
  0.0 103.7 jit_solution(5747596902793478639)
XLA Ops:
  6.5 0.0 all-gather.2.cloned.1.call-start
  6.5 0.7 all-gather.2.cloned.1.call-update
  7.3 1.1 %constant_dynamic-slice_fusion.1 = bf16[384,768]{1,0:T(8,128)(2,1)S(1)} fusion(bf16[1536,768]{1,0:T(8,128)(2,1)} %wq.1, s32[]{:T(128)S(6)} %select_n.67), kind=kLoop, calls=%fused_computation.31 | loop fusion | bytes 1179652 | tf_op jit(solution)/shard_map/dynamic_slice | solution.py:396
  8.4 3.0 %collective-permute-start = (bf16[384,768]{1,0:T(8,128)(2,1)S(1)}, bf16[384,768]{1,0:T(8,128)(2,1)S(1)}, u32[]{:S(2)}, u32[]{:S(2)}) collective-permute-start(bf16[384,768]{1,0:T(8,128)(2,1)S(1)} %constant_dynamic-slice_fusion.1), channel_id=1, source_target_pairs={{0,1},{1,0},{2,3},{3,2},{4,5},{5,4},{6,7},{7,6},{8,9},{9,8},{10,11... | collective-permute-start | bytes 1769480 | tf_op jit(solution)/shard_map/ppermute | solution.py:396
  12.1 0.0 copy-done.18
  12.1 0.1 pad_maximum_fusion
  12.2 0.3 fusion
  12.5 0.0 copy-start.15
  12.5 1.7 %copy-done.15 = bf16[1536,768]{1,0:T(8,128)(2,1)S(1)} copy-done((bf16[1536,768]{1,0:T(8,128)(2,1)S(1)}, bf16[1536,768]{1,0:T(8,128)(2,1)}, u32[]{:S(2)}) %copy-start.15) | copy-done | bytes 2359320
  14.2 1.4 %copy-done.16 = bf16[1,512,1536]{2,1,0:T(8,128)(2,1)S(1)} copy-done((bf16[1,512,1536]{2,1,0:T(8,128)(2,1)S(1)}, bf16[1,512,1536]{2,1,0:T(8,128)(2,1)}, u32[]{:S(2)}) %copy-start.16) | copy-done | bytes 1572888
  15.6 1.4 %copy-done.17 = bf16[1536,512]{1,0:T(8,128)(2,1)S(1)} copy-done((bf16[1536,512]{1,0:T(8,128)(2,1)S(1)}, bf16[1536,512]{1,0:T(8,128)(2,1)}, u32[]{:S(2)}) %copy-start.17) | copy-done | bytes 1572888
  17.0 3.1 %project_own.1 = (bf16[512,1536]{1,0:T(8,128)(2,1)S(1)}, bf16[512,768]{1,0:T(8,128)(2,1)S(1)}, bf16[512,512]{1,0:T(8,128)(2,1)}, f32[512,256]{1,0:T(8,128)S(1)}, f32[512,256]{1,0:T(8,128)S(1)}) custom-call(bf16[512,1536]{1,0:T(8,128)(2,1)S(1)} %bitcast.14, f32[1,1536]{1,0:T(1,128)S(1)} %reshape.34.gain, bf16[1536,768]{1,0:T(8,128)(2,1)S(1)} %copy-done.15, ...), custom_call_target="tpu_custom_call" | custom-call | flops 2013265920 | bytes 10485760 | tf_op jit(solution)/shard_map/project_own/pallas_call | solution.py:79
  20.0 1.1 %copy-done.1 = bf16[512,1536]{1,0:T(8,128)(2,1)} copy-done((bf16[512,1536]{1,0:T(8,128)(2,1)}, bf16[512,1536]{1,0:T(8,128)(2,1)S(1)}, u32[]{:S(2)}) %copy-start.1) | copy-done | bytes 1572888
  21.2 0.9 copy-done.5
  22.0 2.7 %collective-permute-done.w0 = bf16[384,768]{1,0:T(8,128)(2,1)S(1)} collective-permute-done((bf16[384,768]{1,0:T(8,128)(2,1)S(1)}, bf16[384,768]{1,0:T(8,128)(2,1)S(1)}, u32[]{:S(2)}, u32[]{:S(2)}) %collective-permute-start) | collective-permute-done | bytes 589856 | tf_op jit(solution)/shard_map/ppermute | solution.py:396
  24.8 1.7 %collective-permute-start.2 = (bf16[384,768]{1,0:T(8,128)(2,1)S(1)}, bf16[384,768]{1,0:T(8,128)(2,1)S(1)}, u32[]{:S(2)}, u32[]{:S(2)}) collective-permute-start(bf16[384,768]{1,0:T(8,128)(2,1)S(1)} %collective-permute-done.w0), channel_id=1, source_target_pairs={{0,16},{16,0},{1,17},{17,1},{2,18},{18,2},{3,19},{19,3},{4,20},{20... | collective-permute-start | bytes 1769480 | tf_op jit(solution)/shard_map/ppermute | solution.py:406
  26.5 0.0 copy-done
  26.5 1.1 %constant_dynamic-slice_fusion = bf16[384,1536]{1,0:T(8,128)(2,1)} fusion(bf16[768,1536]{1,0:T(8,128)(2,1)S(1)} %copy-done, s32[]{:T(128)S(6)} %select_n.73), kind=kLoop, calls=%fused_computation.30 | loop fusion | bytes 2359300 | tf_op jit(solution)/shard_map/dynamic_slice | solution.py:396
  27.6 1.5 %collective-permute-start.1 = (bf16[384,1536]{1,0:T(8,128)(2,1)}, bf16[384,1536]{1,0:T(8,128)(2,1)}, u32[]{:S(2)}, u32[]{:S(2)}) collective-permute-start(bf16[384,1536]{1,0:T(8,128)(2,1)} %constant_dynamic-slice_fusion), channel_id=1, source_target_pairs={{0,1},{1,0},{2,3},{3,2},{4,5},{5,4},{6,7},{7,6},{8,9},{9,8},{10,11... | collective-permute-start | bytes 3538952 | tf_op jit(solution)/shard_map/ppermute | solution.py:396
  29.1 0.0 collective-permute-start.3
  29.1 10.3 %collective-permute-done.2.w1 = bf16[384,768]{1,0:T(8,128)(2,1)S(1)} collective-permute-done((bf16[384,768]{1,0:T(8,128)(2,1)S(1)}, bf16[384,768]{1,0:T(8,128)(2,1)S(1)}, u32[]{:S(2)}, u32[]{:S(2)}) %collective-permute-start.2) | collective-permute-done | bytes 589856 | tf_op jit(solution)/shard_map/ppermute | solution.py:406
  39.4 0.0 copy-done.11
  39.4 0.0 copy-done.13
  39.4 0.0 collective-permute-start.4
  39.4 0.0 copy-start.9
  39.4 0.8 copy-done.9
  40.2 0.1 pad_add_fusion.1.order
  40.3 0.0 collective-permute-done.3.w2
  40.3 1.2 %collective-permute-done.4.w3 = bf16[384,768]{1,0:T(8,128)(2,1)} collective-permute-done((bf16[384,768]{1,0:T(8,128)(2,1)S(1)}, bf16[384,768]{1,0:T(8,128)(2,1)}, u32[]{:S(2)}, u32[]{:S(2)}) %collective-permute-start.4) | collective-permute-done | bytes 589856 | tf_op jit(solution)/shard_map/ppermute | solution.py:410
  41.5 0.0 copy-done.7
  41.5 1.5 %copy-done.2 = bf16[512,1536]{1,0:T(8,128)(2,1)S(1)} copy-done((bf16[512,1536]{1,0:T(8,128)(2,1)S(1)}, bf16[512,1536]{1,0:T(8,128)(2,1)}, u32[]{:S(2)}) %copy-start.2) | copy-done | bytes 1572888
  43.0 1.1 %copy-done.8 = bf16[384,768]{1,0:T(8,128)(2,1)S(1)} copy-done((bf16[384,768]{1,0:T(8,128)(2,1)S(1)}, bf16[384,768]{1,0:T(8,128)(2,1)}, u32[]{:S(2)}) %copy-start.8) | copy-done | bytes 589848
  44.0 1.1 %copy-done.10 = bf16[384,768]{1,0:T(8,128)(2,1)S(1)} copy-done((bf16[384,768]{1,0:T(8,128)(2,1)S(1)}, bf16[384,768]{1,0:T(8,128)(2,1)}, u32[]{:S(2)}) %copy-start.10) | copy-done | bytes 589848
  45.1 1.0 %copy-done.12 = f32[512,256]{1,0:T(8,128)S(1)} copy-done((f32[512,256]{1,0:T(8,128)S(1)}, f32[512,256]{1,0:T(8,128)}, u32[]{:S(2)}) %copy-start.12) | copy-done | bytes 524312
  46.1 1.0 %copy-done.14 = f32[512,256]{1,0:T(8,128)S(1)} copy-done((f32[512,256]{1,0:T(8,128)S(1)}, f32[512,256]{1,0:T(8,128)}, u32[]{:S(2)}) %copy-start.14) | copy-done | bytes 524312
  47.2 3.4 %project_other.1.qb = bf16[512,768]{1,0:T(8,128)(2,1)S(1)} custom-call(s32[4]{0:T(128)S(1)} %pad_add_fusion.1.order, bf16[512,1536]{1,0:T(8,128)(2,1)S(1)} %copy-done.2, bf16[384,768]{1,0:T(8,128)(2,1)S(1)} %copy-done.8, bf16[384,768]{1,0:T(8,128)(2,1)S(1)} %copy-done.10, bf16[384,768]{1,0:T(8,128)(2,1)} %collective-permute-done.3.w2, ...), custom_call_target="tpu_custom_call" | custom-call | flops 1207959552 | bytes 6291456 | tf_op jit(solution)/shard_map/project_other/pallas_call | solution.py:120
  50.6 4.0 %collective-permute-done.1.wob0 = bf16[384,1536]{1,0:T(8,128)(2,1)} collective-permute-done((bf16[384,1536]{1,0:T(8,128)(2,1)}, bf16[384,1536]{1,0:T(8,128)(2,1)}, u32[]{:S(2)}, u32[]{:S(2)}) %collective-permute-start.1) | collective-permute-done | bytes 1179680 | tf_op jit(solution)/shard_map/ppermute | solution.py:396
  54.6 0.0 collective-permute-start.5
  54.6 0.0 copy-done.19
  54.6 0.6 collective-permute-start.6
  55.2 0.5 and_select_fusion.1.idx
  55.7 1.4 %collective-permute-start.8 = (bf16[512,512]{1,0:T(8,128)(2,1)}, bf16[512,512]{1,0:T(8,128)(2,1)}, u32[]{:S(2)}, u32[]{:S(2)}) collective-permute-start(bf16[512,512]{1,0:T(8,128)(2,1)} %get-tuple-element.49.own), channel_id=1, source_target_pairs={{0,1},{1,0},{2,3},{3,2},{4,5},{5,4},{6,7},{7,6},{8,9},{9,8},{10,11... | collective-permute-start | bytes 1572872 | tf_op jit(solution)/shard_map/ppermute | solution.py:417
  57.2 0.9 collective-permute-done.6
  58.1 0.5 and_select_fusion.idx
  58.6 0.0 collective-permute-done.5.wob1
  58.6 1.0 copy-done.3
  59.6 2.6 %pick_pages.2 = (bf16[8,64,256]{2,1,0:T(8,128)(2,1)}, bf16[8,64,256]{2,1,0:T(8,128)(2,1)}) custom-call(s32[8]{0:T(128)} %and_select_fusion.idx, bf16[64,64,512]{2,1,0:T(8,128)(2,1)} %all-gather.2.cloned.1.call-done.pool), custom_call_target="tpu_custom_call" | custom-call | bytes 1048576 | tf_op jit(solution)/shard_map/pick_pages/pallas_call | solution.py:150
  62.3 0.7 collective-permute-start.10
  63.0 1.4 %collective-permute-start.7 = (bf16[8,64,256]{2,1,0:T(8,128)(2,1)}, bf16[8,64,256]{2,1,0:T(8,128)(2,1)S(1)}, u32[]{:S(2)}, u32[]{:S(2)}) collective-permute-start(bf16[8,64,256]{2,1,0:T(8,128)(2,1)} %get-tuple-element.48), channel_id=1, source_target_pairs={{0,16},{16,0},{1,17},{17,1},{2,18},{18,2},{3,19},{19,3},{4,20},{20... | collective-permute-start | bytes 786440 | tf_op jit(solution)/shard_map/ppermute | solution.py:426
  64.5 2.7 %pick_pages.3 = (bf16[8,64,256]{2,1,0:T(8,128)(2,1)}, bf16[8,64,256]{2,1,0:T(8,128)(2,1)}) custom-call(s32[8]{0:T(128)} %and_select_fusion.1.idx, bf16[64,64,512]{2,1,0:T(8,128)(2,1)} %all-gather.2.cloned.1.call-done.pool), custom_call_target="tpu_custom_call" | custom-call | bytes 1048576 | tf_op jit(solution)/shard_map/pick_pages/pallas_call | solution.py:150
  67.2 0.0 copy-start.4
  67.2 4.7 %collective-permute-done.10 = bf16[8,64,256]{2,1,0:T(8,128)(2,1)} collective-permute-done((bf16[8,64,256]{2,1,0:T(8,128)(2,1)}, bf16[8,64,256]{2,1,0:T(8,128)(2,1)}, u32[]{:S(2)}, u32[]{:S(2)}) %collective-permute-start.10) | collective-permute-done | bytes 262176 | tf_op jit(solution)/shard_map/ppermute | solution.py:427
  71.9 1.0 broadcast_select_fusion.v_mine
  72.9 1.6 %collective-permute-start.11 = (bf16[8,64,256]{2,1,0:T(8,128)(2,1)S(1)}, bf16[8,64,256]{2,1,0:T(8,128)(2,1)S(1)}, u32[]{:S(2)}, u32[]{:S(2)}) collective-permute-start(bf16[8,64,256]{2,1,0:T(8,128)(2,1)S(1)} %broadcast_select_fusion.v_mine), channel_id=1, source_target_pairs={{0,1},{1,0},{2,3},{3,2},{4,5},{5,4},{6,7},{7,6},{8,9},{9,8},{10,11... | collective-permute-start | bytes 786440 | tf_op jit(solution)/shard_map/ppermute | solution.py:433
  74.5 0.0 collective-permute-done.8.peer
  74.5 1.4 %collective-permute-done.7 = bf16[8,64,256]{2,1,0:T(8,128)(2,1)S(1)} collective-permute-done((bf16[8,64,256]{2,1,0:T(8,128)(2,1)}, bf16[8,64,256]{2,1,0:T(8,128)(2,1)S(1)}, u32[]{:S(2)}, u32[]{:S(2)}) %collective-permute-start.7) | collective-permute-done | bytes 262176 | tf_op jit(solution)/shard_map/ppermute | solution.py:426
  75.8 1.0 broadcast_select_fusion.1.k_mine
  76.8 1.5 %collective-permute-start.9 = (bf16[8,64,256]{2,1,0:T(8,128)(2,1)S(1)}, bf16[8,64,256]{2,1,0:T(8,128)(2,1)S(1)}, u32[]{:S(2)}, u32[]{:S(2)}) collective-permute-start(bf16[8,64,256]{2,1,0:T(8,128)(2,1)S(1)} %broadcast_select_fusion.1.k_mine), channel_id=1, source_target_pairs={{0,1},{1,0},{2,3},{3,2},{4,5},{5,4},{6,7},{7,6},{8,9},{9,8},{10,11... | collective-permute-start | bytes 786440 | tf_op jit(solution)/shard_map/ppermute | solution.py:431
  79.0 0.1 pad_add_fusion.info
  79.1 1.1 %copy-done.6 = bf16[512,768]{1,0:T(8,128)(2,1)S(1)} copy-done((bf16[512,768]{1,0:T(8,128)(2,1)S(1)}, bf16[512,768]{1,0:T(8,128)(2,1)}, u32[]{:S(2)}) %copy-start.6) | copy-done | bytes 786456
  80.2 2.4 %hold.1 = (bf16[512,768]{1,0:T(8,128)(2,1)S(1)}, bf16[512,768]{1,0:T(8,128)(2,1)S(1)}, bf16[512,512]{1,0:T(8,128)(2,1)S(1)}, bf16[512,512]{1,0:T(8,128)(2,1)S(1)...) custom-call(s32[3]{0:T(128)S(1)} %pad_add_fusion.info, bf16[512,768]{1,0:T(8,128)(2,1)S(1)} %copy-done.6, ...), custom_call_target="tpu_custom_call" | custom-call | bytes 8388608 | tf_op jit(solution)/shard_map/hold/pallas_call | solution.py:183
  82.6 0.0 collective-permute-done.11.v_peer
  82.6 2.3 %collective-permute-done.9.k_peer = bf16[8,64,256]{2,1,0:T(8,128)(2,1)S(1)} collective-permute-done((bf16[8,64,256]{2,1,0:T(8,128)(2,1)S(1)}, bf16[8,64,256]{2,1,0:T(8,128)(2,1)S(1)}, u32[]{:S(2)}, u32[]{:S(2)}) %collective-permute-start.9) | collective-permute-done | bytes 262176 | tf_op jit(solution)/shard_map/ppermute | solution.py:431
  84.9 11.9 %attend_and_out.1 = bf16[512,1536]{1,0:T(8,128)(2,1)} custom-call(s32[3]{0:T(128)S(1)} %pad_add_fusion.info, bf16[512,768]{1,0:T(8,128)(2,1)S(1)} %get-tuple-element.60.qa, bf16[512,768]{1,0:T(8,128)(2,1)S(1)} %get-tuple-element.61.qb, bf16[8,64,256]{2,1,0:T(8,128)(2,1)S(1)} %broadcast_select_fusion.1.k_mine, ...), custom_call_target="tpu_custom_call" | custom-call | flops 6442450944 | bytes 12582912 | tf_op jit(solution)/shard_map/attend_and_out/pallas_call | solution.py:353
  (23 shorter events, 0.1 us)
Async XLA Ops:
  6.5 5.5 %copy-start.18 = (f32[1536]{0:T(1024)S(1)}, f32[1536]{0:T(1024)}, u32[]{:S(2)}) copy-start(f32[1536]{0:T(1024)} %param.10) | copy-start | bytes 18436
  6.5 53.1 %all-gather.2.cloned.1.call-start = ((), (), s32[]{:S(2)}) async-start(), calls=%async_computation | async-start | bytes 4718592 | tf_op jit(solution)/shard_map/all_gather | solution.py:392
  8.4 16.4 %collective-permute-start = (bf16[384,768]{1,0:T(8,128)(2,1)S(1)}, bf16[384,768]{1,0:T(8,128)(2,1)S(1)}, u32[]{:S(2)}, u32[]{:S(2)}) collective-permute-start(bf16[384,768]{1,0:T(8,128)(2,1)S(1)} %constant_dynamic-slice_fusion.1), channel_id=1, source_target_pairs={{0,1},{1,0},{2,3},{3,2},{4,5},{5,4},{6,7},{7,6},{8,9},{9,8},{10,11... | collective-permute-start | bytes 1769480 | tf_op jit(solution)/shard_map/ppermute | solution.py:396
  12.5 1.7 %copy-start.15 = (bf16[1536,768]{1,0:T(8,128)(2,1)S(1)}, bf16[1536,768]{1,0:T(8,128)(2,1)}, u32[]{:S(2)}) copy-start(bf16[1536,768]{1,0:T(8,128)(2,1)} %wq.1) | copy-start | bytes 7077892
  14.2 1.4 %copy-start.16 = (bf16[1,512,1536]{2,1,0:T(8,128)(2,1)S(1)}, bf16[1,512,1536]{2,1,0:T(8,128)(2,1)}, u32[]{:S(2)}) copy-start(bf16[1,512,1536]{2,1,0:T(8,128)(2,1)} %param.9) | copy-start | bytes 4718596
  15.6 1.4 %copy-start.17 = (bf16[1536,512]{1,0:T(8,128)(2,1)S(1)}, bf16[1536,512]{1,0:T(8,128)(2,1)}, u32[]{:S(2)}) copy-start(bf16[1536,512]{1,0:T(8,128)(2,1)} %wkv.1) | copy-start | bytes 4718596
  17.0 9.5 %copy-start = (bf16[768,1536]{1,0:T(8,128)(2,1)S(1)}, bf16[768,1536]{1,0:T(8,128)(2,1)}, u32[]{:S(2)}) copy-start(bf16[768,1536]{1,0:T(8,128)(2,1)} %woa.1) | copy-start | bytes 7077892
  20.0 1.1 %copy-start.1 = (bf16[512,1536]{1,0:T(8,128)(2,1)}, bf16[512,1536]{1,0:T(8,128)(2,1)S(1)}, u32[]{:S(2)}) copy-start(bf16[512,1536]{1,0:T(8,128)(2,1)S(1)} %get-tuple-element.40.normed) | copy-start | bytes 4718596
  21.2 0.9 copy-start.5
  22.0 17.3 %copy-start.11 = (f32[512,256]{1,0:T(8,128)}, f32[512,256]{1,0:T(8,128)S(1)}, u32[]{:S(2)}) copy-start(f32[512,256]{1,0:T(8,128)S(1)} %get-tuple-element.42.cos) | copy-start | bytes 1572868
  22.0 17.3 %copy-start.13 = (f32[512,256]{1,0:T(8,128)}, f32[512,256]{1,0:T(8,128)S(1)}, u32[]{:S(2)}) copy-start(f32[512,256]{1,0:T(8,128)S(1)} %get-tuple-element.43.sin) | copy-start | bytes 1572868
  24.8 16.8 %copy-start.7 = (bf16[384,768]{1,0:T(8,128)(2,1)}, bf16[384,768]{1,0:T(8,128)(2,1)S(1)}, u32[]{:S(2)}) copy-start(bf16[384,768]{1,0:T(8,128)(2,1)S(1)} %collective-permute-done.w0) | copy-start | bytes 1769476
  24.8 14.6 %collective-permute-start.2 = (bf16[384,768]{1,0:T(8,128)(2,1)S(1)}, bf16[384,768]{1,0:T(8,128)(2,1)S(1)}, u32[]{:S(2)}, u32[]{:S(2)}) collective-permute-start(bf16[384,768]{1,0:T(8,128)(2,1)S(1)} %collective-permute-done.w0), channel_id=1, source_target_pairs={{0,16},{16,0},{1,17},{17,1},{2,18},{18,2},{3,19},{19,3},{4,20},{20... | collective-permute-start | bytes 1769480 | tf_op jit(solution)/shard_map/ppermute | solution.py:406
  27.6 27.0 %collective-permute-start.1 = (bf16[384,1536]{1,0:T(8,128)(2,1)}, bf16[384,1536]{1,0:T(8,128)(2,1)}, u32[]{:S(2)}, u32[]{:S(2)}) collective-permute-start(bf16[384,1536]{1,0:T(8,128)(2,1)} %constant_dynamic-slice_fusion), channel_id=1, source_target_pairs={{0,1},{1,0},{2,3},{3,2},{4,5},{5,4},{6,7},{7,6},{8,9},{9,8},{10,11... | collective-permute-start | bytes 3538952 | tf_op jit(solution)/shard_map/ppermute | solution.py:396
  29.1 11.2 %collective-permute-start.3 = (bf16[384,768]{1,0:T(8,128)(2,1)S(1)}, bf16[384,768]{1,0:T(8,128)(2,1)}, u32[]{:S(2)}, u32[]{:S(2)}) collective-permute-start(bf16[384,768]{1,0:T(8,128)(2,1)S(1)} %collective-permute-done.w0), channel_id=1, source_target_pairs={{0,2},{2,0},{4,6},{6,4},{8,10},{10,8},{12,14},{14,12},{1,3},{3,1},... | collective-permute-start | bytes 1769480 | tf_op jit(solution)/shard_map/ppermute | solution.py:410
  39.4 2.1 %collective-permute-start.4 = (bf16[384,768]{1,0:T(8,128)(2,1)S(1)}, bf16[384,768]{1,0:T(8,128)(2,1)}, u32[]{:S(2)}, u32[]{:S(2)}) collective-permute-start(bf16[384,768]{1,0:T(8,128)(2,1)S(1)} %collective-permute-done.2.w1), channel_id=1, source_target_pairs={{0,2},{2,0},{4,6},{6,4},{8,10},{10,8},{12,14},{14,12},{1,3},{3,1},... | collective-permute-start | bytes 1769480 | tf_op jit(solution)/shard_map/ppermute | solution.py:410
  39.4 0.8 copy-start.9
  41.5 1.5 %copy-start.2 = (bf16[512,1536]{1,0:T(8,128)(2,1)S(1)}, bf16[512,1536]{1,0:T(8,128)(2,1)}, u32[]{:S(2)}) copy-start(bf16[512,1536]{1,0:T(8,128)(2,1)} %copy-done.1) | copy-start | bytes 4718596
  43.0 1.1 %copy-start.8 = (bf16[384,768]{1,0:T(8,128)(2,1)S(1)}, bf16[384,768]{1,0:T(8,128)(2,1)}, u32[]{:S(2)}) copy-start(bf16[384,768]{1,0:T(8,128)(2,1)} %copy-done.7) | copy-start | bytes 1769476
  44.0 1.1 %copy-start.10 = (bf16[384,768]{1,0:T(8,128)(2,1)S(1)}, bf16[384,768]{1,0:T(8,128)(2,1)}, u32[]{:S(2)}) copy-start(bf16[384,768]{1,0:T(8,128)(2,1)} %copy-done.9) | copy-start | bytes 1769476
  45.1 1.0 %copy-start.12 = (f32[512,256]{1,0:T(8,128)S(1)}, f32[512,256]{1,0:T(8,128)}, u32[]{:S(2)}) copy-start(f32[512,256]{1,0:T(8,128)} %copy-done.11) | copy-start | bytes 1572868
  46.1 1.0 %copy-start.14 = (f32[512,256]{1,0:T(8,128)S(1)}, f32[512,256]{1,0:T(8,128)}, u32[]{:S(2)}) copy-start(f32[512,256]{1,0:T(8,128)} %copy-done.13) | copy-start | bytes 1572868
  47.2 7.4 %copy-start.19 = (s32[1,8]{1,0:T(1,128)S(1)}, s32[1,8]{1,0:T(1,128)}, u32[]{:S(2)}) copy-start(s32[1,8]{1,0:T(1,128)} %param.15) | copy-start | bytes 100
  54.6 4.1 %collective-permute-start.5 = (bf16[384,1536]{1,0:T(8,128)(2,1)}, bf16[384,1536]{1,0:T(8,128)(2,1)S(1)}, u32[]{:S(2)}, u32[]{:S(2)}) collective-permute-start(bf16[384,1536]{1,0:T(8,128)(2,1)} %collective-permute-done.1.wob0), channel_id=1, source_target_pairs={{0,2},{2,0},{4,6},{6,4},{8,10},{10,8},{12,14},{14,12},{1,3},{3,1},... | collective-permute-start | bytes 3538952 | tf_op jit(solution)/shard_map/ppermute | solution.py:416
  54.6 3.5 %collective-permute-start.6 = (s32[8]{0:T(128)S(1)}, s32[8]{0:T(128)S(1)}, u32[]{:S(2)}, u32[]{:S(2)}) collective-permute-start(s32[8]{0:T(128)S(1)} %bitcast.15), channel_id=1, source_target_pairs={{0,16},{16,0},{1,17},{17,1},{2,18},{18,2},{3,19},{19,3},{4,20},{20... | collective-permute-start | bytes 104 | tf_op jit(solution)/shard_map/ppermute | solution.py:409
  55.7 18.7 %collective-permute-start.8 = (bf16[512,512]{1,0:T(8,128)(2,1)}, bf16[512,512]{1,0:T(8,128)(2,1)}, u32[]{:S(2)}, u32[]{:S(2)}) collective-permute-start(bf16[512,512]{1,0:T(8,128)(2,1)} %get-tuple-element.49.own), channel_id=1, source_target_pairs={{0,1},{1,0},{2,3},{3,2},{4,5},{5,4},{6,7},{7,6},{8,9},{9,8},{10,11... | collective-permute-start | bytes 1572872 | tf_op jit(solution)/shard_map/ppermute | solution.py:417
  58.6 1.0 copy-start.3
  62.3 9.6 %collective-permute-start.10 = (bf16[8,64,256]{2,1,0:T(8,128)(2,1)}, bf16[8,64,256]{2,1,0:T(8,128)(2,1)}, u32[]{:S(2)}, u32[]{:S(2)}) collective-permute-start(bf16[8,64,256]{2,1,0:T(8,128)(2,1)} %get-tuple-element.64), channel_id=1, source_target_pairs={{0,16},{16,0},{1,17},{17,1},{2,18},{18,2},{3,19},{19,3},{4,20},{20... | collective-permute-start | bytes 786440 | tf_op jit(solution)/shard_map/ppermute | solution.py:427
  63.0 12.8 %collective-permute-start.7 = (bf16[8,64,256]{2,1,0:T(8,128)(2,1)}, bf16[8,64,256]{2,1,0:T(8,128)(2,1)S(1)}, u32[]{:S(2)}, u32[]{:S(2)}) collective-permute-start(bf16[8,64,256]{2,1,0:T(8,128)(2,1)} %get-tuple-element.48), channel_id=1, source_target_pairs={{0,16},{16,0},{1,17},{17,1},{2,18},{18,2},{3,19},{19,3},{4,20},{20... | collective-permute-start | bytes 786440 | tf_op jit(solution)/shard_map/ppermute | solution.py:426
  67.2 11.9 %copy-start.4 = (bf16[384,1536]{1,0:T(8,128)(2,1)S(1)}, bf16[384,1536]{1,0:T(8,128)(2,1)}, u32[]{:S(2)}) copy-start(bf16[384,1536]{1,0:T(8,128)(2,1)} %copy-done.3) | copy-start | bytes 3538948
  72.9 9.8 %collective-permute-start.11 = (bf16[8,64,256]{2,1,0:T(8,128)(2,1)S(1)}, bf16[8,64,256]{2,1,0:T(8,128)(2,1)S(1)}, u32[]{:S(2)}, u32[]{:S(2)}) collective-permute-start(bf16[8,64,256]{2,1,0:T(8,128)(2,1)S(1)} %broadcast_select_fusion.v_mine), channel_id=1, source_target_pairs={{0,1},{1,0},{2,3},{3,2},{4,5},{5,4},{6,7},{7,6},{8,9},{9,8},{10,11... | collective-permute-start | bytes 786440 | tf_op jit(solution)/shard_map/ppermute | solution.py:433
  76.8 8.1 %collective-permute-start.9 = (bf16[8,64,256]{2,1,0:T(8,128)(2,1)S(1)}, bf16[8,64,256]{2,1,0:T(8,128)(2,1)S(1)}, u32[]{:S(2)}, u32[]{:S(2)}) collective-permute-start(bf16[8,64,256]{2,1,0:T(8,128)(2,1)S(1)} %broadcast_select_fusion.1.k_mine), channel_id=1, source_target_pairs={{0,1},{1,0},{2,3},{3,2},{4,5},{5,4},{6,7},{7,6},{8,9},{9,8},{10,11... | collective-permute-start | bytes 786440 | tf_op jit(solution)/shard_map/ppermute | solution.py:431
  79.1 1.1 %copy-start.6 = (bf16[512,768]{1,0:T(8,128)(2,1)S(1)}, bf16[512,768]{1,0:T(8,128)(2,1)}, u32[]{:S(2)}) copy-start(bf16[512,768]{1,0:T(8,128)(2,1)} %copy-done.5) | copy-start | bytes 2359300
Sparse Core Ops, SparseCore 0:
  9.0 49.8 all-gather.1

commit v11 on v10

--- a/solution.py
+++ b/solution.py
@@ -207,6 +207,7 @@
     wb,
     out_hbm,
     keys,
+    turned,
     vals,
     mix,
     out,
@@ -262,12 +263,8 @@
         q = (qa, qb)[n][pl.ds(i * tile, tile), h * head_size : (h + 1) * head_size]
         top = None
         for lo in range(0, span, tile):
-            s = lax.dot_general(
-                q,
-                keys[pl.ds(i * tile + lo, tile), :],
-                (((1,), (1,)), ((), ())),
-                preferred_element_type=F32,
-            )
+            at = i * tile + lo
+            s = jnp.dot(q, turned[:, at : at + tile], preferred_element_type=F32)
             if lo == 0:
                 s = jnp.where(gap >= 1, s, MASKED)
             if lo + tile == span:
@@ -316,6 +313,8 @@
         stores[i].start()
 
     finish(keys, ksem)
+    for lo in range(0, window + rows, tile):
+        turned[:, lo : lo + tile] = keys[lo : lo + tile, :].T
     score(0)
     ready = []
     for m in range(len(order)):
@@ -357,6 +356,7 @@
         out_specs=spec(ANY),
         scratch_shapes=[
             pltpu.VMEM((window + rows, head_size), BF16),
+            pltpu.VMEM((head_size, window + rows), BF16),
             pltpu.VMEM((window + rows, head_size), BF16),
             pltpu.VMEM((2, rows, half), BF16),
             pltpu.VMEM((rows, width), BF16),

time: 104 us -> 104 us (level)
  no operation moved by 1% of the time
where the time goes in v11:
time: 104 us
  waiting for transfers between devices  28.2 us (27%)
  Pallas kernels  26 us (25%)
  local copies, waits for them, and re-layouts  17.4 us (17%)
  between operations  15.1 us (15%)
  starting transfers between devices  13.5 us (13%)
  other arithmetic  3.55 us (3%)
    unnamed x40, local copies, waits for them, and re-layouts  15.1 us
    pallas_call x1, Pallas kernels, attend_pages(): pl.pallas_call(functools.partial(attend_kernel, head_size), out_shape=jax...  11.9 us
    ppermute x1, waiting for transfers between devices, pair_shards(): b = lax.ppermute(a, 'rep', swap)  10.3 us
    ppermute x2, waiting for transfers between devices, peer_rows(): lax.ppermute(lax.dynamic_slice_in_dim(w, at * deep, deep, 0), 'tensor', s...  6.65 us
    pallas_call x2, Pallas kernels, pick(): pl.pallas_call(pick_kernel, out_shape=(half, half), in_specs=[spec(pltpu....  5.27 us
    ppermute x1, waiting for transfers between devices, pair_shards(): v_came = lax.ppermute(v_sent, 'rep', swap)  4.69 us
    ppermute x2, starting transfers between devices, peer_rows(): lax.ppermute(lax.dynamic_slice_in_dim(w, at * deep, deep, 0), 'tensor', s...  4.55 us
    pallas_call x1, Pallas kernels, project_other(): pl.pallas_call(functools.partial(other_kernel, head_size, score_factor(he...  3.4 us
  transfers between devices with their start and end apart: 13, of which 8 were waited for; matrix products, arithmetic and copies ran while one was open for 6% of the time, Pallas kernels for 14%

profile of v11, /device:TPU:0, one launch (start us, length us, event | category | flops | bytes accessed | tf_op | source)
XLA Modules:
  0.0 103.7 jit_solution(5145714295327877530)
XLA Ops:
  6.5 0.0 all-gather.2.cloned.1.call-start
  6.5 0.7 all-gather.2.cloned.1.call-update
  7.3 1.1 %constant_dynamic-slice_fusion.1 = bf16[384,768]{1,0:T(8,128)(2,1)S(1)} fusion(bf16[1536,768]{1,0:T(8,128)(2,1)} %wq.1, s32[]{:T(128)S(6)} %select_n.67), kind=kLoop, calls=%fused_computation.31 | loop fusion | bytes 1179652 | tf_op jit(solution)/shard_map/dynamic_slice | solution.py:396
  8.4 3.0 %collective-permute-start = (bf16[384,768]{1,0:T(8,128)(2,1)S(1)}, bf16[384,768]{1,0:T(8,128)(2,1)S(1)}, u32[]{:S(2)}, u32[]{:S(2)}) collective-permute-start(bf16[384,768]{1,0:T(8,128)(2,1)S(1)} %constant_dynamic-slice_fusion.1), channel_id=1, source_target_pairs={{0,1},{1,0},{2,3},{3,2},{4,5},{5,4},{6,7},{7,6},{8,9},{9,8},{10,11... | collective-permute-start | bytes 1769480 | tf_op jit(solution)/shard_map/ppermute | solution.py:396
  12.1 0.0 copy-done.18
  12.1 0.1 pad_maximum_fusion
  12.2 0.3 fusion
  12.5 0.0 copy-start.15
  12.5 1.7 %copy-done.15 = bf16[1536,768]{1,0:T(8,128)(2,1)S(1)} copy-done((bf16[1536,768]{1,0:T(8,128)(2,1)S(1)}, bf16[1536,768]{1,0:T(8,128)(2,1)}, u32[]{:S(2)}) %copy-start.15) | copy-done | bytes 2359320
  14.2 1.4 %copy-done.16 = bf16[1,512,1536]{2,1,0:T(8,128)(2,1)S(1)} copy-done((bf16[1,512,1536]{2,1,0:T(8,128)(2,1)S(1)}, bf16[1,512,1536]{2,1,0:T(8,128)(2,1)}, u32[]{:S(2)}) %copy-start.16) | copy-done | bytes 1572888
  15.6 1.4 %copy-done.17 = bf16[1536,512]{1,0:T(8,128)(2,1)S(1)} copy-done((bf16[1536,512]{1,0:T(8,128)(2,1)S(1)}, bf16[1536,512]{1,0:T(8,128)(2,1)}, u32[]{:S(2)}) %copy-start.17) | copy-done | bytes 1572888
  17.0 3.1 %project_own.1 = (bf16[512,1536]{1,0:T(8,128)(2,1)S(1)}, bf16[512,768]{1,0:T(8,128)(2,1)S(1)}, bf16[512,512]{1,0:T(8,128)(2,1)}, f32[512,256]{1,0:T(8,128)S(1)}, f32[512,256]{1,0:T(8,128)S(1)}) custom-call(bf16[512,1536]{1,0:T(8,128)(2,1)S(1)} %bitcast.14, f32[1,1536]{1,0:T(1,128)S(1)} %reshape.34.gain, bf16[1536,768]{1,0:T(8,128)(2,1)S(1)} %copy-done.15, ...), custom_call_target="tpu_custom_call" | custom-call | flops 2013265920 | bytes 10485760 | tf_op jit(solution)/shard_map/project_own/pallas_call | solution.py:79
  20.0 1.1 %copy-done.1 = bf16[512,1536]{1,0:T(8,128)(2,1)} copy-done((bf16[512,1536]{1,0:T(8,128)(2,1)}, bf16[512,1536]{1,0:T(8,128)(2,1)S(1)}, u32[]{:S(2)}) %copy-start.1) | copy-done | bytes 1572888
  21.2 0.9 copy-done.5
  22.0 2.7 %collective-permute-done.w0 = bf16[384,768]{1,0:T(8,128)(2,1)S(1)} collective-permute-done((bf16[384,768]{1,0:T(8,128)(2,1)S(1)}, bf16[384,768]{1,0:T(8,128)(2,1)S(1)}, u32[]{:S(2)}, u32[]{:S(2)}) %collective-permute-start) | collective-permute-done | bytes 589856 | tf_op jit(solution)/shard_map/ppermute | solution.py:396
  24.8 1.7 %collective-permute-start.2 = (bf16[384,768]{1,0:T(8,128)(2,1)S(1)}, bf16[384,768]{1,0:T(8,128)(2,1)S(1)}, u32[]{:S(2)}, u32[]{:S(2)}) collective-permute-start(bf16[384,768]{1,0:T(8,128)(2,1)S(1)} %collective-permute-done.w0), channel_id=1, source_target_pairs={{0,16},{16,0},{1,17},{17,1},{2,18},{18,2},{3,19},{19,3},{4,20},{20... | collective-permute-start | bytes 1769480 | tf_op jit(solution)/shard_map/ppermute | solution.py:406
  26.5 0.0 copy-done
  26.5 1.1 %constant_dynamic-slice_fusion = bf16[384,1536]{1,0:T(8,128)(2,1)} fusion(bf16[768,1536]{1,0:T(8,128)(2,1)S(1)} %copy-done, s32[]{:T(128)S(6)} %select_n.73), kind=kLoop, calls=%fused_computation.30 | loop fusion | bytes 2359300 | tf_op jit(solution)/shard_map/dynamic_slice | solution.py:396
  27.6 1.5 %collective-permute-start.1 = (bf16[384,1536]{1,0:T(8,128)(2,1)}, bf16[384,1536]{1,0:T(8,128)(2,1)}, u32[]{:S(2)}, u32[]{:S(2)}) collective-permute-start(bf16[384,1536]{1,0:T(8,128)(2,1)} %constant_dynamic-slice_fusion), channel_id=1, source_target_pairs={{0,1},{1,0},{2,3},{3,2},{4,5},{5,4},{6,7},{7,6},{8,9},{9,8},{10,11... | collective-permute-start | bytes 3538952 | tf_op jit(solution)/shard_map/ppermute | solution.py:396
  29.1 0.0 collective-permute-start.3
  29.1 10.3 %collective-permute-done.2.w1 = bf16[384,768]{1,0:T(8,128)(2,1)S(1)} collective-permute-done((bf16[384,768]{1,0:T(8,128)(2,1)S(1)}, bf16[384,768]{1,0:T(8,128)(2,1)S(1)}, u32[]{:S(2)}, u32[]{:S(2)}) %collective-permute-start.2) | collective-permute-done | bytes 589856 | tf_op jit(solution)/shard_map/ppermute | solution.py:406
  39.4 0.0 copy-done.11
  39.4 0.0 copy-done.13
  39.4 0.0 collective-permute-start.4
  39.4 0.0 copy-start.9
  39.4 0.8 copy-done.9
  40.2 0.1 pad_add_fusion.1.order
  40.3 0.0 collective-permute-done.3.w2
  40.3 1.2 %collective-permute-done.4.w3 = bf16[384,768]{1,0:T(8,128)(2,1)} collective-permute-done((bf16[384,768]{1,0:T(8,128)(2,1)S(1)}, bf16[384,768]{1,0:T(8,128)(2,1)}, u32[]{:S(2)}, u32[]{:S(2)}) %collective-permute-start.4) | collective-permute-done | bytes 589856 | tf_op jit(solution)/shard_map/ppermute | solution.py:410
  41.5 0.0 copy-done.7
  41.5 1.5 %copy-done.2 = bf16[512,1536]{1,0:T(8,128)(2,1)S(1)} copy-done((bf16[512,1536]{1,0:T(8,128)(2,1)S(1)}, bf16[512,1536]{1,0:T(8,128)(2,1)}, u32[]{:S(2)}) %copy-start.2) | copy-done | bytes 1572888
  43.0 1.1 %copy-done.8 = bf16[384,768]{1,0:T(8,128)(2,1)S(1)} copy-done((bf16[384,768]{1,0:T(8,128)(2,1)S(1)}, bf16[384,768]{1,0:T(8,128)(2,1)}, u32[]{:S(2)}) %copy-start.8) | copy-done | bytes 589848
  44.0 1.1 %copy-done.10 = bf16[384,768]{1,0:T(8,128)(2,1)S(1)} copy-done((bf16[384,768]{1,0:T(8,128)(2,1)S(1)}, bf16[384,768]{1,0:T(8,128)(2,1)}, u32[]{:S(2)}) %copy-start.10) | copy-done | bytes 589848
  45.1 1.0 %copy-done.12 = f32[512,256]{1,0:T(8,128)S(1)} copy-done((f32[512,256]{1,0:T(8,128)S(1)}, f32[512,256]{1,0:T(8,128)}, u32[]{:S(2)}) %copy-start.12) | copy-done | bytes 524312
  46.1 1.0 %copy-done.14 = f32[512,256]{1,0:T(8,128)S(1)} copy-done((f32[512,256]{1,0:T(8,128)S(1)}, f32[512,256]{1,0:T(8,128)}, u32[]{:S(2)}) %copy-start.14) | copy-done | bytes 524312
  47.2 3.4 %project_other.1.qb = bf16[512,768]{1,0:T(8,128)(2,1)S(1)} custom-call(s32[4]{0:T(128)S(1)} %pad_add_fusion.1.order, bf16[512,1536]{1,0:T(8,128)(2,1)S(1)} %copy-done.2, bf16[384,768]{1,0:T(8,128)(2,1)S(1)} %copy-done.8, bf16[384,768]{1,0:T(8,128)(2,1)S(1)} %copy-done.10, bf16[384,768]{1,0:T(8,128)(2,1)} %collective-permute-done.3.w2, ...), custom_call_target="tpu_custom_call" | custom-call | flops 1207959552 | bytes 6291456 | tf_op jit(solution)/shard_map/project_other/pallas_call | solution.py:120
  50.6 4.0 %collective-permute-done.1.wob0 = bf16[384,1536]{1,0:T(8,128)(2,1)} collective-permute-done((bf16[384,1536]{1,0:T(8,128)(2,1)}, bf16[384,1536]{1,0:T(8,128)(2,1)}, u32[]{:S(2)}, u32[]{:S(2)}) %collective-permute-start.1) | collective-permute-done | bytes 1179680 | tf_op jit(solution)/shard_map/ppermute | solution.py:396
  54.6 0.0 collective-permute-start.5
  54.6 0.0 copy-done.19
  54.6 0.6 collective-permute-start.6
  55.2 0.5 and_select_fusion.1.idx
  55.7 1.4 %collective-permute-start.8 = (bf16[512,512]{1,0:T(8,128)(2,1)}, bf16[512,512]{1,0:T(8,128)(2,1)}, u32[]{:S(2)}, u32[]{:S(2)}) collective-permute-start(bf16[512,512]{1,0:T(8,128)(2,1)} %get-tuple-element.49.own), channel_id=1, source_target_pairs={{0,1},{1,0},{2,3},{3,2},{4,5},{5,4},{6,7},{7,6},{8,9},{9,8},{10,11... | collective-permute-start | bytes 1572872 | tf_op jit(solution)/shard_map/ppermute | solution.py:417
  57.2 0.9 collective-permute-done.6
  58.1 0.5 and_select_fusion.idx
  58.6 0.0 collective-permute-done.5.wob1
  58.6 1.0 copy-done.3
  59.6 2.6 %pick_pages.2 = (bf16[8,64,256]{2,1,0:T(8,128)(2,1)}, bf16[8,64,256]{2,1,0:T(8,128)(2,1)}) custom-call(s32[8]{0:T(128)} %and_select_fusion.idx, bf16[64,64,512]{2,1,0:T(8,128)(2,1)} %all-gather.2.cloned.1.call-done.pool), custom_call_target="tpu_custom_call" | custom-call | bytes 1048576 | tf_op jit(solution)/shard_map/pick_pages/pallas_call | solution.py:150
  62.3 0.7 collective-permute-start.10
  63.0 1.4 %collective-permute-start.7 = (bf16[8,64,256]{2,1,0:T(8,128)(2,1)}, bf16[8,64,256]{2,1,0:T(8,128)(2,1)S(1)}, u32[]{:S(2)}, u32[]{:S(2)}) collective-permute-start(bf16[8,64,256]{2,1,0:T(8,128)(2,1)} %get-tuple-element.48), channel_id=1, source_target_pairs={{0,16},{16,0},{1,17},{17,1},{2,18},{18,2},{3,19},{19,3},{4,20},{20... | collective-permute-start | bytes 786440 | tf_op jit(solution)/shard_map/ppermute | solution.py:426
  64.5 2.7 %pick_pages.3 = (bf16[8,64,256]{2,1,0:T(8,128)(2,1)}, bf16[8,64,256]{2,1,0:T(8,128)(2,1)}) custom-call(s32[8]{0:T(128)} %and_select_fusion.1.idx, bf16[64,64,512]{2,1,0:T(8,128)(2,1)} %all-gather.2.cloned.1.call-done.pool), custom_call_target="tpu_custom_call" | custom-call | bytes 1048576 | tf_op jit(solution)/shard_map/pick_pages/pallas_call | solution.py:150
  67.2 0.0 copy-start.4
  67.2 4.7 %collective-permute-done.10 = bf16[8,64,256]{2,1,0:T(8,128)(2,1)} collective-permute-done((bf16[8,64,256]{2,1,0:T(8,128)(2,1)}, bf16[8,64,256]{2,1,0:T(8,128)(2,1)}, u32[]{:S(2)}, u32[]{:S(2)}) %collective-permute-start.10) | collective-permute-done | bytes 262176 | tf_op jit(solution)/shard_map/ppermute | solution.py:427
  71.9 1.0 broadcast_select_fusion.v_mine
  72.9 1.6 %collective-permute-start.11 = (bf16[8,64,256]{2,1,0:T(8,128)(2,1)S(1)}, bf16[8,64,256]{2,1,0:T(8,128)(2,1)S(1)}, u32[]{:S(2)}, u32[]{:S(2)}) collective-permute-start(bf16[8,64,256]{2,1,0:T(8,128)(2,1)S(1)} %broadcast_select_fusion.v_mine), channel_id=1, source_target_pairs={{0,1},{1,0},{2,3},{3,2},{4,5},{5,4},{6,7},{7,6},{8,9},{9,8},{10,11... | collective-permute-start | bytes 786440 | tf_op jit(solution)/shard_map/ppermute | solution.py:433
  74.5 0.0 collective-permute-done.8.peer
  74.5 1.4 %collective-permute-done.7 = bf16[8,64,256]{2,1,0:T(8,128)(2,1)S(1)} collective-permute-done((bf16[8,64,256]{2,1,0:T(8,128)(2,1)}, bf16[8,64,256]{2,1,0:T(8,128)(2,1)S(1)}, u32[]{:S(2)}, u32[]{:S(2)}) %collective-permute-start.7) | collective-permute-done | bytes 262176 | tf_op jit(solution)/shard_map/ppermute | solution.py:426
  75.8 1.0 broadcast_select_fusion.1.k_mine
  76.8 1.5 %collective-permute-start.9 = (bf16[8,64,256]{2,1,0:T(8,128)(2,1)S(1)}, bf16[8,64,256]{2,1,0:T(8,128)(2,1)S(1)}, u32[]{:S(2)}, u32[]{:S(2)}) collective-permute-start(bf16[8,64,256]{2,1,0:T(8,128)(2,1)S(1)} %broadcast_select_fusion.1.k_mine), channel_id=1, source_target_pairs={{0,1},{1,0},{2,3},{3,2},{4,5},{5,4},{6,7},{7,6},{8,9},{9,8},{10,11... | collective-permute-start | bytes 786440 | tf_op jit(solution)/shard_map/ppermute | solution.py:431
  79.0 0.1 pad_add_fusion.info
  79.1 1.1 %copy-done.6 = bf16[512,768]{1,0:T(8,128)(2,1)S(1)} copy-done((bf16[512,768]{1,0:T(8,128)(2,1)S(1)}, bf16[512,768]{1,0:T(8,128)(2,1)}, u32[]{:S(2)}) %copy-start.6) | copy-done | bytes 786456
  80.2 2.4 %hold.1 = (bf16[512,768]{1,0:T(8,128)(2,1)S(1)}, bf16[512,768]{1,0:T(8,128)(2,1)S(1)}, bf16[512,512]{1,0:T(8,128)(2,1)S(1)}, bf16[512,512]{1,0:T(8,128)(2,1)S(1)...) custom-call(s32[3]{0:T(128)S(1)} %pad_add_fusion.info, bf16[512,768]{1,0:T(8,128)(2,1)S(1)} %copy-done.6, ...), custom_call_target="tpu_custom_call" | custom-call | bytes 8388608 | tf_op jit(solution)/shard_map/hold/pallas_call | solution.py:183
  82.6 0.0 collective-permute-done.11.v_peer
  82.6 2.3 %collective-permute-done.9.k_peer = bf16[8,64,256]{2,1,0:T(8,128)(2,1)S(1)} collective-permute-done((bf16[8,64,256]{2,1,0:T(8,128)(2,1)S(1)}, bf16[8,64,256]{2,1,0:T(8,128)(2,1)S(1)}, u32[]{:S(2)}, u32[]{:S(2)}) %collective-permute-start.9) | collective-permute-done | bytes 262176 | tf_op jit(solution)/shard_map/ppermute | solution.py:431
  84.9 11.9 %attend_and_out.1 = bf16[512,1536]{1,0:T(8,128)(2,1)} custom-call(s32[3]{0:T(128)S(1)} %pad_add_fusion.info, bf16[512,768]{1,0:T(8,128)(2,1)S(1)} %get-tuple-element.60.qa, bf16[512,768]{1,0:T(8,128)(2,1)S(1)} %get-tuple-element.61.qb, bf16[8,64,256]{2,1,0:T(8,128)(2,1)S(1)} %broadcast_select_fusion.1.k_mine, ...), custom_call_target="tpu_custom_call" | custom-call | flops 6442450944 | bytes 12582912 | tf_op jit(solution)/shard_map/attend_and_out/pallas_call | solution.py:352
  (23 shorter events, 0.1 us)
Async XLA Ops:
  6.5 5.5 %copy-start.18 = (f32[1536]{0:T(1024)S(1)}, f32[1536]{0:T(1024)}, u32[]{:S(2)}) copy-start(f32[1536]{0:T(1024)} %param.10) | copy-start | bytes 18436
  6.5 53.1 %all-gather.2.cloned.1.call-start = ((), (), s32[]{:S(2)}) async-start(), calls=%async_computation | async-start | bytes 4718592 | tf_op jit(solution)/shard_map/all_gather | solution.py:392
  8.4 16.4 %collective-permute-start = (bf16[384,768]{1,0:T(8,128)(2,1)S(1)}, bf16[384,768]{1,0:T(8,128)(2,1)S(1)}, u32[]{:S(2)}, u32[]{:S(2)}) collective-permute-start(bf16[384,768]{1,0:T(8,128)(2,1)S(1)} %constant_dynamic-slice_fusion.1), channel_id=1, source_target_pairs={{0,1},{1,0},{2,3},{3,2},{4,5},{5,4},{6,7},{7,6},{8,9},{9,8},{10,11... | collective-permute-start | bytes 1769480 | tf_op jit(solution)/shard_map/ppermute | solution.py:396
  12.5 1.7 %copy-start.15 = (bf16[1536,768]{1,0:T(8,128)(2,1)S(1)}, bf16[1536,768]{1,0:T(8,128)(2,1)}, u32[]{:S(2)}) copy-start(bf16[1536,768]{1,0:T(8,128)(2,1)} %wq.1) | copy-start | bytes 7077892
  14.2 1.4 %copy-start.16 = (bf16[1,512,1536]{2,1,0:T(8,128)(2,1)S(1)}, bf16[1,512,1536]{2,1,0:T(8,128)(2,1)}, u32[]{:S(2)}) copy-start(bf16[1,512,1536]{2,1,0:T(8,128)(2,1)} %param.9) | copy-start | bytes 4718596
  15.6 1.4 %copy-start.17 = (bf16[1536,512]{1,0:T(8,128)(2,1)S(1)}, bf16[1536,512]{1,0:T(8,128)(2,1)}, u32[]{:S(2)}) copy-start(bf16[1536,512]{1,0:T(8,128)(2,1)} %wkv.1) | copy-start | bytes 4718596
  17.0 9.5 %copy-start = (bf16[768,1536]{1,0:T(8,128)(2,1)S(1)}, bf16[768,1536]{1,0:T(8,128)(2,1)}, u32[]{:S(2)}) copy-start(bf16[768,1536]{1,0:T(8,128)(2,1)} %woa.1) | copy-start | bytes 7077892
  20.0 1.1 %copy-start.1 = (bf16[512,1536]{1,0:T(8,128)(2,1)}, bf16[512,1536]{1,0:T(8,128)(2,1)S(1)}, u32[]{:S(2)}) copy-start(bf16[512,1536]{1,0:T(8,128)(2,1)S(1)} %get-tuple-element.40.normed) | copy-start | bytes 4718596
  21.2 0.9 copy-start.5
  22.0 17.3 %copy-start.11 = (f32[512,256]{1,0:T(8,128)}, f32[512,256]{1,0:T(8,128)S(1)}, u32[]{:S(2)}) copy-start(f32[512,256]{1,0:T(8,128)S(1)} %get-tuple-element.42.cos) | copy-start | bytes 1572868
  22.0 17.3 %copy-start.13 = (f32[512,256]{1,0:T(8,128)}, f32[512,256]{1,0:T(8,128)S(1)}, u32[]{:S(2)}) copy-start(f32[512,256]{1,0:T(8,128)S(1)} %get-tuple-element.43.sin) | copy-start | bytes 1572868
  24.8 16.8 %copy-start.7 = (bf16[384,768]{1,0:T(8,128)(2,1)}, bf16[384,768]{1,0:T(8,128)(2,1)S(1)}, u32[]{:S(2)}) copy-start(bf16[384,768]{1,0:T(8,128)(2,1)S(1)} %collective-permute-done.w0) | copy-start | bytes 1769476
  24.8 14.6 %collective-permute-start.2 = (bf16[384,768]{1,0:T(8,128)(2,1)S(1)}, bf16[384,768]{1,0:T(8,128)(2,1)S(1)}, u32[]{:S(2)}, u32[]{:S(2)}) collective-permute-start(bf16[384,768]{1,0:T(8,128)(2,1)S(1)} %collective-permute-done.w0), channel_id=1, source_target_pairs={{0,16},{16,0},{1,17},{17,1},{2,18},{18,2},{3,19},{19,3},{4,20},{20... | collective-permute-start | bytes 1769480 | tf_op jit(solution)/shard_map/ppermute | solution.py:406
  27.6 27.0 %collective-permute-start.1 = (bf16[384,1536]{1,0:T(8,128)(2,1)}, bf16[384,1536]{1,0:T(8,128)(2,1)}, u32[]{:S(2)}, u32[]{:S(2)}) collective-permute-start(bf16[384,1536]{1,0:T(8,128)(2,1)} %constant_dynamic-slice_fusion), channel_id=1, source_target_pairs={{0,1},{1,0},{2,3},{3,2},{4,5},{5,4},{6,7},{7,6},{8,9},{9,8},{10,11... | collective-permute-start | bytes 3538952 | tf_op jit(solution)/shard_map/ppermute | solution.py:396
  29.1 11.2 %collective-permute-start.3 = (bf16[384,768]{1,0:T(8,128)(2,1)S(1)}, bf16[384,768]{1,0:T(8,128)(2,1)}, u32[]{:S(2)}, u32[]{:S(2)}) collective-permute-start(bf16[384,768]{1,0:T(8,128)(2,1)S(1)} %collective-permute-done.w0), channel_id=1, source_target_pairs={{0,2},{2,0},{4,6},{6,4},{8,10},{10,8},{12,14},{14,12},{1,3},{3,1},... | collective-permute-start | bytes 1769480 | tf_op jit(solution)/shard_map/ppermute | solution.py:410
  39.4 2.1 %collective-permute-start.4 = (bf16[384,768]{1,0:T(8,128)(2,1)S(1)}, bf16[384,768]{1,0:T(8,128)(2,1)}, u32[]{:S(2)}, u32[]{:S(2)}) collective-permute-start(bf16[384,768]{1,0:T(8,128)(2,1)S(1)} %collective-permute-done.2.w1), channel_id=1, source_target_pairs={{0,2},{2,0},{4,6},{6,4},{8,10},{10,8},{12,14},{14,12},{1,3},{3,1},... | collective-permute-start | bytes 1769480 | tf_op jit(solution)/shard_map/ppermute | solution.py:410
  39.4 0.8 copy-start.9
  41.5 1.5 %copy-start.2 = (bf16[512,1536]{1,0:T(8,128)(2,1)S(1)}, bf16[512,1536]{1,0:T(8,128)(2,1)}, u32[]{:S(2)}) copy-start(bf16[512,1536]{1,0:T(8,128)(2,1)} %copy-done.1) | copy-start | bytes 4718596
  43.0 1.1 %copy-start.8 = (bf16[384,768]{1,0:T(8,128)(2,1)S(1)}, bf16[384,768]{1,0:T(8,128)(2,1)}, u32[]{:S(2)}) copy-start(bf16[384,768]{1,0:T(8,128)(2,1)} %copy-done.7) | copy-start | bytes 1769476
  44.0 1.1 %copy-start.10 = (bf16[384,768]{1,0:T(8,128)(2,1)S(1)}, bf16[384,768]{1,0:T(8,128)(2,1)}, u32[]{:S(2)}) copy-start(bf16[384,768]{1,0:T(8,128)(2,1)} %copy-done.9) | copy-start | bytes 1769476
  45.1 1.0 %copy-start.12 = (f32[512,256]{1,0:T(8,128)S(1)}, f32[512,256]{1,0:T(8,128)}, u32[]{:S(2)}) copy-start(f32[512,256]{1,0:T(8,128)} %copy-done.11) | copy-start | bytes 1572868
  46.1 1.0 %copy-start.14 = (f32[512,256]{1,0:T(8,128)S(1)}, f32[512,256]{1,0:T(8,128)}, u32[]{:S(2)}) copy-start(f32[512,256]{1,0:T(8,128)} %copy-done.13) | copy-start | bytes 1572868
  47.2 7.4 %copy-start.19 = (s32[1,8]{1,0:T(1,128)S(1)}, s32[1,8]{1,0:T(1,128)}, u32[]{:S(2)}) copy-start(s32[1,8]{1,0:T(1,128)} %param.15) | copy-start | bytes 100
  54.6 4.1 %collective-permute-start.5 = (bf16[384,1536]{1,0:T(8,128)(2,1)}, bf16[384,1536]{1,0:T(8,128)(2,1)S(1)}, u32[]{:S(2)}, u32[]{:S(2)}) collective-permute-start(bf16[384,1536]{1,0:T(8,128)(2,1)} %collective-permute-done.1.wob0), channel_id=1, source_target_pairs={{0,2},{2,0},{4,6},{6,4},{8,10},{10,8},{12,14},{14,12},{1,3},{3,1},... | collective-permute-start | bytes 3538952 | tf_op jit(solution)/shard_map/ppermute | solution.py:416
  54.6 3.5 %collective-permute-start.6 = (s32[8]{0:T(128)S(1)}, s32[8]{0:T(128)S(1)}, u32[]{:S(2)}, u32[]{:S(2)}) collective-permute-start(s32[8]{0:T(128)S(1)} %bitcast.15), channel_id=1, source_target_pairs={{0,16},{16,0},{1,17},{17,1},{2,18},{18,2},{3,19},{19,3},{4,20},{20... | collective-permute-start | bytes 104 | tf_op jit(solution)/shard_map/ppermute | solution.py:409
  55.7 18.7 %collective-permute-start.8 = (bf16[512,512]{1,0:T(8,128)(2,1)}, bf16[512,512]{1,0:T(8,128)(2,1)}, u32[]{:S(2)}, u32[]{:S(2)}) collective-permute-start(bf16[512,512]{1,0:T(8,128)(2,1)} %get-tuple-element.49.own), channel_id=1, source_target_pairs={{0,1},{1,0},{2,3},{3,2},{4,5},{5,4},{6,7},{7,6},{8,9},{9,8},{10,11... | collective-permute-start | bytes 1572872 | tf_op jit(solution)/shard_map/ppermute | solution.py:417
  58.6 1.0 copy-start.3
  62.3 9.6 %collective-permute-start.10 = (bf16[8,64,256]{2,1,0:T(8,128)(2,1)}, bf16[8,64,256]{2,1,0:T(8,128)(2,1)}, u32[]{:S(2)}, u32[]{:S(2)}) collective-permute-start(bf16[8,64,256]{2,1,0:T(8,128)(2,1)} %get-tuple-element.64), channel_id=1, source_target_pairs={{0,16},{16,0},{1,17},{17,1},{2,18},{18,2},{3,19},{19,3},{4,20},{20... | collective-permute-start | bytes 786440 | tf_op jit(solution)/shard_map/ppermute | solution.py:427
  63.0 12.8 %collective-permute-start.7 = (bf16[8,64,256]{2,1,0:T(8,128)(2,1)}, bf16[8,64,256]{2,1,0:T(8,128)(2,1)S(1)}, u32[]{:S(2)}, u32[]{:S(2)}) collective-permute-start(bf16[8,64,256]{2,1,0:T(8,128)(2,1)} %get-tuple-element.48), channel_id=1, source_target_pairs={{0,16},{16,0},{1,17},{17,1},{2,18},{18,2},{3,19},{19,3},{4,20},{20... | collective-permute-start | bytes 786440 | tf_op jit(solution)/shard_map/ppermute | solution.py:426
  67.2 11.9 %copy-start.4 = (bf16[384,1536]{1,0:T(8,128)(2,1)S(1)}, bf16[384,1536]{1,0:T(8,128)(2,1)}, u32[]{:S(2)}) copy-start(bf16[384,1536]{1,0:T(8,128)(2,1)} %copy-done.3) | copy-start | bytes 3538948
  72.9 9.8 %collective-permute-start.11 = (bf16[8,64,256]{2,1,0:T(8,128)(2,1)S(1)}, bf16[8,64,256]{2,1,0:T(8,128)(2,1)S(1)}, u32[]{:S(2)}, u32[]{:S(2)}) collective-permute-start(bf16[8,64,256]{2,1,0:T(8,128)(2,1)S(1)} %broadcast_select_fusion.v_mine), channel_id=1, source_target_pairs={{0,1},{1,0},{2,3},{3,2},{4,5},{5,4},{6,7},{7,6},{8,9},{9,8},{10,11... | collective-permute-start | bytes 786440 | tf_op jit(solution)/shard_map/ppermute | solution.py:433
  76.8 8.1 %collective-permute-start.9 = (bf16[8,64,256]{2,1,0:T(8,128)(2,1)S(1)}, bf16[8,64,256]{2,1,0:T(8,128)(2,1)S(1)}, u32[]{:S(2)}, u32[]{:S(2)}) collective-permute-start(bf16[8,64,256]{2,1,0:T(8,128)(2,1)S(1)} %broadcast_select_fusion.1.k_mine), channel_id=1, source_target_pairs={{0,1},{1,0},{2,3},{3,2},{4,5},{5,4},{6,7},{7,6},{8,9},{9,8},{10,11... | collective-permute-start | bytes 786440 | tf_op jit(solution)/shard_map/ppermute | solution.py:431
  79.1 1.1 %copy-start.6 = (bf16[512,768]{1,0:T(8,128)(2,1)S(1)}, bf16[512,768]{1,0:T(8,128)(2,1)}, u32[]{:S(2)}) copy-start(bf16[512,768]{1,0:T(8,128)(2,1)} %copy-done.5) | copy-start | bytes 2359300
Sparse Core Ops, SparseCore 0:
  9.0 49.8 all-gather.1
